TPU v7x, 32 devices: a whole 2x2x4 slice. The times are simulated.
32 devices in a mesh: grp: 8 (over y, x, core), tp: 4 (over z).
Axes of the slice: x: 2, y: 2, z: 4, core: 2. Of those that a mesh axis runs over, the one named last changes fastest.
Arguments:
- comp_queries: bfloat16 [2048, 8192], P('grp', 'tp'), may hold values from -6 to 6
- comp_keys: bfloat16 [2048, 1024], P('grp', 'tp'), may hold values from -6 to 6
- comp_values: bfloat16 [2048, 1024], P('grp', 'tp'), may hold values from -6 to 6
- prompt_keys: bfloat16 [768, 1024], P('grp', 'tp'), may hold values from -6 to 6
- prompt_values: bfloat16 [768, 1024], P('grp', 'tp'), may hold values from -6 to 6
- query_gain: float32 [128], replicated, may hold values from 0.5 to 6
- key_gain: float32 [128], replicated, may hold values from 0.5 to 6
- out_grad: bfloat16 [2048, 8192], P('grp', 'tp'), may hold values from -18 to 18
- live_counts: int32 [8], P('grp'), may hold values from 1 to 4, as said below
- slot_prompts: int32 [32], P('grp'), may hold values from 0 to 1, as said below
Outputs:
- attended: bfloat16 [2048, 8192], P('grp', 'tp')
- query_grads: bfloat16 [2048, 8192], P('grp', 'tp')
- comp_key_grads: bfloat16 [2048, 1024], P('grp', 'tp')
- comp_value_grads: bfloat16 [2048, 1024], P('grp', 'tp')
- prompt_key_grads: float32 [768, 1024], P('grp', 'tp')
- prompt_value_grads: float32 [768, 1024], P('grp', 'tp')
- query_gain_grad: float32 [128], replicated
- key_gain_grad: float32 [128], replicated
Inputs may be any that keep to these rules, and one draw needn't show every extreme that they name: Slot j of index s of grp is live exactly when j < live_counts[s]; some index has all 4 live and some has one. `slot_prompts`: the first slot of every index of grp is live; every prompt is named by some first slot.
All inputs are finite; a program needn't handle non-finite values.
Results may differ from a plain program's by a relative error of at most 0.033.
The roundings to bfloat16 on the way count: a program that leaves them out, or rounds other values in their place, can miss the bound.
Values may be sent and summed in bfloat16 or wider, within the bound.
No kernel may reach another device: no remote copies, remote signals or barrier semaphores. Data moves between devices by JAX's collectives and lax.ppermute only.
A program may use at most 64 MiB of HBM per device.

v0:
```python
import math

import jax
import jax.numpy as jnp
from jax import lax
from jax.experimental import pallas as pl
from jax.experimental.pallas import tpu as pltpu
from jax.sharding import PartitionSpec as P

PL = 384
CL = 64
EPS = 1e-06
TAIL = 16
VMEM_LIMIT = 48 * 1024 * 1024
F32 = jnp.float32
BF16 = jnp.bfloat16


def dot(left, right):
    return jnp.dot(left, right, preferred_element_type=F32)


def dot_nt(left, right):
    return lax.dot_general(left, right, (((1,), (1,)), ((), ())), preferred_element_type=F32)


def unit(raw):
    recip = lax.rsqrt(jnp.mean(raw * raw, axis=-1, keepdims=True) + EPS)
    return raw * recip, recip


def norm_back(upstream, unit_rows, recip, gain):
    scaled = upstream * gain
    return recip * (scaled - unit_rows * jnp.mean(unit_rows * scaled, axis=-1, keepdims=True))


def attention_kernel(
    live_ref, prompt_ref,
    q_ref, do_ref, ck_ref, cv_ref, pool_ref, qg_ref, kg_ref,
    att_ref, dq_ref, dk_ref, dv_ref, send_ref,
    acc, pool_unit, pool_keys, pool_keys_t, pool_values_t, qgain_col, qpart, kpart,
):
    slot = pl.program_id(0)
    size = qg_ref.shape[1]
    heads = ck_ref.shape[1] // size
    width = heads * size
    group = q_ref.shape[1] // width
    score_scale = 1.0 / math.sqrt(size)
    chunk_heads = min(group, 4)
    chunk = chunk_heads * CL

    @pl.when(slot == 0)
    def _():
        qgain_col[...] = jnp.broadcast_to(qg_ref[...], (size, size)).T
        qpart[...] = jnp.zeros_like(qpart)
        kpart[...] = jnp.zeros_like(kpart)
        acc[...] = jnp.zeros_like(acc)
        for head in range(heads):
            columns = slice(head * size, (head + 1) * size)
            unit_rows, _ = unit(pool_ref[:, columns].astype(F32))
            pool_unit[:, columns] = unit_rows
            keys = (unit_rows * kg_ref[...]).astype(BF16)
            pool_keys[:, columns] = keys
            pool_keys_t[columns, :] = keys.T
            pool_values_t[columns, :] = pool_ref[:, width + head * size:width + (head + 1) * size].T

    alive = slot < live_ref[0]

    @pl.when(jnp.logical_not(alive))
    def _():
        for ref in (att_ref, dq_ref, dk_ref, dv_ref):
            ref[...] = jnp.zeros_like(ref)

    @pl.when(alive)
    def _():
        first = pl.multiple_of(prompt_ref[slot] * PL, PL)
        rows = pl.ds(first, PL)
        gain_col = jnp.concatenate([qgain_col[...]] * (chunk // size), axis=1)

        def load_head(head):
            columns = slice(head * size, (head + 1) * size)
            own_unit, own_recip = unit(ck_ref[:, columns].astype(F32))
            own_keys = (own_unit * kg_ref[...]).astype(BF16)
            own_values = cv_ref[:, columns]
            keys = jnp.concatenate([pool_keys[rows, columns], own_keys], axis=0)
            values = jnp.concatenate(
                [pool_ref[rows, width + head * size:width + (head + 1) * size], own_values], axis=0
            )
            keys_t = jnp.concatenate([pool_keys_t[columns, rows], own_keys.T], axis=1)
            values_t = jnp.concatenate([pool_values_t[columns, rows], own_values.T], axis=1)
            values_t = jnp.concatenate([values_t, jnp.ones((16, PL + CL), BF16)], axis=0)
            return own_unit, own_recip, keys, values, keys_t, values_t

        def places(head, at):
            start = (head * group + at * chunk_heads) * size
            return [slice(start + g * size, start + (g + 1) * size) for g in range(chunk_heads)]

        def stack(ref, where):
            return jnp.concatenate([ref[:, place] for place in where], axis=0)

        def unstack(ref, where, values):
            for g, place in enumerate(where):
                ref[:, place] = values[g * CL:(g + 1) * CL]

        def begin(state):
            raw_t = stack(q_ref, state["where"]).T.astype(F32)
            state["recip"] = lax.rsqrt(jnp.mean(raw_t * raw_t, axis=0, keepdims=True) + EPS)
            state["unit"] = raw_t * state["recip"]
            state["queries"] = (state["unit"] * gain_col).astype(BF16)
            state["scores"] = dot(state["head"][2], state["queries"])

        def weigh(state):
            scores = state.pop("scores")
            own = scores[PL:]
            key_no = lax.broadcasted_iota(jnp.int32, own.shape, 0)
            token_no = lax.broadcasted_iota(jnp.int32, own.shape, 1) % CL
            own = jnp.where(key_no <= token_no, own, -jnp.inf)
            scores = jnp.concatenate([scores[:PL], own], axis=0)
            high = jnp.max(scores, axis=0, keepdims=True)
            state["weights"] = jnp.exp2((scores - high) * (score_scale * math.log2(math.e)))
            state["half"] = state["weights"].astype(BF16)
            state["summed"] = dot(state["head"][5], state["half"])

        def attend(state):
            summed = state.pop("summed")
            inverse = 1.0 / summed[size:size + 1]
            attended = (summed[:size] * inverse).astype(BF16)
            unstack(att_ref, state["where"], attended.T)
            grads = (stack(do_ref, state["where"]).T.astype(F32) * inverse).astype(BF16)
            state["grads"] = grads
            state["delta"] = jnp.sum(grads.astype(F32) * attended.astype(F32), axis=0, keepdims=True)
            state["prob_grad"] = dot(state["head"][3], grads)

        def back(state):
            state["value_grad"] = dot_nt(state.pop("half"), state.pop("grads"))
            score_grad = (state.pop("weights") * (state.pop("prob_grad") - state.pop("delta"))).astype(BF16)
            state["query_grad"] = dot(state["head"][4], score_grad)
            state["key_grad"] = dot_nt(score_grad, state.pop("queries"))

        def end(state):
            query_grad = state.pop("query_grad") * score_scale
            query_unit = state.pop("unit")
            part = query_grad * query_unit
            for at in range(0, chunk, size):
                qpart[...] += part[:, at:at + size]
            mean = jnp.mean(part * gain_col, axis=0, keepdims=True)
            query_out = state.pop("recip") * (query_grad * gain_col - query_unit * mean)
            unstack(dq_ref, state["where"], query_out.astype(BF16).T)

        loaded = [load_head(head) for head in range(heads)]
        states = [
            {"head": loaded[head], "where": places(head, at)}
            for head in range(heads)
            for at in range(group // chunk_heads)
        ]
        stages = (begin, weigh, attend, back, end)
        for tick in range(len(states) + len(stages) - 1):
            for number in range(len(stages)):
                if 0 <= tick - number < len(states):
                    stages[number](states[tick - number])

        per_head = group // chunk_heads
        for head in range(heads):
            own_unit, own_recip = loaded[head][:2]
            mine = states[head * per_head:(head + 1) * per_head]
            key_grad = sum(state["key_grad"] for state in mine) * score_scale
            value_grad = sum(state["value_grad"] for state in mine)
            start = 2 * head * size
            acc[rows, start:start + size] += key_grad[:PL]
            acc[rows, start + size:start + 2 * size] += value_grad[:PL]
            own_grad = key_grad[PL:]
            kpart[...] += jnp.sum(own_grad * own_unit, axis=0, keepdims=True)
            columns = slice(head * size, (head + 1) * size)
            dk_ref[:, columns] = norm_back(own_grad, own_unit, own_recip, kg_ref[...]).astype(BF16)
            dv_ref[:, columns] = value_grad[PL:].astype(BF16)

    @pl.when(slot == pl.num_programs(0) - 1)
    def _():
        key_part = kpart[...]
        for head in range(heads):
            terms = acc[:, 2 * head * size:(2 * head + 1) * size] * pool_unit[:, head * size:(head + 1) * size]
            key_part = key_part + jnp.sum(terms, axis=0, keepdims=True)
        query_part = jnp.sum(qpart[...].T, axis=0, keepdims=True)
        tail = []
        for part in (query_part, key_part):
            upper = part.astype(BF16).astype(F32)
            tail += [upper, part - upper]
        row = jnp.concatenate(tail + [jnp.zeros((1, 2 * width - 4 * size), F32)] * (2 * width > 4 * size), axis=1)
        row = jnp.broadcast_to(row, (TAIL, 2 * width))
        row = jnp.where(lax.broadcasted_iota(jnp.int32, row.shape, 0) == 0, row, 0.0).astype(BF16)
        blocks = send_ref.shape[0]
        shard = (send_ref.shape[1] - TAIL) if blocks > 1 else acc.shape[0]
        for at in range(blocks):
            send_ref[at, :shard, :] = acc[at * shard:(at + 1) * shard, :].astype(BF16)
            send_ref[at, shard:, :] = row


def attention(live_counts, slot_prompts, queries, out_grad, keys, values, pool, query_gain, key_gain, blocks):
    size = query_gain.shape[0]
    slots = slot_prompts.shape[0]
    width = keys.shape[1]
    pool_rows = pool.shape[0]
    smem = pl.BlockSpec(memory_space=pltpu.SMEM)
    token = pl.BlockSpec((CL, queries.shape[1]), lambda j: (j, 0))
    own = pl.BlockSpec((CL, width), lambda j: (j, 0))
    gain = pl.BlockSpec((1, size), lambda j: (0, 0))
    send = (blocks, pool_rows // blocks + TAIL, 2 * width)
    return pl.pallas_call(
        attention_kernel,
        grid=(slots,),
        in_specs=[smem, smem, token, token, own, own, pl.BlockSpec(pool.shape, lambda j: (0, 0)), gain, gain],
        out_specs=[token, token, own, own, pl.BlockSpec(send, lambda j: (0, 0, 0))],
        out_shape=[
            jax.ShapeDtypeStruct(queries.shape, BF16),
            jax.ShapeDtypeStruct(queries.shape, BF16),
            jax.ShapeDtypeStruct(keys.shape, BF16),
            jax.ShapeDtypeStruct(keys.shape, BF16),
            jax.ShapeDtypeStruct(send, BF16),
        ],
        scratch_shapes=[
            pltpu.VMEM((pool_rows, 2 * width), F32),
            pltpu.VMEM((pool_rows, width), F32),
            pltpu.VMEM((pool_rows, width), BF16),
            pltpu.VMEM((width, pool_rows), BF16),
            pltpu.VMEM((width, pool_rows), BF16),
            pltpu.VMEM((size, size), F32),
            pltpu.VMEM((size, size), F32),
            pltpu.VMEM((1, size), F32),
        ],
        compiler_params=pltpu.CompilerParams(vmem_limit_bytes=VMEM_LIMIT),
        name="attention",
    )(
        live_counts, slot_prompts, queries, out_grad, keys, values, pool,
        query_gain.reshape(1, size), key_gain.reshape(1, size),
    )


def finish_kernel(parts_ref, raw_ref, kg_ref, key_ref, value_ref):
    size = kg_ref.shape[1]
    shard = raw_ref.shape[0]
    total = parts_ref[0, :shard, :].astype(F32)
    for at in range(1, parts_ref.shape[0]):
        total = total + parts_ref[at, :shard, :].astype(F32)
    for head in range(raw_ref.shape[1] // size):
        columns = slice(head * size, (head + 1) * size)
        unit_rows, recip = unit(raw_ref[:, columns].astype(F32))
        at = 2 * head * size
        key_ref[:, columns] = norm_back(total[:, at:at + size], unit_rows, recip, kg_ref[...])
        value_ref[:, columns] = total[:, at + size:at + 2 * size]


def finish(parts, raw, key_gain):
    shape = jax.ShapeDtypeStruct(raw.shape, F32)
    return pl.pallas_call(
        finish_kernel,
        out_shape=[shape, shape],
        compiler_params=pltpu.CompilerParams(vmem_limit_bytes=VMEM_LIMIT),
        cost_estimate=pl.CostEstimate(flops=20 * raw.size, bytes_accessed=2 * parts.size, transcendentals=0),
        name="finish",
    )(parts, raw, key_gain.reshape(1, -1))


def sum_over(values, axis):
    count = lax.axis_size(axis)
    terms = [values] + [
        lax.ppermute(values, axis, [(i, i ^ step) for i in range(count)]) for step in range(1, count)
    ]
    while len(terms) > 1:
        terms = [left + right for left, right in zip(terms[::2], terms[1::2])]
    return terms[0]


def local(
    comp_queries, comp_keys, comp_values, prompt_keys, prompt_values,
    query_gain, key_gain, out_grad, live_counts, slot_prompts,
):
    grp = lax.axis_size("grp")
    shard, width = prompt_keys.shape
    size = query_gain.shape[0]
    mine = jnp.concatenate([prompt_keys, prompt_values], axis=1)
    copies = jnp.broadcast_to(mine, (grp,) + mine.shape)
    pool = lax.all_to_all(copies, "grp", 0, 0, tiled=True).reshape(grp * shard, 2 * width)
    blocks = grp if shard % TAIL == 0 else 1
    attended, query_grads, key_grads, value_grads, send = attention(
        live_counts, slot_prompts, comp_queries, out_grad, comp_keys, comp_values, pool,
        query_gain, key_gain, blocks,
    )
    if blocks == 1:
        tail = jnp.broadcast_to(send[:, grp * shard:], (grp, TAIL, 2 * width))
        send = jnp.concatenate([send[0, :grp * shard].reshape(grp, shard, 2 * width), tail], axis=1)
    parts = lax.all_to_all(send, "grp", 0, 0, tiled=True)
    gains = jnp.sum(parts[:, shard, :4 * size].astype(F32).reshape(grp, 2, 2, size), axis=(0, 2))
    gains = sum_over(gains, "tp")
    prompt_key_grads, prompt_value_grads = finish(parts, prompt_keys, key_gain)
    return (
        attended, query_grads, key_grads, value_grads,
        prompt_key_grads, prompt_value_grads, gains[0], gains[1],
    )


def solution(mesh):
    split, whole = P("grp", "tp"), P()
    return jax.shard_map(
        local,
        mesh=mesh,
        in_specs=(split, split, split, split, split, whole, whole, split, P("grp"), P("grp")),
        out_specs=(split, split, split, split, split, split, whole, whole),
        check_vma=False,
    )
```

profile of v0, /device:TPU:0, one launch (start us, length us, event | category | flops | bytes accessed | tf_op | source)
XLA Modules:
  0.0 56.5 jit_solution(6415838351341358924)
XLA Ops:
  0.6 0.8 %pad_maximum_fusion = bf16[96,512]{1,0:T(8,128)(2,1)S(1)} fusion(bf16[96,256]{1,0:T(8,128)(2,1)} %param.14, bf16[96,256]{1,0:T(8,128)(2,1)} %raw_ref.1), kind=kLoop, calls=%fused_computation | loop fusion | flops 196608 | bytes 196608 | tf_op jit(solution)/shard_map/concatenate | solution.py:280
  1.5 0.0 copy-start
  1.5 0.0 copy-start.1
  1.5 0.9 %broadcast_in_dim.3 = bf16[8,96,512]{2,1,0:T(8,128)(2,1)} broadcast(bf16[96,512]{1,0:T(8,128)(2,1)S(1)} %pad_maximum_fusion), dimensions={1,2} | broadcast | bytes 884736 | tf_op jit(solution)/shard_map/broadcast_in_dim | solution.py:281
  2.4 0.0 copy-start.3
  2.4 0.0 copy-start.4
  2.4 5.3 %all-to-all-start = ((bf16[8,96,512]{2,1,0:T(8,128)(2,1)}), bf16[8,96,512]{2,1,0:T(8,128)(2,1)S(1)}, u32[]{:S(2)}, u32[]{:S(2)}) async-start(bf16[8,96,512]{2,1,0:T(8,128)(2,1)} %broadcast_in_dim.3), calls=%async_computation | async-start | bytes 1572864 | tf_op jit(solution)/shard_map/all_to_all | solution.py:282
  8.4 12.0 %all-to-all-done = bf16[8,96,512]{2,1,0:T(8,128)(2,1)S(1)} async-done(((bf16[8,96,512]{2,1,0:T(8,128)(2,1)}), bf16[8,96,512]{2,1,0:T(8,128)(2,1)S(1)}, u32[]{:S(2)}, u32[]{:S(2)}) %all-to-all-start) | async-done | bytes 786464 | tf_op jit(solution)/shard_map/all_to_all | solution.py:282
  20.3 0.0 copy-start.5
  20.3 0.0 copy-start.6
  20.3 0.0 copy-start.7
  20.3 0.0 copy-done
  20.3 0.0 copy-done.1
  20.4 0.0 copy-done.3
  20.4 0.0 copy-done.4
  20.4 0.6 %copy-done.5 = f32[128]{0:T(128)S(1)} copy-done((f32[128]{0:T(128)S(1)}, f32[128]{0:T(128)}, u32[]{:S(2)}) %copy-start.5) | copy-done | bytes 536
  21.0 0.0 copy-done.6
  21.0 0.0 copy-done.7
  21.0 7.4 %attention.1 = (bf16[256,2048]{1,0:T(8,128)(2,1)}, bf16[256,2048]{1,0:T(8,128)(2,1)}, bf16[256,256]{1,0:T(8,128)(2,1)}, bf16[256,256]{1,0:T(8,128)(2,1)}, bf16[8,112,512]{2,1,0:T(8,128)(2,1)S(1)}) custom-call(s32[1]{0:T(128)S(6)} %copy.18.live_ref, s32[4]{0:T(128)S(1)} %copy-done.6, bf16[256,2048]{1,0:T(8,128)(2,1)S(1)} %copy-done, ...), custom_call_target="tpu_custom_call" | custom-call | tf_op jit(solution)/shard_map/attention/pallas_call | solution.py:208
  28.4 0.0 copy-start.2
  28.4 19.3 %all_to_all.10.parts_ref = bf16[8,112,512]{2,1,0:T(8,128)(2,1)S(1)} all-to-all(bf16[8,112,512]{2,1,0:T(8,128)(2,1)S(1)} %get-tuple-element.19), channel_id=1, replica_groups=mesh['grp'=8,'tp'=4] {'grp'}, dimensions={0} | all-to-all | bytes 1835008 | tf_op jit(solution)/shard_map/all_to_all | solution.py:291
  47.8 3.7 %collective-permute-start.2 = (f32[2,128]{1,0:T(2,128)S(1)}, f32[2,128]{1,0:T(2,128)S(1)}, u32[]{:S(2)}, u32[]{:S(2)}) collective-permute-start(f32[2,128]{1,0:T(2,128)S(1)} %reduce_sum.18), channel_id=1, source_target_pairs={{0,3},{1,2},{2,1},{3,0},{4,7},{5,6},{6,5},{7,4},{8,11},{9,10},{10,... | collective-permute-start | bytes 3080 | tf_op jit(solution)/shard_map/ppermute | solution.py:266
  51.5 0.0 collective-permute-start.1
  51.5 0.8 %collective-permute-start = (f32[2,128]{1,0:T(2,128)S(1)}, f32[2,128]{1,0:T(2,128)S(1)}, u32[]{:S(2)}, u32[]{:S(2)}) collective-permute-start(f32[2,128]{1,0:T(2,128)S(1)} %reduce_sum.18), channel_id=1, source_target_pairs={{0,1},{1,0},{2,3},{3,2},{4,5},{5,4},{6,7},{7,6},{8,9},{9,8},{10,11... | collective-permute-start | bytes 3080 | tf_op jit(solution)/shard_map/ppermute | solution.py:266
  52.2 0.0 copy-done.2
  52.2 0.9 %finish.1 = (f32[96,256]{1,0:T(8,128)}, f32[96,256]{1,0:T(8,128)}) custom-call(bf16[8,112,512]{2,1,0:T(8,128)(2,1)S(1)} %all_to_all.10.parts_ref, bf16[96,256]{1,0:T(8,128)(2,1)S(1)} %copy-done.2, f32[1,128]{1,0:T(1,128)S(1)} %bitcast.10), custom_call_target="tpu_custom_call" | custom-call | flops 491520 | bytes 917504 | tf_op jit(solution)/shard_map/finish/pallas_call | solution.py:254
  53.1 0.1 collective-permute-done.2
  53.2 2.7 %collective-permute-done.1 = f32[2,128]{1,0:T(2,128)S(1)} collective-permute-done((f32[2,128]{1,0:T(2,128)S(1)}, f32[2,128]{1,0:T(2,128)S(1)}, u32[]{:S(2)}, u32[]{:S(2)}) %collective-permute-start.1) | collective-permute-done | bytes 1056 | tf_op jit(solution)/shard_map/ppermute | solution.py:266
  55.9 0.0 collective-permute-done
  55.9 0.5 slice_bitcast_fusion
  (3 shorter events, 0.1 us)
Async XLA Ops:
  1.5 18.9 %copy-start = (bf16[256,2048]{1,0:T(8,128)(2,1)S(1)}, bf16[256,2048]{1,0:T(8,128)(2,1)}, u32[]{:S(2)}) copy-start(bf16[256,2048]{1,0:T(8,128)(2,1)} %q_ref.1) | copy-start | bytes 3145732
  1.5 18.9 %copy-start.1 = (bf16[256,2048]{1,0:T(8,128)(2,1)S(1)}, bf16[256,2048]{1,0:T(8,128)(2,1)}, u32[]{:S(2)}) copy-start(bf16[256,2048]{1,0:T(8,128)(2,1)} %do_ref.1) | copy-start | bytes 3145732
  2.4 17.9 %copy-start.3 = (bf16[256,256]{1,0:T(8,128)(2,1)S(1)}, bf16[256,256]{1,0:T(8,128)(2,1)}, u32[]{:S(2)}) copy-start(bf16[256,256]{1,0:T(8,128)(2,1)} %ck_ref.1) | copy-start | bytes 393220
  2.4 17.9 %copy-start.4 = (bf16[256,256]{1,0:T(8,128)(2,1)S(1)}, bf16[256,256]{1,0:T(8,128)(2,1)}, u32[]{:S(2)}) copy-start(bf16[256,256]{1,0:T(8,128)(2,1)} %cv_ref.1) | copy-start | bytes 393220
  2.4 17.9 %all-to-all-start = ((bf16[8,96,512]{2,1,0:T(8,128)(2,1)}), bf16[8,96,512]{2,1,0:T(8,128)(2,1)S(1)}, u32[]{:S(2)}, u32[]{:S(2)}) async-start(bf16[8,96,512]{2,1,0:T(8,128)(2,1)} %broadcast_in_dim.3), calls=%async_computation | async-start | bytes 1572864 | tf_op jit(solution)/shard_map/all_to_all | solution.py:282
  20.3 0.7 %copy-start.5 = (f32[128]{0:T(128)S(1)}, f32[128]{0:T(128)}, u32[]{:S(2)}) copy-start(f32[128]{0:T(128)} %param.16) | copy-start | bytes 1540
  20.3 0.7 %copy-start.6 = (s32[4]{0:T(128)S(1)}, s32[4]{0:T(128)}, u32[]{:S(2)}) copy-start(s32[4]{0:T(128)} %prompt_ref.1) | copy-start | bytes 52
  20.3 0.7 %copy-start.7 = (f32[128]{0:T(128)S(1)}, f32[128]{0:T(128)}, u32[]{:S(2)}) copy-start(f32[128]{0:T(128)} %param.15) | copy-start | bytes 1540
  28.4 23.8 %copy-start.2 = (bf16[96,256]{1,0:T(8,128)(2,1)S(1)}, bf16[96,256]{1,0:T(8,128)(2,1)}, u32[]{:S(2)}) copy-start(bf16[96,256]{1,0:T(8,128)(2,1)} %raw_ref.1) | copy-start | bytes 147460
  47.8 5.4 %collective-permute-start.2 = (f32[2,128]{1,0:T(2,128)S(1)}, f32[2,128]{1,0:T(2,128)S(1)}, u32[]{:S(2)}, u32[]{:S(2)}) collective-permute-start(f32[2,128]{1,0:T(2,128)S(1)} %reduce_sum.18), channel_id=1, source_target_pairs={{0,3},{1,2},{2,1},{3,0},{4,7},{5,6},{6,5},{7,4},{8,11},{9,10},{10,... | collective-permute-start | bytes 3080 | tf_op jit(solution)/shard_map/ppermute | solution.py:266
  51.5 4.5 %collective-permute-start.1 = (f32[2,128]{1,0:T(2,128)S(1)}, f32[2,128]{1,0:T(2,128)S(1)}, u32[]{:S(2)}, u32[]{:S(2)}) collective-permute-start(f32[2,128]{1,0:T(2,128)S(1)} %reduce_sum.18), channel_id=1, source_target_pairs={{0,2},{1,3},{2,0},{3,1},{4,6},{5,7},{6,4},{7,5},{8,10},{9,11},{10,... | collective-permute-start | bytes 3080 | tf_op jit(solution)/shard_map/ppermute | solution.py:266
  51.5 4.5 %collective-permute-start = (f32[2,128]{1,0:T(2,128)S(1)}, f32[2,128]{1,0:T(2,128)S(1)}, u32[]{:S(2)}, u32[]{:S(2)}) collective-permute-start(f32[2,128]{1,0:T(2,128)S(1)} %reduce_sum.18), channel_id=1, source_target_pairs={{0,1},{1,0},{2,3},{3,2},{4,5},{5,4},{6,7},{7,6},{8,9},{9,8},{10,11... | collective-permute-start | bytes 3080 | tf_op jit(solution)/shard_map/ppermute | solution.py:266
where the time goes:
time: 56.8 us; the launch traced here: 56.5 us
  blocking collectives  19.3 us (34%)
  waiting for transfers between devices  14.8 us (26%)
  starting transfers between devices  9.75 us (17%)
  Pallas kernels  8.23 us (14%)
  local copies, waits for them, and re-layouts  2.14 us (4%)
  between operations  1.34 us (2%)
  other arithmetic  0.89 us (2%)
    all_to_all x1, blocking collectives, local(): parts = lax.all_to_all(send, 'grp', 0, 0, tiled=True)  19.3 us
    all_to_all x1, waiting for transfers between devices, local(): lax.all_to_all(copies, 'grp', 0, 0, tiled=True)  12 us
    pallas_call x1, Pallas kernels, attention(): pl.pallas_call(attention_kernel, grid=(slots,), in_specs=[smem, smem, tok...  7.38 us
    all_to_all x1, starting transfers between devices, local(): lax.all_to_all(copies, 'grp', 0, 0, tiled=True)  5.3 us
    ppermute x3, starting transfers between devices, sum_over(): lax.ppermute(values, axis, [(i, i ^ step) for i in range(count)])  4.45 us
    ppermute x3, waiting for transfers between devices, sum_over(): lax.ppermute(values, axis, [(i, i ^ step) for i in range(count)])  2.83 us
  transfers between devices with their start and end apart: 4, of which 3 were waited for; matrix products, arithmetic and copies ran while one was open for 0% of the time, Pallas kernels for 2%

commit v1 on v0

v1 whole, which is shorter than its diff:
```python
import functools
import math

import jax
import jax.numpy as jnp
from jax import lax
from jax.experimental import pallas as pl
from jax.experimental.pallas import tpu as pltpu
from jax.sharding import PartitionSpec as P

PL = 384
CL = 64
EPS = 1e-06
TAIL = 16
CHUNK = 256
VMEM_LIMIT = 24 * 1024 * 1024
F32 = jnp.float32
BF16 = jnp.bfloat16
SMEM_SPEC = pl.BlockSpec(memory_space=pltpu.SMEM)
VMEM_SPEC = pl.BlockSpec(memory_space=pltpu.VMEM)
HBM_SPEC = pl.BlockSpec(memory_space=pltpu.HBM)


def dot(left, right):
    return jnp.dot(left, right, preferred_element_type=F32)


def dot_nt(left, right):
    return lax.dot_general(left, right, (((1,), (1,)), ((), ())), preferred_element_type=F32)


def unit(raw):
    recip = lax.rsqrt(jnp.mean(raw * raw, axis=-1, keepdims=True) + EPS)
    return raw * recip, recip


def norm_back(upstream, unit_rows, recip, gain):
    scaled = upstream * gain
    return recip * (scaled - unit_rows * jnp.mean(unit_rows * scaled, axis=-1, keepdims=True))


def halves(row):
    upper = row.astype(BF16)
    return [upper, (row - upper.astype(F32)).astype(BF16)]


def gain_rows(term, wide):
    row = jnp.concatenate([part.astype(F32) for part in halves(term)], axis=1)
    if wide > row.shape[1]:
        row = jnp.concatenate([row, jnp.zeros((1, wide - row.shape[1]), F32)], axis=1)
    rows = jnp.broadcast_to(row, (TAIL, wide))
    return jnp.where(lax.broadcasted_iota(jnp.int32, rows.shape, 0) == 0, rows, 0.0).astype(BF16)


def gain_term(rows, size):
    row = rows.astype(F32)[0:1]
    return row[:, :size] + row[:, size:2 * size]


def params(limit=VMEM_LIMIT):
    return pltpu.CompilerParams(vmem_limit_bytes=limit)


def cost(flops, size):
    return pl.CostEstimate(flops=flops, bytes_accessed=size, transcendentals=0)


def gains_kernel(qg_ref, kg_ref, query_col_ref, key_row_ref):
    size = qg_ref.shape[1]
    column = jnp.broadcast_to(qg_ref[...], (size, size)).T
    for at in range(0, query_col_ref.shape[1], size):
        query_col_ref[:, at:at + size] = column
    key_row_ref[...] = jnp.broadcast_to(kg_ref[...], key_row_ref.shape)


def spread_gains(query_gain, key_gain, lanes):
    size = query_gain.shape[0]
    return pl.pallas_call(
        gains_kernel,
        in_specs=[VMEM_SPEC] * 2,
        out_specs=[VMEM_SPEC] * 2,
        out_shape=[jax.ShapeDtypeStruct((size, lanes), F32), jax.ShapeDtypeStruct((8, size), F32)],
        compiler_params=params(),
        cost_estimate=cost(4 * 10**9, 10**6),
        name="spread_gains",
    )(query_gain.reshape(1, size), key_gain.reshape(1, size))


def pack_kernel(keys_ref, values_ref, kg_ref, out_ref):
    size, width = kg_ref.shape[1], keys_ref.shape[1]
    for head in range(width // size):
        columns = slice(head * size, (head + 1) * size)
        unit_rows, _ = unit(keys_ref[:, columns].astype(F32))
        out_ref[:, columns] = (unit_rows * kg_ref[0:1, :]).astype(BF16)
    out_ref[:, width:] = values_ref[...]


def pack(keys, values, key_row):
    return pl.pallas_call(
        pack_kernel,
        in_specs=[VMEM_SPEC] * 3,
        out_specs=VMEM_SPEC,
        out_shape=jax.ShapeDtypeStruct((keys.shape[0], 2 * keys.shape[1]), BF16),
        compiler_params=params(),
        cost_estimate=cost(4 * 10**9, 10**6),
        name="pack",
    )(keys, values, key_row)


def head_columns(head, group, size):
    return [slice((head * group + g) * size, (head * group + g + 1) * size) for g in range(group)]


def slot_rows(slot):
    return pl.ds(pl.multiple_of(slot * CL, CL), CL)


def prepare_kernel(live_ref, q_ref, do_ref, col_ref, raw_ref, recip_ref, queries_ref, grads_ref):
    size = col_ref.shape[0]
    heads = raw_ref.shape[1] // size
    group = q_ref.shape[1] // raw_ref.shape[1]

    def live(slot, carry):
        for head in range(heads):
            places = head_columns(head, group, size)
            rows = slice(head * size, (head + 1) * size)
            half = jnp.concatenate([q_ref[slot_rows(slot), place] for place in places], axis=0).T
            raw_ref[slot, rows, :] = half
            raw = half.astype(F32)
            recip = lax.rsqrt(jnp.mean(raw * raw, axis=0, keepdims=True) + EPS)
            recip_ref[slot, head:head + 1, :] = recip
            queries_ref[slot, rows, :] = (raw * recip * col_ref[...]).astype(BF16)
            grads_ref[slot, rows, :] = jnp.concatenate([do_ref[slot_rows(slot), place] for place in places], axis=0).T
        return carry

    lax.fori_loop(0, live_ref[0], live, 0)


def prepare(live_counts, queries, out_grad, query_col, slots, width):
    lanes = query_col.shape[1]
    turned = jax.ShapeDtypeStruct((slots, width, lanes), BF16)
    return pl.pallas_call(
        prepare_kernel,
        in_specs=[SMEM_SPEC] + [VMEM_SPEC] * 3,
        out_specs=[VMEM_SPEC] * 4,
        out_shape=[turned, jax.ShapeDtypeStruct((slots, 8, lanes), F32), turned, turned],
        compiler_params=params(),
        cost_estimate=cost(2 * 10**9, 6 * queries.size),
        name="prepare",
    )(live_counts, queries, out_grad, query_col)


def attention_kernel(*refs, parts, heads):
    live_ref, prompt_ref, me_ref, queries_ref, grads_ref, ck_ref, cv_ref, kg_ref = refs[:8]
    pieces, refs = refs[8:8 + parts], refs[8 + parts:]
    att_ref, ds_ref, pool_keys, own_keys_ref, dk_ref, dv_ref, keep_ref, send_ref = refs[:8]
    acc, pool_values, pool_values_t, term = refs[8:]
    size = kg_ref.shape[1]
    width = heads * size
    slots, _, lanes = queries_ref.shape
    per_head = lanes // CHUNK
    score_scale = 1.0 / math.sqrt(size)
    shard = pieces[0].shape[0]
    gain = kg_ref[0:1, :]

    def piece_rows(piece_no):
        return pl.ds(pl.multiple_of((me_ref[0] ^ piece_no) * shard, shard), shard)

    term[...] = jnp.zeros_like(term)
    acc[...] = jnp.zeros_like(acc)
    for piece_no, piece in enumerate(pieces):
        pool_keys[piece_rows(piece_no), :] = piece[:, :width]
        pool_values[piece_rows(piece_no), :] = piece[:, width:]
    for head in range(heads):
        columns = slice(head * size, (head + 1) * size)
        pool_values_t[columns, :] = pool_values[:, columns].T

    def dead(slot, carry):
        dk_ref[slot_rows(slot), :] = jnp.zeros((CL, width), BF16)
        dv_ref[slot_rows(slot), :] = jnp.zeros((CL, width), BF16)
        return carry

    def live(slot, carry):
        rows = pl.ds(pl.multiple_of(prompt_ref[slot] * PL, PL), PL)

        def load_head(head):
            columns = slice(head * size, (head + 1) * size)
            own_unit, own_recip = unit(ck_ref[slot_rows(slot), columns].astype(F32))
            own_keys = (own_unit * gain).astype(BF16)
            own_keys_ref[slot_rows(slot), columns] = own_keys
            own_values = cv_ref[slot_rows(slot), columns]
            keys = jnp.concatenate([pool_keys[rows, columns], own_keys], axis=0)
            values = jnp.concatenate([pool_values[rows, columns], own_values], axis=0)
            values_t = jnp.concatenate([pool_values_t[columns, rows], own_values.T], axis=1)
            values_t = jnp.concatenate([values_t, jnp.ones((TAIL, PL + CL), BF16)], axis=0)
            return own_unit, own_recip, keys, values, values_t

        def begin(state):
            state["queries"] = queries_ref[slot, state["rows"], state["lanes"]]
            state["scores"] = dot(state["head"][2], state["queries"])

        def weigh(state):
            scores = state.pop("scores")
            own = scores[PL:]
            key_no = lax.broadcasted_iota(jnp.int32, own.shape, 0)
            token_no = lax.broadcasted_iota(jnp.int32, own.shape, 1) % CL
            own = jnp.where(key_no <= token_no, own, -jnp.inf)
            scores = jnp.concatenate([scores[:PL], own], axis=0)
            high = jnp.max(scores, axis=0, keepdims=True)
            state["weights"] = jnp.exp2((scores - high) * (score_scale * math.log2(math.e)))
            state["half"] = state["weights"].astype(BF16)
            state["summed"] = dot(state["head"][4], state["half"])

        def attend(state):
            summed = state.pop("summed")
            inverse = 1.0 / summed[size:size + 1]
            attended = (summed[:size] * inverse).astype(BF16)
            att_ref[slot, state["rows"], state["lanes"]] = attended
            grads = (grads_ref[slot, state["rows"], state["lanes"]].astype(F32) * inverse).astype(BF16)
            state["grads"] = grads
            state["delta"] = jnp.sum(grads.astype(F32) * attended.astype(F32), axis=0, keepdims=True)
            state["prob_grad"] = dot(state["head"][3], grads)

        def back(state):
            state["value_grad"] = dot_nt(state.pop("half"), state.pop("grads"))
            score_grad = (state.pop("weights") * (state.pop("prob_grad") - state.pop("delta"))).astype(BF16)
            ds_ref[slot, state["head_no"], :, state["lanes"]] = score_grad
            state["key_grad"] = dot_nt(score_grad, state.pop("queries"))

        loaded = [load_head(head) for head in range(heads)]
        states = [
            {
                "head": loaded[head],
                "head_no": head,
                "rows": slice(head * size, (head + 1) * size),
                "lanes": slice(at * CHUNK, (at + 1) * CHUNK),
            }
            for head in range(heads)
            for at in range(per_head)
        ]
        stages = (begin, weigh, attend, back)
        for tick in range(len(states) + len(stages) - 1):
            for number in range(len(stages)):
                if 0 <= tick - number < len(states):
                    stages[number](states[tick - number])

        for head in range(heads):
            own_unit, own_recip, keys = loaded[head][:3]
            mine = states[head * per_head:(head + 1) * per_head]
            key_grad = sum(state["key_grad"] for state in mine) * score_scale
            value_grad = sum(state["value_grad"] for state in mine)
            columns = slice(head * size, (head + 1) * size)
            acc[rows, columns] += key_grad[:PL]
            acc[rows, width + head * size:width + (head + 1) * size] += value_grad[:PL]
            own_grad = key_grad[PL:]
            term[...] += jnp.sum(own_grad * keys[PL:].astype(F32), axis=0, keepdims=True)
            dk_ref[slot_rows(slot), columns] = norm_back(own_grad, own_unit, own_recip, gain).astype(BF16)
            dv_ref[slot_rows(slot), columns] = value_grad[PL:].astype(BF16)
        return carry

    lax.fori_loop(0, live_ref[0], live, 0)
    lax.fori_loop(live_ref[0], slots, dead, 0)

    total = term[...]
    for head in range(heads):
        columns = slice(head * size, (head + 1) * size)
        total = total + jnp.sum(acc[:, columns] * pool_keys[:, columns].astype(F32), axis=0, keepdims=True)
    if parts == 1:
        keep_ref[...] = acc[...]
        send_ref[...] = jnp.concatenate([total, jnp.zeros((7, size), F32)], axis=0)
    else:
        for piece_no in range(parts):
            place = slice(piece_no // 2 * shard, (piece_no // 2 + 1) * shard)
            if piece_no % 2 == 0:
                keep_ref[place, :] = acc[piece_rows(piece_no), :]
            else:
                send_ref[place, :] = acc[piece_rows(piece_no), :].astype(BF16)
        tail = gain_rows(total, 2 * width)
        send_ref[parts // 2 * shard:, :] = tail
        keep_ref[parts // 2 * shard:, :] = tail.astype(F32)


def attention(live_counts, slot_prompts, me, queries, grads, keys, values, key_row, pieces):
    size = key_row.shape[1]
    slots, width, lanes = queries.shape
    heads = width // size
    parts = len(pieces)
    pool_rows = parts * pieces[0].shape[0]
    own = jax.ShapeDtypeStruct(keys.shape, BF16)
    out_shape = [
        jax.ShapeDtypeStruct(queries.shape, BF16),
        jax.ShapeDtypeStruct((slots, heads, PL + CL, lanes), BF16),
        jax.ShapeDtypeStruct((pool_rows, width), BF16),
        own, own, own,
    ]
    if parts > 1:
        half = (pool_rows // 2 + TAIL, 2 * width)
        out_shape += [jax.ShapeDtypeStruct(half, F32), jax.ShapeDtypeStruct(half, BF16)]
    else:
        out_shape += [jax.ShapeDtypeStruct((pool_rows, 2 * width), F32), jax.ShapeDtypeStruct((8, size), F32)]
    return pl.pallas_call(
        functools.partial(attention_kernel, parts=parts, heads=heads),
        in_specs=[SMEM_SPEC] * 3 + [VMEM_SPEC] * (5 + parts),
        out_specs=[VMEM_SPEC] * 8,
        out_shape=out_shape,
        scratch_shapes=[
            pltpu.VMEM((pool_rows, 2 * width), F32),
            pltpu.VMEM((pool_rows, width), BF16),
            pltpu.VMEM((width, pool_rows), BF16),
            pltpu.VMEM((1, size), F32),
        ],
        compiler_params=params(),
        cost_estimate=cost(3 * 10**9, 10**7),
        name="attention",
    )(live_counts, slot_prompts, me, queries, grads, keys, values, key_row, *pieces)


def post_kernel(
    live_ref, prompt_ref, att_t_ref, ds_ref, pool_keys, own_keys_ref, raw_ref, recip_ref, col_ref,
    att_ref, dq_ref, att_out, dq_out, sems,
):
    slots, width, lanes = raw_ref.shape
    size = col_ref.shape[0]
    heads = width // size
    group = att_ref.shape[1] // width
    score_scale = 1.0 / math.sqrt(size)

    def copy_out(slot, which):
        source, target = ((att_out, att_ref), (dq_out, dq_ref))[which]
        return pltpu.make_async_copy(source.at[slot], target.at[slot_rows(slot), :], sems.at[which, slot])

    def dead(slot, carry):
        att_out[slot] = jnp.zeros(att_out.shape[1:], BF16)
        dq_out[slot] = jnp.zeros(dq_out.shape[1:], BF16)
        for which in range(2):
            copy_out(slot, which).start()
        return carry

    def live(slot, carry):
        rows = pl.ds(pl.multiple_of(prompt_ref[slot] * PL, PL), PL)
        for head in range(heads):
            columns = slice(head * size, (head + 1) * size)
            keys_t = jnp.concatenate([pool_keys[rows, columns], own_keys_ref[slot_rows(slot), columns]], axis=0).T
            query_grad = dot(keys_t, ds_ref[slot, head]) * score_scale
            recip = recip_ref[slot, head:head + 1, :]
            query_unit = raw_ref[slot, columns, :].astype(F32) * recip
            scaled = query_grad * col_ref[...]
            mean = jnp.mean(query_unit * scaled, axis=0, keepdims=True)
            query_out = (recip * (scaled - query_unit * mean)).astype(BF16).T
            attended = att_t_ref[slot, columns, :].T
            for g, place in enumerate(head_columns(head, group, size)):
                att_out[slot, :, place] = attended[g * CL:(g + 1) * CL]
                dq_out[slot, :, place] = query_out[g * CL:(g + 1) * CL]
        for which in range(2):
            copy_out(slot, which).start()
        return carry

    lax.fori_loop(live_ref[0], slots, dead, 0)
    lax.fori_loop(0, live_ref[0], live, 0)
    for slot in range(slots):
        for which in range(2):
            copy_out(slot, which).wait()


def post(live_counts, slot_prompts, att_t, score_grads, pool_keys, own_keys, raw, recip, query_col, shape):
    slots = raw.shape[0]
    out = jax.ShapeDtypeStruct(shape, BF16)
    slab = pltpu.VMEM((slots, CL, shape[1]), BF16)
    return pl.pallas_call(
        post_kernel,
        in_specs=[SMEM_SPEC] * 2 + [VMEM_SPEC] * 7,
        out_specs=[HBM_SPEC] * 2,
        out_shape=[out, out],
        scratch_shapes=[slab, slab, pltpu.SemaphoreType.DMA((2, slots))],
        compiler_params=params(),
        cost_estimate=cost(3 * 10**9, 4 * 10**6),
        name="post",
    )(live_counts, slot_prompts, att_t, score_grads, pool_keys, own_keys, raw, recip, query_col)


def tree(terms):
    while len(terms) > 1:
        terms = [left + right for left, right in zip(terms[::2], terms[1::2])]
    return terms[0]


def add_kernel(keep_ref, came_ref, own_ref, *send_refs, size):
    blocks = len(send_refs) + 1
    shard = (keep_ref.shape[0] - TAIL) // blocks
    mine = gain_term(keep_ref[blocks * shard:, :], size)
    other = gain_term(came_ref[blocks * shard:, :], size)
    tail = gain_rows(mine + other, keep_ref.shape[1])
    for at in range(blocks):
        place = slice(at * shard, (at + 1) * shard)
        total = keep_ref[place, :] + came_ref[place, :].astype(F32)
        if at == 0:
            own_ref[:shard, :] = total
            own_ref[shard:, :] = tail.astype(F32)
        else:
            send_refs[at - 1][:shard, :] = total.astype(BF16)
            send_refs[at - 1][shard:, :] = tail


def add(keep, came, blocks, size):
    wide = keep.shape[1]
    shape = ((keep.shape[0] - TAIL) // blocks + TAIL, wide)
    return pl.pallas_call(
        functools.partial(add_kernel, size=size),
        in_specs=[VMEM_SPEC] * 2,
        out_specs=[VMEM_SPEC] * blocks,
        out_shape=[jax.ShapeDtypeStruct(shape, F32)] + [jax.ShapeDtypeStruct(shape, BF16)] * (blocks - 1),
        compiler_params=params(),
        name="add",
    )(keep, came)


def chips_kernel(*refs, size):
    total = tree([gain_term(ref[ref.shape[0] - TAIL:, :], size) for ref in refs[:-1]])
    refs[-1][...] = jnp.broadcast_to(total, refs[-1].shape)


def sum_chips(blocks, size):
    return pl.pallas_call(
        functools.partial(chips_kernel, size=size),
        in_specs=[VMEM_SPEC] * len(blocks),
        out_specs=VMEM_SPEC,
        out_shape=jax.ShapeDtypeStruct((8, size), F32),
        compiler_params=params(),
        name="sum_chips",
    )(*blocks)


def last_kernel(*refs):
    terms, (qg_ref, kg_ref, query_ref, key_ref) = refs[:-4], refs[-4:]
    total = tree([ref[0:1, :] for ref in terms])
    query_ref[...] = total / qg_ref[...]
    key_ref[...] = total / kg_ref[...]


def gain_grads(terms, query_gain, key_gain):
    row = jax.ShapeDtypeStruct((1, query_gain.shape[0]), F32)
    return pl.pallas_call(
        last_kernel,
        in_specs=[VMEM_SPEC] * (len(terms) + 2),
        out_specs=[VMEM_SPEC] * 2,
        out_shape=[row, row],
        compiler_params=params(),
        name="gain_grads",
    )(*terms, query_gain.reshape(1, -1), key_gain.reshape(1, -1))


def finish_kernel(*refs):
    parts, (raw_ref, kg_ref, key_ref, value_ref) = refs[:-4], refs[-4:]
    size = kg_ref.shape[1]
    shard, width = raw_ref.shape
    total = parts[0][:shard, :]
    for ref in parts[1:]:
        total = total + ref[:shard, :].astype(F32)
    for head in range(width // size):
        columns = slice(head * size, (head + 1) * size)
        unit_rows, recip = unit(raw_ref[:, columns].astype(F32))
        key_ref[:, columns] = norm_back(total[:, columns], unit_rows, recip, kg_ref[0:1, :])
    value_ref[...] = total[:, width:]


def finish(blocks, raw, key_row):
    shape = jax.ShapeDtypeStruct(raw.shape, F32)
    return pl.pallas_call(
        finish_kernel,
        in_specs=[VMEM_SPEC] * (len(blocks) + 2),
        out_specs=[VMEM_SPEC] * 2,
        out_shape=[shape, shape],
        compiler_params=params(),
        cost_estimate=cost(10**8, 10**6),
        name="finish",
    )(*blocks, raw, key_row)


def swap(values, axis, step):
    return lax.ppermute(values, axis, [(i, i ^ step) for i in range(lax.axis_size(axis))])


def local(
    comp_queries, comp_keys, comp_values, prompt_keys, prompt_values,
    query_gain, key_gain, out_grad, live_counts, slot_prompts,
):
    grp, tp = lax.axis_size("grp"), lax.axis_size("tp")
    shard = prompt_keys.shape[0]
    size = query_gain.shape[0]
    by_permute = shard % 16 == 0 and grp > 1 and grp & (grp - 1) == 0 and tp & (tp - 1) == 0
    slots, width = slot_prompts.shape[0], comp_keys.shape[1]
    query_col, key_row = spread_gains(query_gain, key_gain, comp_queries.shape[1] // width * CL)
    mine = pack(prompt_keys, prompt_values, key_row)
    raw, recip, queries, grads = prepare(live_counts, comp_queries, out_grad, query_col, slots, width)
    if by_permute:
        me = lax.axis_index("grp").astype(jnp.int32).reshape(1)
        even = [mine] + [swap(mine, "grp", step) for step in range(2, grp, 2)]
        odd = [swap(mine, "grp", 1)]
        even, queries = lax.optimization_barrier((even, queries))
        odd += [swap(piece, "grp", 1) for piece in even[1:]]
        pieces = [piece for pair in zip(even, odd) for piece in pair]
    else:
        me = jnp.zeros((1,), jnp.int32)
        pieces = [lax.all_gather(mine, "grp", axis=0, tiled=True)]
    att_t, score_grads, pool_keys, own_keys, key_grads, value_grads, keep, send = attention(
        live_counts, slot_prompts, me, queries, grads, comp_keys, comp_values, key_row, pieces,
    )
    attended, query_grads = post(
        live_counts, slot_prompts, att_t, score_grads, pool_keys, own_keys, raw, recip, query_col, comp_queries.shape,
    )
    if by_permute:
        own, *blocks = add(keep, swap(send, "grp", 1), grp // 2, size)
        blocks = [own] + [swap(block, "grp", 2 * at + 2) for at, block in enumerate(blocks)]
        blocks, attended = lax.optimization_barrier((blocks, attended))
        total = sum_chips(blocks, size)
        terms = [total] + [swap(total, "tp", step) for step in range(1, tp)]
    else:
        blocks = [lax.psum_scatter(keep, "grp", scatter_dimension=0, tiled=True)]
        terms = [lax.psum(send, ("grp", "tp"))]
    prompt_key_grads, prompt_value_grads = finish(blocks, prompt_keys, key_row)
    query_gain_grad, key_gain_grad = gain_grads(terms, query_gain, key_gain)
    return (
        attended, query_grads, key_grads, value_grads, prompt_key_grads, prompt_value_grads,
        query_gain_grad.reshape(size), key_gain_grad.reshape(size),
    )


def solution(mesh):
    split, whole = P("grp", "tp"), P()
    return jax.shard_map(
        local,
        mesh=mesh,
        in_specs=(split, split, split, split, split, whole, whole, split, P("grp"), P("grp")),
        out_specs=(split, split, split, split, split, split, whole, whole),
        check_vma=False,
    )
```

time: 56.8 us -> 44.4 us (0.78)
  blocking collectives: 19.3 us -> 0 us
  Pallas kernels: 8.23 us -> 15.1 us
  waiting for transfers between devices: 14.8 us -> 10.4 us
  starting transfers between devices: 9.75 us -> 13.2 us
  local copies, waits for them, and re-layouts: 2.14 us -> 4.24 us
  other arithmetic: 0.89 us -> 0 us
    all_to_all x1 -> x0, blocking collectives: 19.3 us -> none  [local(): parts = lax.all_to_all(send, 'grp', 0, 0, tiled=True)]
    all_to_all x1 -> x0, waiting for transfers between devices: 12 us -> none  [local(): lax.all_to_all(copies, 'grp', 0, 0, tiled=True)]
    ppermute x3 -> x14, starting transfers between devices: 4.45 us -> 13.2 us  [swap(): lax.ppermute(values, axis, [(i, i ^ step) for i in range(lax.axis_size(ax...]
    ppermute x3 -> x14, waiting for transfers between devices: 2.83 us -> 10.4 us  [swap(): lax.ppermute(values, axis, [(i, i ^ step) for i in range(lax.axis_size(ax...]
    pallas_call x2 -> x9, Pallas kernels: 8.23 us -> 15.1 us  [the longest x1 9.01 us: attention(): pl.pallas_call(functools.partial(attention_kernel, parts=parts, heads=hea...]
    all_to_all x1 -> x0, starting transfers between devices: 5.3 us -> none  [local(): lax.all_to_all(copies, 'grp', 0, 0, tiled=True)]
    unnamed x16 -> x26, local copies, waits for them, and re-layouts: 0.67 us -> 4.24 us
    broadcast_in_dim x1 -> x0, local copies, waits for them, and re-layouts: 0.95 us -> none  [local(): copies = jnp.broadcast_to(mine, (grp,) + mine.shape)]
  transfers between devices with their start and end apart: 4 -> 14, of which waited for: 3 -> 10; matrix products, arithmetic and copies ran while one was open for 0% -> 0% of each run, Pallas kernels for 2% -> 12%
where the time goes in v1:
time: 44.4 us; the launch traced here: 44.3 us
  Pallas kernels  15.1 us (34%)
  starting transfers between devices  13.2 us (30%)
  waiting for transfers between devices  10.4 us (23%)
  local copies, waits for them, and re-layouts  4.24 us (10%)
  between operations  1.42 us (3%)
    ppermute x14, starting transfers between devices, swap(): lax.ppermute(values, axis, [(i, i ^ step) for i in range(lax.axis_size(ax...  13.2 us
    ppermute x14, waiting for transfers between devices, swap(): lax.ppermute(values, axis, [(i, i ^ step) for i in range(lax.axis_size(ax...  10.4 us
    pallas_call x1, Pallas kernels, attention(): pl.pallas_call(functools.partial(attention_kernel, parts=parts, heads=hea...  9.01 us
    unnamed x26, local copies, waits for them, and re-layouts  4.24 us
    pallas_call x1, Pallas kernels, post(): pl.pallas_call(post_kernel, in_specs=[SMEM_SPEC] * 2 + [VMEM_SPEC] * 7, o...  3.41 us
    pallas_call x1, Pallas kernels, prepare(): pl.pallas_call(prepare_kernel, in_specs=[SMEM_SPEC] + [VMEM_SPEC] * 3, ou...  0.96 us
  transfers between devices with their start and end apart: 14, of which 10 were waited for; matrix products, arithmetic and copies ran while one was open for 0% of the time, Pallas kernels for 12%

profile of v1, /device:TPU:0, one launch (start us, length us, event | category | flops | bytes accessed | tf_op | source)
XLA Modules:
  0.0 44.3 jit_solution(4724366548883594991)
XLA Ops:
  0.6 0.0 copy-start.1
  0.6 0.6 %copy-done.1 = f32[128]{0:T(128)S(1)} copy-done((f32[128]{0:T(128)S(1)}, f32[128]{0:T(128)}, u32[]{:S(2)}) %copy-start.1) | copy-done | bytes 536
  1.3 0.0 copy-start.3
  1.3 0.7 %copy-done.3 = f32[128]{0:T(128)S(1)} copy-done((f32[128]{0:T(128)S(1)}, f32[128]{0:T(128)}, u32[]{:S(2)}) %copy-start.3) | copy-done | bytes 536
  1.9 0.0 copy-start
  1.9 0.0 copy-start.9
  2.0 0.1 spread_gains.1
  2.1 0.7 %copy-done = bf16[96,256]{1,0:T(8,128)(2,1)S(1)} copy-done((bf16[96,256]{1,0:T(8,128)(2,1)S(1)}, bf16[96,256]{1,0:T(8,128)(2,1)}, u32[]{:S(2)}) %copy-start) | copy-done | bytes 49176
  2.7 0.0 copy-done.9
  2.8 0.0 copy-start.5
  2.8 0.0 copy-start.6
  2.8 0.1 pack.1.refs_8_
  2.9 0.5 %collective-permute-start.3 = (bf16[96,512]{1,0:T(8,128)(2,1)S(1)}, bf16[96,512]{1,0:T(8,128)(2,1)S(1)}, u32[]{:S(2)}, u32[]{:S(2)}) collective-permute-start(bf16[96,512]{1,0:T(8,128)(2,1)S(1)} %pack.1.refs_8_), channel_id=1, source_target_pairs={{0,4},{4,0},{8,12},{12,8},{16,20},{20,16},{24,28},{28,24},{1,5},{5... | collective-permute-start | bytes 294920 | tf_op jit(solution)/shard_map/ppermute | solution.py:480
  3.4 3.5 %collective-permute-start.2 = (bf16[96,512]{1,0:T(8,128)(2,1)S(1)}, bf16[96,512]{1,0:T(8,128)(2,1)S(1)}, u32[]{:S(2)}, u32[]{:S(2)}) collective-permute-start(bf16[96,512]{1,0:T(8,128)(2,1)S(1)} %pack.1.refs_8_), channel_id=1, source_target_pairs={{0,24},{4,28},{8,16},{12,20},{16,8},{20,12},{24,0},{28,4},{1,25},{... | collective-permute-start | bytes 294920 | tf_op jit(solution)/shard_map/ppermute | solution.py:480
  6.9 0.5 %collective-permute-start.1 = (bf16[96,512]{1,0:T(8,128)(2,1)S(1)}, bf16[96,512]{1,0:T(8,128)(2,1)S(1)}, u32[]{:S(2)}, u32[]{:S(2)}) collective-permute-start(bf16[96,512]{1,0:T(8,128)(2,1)S(1)} %pack.1.refs_8_), channel_id=1, source_target_pairs={{0,16},{4,20},{8,24},{12,28},{16,0},{20,4},{24,8},{28,12},{1,17},{... | collective-permute-start | bytes 294920 | tf_op jit(solution)/shard_map/ppermute | solution.py:480
  7.4 0.1 collective-permute-start
  8.2 0.0 copy-done.5
  8.2 0.0 copy-done.6
  8.2 0.0 copy-start.7
  8.3 0.0 copy-start.8
  8.3 0.0 copy-start.10
  8.3 1.0 %prepare.1 = (bf16[4,256,512]{2,1,0:T(8,128)(2,1)S(1)}, f32[4,8,512]{2,1,0:T(8,128)S(1)}, bf16[4,256,512]{2,1,0:T(8,128)(2,1)S(1)}, bf16[4,256,512]{2,1,0:T(8,128)(2,1)S(1)}) custom-call(s32[1]{0:T(128)S(6)} %copy.18.live_ref.refs_0_, bf16[256,2048]{1,0:T(8,128)(2,1)S(1)} %copy-done.5, bf16[256,2048]{1,0:T(8,128)(2,1)S(1)} %copy-done.6, ...), custom_call_target="tpu_custom_call" | custom-call | flops 2000000000 | bytes 3145728 | tf_op jit(solution)/shard_map/prepare/pallas_call | solution.py:142
  9.2 0.0 copy-start.11
  9.3 1.0 %copy-done.11 = bf16[4,256,512]{2,1,0:T(8,128)(2,1)} copy-done((bf16[4,256,512]{2,1,0:T(8,128)(2,1)}, bf16[4,256,512]{2,1,0:T(8,128)(2,1)S(1)}, u32[]{:S(2)}) %copy-start.11) | copy-done | bytes 1048600
  10.2 0.2 collective-permute-done.2.refs_14_
  10.4 2.0 %collective-permute-done.1.refs_12_ = bf16[96,512]{1,0:T(8,128)(2,1)S(1)} collective-permute-done((bf16[96,512]{1,0:T(8,128)(2,1)S(1)}, bf16[96,512]{1,0:T(8,128)(2,1)S(1)}, u32[]{:S(2)}, u32[]{:S(2)}) %collective-permute-start.1) | collective-permute-done | bytes 98336 | tf_op jit(solution)/shard_map/ppermute | solution.py:480
  12.4 0.3 collective-permute-done.refs_10_
  12.7 0.0 collective-permute-start.4
  12.7 0.5 %collective-permute-start.5 = (bf16[96,512]{1,0:T(8,128)(2,1)S(1)}, bf16[96,512]{1,0:T(8,128)(2,1)S(1)}, u32[]{:S(2)}, u32[]{:S(2)}) collective-permute-start(bf16[96,512]{1,0:T(8,128)(2,1)S(1)} %collective-permute-done.1.refs_12_), channel_id=1, source_target_pairs={{0,4},{4,0},{8,12},{12,8},{16,20},{20,16},{24,28},{28,24},{1,5},{5... | collective-permute-start | bytes 294920 | tf_op jit(solution)/shard_map/ppermute | solution.py:480
  13.2 0.0 collective-permute-start.6
  13.2 0.0 collective-permute-done.3.refs_9_
  13.2 0.8 %collective-permute-done.4.refs_11_ = bf16[96,512]{1,0:T(8,128)(2,1)S(1)} collective-permute-done((bf16[96,512]{1,0:T(8,128)(2,1)S(1)}, bf16[96,512]{1,0:T(8,128)(2,1)S(1)}, u32[]{:S(2)}, u32[]{:S(2)}) %collective-permute-start.4) | collective-permute-done | bytes 98336 | tf_op jit(solution)/shard_map/ppermute | solution.py:480
  14.0 0.2 collective-permute-done.5.refs_13_
  14.1 0.4 collective-permute-done.6.refs_15_
  14.5 0.0 copy-done.7
  14.5 0.0 copy-done.8
  14.5 0.0 copy-done.10
  14.5 0.0 copy-start.12
  14.5 1.2 %copy-done.12 = bf16[4,256,512]{2,1,0:T(8,128)(2,1)S(1)} copy-done((bf16[4,256,512]{2,1,0:T(8,128)(2,1)S(1)}, bf16[4,256,512]{2,1,0:T(8,128)(2,1)}, u32[]{:S(2)}) %copy-start.12) | copy-done | bytes 1048600
  15.7 9.0 %attention.1 = (bf16[4,256,512]{2,1,0:T(8,128)(2,1)S(1)}, bf16[4,2,448,512]{3,2,1,0:T(8,128)(2,1)S(1)}, bf16[768,256]{1,0:T(8,128)(2,1)S(1)}, bf16[256,256]{1,0:...) custom-call(s32[1]{0:T(128)S(6)} %copy.18.live_ref.refs_0_, ...), custom_call_target="tpu_custom_call" | custom-call | flops 3000000000 | bytes 10000000 | tf_op jit(solution)/shard_map/attention/pallas_call | solution.py:301
  24.8 0.0 collective-permute-start.7
  24.8 1.7 %collective-permute-done.7.came_ref = bf16[400,512]{1,0:T(8,128)(2,1)S(1)} collective-permute-done((bf16[400,512]{1,0:T(8,128)(2,1)S(1)}, bf16[400,512]{1,0:T(8,128)(2,1)S(1)}, u32[]{:S(2)}, u32[]{:S(2)}) %collective-permute-start.7) | collective-permute-done | bytes 409632 | tf_op jit(solution)/shard_map/ppermute | solution.py:480
  26.5 0.1 add.1
  26.6 1.6 %collective-permute-start.8 = (bf16[112,512]{1,0:T(8,128)(2,1)S(1)}, bf16[112,512]{1,0:T(8,128)(2,1)S(1)}, u32[]{:S(2)}, u32[]{:S(2)}) collective-permute-start(bf16[112,512]{1,0:T(8,128)(2,1)S(1)} %get-tuple-element.54), channel_id=1, source_target_pairs={{0,8},{4,12},{8,0},{12,4},{16,24},{20,28},{24,16},{28,20},{1,9},{5... | collective-permute-start | bytes 344072 | tf_op jit(solution)/shard_map/ppermute | solution.py:480
  28.2 0.0 collective-permute-start.9
  28.3 1.9 %collective-permute-start.10 = (bf16[112,512]{1,0:T(8,128)(2,1)S(1)}, bf16[112,512]{1,0:T(8,128)(2,1)S(1)}, u32[]{:S(2)}, u32[]{:S(2)}) collective-permute-start(bf16[112,512]{1,0:T(8,128)(2,1)S(1)} %get-tuple-element.56), channel_id=1, source_target_pairs={{0,24},{4,28},{8,16},{12,20},{16,8},{20,12},{24,0},{28,4},{1,25},{... | collective-permute-start | bytes 344072 | tf_op jit(solution)/shard_map/ppermute | solution.py:480
  30.2 0.0 copy-start.2
  30.2 0.0 copy-start.4
  30.2 3.4 %post.1 = (bf16[256,2048]{1,0:T(8,128)(2,1)}, bf16[256,2048]{1,0:T(8,128)(2,1)}) custom-call(s32[1]{0:T(128)S(6)} %copy.18.live_ref.refs_0_, s32[4]{0:T(128)S(1)} %copy-done.10, bf16[4,256,512]{2,1,0:T(8,128)(2,1)S(1)} %get-tuple-element.57.att_t_ref, bf16[4,2,448,512]{3,2,1,0:T(8,128)(2,1)S(1)} %get-tuple-element.58.ds_ref, ...), custom_call_target="tpu_custom_call" | custom-call | flops 3000000000 | bytes 4000000 | tf_op jit(solution)/shard_map/post/pallas_call | solution.py:369
  33.6 0.0 collective-permute-done.8.refs_1_
  33.6 2.0 %collective-permute-done.9.refs_2_ = bf16[112,512]{1,0:T(8,128)(2,1)S(1)} collective-permute-done((bf16[112,512]{1,0:T(8,128)(2,1)S(1)}, bf16[112,512]{1,0:T(8,128)(2,1)S(1)}, u32[]{:S(2)}, u32[]{:S(2)}) %collective-permute-start.9) | collective-permute-done | bytes 114720 | tf_op jit(solution)/shard_map/ppermute | solution.py:480
  35.6 0.0 collective-permute-done.10.refs_3_
  35.6 3.7 %collective-permute-start.13 = (f32[8,128]{1,0:T(8,128)S(1)}, f32[8,128]{1,0:T(8,128)S(1)}, u32[]{:S(2)}, u32[]{:S(2)}) collective-permute-start(f32[8,128]{1,0:T(8,128)S(1)} %sum_chips.1.refs_0_), channel_id=1, source_target_pairs={{0,3},{1,2},{2,1},{3,0},{4,7},{5,6},{6,5},{7,4},{8,11},{9,10},{10,... | collective-permute-start | bytes 12296 | tf_op jit(solution)/shard_map/ppermute | solution.py:480
  39.3 0.0 collective-permute-start.12
  39.3 0.8 %collective-permute-start.11 = (f32[8,128]{1,0:T(8,128)S(1)}, f32[8,128]{1,0:T(8,128)S(1)}, u32[]{:S(2)}, u32[]{:S(2)}) collective-permute-start(f32[8,128]{1,0:T(8,128)S(1)} %sum_chips.1.refs_0_), channel_id=1, source_target_pairs={{0,1},{1,0},{2,3},{3,2},{4,5},{5,4},{6,7},{7,6},{8,9},{9,8},{10,11... | collective-permute-start | bytes 12296 | tf_op jit(solution)/shard_map/ppermute | solution.py:480
  40.1 0.8 %finish.1 = (f32[96,256]{1,0:T(8,128)}, f32[96,256]{1,0:T(8,128)}) custom-call(f32[112,512]{1,0:T(8,128)S(1)} %get-tuple-element.68.refs_0_, bf16[112,512]{1,0:T(8,128)(2,1)S(1)} %collective-permute-done.8.refs_1_, bf16[112,512]{1,0:T(8,128)(2,1)S(1)} %collective-permute-done.9.refs_2_, bf16[112,512]{1,0:T(8,128)(2,1)S(1)} %collective-permute-done.10.refs_3_, ...), custom_call_target="tpu_custom_call" | custom-call | flops 100000000 | bytes 1000000 | tf_op jit(solution)/shard_map/finish/pallas_call | solution.py:468
  40.9 0.2 collective-permute-done.13.refs_3_
  41.1 2.7 %collective-permute-done.12.refs_2_ = f32[8,128]{1,0:T(8,128)S(1)} collective-permute-done((f32[8,128]{1,0:T(8,128)S(1)}, f32[8,128]{1,0:T(8,128)S(1)}, u32[]{:S(2)}, u32[]{:S(2)}) %collective-permute-start.12) | collective-permute-done | bytes 4128 | tf_op jit(solution)/shard_map/ppermute | solution.py:480
  43.8 0.0 collective-permute-done.11.refs_1_
  43.8 0.0 copy-done.2
  43.8 0.0 copy-done.4
  43.8 0.5 %gain_grads.1 = (f32[1,128]{1,0:T(1,128)}, f32[1,128]{1,0:T(1,128)}) custom-call(f32[8,128]{1,0:T(8,128)S(1)} %sum_chips.1.refs_0_, f32[8,128]{1,0:T(8,128)S(1)} %collective-permute-done.11.refs_1_, f32[8,128]{1,0:T(8,128)S(1)} %collective-permute-done.12.refs_2_, f32[8,128]{1,0:T(8,128)S(1)} %collective-permute-done.13.refs_3_, f32[1,128]{1,0:T(1,128)S(1)} %bitcast.6, ...), custom_call_target="tpu_custom_call" | custom-call | tf_op jit(solution)/shard_map/gain_grads/pallas_call | solution.py:442
  (1 shorter events, 0.0 us)
Async XLA Ops:
  0.6 0.7 %copy-start.1 = (f32[128]{0:T(128)S(1)}, f32[128]{0:T(128)}, u32[]{:S(2)}) copy-start(f32[128]{0:T(128)} %param.15) | copy-start | bytes 1540
  1.3 0.7 %copy-start.3 = (f32[128]{0:T(128)S(1)}, f32[128]{0:T(128)}, u32[]{:S(2)}) copy-start(f32[128]{0:T(128)} %param.16) | copy-start | bytes 1540
  1.9 0.8 %copy-start = (bf16[96,256]{1,0:T(8,128)(2,1)S(1)}, bf16[96,256]{1,0:T(8,128)(2,1)}, u32[]{:S(2)}) copy-start(bf16[96,256]{1,0:T(8,128)(2,1)} %refs_4_.1) | copy-start | bytes 147460
  1.9 0.8 %copy-start.9 = (bf16[96,256]{1,0:T(8,128)(2,1)S(1)}, bf16[96,256]{1,0:T(8,128)(2,1)}, u32[]{:S(2)}) copy-start(bf16[96,256]{1,0:T(8,128)(2,1)} %values_ref.1) | copy-start | bytes 147460
  2.8 5.5 %copy-start.5 = (bf16[256,2048]{1,0:T(8,128)(2,1)S(1)}, bf16[256,2048]{1,0:T(8,128)(2,1)}, u32[]{:S(2)}) copy-start(bf16[256,2048]{1,0:T(8,128)(2,1)} %q_ref.1) | copy-start | bytes 3145732
  2.8 5.5 %copy-start.6 = (bf16[256,2048]{1,0:T(8,128)(2,1)S(1)}, bf16[256,2048]{1,0:T(8,128)(2,1)}, u32[]{:S(2)}) copy-start(bf16[256,2048]{1,0:T(8,128)(2,1)} %do_ref.1) | copy-start | bytes 3145732
  2.9 10.3 %collective-permute-start.3 = (bf16[96,512]{1,0:T(8,128)(2,1)S(1)}, bf16[96,512]{1,0:T(8,128)(2,1)S(1)}, u32[]{:S(2)}, u32[]{:S(2)}) collective-permute-start(bf16[96,512]{1,0:T(8,128)(2,1)S(1)} %pack.1.refs_8_), channel_id=1, source_target_pairs={{0,4},{4,0},{8,12},{12,8},{16,20},{20,16},{24,28},{28,24},{1,5},{5... | collective-permute-start | bytes 294920 | tf_op jit(solution)/shard_map/ppermute | solution.py:480
  3.4 7.0 %collective-permute-start.2 = (bf16[96,512]{1,0:T(8,128)(2,1)S(1)}, bf16[96,512]{1,0:T(8,128)(2,1)S(1)}, u32[]{:S(2)}, u32[]{:S(2)}) collective-permute-start(bf16[96,512]{1,0:T(8,128)(2,1)S(1)} %pack.1.refs_8_), channel_id=1, source_target_pairs={{0,24},{4,28},{8,16},{12,20},{16,8},{20,12},{24,0},{28,4},{1,25},{... | collective-permute-start | bytes 294920 | tf_op jit(solution)/shard_map/ppermute | solution.py:480
  6.9 5.5 %collective-permute-start.1 = (bf16[96,512]{1,0:T(8,128)(2,1)S(1)}, bf16[96,512]{1,0:T(8,128)(2,1)S(1)}, u32[]{:S(2)}, u32[]{:S(2)}) collective-permute-start(bf16[96,512]{1,0:T(8,128)(2,1)S(1)} %pack.1.refs_8_), channel_id=1, source_target_pairs={{0,16},{4,20},{8,24},{12,28},{16,0},{20,4},{24,8},{28,12},{1,17},{... | collective-permute-start | bytes 294920 | tf_op jit(solution)/shard_map/ppermute | solution.py:480
  7.4 5.3 %collective-permute-start = (bf16[96,512]{1,0:T(8,128)(2,1)S(1)}, bf16[96,512]{1,0:T(8,128)(2,1)S(1)}, u32[]{:S(2)}, u32[]{:S(2)}) collective-permute-start(bf16[96,512]{1,0:T(8,128)(2,1)S(1)} %pack.1.refs_8_), channel_id=1, source_target_pairs={{0,8},{4,12},{8,0},{12,4},{16,24},{20,28},{24,16},{28,20},{1,9},{5... | collective-permute-start | bytes 294920 | tf_op jit(solution)/shard_map/ppermute | solution.py:480
  8.2 6.3 %copy-start.7 = (bf16[256,256]{1,0:T(8,128)(2,1)S(1)}, bf16[256,256]{1,0:T(8,128)(2,1)}, u32[]{:S(2)}) copy-start(bf16[256,256]{1,0:T(8,128)(2,1)} %refs_5_.1) | copy-start | bytes 393220
  8.3 6.3 %copy-start.8 = (bf16[256,256]{1,0:T(8,128)(2,1)S(1)}, bf16[256,256]{1,0:T(8,128)(2,1)}, u32[]{:S(2)}) copy-start(bf16[256,256]{1,0:T(8,128)(2,1)} %refs_6_.1) | copy-start | bytes 393220
  8.3 6.2 %copy-start.10 = (s32[4]{0:T(128)S(1)}, s32[4]{0:T(128)}, u32[]{:S(2)}) copy-start(s32[4]{0:T(128)} %prompt_ref.1) | copy-start | bytes 52
  9.2 1.0 %copy-start.11 = (bf16[4,256,512]{2,1,0:T(8,128)(2,1)}, bf16[4,256,512]{2,1,0:T(8,128)(2,1)S(1)}, u32[]{:S(2)}) copy-start(bf16[4,256,512]{2,1,0:T(8,128)(2,1)S(1)} %get-tuple-element.46.refs_4_) | copy-start | bytes 3145732
  12.7 1.3 %collective-permute-start.4 = (bf16[96,512]{1,0:T(8,128)(2,1)S(1)}, bf16[96,512]{1,0:T(8,128)(2,1)S(1)}, u32[]{:S(2)}, u32[]{:S(2)}) collective-permute-start(bf16[96,512]{1,0:T(8,128)(2,1)S(1)} %collective-permute-done.refs_10_), channel_id=1, source_target_pairs={{0,4},{4,0},{8,12},{12,8},{16,20},{20,16},{24,28},{28,24},{1,5},{5... | collective-permute-start | bytes 294920 | tf_op jit(solution)/shard_map/ppermute | solution.py:480
  12.7 1.5 %collective-permute-start.5 = (bf16[96,512]{1,0:T(8,128)(2,1)S(1)}, bf16[96,512]{1,0:T(8,128)(2,1)S(1)}, u32[]{:S(2)}, u32[]{:S(2)}) collective-permute-start(bf16[96,512]{1,0:T(8,128)(2,1)S(1)} %collective-permute-done.1.refs_12_), channel_id=1, source_target_pairs={{0,4},{4,0},{8,12},{12,8},{16,20},{20,16},{24,28},{28,24},{1,5},{5... | collective-permute-start | bytes 294920 | tf_op jit(solution)/shard_map/ppermute | solution.py:480
  13.2 1.3 %collective-permute-start.6 = (bf16[96,512]{1,0:T(8,128)(2,1)S(1)}, bf16[96,512]{1,0:T(8,128)(2,1)S(1)}, u32[]{:S(2)}, u32[]{:S(2)}) collective-permute-start(bf16[96,512]{1,0:T(8,128)(2,1)S(1)} %collective-permute-done.2.refs_14_), channel_id=1, source_target_pairs={{0,4},{4,0},{8,12},{12,8},{16,20},{20,16},{24,28},{28,24},{1,5},{5... | collective-permute-start | bytes 294920 | tf_op jit(solution)/shard_map/ppermute | solution.py:480
  14.5 1.2 %copy-start.12 = (bf16[4,256,512]{2,1,0:T(8,128)(2,1)S(1)}, bf16[4,256,512]{2,1,0:T(8,128)(2,1)}, u32[]{:S(2)}) copy-start(bf16[4,256,512]{2,1,0:T(8,128)(2,1)} %copy-done.11) | copy-start | bytes 3145732
  24.8 1.7 %collective-permute-start.7 = (bf16[400,512]{1,0:T(8,128)(2,1)S(1)}, bf16[400,512]{1,0:T(8,128)(2,1)S(1)}, u32[]{:S(2)}, u32[]{:S(2)}) collective-permute-start(bf16[400,512]{1,0:T(8,128)(2,1)S(1)} %get-tuple-element.52), channel_id=1, source_target_pairs={{0,4},{4,0},{8,12},{12,8},{16,20},{20,16},{24,28},{28,24},{1,5},{5... | collective-permute-start | bytes 1228808 | tf_op jit(solution)/shard_map/ppermute | solution.py:480
  26.6 7.0 %collective-permute-start.8 = (bf16[112,512]{1,0:T(8,128)(2,1)S(1)}, bf16[112,512]{1,0:T(8,128)(2,1)S(1)}, u32[]{:S(2)}, u32[]{:S(2)}) collective-permute-start(bf16[112,512]{1,0:T(8,128)(2,1)S(1)} %get-tuple-element.54), channel_id=1, source_target_pairs={{0,8},{4,12},{8,0},{12,4},{16,24},{20,28},{24,16},{28,20},{1,9},{5... | collective-permute-start | bytes 344072 | tf_op jit(solution)/shard_map/ppermute | solution.py:480
  28.2 7.4 %collective-permute-start.9 = (bf16[112,512]{1,0:T(8,128)(2,1)S(1)}, bf16[112,512]{1,0:T(8,128)(2,1)S(1)}, u32[]{:S(2)}, u32[]{:S(2)}) collective-permute-start(bf16[112,512]{1,0:T(8,128)(2,1)S(1)} %get-tuple-element.55), channel_id=1, source_target_pairs={{0,16},{4,20},{8,24},{12,28},{16,0},{20,4},{24,8},{28,12},{1,17},{... | collective-permute-start | bytes 344072 | tf_op jit(solution)/shard_map/ppermute | solution.py:480
  28.3 7.4 %collective-permute-start.10 = (bf16[112,512]{1,0:T(8,128)(2,1)S(1)}, bf16[112,512]{1,0:T(8,128)(2,1)S(1)}, u32[]{:S(2)}, u32[]{:S(2)}) collective-permute-start(bf16[112,512]{1,0:T(8,128)(2,1)S(1)} %get-tuple-element.56), channel_id=1, source_target_pairs={{0,24},{4,28},{8,16},{12,20},{16,8},{20,12},{24,0},{28,4},{1,25},{... | collective-permute-start | bytes 344072 | tf_op jit(solution)/shard_map/ppermute | solution.py:480
  30.2 13.6 %copy-start.2 = (f32[128]{0:T(128)S(1)}, f32[128]{0:T(128)}, u32[]{:S(2)}) copy-start(f32[128]{0:T(128)} %param.15) | copy-start | bytes 1540
  30.2 13.6 %copy-start.4 = (f32[128]{0:T(128)S(1)}, f32[128]{0:T(128)}, u32[]{:S(2)}) copy-start(f32[128]{0:T(128)} %param.16) | copy-start | bytes 1540
  35.6 5.5 %collective-permute-start.13 = (f32[8,128]{1,0:T(8,128)S(1)}, f32[8,128]{1,0:T(8,128)S(1)}, u32[]{:S(2)}, u32[]{:S(2)}) collective-permute-start(f32[8,128]{1,0:T(8,128)S(1)} %sum_chips.1.refs_0_), channel_id=1, source_target_pairs={{0,3},{1,2},{2,1},{3,0},{4,7},{5,6},{6,5},{7,4},{8,11},{9,10},{10,... | collective-permute-start | bytes 12296 | tf_op jit(solution)/shard_map/ppermute | solution.py:480
  39.3 4.5 %collective-permute-start.12 = (f32[8,128]{1,0:T(8,128)S(1)}, f32[8,128]{1,0:T(8,128)S(1)}, u32[]{:S(2)}, u32[]{:S(2)}) collective-permute-start(f32[8,128]{1,0:T(8,128)S(1)} %sum_chips.1.refs_0_), channel_id=1, source_target_pairs={{0,2},{1,3},{2,0},{3,1},{4,6},{5,7},{6,4},{7,5},{8,10},{9,11},{10,... | collective-permute-start | bytes 12296 | tf_op jit(solution)/shard_map/ppermute | solution.py:480
  39.3 4.5 %collective-permute-start.11 = (f32[8,128]{1,0:T(8,128)S(1)}, f32[8,128]{1,0:T(8,128)S(1)}, u32[]{:S(2)}, u32[]{:S(2)}) collective-permute-start(f32[8,128]{1,0:T(8,128)S(1)} %sum_chips.1.refs_0_), channel_id=1, source_target_pairs={{0,1},{1,0},{2,3},{3,2},{4,5},{5,4},{6,7},{7,6},{8,9},{9,8},{10,11... | collective-permute-start | bytes 12296 | tf_op jit(solution)/shard_map/ppermute | solution.py:480

commit v2 on v1

v2 whole, which is shorter than its diff:
```python
import functools
import math

import jax
import jax.numpy as jnp
from jax import lax
from jax.experimental import pallas as pl
from jax.experimental.pallas import tpu as pltpu
from jax.sharding import PartitionSpec as P

PL = 384
CL = 64
EPS = 1e-06
TAIL = 16
CHUNK = 256
VMEM_LIMIT = 24 * 1024 * 1024
F32 = jnp.float32
BF16 = jnp.bfloat16
SMEM_SPEC = pl.BlockSpec(memory_space=pltpu.SMEM)
VMEM_SPEC = pl.BlockSpec(memory_space=pltpu.VMEM)
HBM_SPEC = pl.BlockSpec(memory_space=pltpu.HBM)


def dot(left, right):
    return jnp.dot(left, right, preferred_element_type=F32)


def dot_nt(left, right):
    return lax.dot_general(left, right, (((1,), (1,)), ((), ())), preferred_element_type=F32)


def unit(raw):
    recip = lax.rsqrt(jnp.mean(raw * raw, axis=-1, keepdims=True) + EPS)
    return raw * recip, recip


def norm_back(upstream, unit_rows, recip, gain):
    scaled = upstream * gain
    return recip * (scaled - unit_rows * jnp.mean(unit_rows * scaled, axis=-1, keepdims=True))


def halves(row):
    upper = row.astype(BF16)
    return [upper, (row - upper.astype(F32)).astype(BF16)]


def gain_rows(term, wide):
    row = jnp.concatenate([part.astype(F32) for part in halves(term)], axis=1)
    if wide > row.shape[1]:
        row = jnp.concatenate([row, jnp.zeros((1, wide - row.shape[1]), F32)], axis=1)
    rows = jnp.broadcast_to(row, (TAIL, wide))
    return jnp.where(lax.broadcasted_iota(jnp.int32, rows.shape, 0) == 0, rows, 0.0).astype(BF16)


def gain_term(rows, size):
    row = rows.astype(F32)[0:1]
    return row[:, :size] + row[:, size:2 * size]


def params(limit=VMEM_LIMIT):
    return pltpu.CompilerParams(vmem_limit_bytes=limit)


def cost(flops, size):
    return pl.CostEstimate(flops=flops, bytes_accessed=size, transcendentals=0)


def causal_kernel(mask_ref):
    key_no = lax.broadcasted_iota(jnp.int32, mask_ref.shape, 0)
    token_no = lax.broadcasted_iota(jnp.int32, mask_ref.shape, 1) % CL
    mask_ref[...] = jnp.where(key_no <= token_no, 0.0, -jnp.inf)


def causal():
    return pl.pallas_call(
        causal_kernel,
        out_specs=VMEM_SPEC,
        out_shape=jax.ShapeDtypeStruct((CL, CHUNK), F32),
        compiler_params=params(),
        cost_estimate=cost(4 * 10**9, 10**6),
        name="causal",
    )()


def pack_kernel(keys_ref, values_ref, kg_ref, out_ref):
    size, width = kg_ref.shape[1], keys_ref.shape[1]
    for head in range(width // size):
        columns = slice(head * size, (head + 1) * size)
        unit_rows, _ = unit(keys_ref[:, columns].astype(F32))
        out_ref[:, columns] = (unit_rows * kg_ref[...]).astype(BF16)
    out_ref[:, width:] = values_ref[...]


def pack(keys, values, key_gain):
    return pl.pallas_call(
        pack_kernel,
        in_specs=[VMEM_SPEC] * 3,
        out_specs=VMEM_SPEC,
        out_shape=jax.ShapeDtypeStruct((keys.shape[0], 2 * keys.shape[1]), BF16),
        compiler_params=params(),
        cost_estimate=cost(4 * 10**9, 10**6),
        name="pack",
    )(keys, values, key_gain)


def head_columns(head, group, size):
    return [slice((head * group + g) * size, (head * group + g + 1) * size) for g in range(group)]


def slot_rows(slot):
    return pl.ds(pl.multiple_of(slot * CL, CL), CL)


def prepare_kernel(live_ref, q_ref, do_ref, qg_ref, raw_ref, recip_ref, queries_ref, grads_ref, col_ref):
    size = col_ref.shape[0]
    heads = raw_ref.shape[1] // size
    group = q_ref.shape[1] // raw_ref.shape[1]
    column = jnp.broadcast_to(qg_ref[...], (size, size)).T
    for at in range(0, col_ref.shape[1], size):
        col_ref[:, at:at + size] = column

    def live(slot, carry):
        for head in range(heads):
            places = head_columns(head, group, size)
            rows = slice(head * size, (head + 1) * size)
            half = jnp.concatenate([q_ref[slot_rows(slot), place] for place in places], axis=0).T
            raw_ref[slot, rows, :] = half
            raw = half.astype(F32)
            recip = lax.rsqrt(jnp.mean(raw * raw, axis=0, keepdims=True) + EPS)
            recip_ref[slot, head:head + 1, :] = recip
            queries_ref[slot, rows, :] = (raw * recip * col_ref[...]).astype(BF16)
            grads_ref[slot, rows, :] = jnp.concatenate([do_ref[slot_rows(slot), place] for place in places], axis=0).T
        return carry

    lax.fori_loop(0, live_ref[0], live, 0)


def prepare(live_counts, queries, out_grad, query_gain, slots, width):
    size = query_gain.shape[1]
    lanes = queries.shape[1] // width * CL
    turned = jax.ShapeDtypeStruct((slots, width, lanes), BF16)
    return pl.pallas_call(
        prepare_kernel,
        in_specs=[SMEM_SPEC] + [VMEM_SPEC] * 3,
        out_specs=[VMEM_SPEC] * 5,
        out_shape=[
            turned, jax.ShapeDtypeStruct((slots, 8, lanes), F32), turned, turned,
            jax.ShapeDtypeStruct((size, lanes), F32),
        ],
        compiler_params=params(),
        cost_estimate=cost(2 * 10**9, 6 * queries.size),
        name="prepare",
    )(live_counts, queries, out_grad, query_gain)


def attention_kernel(*refs, parts, heads):
    live_ref, prompt_ref, me_ref, queries_ref, grads_ref, ck_ref, cv_ref, kg_ref, mask_ref = refs[:9]
    pieces, refs = refs[9:9 + parts], refs[9 + parts:]
    att_ref, ds_ref, pool_keys, own_keys, dk_ref, dv_ref, term_ref, keep_ref = refs[:8]
    send_ref, refs = (refs[8], refs[9:]) if parts > 1 else (None, refs[8:])
    acc, own_acc, pool_values, pool_values_t, own_values_t = refs[:5]
    size = kg_ref.shape[1]
    width = heads * size
    slots, _, lanes = queries_ref.shape
    per_head = lanes // CHUNK
    count = heads * per_head
    scores, weights, summed, grads, prob_grads, deltas = (refs[5 + at * count:5 + (at + 1) * count] for at in range(6))
    score_scale = 1.0 / math.sqrt(size)
    shard = pieces[0].shape[0]
    pool_rows = parts * shard

    def columns(head):
        return slice(head * size, (head + 1) * size)

    def piece_rows(piece_no):
        return pl.ds(pl.multiple_of((me_ref[0] ^ piece_no) * shard, shard), shard)

    acc[...] = jnp.zeros_like(acc)
    own_acc[...] = jnp.zeros_like(own_acc)
    for piece_no, piece in enumerate(pieces):
        pool_keys[piece_rows(piece_no), :] = piece[:, :width]
        pool_values[piece_rows(piece_no), :] = piece[:, width:]
    for head in range(heads):
        pool_values_t[columns(head), :] = pool_values[:, columns(head)].T
        own_unit, _ = unit(ck_ref[:, columns(head)].astype(F32))
        own_keys[:, columns(head)] = (own_unit * kg_ref[...]).astype(BF16)
        for slot in range(slots):
            own_values_t[slot, head] = cv_ref[slot * CL:(slot + 1) * CL, columns(head)].T
    alive = live_ref[0]

    def step(turn, carry):
        now, before = jnp.minimum(turn, alive - 1), jnp.maximum(turn - 1, 0)
        slot_of = {True: now, False: before}
        rows_of = {True: prompt_ref[now] * PL, False: prompt_ref[before] * PL}
        target_of = {
            True: jnp.where(turn < alive, rows_of[True], pool_rows),
            False: jnp.where(turn > 0, rows_of[False], pool_rows),
        }
        own_of = {True: jnp.where(turn < alive, turn, slots), False: jnp.where(turn > 0, turn - 1, slots)}

        def prompt_rows(at):
            return pl.ds(pl.multiple_of(at, PL), PL)

        def part(no):
            head = no // per_head
            return head, columns(head), slice(no % per_head * CHUNK, (no % per_head + 1) * CHUNK)

        def begin(no, fresh):
            _, place, span = part(no)
            keys = jnp.concatenate(
                [pool_keys[prompt_rows(rows_of[fresh]), place], own_keys[slot_rows(slot_of[fresh]), place]], axis=0
            )
            scores[no][...] = dot(keys, queries_ref[slot_of[fresh], place, span])

        def weigh(no, fresh):
            head, place, _ = part(no)
            prompt, own = scores[no][:PL, :], scores[no][PL:, :] + mask_ref[...]
            factor = score_scale * math.log2(math.e)
            high = jnp.maximum(jnp.max(prompt, axis=0, keepdims=True), jnp.max(own, axis=0, keepdims=True))
            both = jnp.concatenate([prompt, own], axis=0)
            half = jnp.exp2((both - high) * factor).astype(BF16)
            weights[no][...] = half
            values_t = jnp.concatenate(
                [pool_values_t[place, prompt_rows(rows_of[fresh])], own_values_t[slot_of[fresh], head]], axis=1
            )
            values_t = jnp.concatenate([values_t, jnp.ones((TAIL, PL + CL), BF16)], axis=0)
            summed[no][...] = dot(values_t, half)

        def attend(no, fresh):
            _, place, span = part(no)
            inverse = 1.0 / summed[no][size:size + 1, :]
            attended = (summed[no][:size, :] * inverse).astype(BF16)
            att_ref[slot_of[fresh], place, span] = attended
            scaled = (grads_ref[slot_of[fresh], place, span].astype(F32) * inverse).astype(BF16)
            grads[no][...] = scaled
            delta = jnp.sum(scaled.astype(F32) * attended.astype(F32), axis=0, keepdims=True)
            deltas[no][...] = jnp.broadcast_to(delta, deltas[no].shape)
            values = jnp.concatenate(
                [pool_values[prompt_rows(rows_of[fresh]), place], cv_ref[slot_rows(slot_of[fresh]), place]], axis=0
            )
            prob_grads[no][...] = dot(values, scaled)

        def back(no, fresh):
            head, place, span = part(no)
            half = weights[no][...]
            score_grad = (half.astype(F32) * (prob_grads[no][...] - deltas[no][0:1, :])).astype(BF16)
            ds_ref[slot_of[fresh], head, :, span] = score_grad
            value_grad = dot_nt(half, grads[no][...])
            key_grad = dot_nt(score_grad, queries_ref[slot_of[fresh], place, span])
            target = prompt_rows(target_of[fresh])
            acc[target, place] += key_grad[:PL]
            acc[target, width + head * size:width + (head + 1) * size] += value_grad[:PL]
            own_acc[own_of[fresh], head, 0] += key_grad[PL:]
            own_acc[own_of[fresh], head, 1] += value_grad[PL:]

        stages = (begin, weigh, attend, back)
        for tick in range(count):
            for number, stage in enumerate(stages):
                stage((tick - number) % count, tick >= number)
        return carry

    lax.fori_loop(0, alive + 1, step, 0)

    total = jnp.zeros((1, size), F32)
    for head in range(heads):
        own_grad = own_acc[:slots, head, 0].reshape(slots * CL, size) * score_scale
        own_unit, own_recip = unit(ck_ref[:, columns(head)].astype(F32))
        dk_ref[:, columns(head)] = norm_back(own_grad, own_unit, own_recip, kg_ref[...]).astype(BF16)
        dv_ref[:, columns(head)] = own_acc[:slots, head, 1].reshape(slots * CL, size).astype(BF16)
        total = total + jnp.sum(own_grad * own_keys[:, columns(head)].astype(F32), axis=0, keepdims=True)
        pool_term = acc[:pool_rows, columns(head)] * pool_keys[:, columns(head)].astype(F32)
        total = total + jnp.sum(pool_term, axis=0, keepdims=True) * score_scale
    term_ref[...] = jnp.broadcast_to(total, term_ref.shape)
    if parts == 1:
        keep_ref[:, :width] = acc[:pool_rows, :width] * score_scale
        keep_ref[:, width:] = acc[:pool_rows, width:]
    else:
        for piece_no in range(parts):
            place = slice(piece_no // 2 * shard, (piece_no // 2 + 1) * shard)
            ref = keep_ref if piece_no % 2 == 0 else send_ref
            ref[place, :width] = (acc[piece_rows(piece_no), :width] * score_scale).astype(ref.dtype)
            ref[place, width:] = acc[piece_rows(piece_no), width:].astype(ref.dtype)


def attention(live_counts, slot_prompts, me, queries, grads, keys, values, key_gain, mask, pieces):
    size = key_gain.shape[1]
    slots, width, lanes = queries.shape
    heads = width // size
    parts = len(pieces)
    pool_rows = parts * pieces[0].shape[0]
    count = heads * lanes // CHUNK
    span = PL + CL
    own = jax.ShapeDtypeStruct(keys.shape, BF16)
    out_shape = [
        jax.ShapeDtypeStruct(queries.shape, BF16),
        jax.ShapeDtypeStruct((slots, heads, span, lanes), BF16),
        jax.ShapeDtypeStruct((pool_rows, width), BF16),
        own, own, own,
        jax.ShapeDtypeStruct((8, size), F32),
    ]
    if parts > 1:
        half = (pool_rows // 2, 2 * width)
        out_shape += [jax.ShapeDtypeStruct(half, F32), jax.ShapeDtypeStruct(half, BF16)]
    else:
        out_shape += [jax.ShapeDtypeStruct((pool_rows, 2 * width), F32)]
    kinds = [
        ((span, CHUNK), F32), ((span, CHUNK), BF16), ((size + TAIL, CHUNK), F32),
        ((size, CHUNK), BF16), ((span, CHUNK), F32), ((8, CHUNK), F32),
    ]
    return pl.pallas_call(
        functools.partial(attention_kernel, parts=parts, heads=heads),
        in_specs=[SMEM_SPEC] * 3 + [VMEM_SPEC] * (6 + parts),
        out_specs=[VMEM_SPEC] * len(out_shape),
        out_shape=out_shape,
        scratch_shapes=[
            pltpu.VMEM((pool_rows + PL, 2 * width), F32),
            pltpu.VMEM((slots + 1, heads, 2, CL, size), F32),
            pltpu.VMEM((pool_rows, width), BF16),
            pltpu.VMEM((width, pool_rows), BF16),
            pltpu.VMEM((slots, heads, size, CL), BF16),
        ] + [pltpu.VMEM(shape, kind) for shape, kind in kinds for _ in range(count)],
        compiler_params=params(),
        cost_estimate=cost(3 * 10**9, 10**7),
        name="attention",
    )(live_counts, slot_prompts, me, queries, grads, keys, values, key_gain, mask, *pieces)


def post_kernel(
    live_ref, prompt_ref, att_t_ref, ds_ref, pool_keys, own_keys_ref, raw_ref, recip_ref, col_ref,
    att_ref, dq_ref, att_out, dq_out, sems,
):
    slots, width, lanes = raw_ref.shape
    size = col_ref.shape[0]
    heads = width // size
    group = att_ref.shape[1] // width
    score_scale = 1.0 / math.sqrt(size)

    def copy_out(slot, which):
        source, target = ((att_out, att_ref), (dq_out, dq_ref))[which]
        return pltpu.make_async_copy(source.at[slot], target.at[slot_rows(slot), :], sems.at[which, slot])

    def dead(slot, carry):
        att_out[slot] = jnp.zeros(att_out.shape[1:], BF16)
        dq_out[slot] = jnp.zeros(dq_out.shape[1:], BF16)
        for which in range(2):
            copy_out(slot, which).start()
        return carry

    def live(slot, carry):
        rows = pl.ds(pl.multiple_of(prompt_ref[slot] * PL, PL), PL)
        for head in range(heads):
            columns = slice(head * size, (head + 1) * size)
            keys_t = jnp.concatenate([pool_keys[rows, columns], own_keys_ref[slot_rows(slot), columns]], axis=0).T
            query_grad = dot(keys_t, ds_ref[slot, head]) * score_scale
            recip = recip_ref[slot, head:head + 1, :]
            query_unit = raw_ref[slot, columns, :].astype(F32) * recip
            scaled = query_grad * col_ref[...]
            mean = jnp.mean(query_unit * scaled, axis=0, keepdims=True)
            query_out = (recip * (scaled - query_unit * mean)).astype(BF16).T
            attended = att_t_ref[slot, columns, :].T
            for g, place in enumerate(head_columns(head, group, size)):
                att_out[slot, :, place] = attended[g * CL:(g + 1) * CL]
                dq_out[slot, :, place] = query_out[g * CL:(g + 1) * CL]
        for which in range(2):
            copy_out(slot, which).start()
        return carry

    lax.fori_loop(live_ref[0], slots, dead, 0)
    lax.fori_loop(0, live_ref[0], live, 0)
    for slot in range(slots):
        for which in range(2):
            copy_out(slot, which).wait()


def post(live_counts, slot_prompts, att_t, score_grads, pool_keys, own_keys, raw, recip, query_col, shape):
    slots = raw.shape[0]
    out = jax.ShapeDtypeStruct(shape, BF16)
    slab = pltpu.VMEM((slots, CL, shape[1]), BF16)
    return pl.pallas_call(
        post_kernel,
        in_specs=[SMEM_SPEC] * 2 + [VMEM_SPEC] * 7,
        out_specs=[HBM_SPEC] * 2,
        out_shape=[out, out],
        scratch_shapes=[slab, slab, pltpu.SemaphoreType.DMA((2, slots))],
        compiler_params=params(),
        cost_estimate=cost(3 * 10**9, 4 * 10**6),
        name="post",
    )(live_counts, slot_prompts, att_t, score_grads, pool_keys, own_keys, raw, recip, query_col)


def tree(terms):
    while len(terms) > 1:
        terms = [left + right for left, right in zip(terms[::2], terms[1::2])]
    return terms[0]


def add_kernel(keep_ref, came_ref, *refs, terms, size):
    tail = gain_rows(tree([ref[0:1, :] for ref in refs[:terms]]), keep_ref.shape[1])
    own_ref, send_refs = refs[terms], refs[terms + 1:]
    blocks = len(send_refs) + 1
    shard = keep_ref.shape[0] // blocks
    for at in range(blocks):
        place = slice(at * shard, (at + 1) * shard)
        total = keep_ref[place, :] + came_ref[place, :].astype(F32)
        ref = send_refs[at - 1] if at > 0 else own_ref
        ref[:shard, :] = total.astype(ref.dtype)
        ref[shard:, :] = tail.astype(ref.dtype)


def add(keep, came, terms, blocks):
    shape = (keep.shape[0] // blocks + TAIL, keep.shape[1])
    return pl.pallas_call(
        functools.partial(add_kernel, terms=len(terms), size=terms[0].shape[1]),
        in_specs=[VMEM_SPEC] * (2 + len(terms)),
        out_specs=[VMEM_SPEC] * blocks,
        out_shape=[jax.ShapeDtypeStruct(shape, F32)] + [jax.ShapeDtypeStruct(shape, BF16)] * (blocks - 1),
        compiler_params=params(),
        name="add",
    )(keep, came, *terms)


def chips_kernel(*refs, size):
    total = tree([gain_term(ref[ref.shape[0] - TAIL:, :], size) for ref in refs[:-1]])
    refs[-1][...] = jnp.broadcast_to(total, refs[-1].shape)


def sum_chips(blocks, size):
    return pl.pallas_call(
        functools.partial(chips_kernel, size=size),
        in_specs=[VMEM_SPEC] * len(blocks),
        out_specs=VMEM_SPEC,
        out_shape=jax.ShapeDtypeStruct((8, size), F32),
        compiler_params=params(),
        name="sum_chips",
    )(*blocks)


def last_kernel(*refs):
    terms, (qg_ref, kg_ref, query_ref, key_ref) = refs[:-4], refs[-4:]
    total = tree([ref[0:1, :] for ref in terms])
    query_ref[...] = total / qg_ref[...]
    key_ref[...] = total / kg_ref[...]


def gain_grads(terms, query_gain, key_gain):
    row = jax.ShapeDtypeStruct(query_gain.shape, F32)
    return pl.pallas_call(
        last_kernel,
        in_specs=[VMEM_SPEC] * (len(terms) + 2),
        out_specs=[VMEM_SPEC] * 2,
        out_shape=[row, row],
        compiler_params=params(),
        name="gain_grads",
    )(*terms, query_gain, key_gain)


def finish_kernel(*refs):
    parts, (raw_ref, kg_ref, key_ref, value_ref) = refs[:-4], refs[-4:]
    size = kg_ref.shape[1]
    shard, width = raw_ref.shape
    total = parts[0][:shard, :]
    for ref in parts[1:]:
        total = total + ref[:shard, :].astype(F32)
    for head in range(width // size):
        columns = slice(head * size, (head + 1) * size)
        unit_rows, recip = unit(raw_ref[:, columns].astype(F32))
        key_ref[:, columns] = norm_back(total[:, columns], unit_rows, recip, kg_ref[...])
    value_ref[...] = total[:, width:]


def finish(blocks, raw, key_gain):
    shape = jax.ShapeDtypeStruct(raw.shape, F32)
    return pl.pallas_call(
        finish_kernel,
        in_specs=[VMEM_SPEC] * (len(blocks) + 2),
        out_specs=[VMEM_SPEC] * 2,
        out_shape=[shape, shape],
        compiler_params=params(),
        cost_estimate=cost(10**8, 10**6),
        name="finish",
    )(*blocks, raw, key_gain)


def swap(values, axis, step):
    return lax.ppermute(values, axis, [(i, i ^ step) for i in range(lax.axis_size(axis))])


def local(
    comp_queries, comp_keys, comp_values, prompt_keys, prompt_values,
    query_gain, key_gain, out_grad, live_counts, slot_prompts,
):
    grp, tp = lax.axis_size("grp"), lax.axis_size("tp")
    shard = prompt_keys.shape[0]
    size = query_gain.shape[0]
    by_permute = shard % 16 == 0 and grp > 1 and grp & (grp - 1) == 0 and tp & (tp - 1) == 0
    slots, width = slot_prompts.shape[0], comp_keys.shape[1]
    query_gain, key_gain = query_gain.reshape(1, size), key_gain.reshape(1, size)
    mask = causal()
    mask, keys_in, values_in = lax.optimization_barrier((mask, prompt_keys, prompt_values))
    mine = pack(keys_in, values_in, key_gain)
    raw, recip, queries, grads, query_col = prepare(live_counts, comp_queries, out_grad, query_gain, slots, width)
    if by_permute:
        me = lax.axis_index("grp").astype(jnp.int32).reshape(1)
        even = [mine] + [swap(mine, "grp", step) for step in range(2, grp, 2)]
        odd = [swap(mine, "grp", 1)]
        even, queries, grads, raw, recip, query_col = lax.optimization_barrier(
            (even, queries, grads, raw, recip, query_col)
        )
        odd += [swap(piece, "grp", 1) for piece in even[1:]]
        pieces = [piece for pair in zip(even, odd) for piece in pair]
    else:
        me = jnp.zeros((1,), jnp.int32)
        pieces = [lax.all_gather(mine, "grp", axis=0, tiled=True)]
    att_t, score_grads, pool_keys, own_keys, key_grads, value_grads, term, keep, *send = attention(
        live_counts, slot_prompts, me, queries, grads, comp_keys, comp_values, key_gain, mask, pieces,
    )
    attended, query_grads = post(
        live_counts, slot_prompts, att_t, score_grads, pool_keys, own_keys, raw, recip, query_col, comp_queries.shape,
    )
    if by_permute:
        came = swap(send[0], "grp", 1)
        terms = [term] + [swap(term, "tp", step) for step in range(1, tp)]
        own, *blocks = add(keep, came, terms, grp // 2)
        blocks = [own] + [swap(block, "grp", 2 * at + 2) for at, block in enumerate(blocks)]
        blocks, attended = lax.optimization_barrier((blocks, attended))
        total = sum_chips(blocks, size)
        terms = [total, swap(total, "grp", 1)]
    else:
        blocks = [lax.psum_scatter(keep, "grp", scatter_dimension=0, tiled=True)]
        terms = [lax.psum(term, ("grp", "tp"))]
    prompt_key_grads, prompt_value_grads = finish(blocks, prompt_keys, key_gain)
    query_gain_grad, key_gain_grad = gain_grads(terms, query_gain, key_gain)
    return (
        attended, query_grads, key_grads, value_grads, prompt_key_grads, prompt_value_grads,
        query_gain_grad.reshape(size), key_gain_grad.reshape(size),
    )


def solution(mesh):
    split, whole = P("grp", "tp"), P()
    return jax.shard_map(
        local,
        mesh=mesh,
        in_specs=(split, split, split, split, split, whole, whole, split, P("grp"), P("grp")),
        out_specs=(split, split, split, split, split, split, whole, whole),
        check_vma=False,
    )
```

time: 44.4 us -> 43.1 us (0.971); the launches traced: 44.3 us -> 43.6 us
  waiting for transfers between devices: 10.4 us -> 9.04 us
  Pallas kernels: 15.1 us -> 16.1 us
    ppermute x14 -> x15, waiting for transfers between devices: 10.4 us -> 9.04 us  [swap(): lax.ppermute(values, axis, [(i, i ^ step) for i in range(lax.axis_size(ax...]
    pallas_call x1, Pallas kernels: 9.01 us -> 10 us  [attention(): pl.pallas_call(functools.partial(attention_kernel, parts=parts, heads=hea...]
    ppermute x14 -> x15, starting transfers between devices: 13.2 us -> 13.2 us  [swap(): lax.ppermute(values, axis, [(i, i ^ step) for i in range(lax.axis_size(ax...]
  transfers between devices with their start and end apart: 14 -> 15, of which waited for: 10 -> 10; matrix products, arithmetic and copies ran while one was open for 0% -> 0% of each run, Pallas kernels for 12% -> 12%
where the time goes in v2:
time: 43.1 us; the launch traced here: 43.6 us
  Pallas kernels  16.1 us (37%)
  starting transfers between devices  13.2 us (31%)
  waiting for transfers between devices  9.04 us (21%)
  local copies, waits for them, and re-layouts  3.83 us (9%)
  between operations  1.47 us (3%)
    ppermute x15, starting transfers between devices, swap(): lax.ppermute(values, axis, [(i, i ^ step) for i in range(lax.axis_size(ax...  13.2 us
    pallas_call x1, Pallas kernels, attention(): pl.pallas_call(functools.partial(attention_kernel, parts=parts, heads=hea...  10 us
    ppermute x15, waiting for transfers between devices, swap(): lax.ppermute(values, axis, [(i, i ^ step) for i in range(lax.axis_size(ax...  9.04 us
    unnamed x26, local copies, waits for them, and re-layouts  3.83 us
    pallas_call x1, Pallas kernels, post(): pl.pallas_call(post_kernel, in_specs=[SMEM_SPEC] * 2 + [VMEM_SPEC] * 7, o...  3.41 us
    pallas_call x1, Pallas kernels, prepare(): pl.pallas_call(prepare_kernel, in_specs=[SMEM_SPEC] + [VMEM_SPEC] * 3, ou...  1.05 us
  transfers between devices with their start and end apart: 15, of which 10 were waited for; matrix products, arithmetic and copies ran while one was open for 0% of the time, Pallas kernels for 12%

profile of v2, /device:TPU:0, one launch (start us, length us, event | category | flops | bytes accessed | tf_op | source)
XLA Modules:
  0.0 43.6 jit_solution(2851408392433727866)
XLA Ops:
  0.6 0.0 copy-start
  0.6 0.0 copy-start.7
  0.7 0.0 copy-start.1
  0.7 0.0 copy-start.11
  0.7 0.7 %copy-done = bf16[96,256]{1,0:T(8,128)(2,1)S(1)} copy-done((bf16[96,256]{1,0:T(8,128)(2,1)S(1)}, bf16[96,256]{1,0:T(8,128)(2,1)}, u32[]{:S(2)}) %copy-start) | copy-done | bytes 49176
  1.4 0.0 copy-done.7
  1.5 0.0 copy-done.1
  1.5 0.0 copy-start.2
  1.5 0.0 copy-start.3
  1.5 0.0 copy-start.4
  1.5 0.1 pack.1.refs_9_
  1.6 0.0 copy-done.11
  1.6 0.5 %collective-permute-start.3 = (bf16[96,512]{1,0:T(8,128)(2,1)S(1)}, bf16[96,512]{1,0:T(8,128)(2,1)S(1)}, u32[]{:S(2)}, u32[]{:S(2)}) collective-permute-start(bf16[96,512]{1,0:T(8,128)(2,1)S(1)} %pack.1.refs_9_), channel_id=1, source_target_pairs={{0,4},{4,0},{8,12},{12,8},{16,20},{20,16},{24,28},{28,24},{1,5},{5... | collective-permute-start | bytes 294920 | tf_op jit(solution)/shard_map/ppermute | solution.py:485
  2.1 3.5 %collective-permute-start.2 = (bf16[96,512]{1,0:T(8,128)(2,1)S(1)}, bf16[96,512]{1,0:T(8,128)(2,1)S(1)}, u32[]{:S(2)}, u32[]{:S(2)}) collective-permute-start(bf16[96,512]{1,0:T(8,128)(2,1)S(1)} %pack.1.refs_9_), channel_id=1, source_target_pairs={{0,24},{4,28},{8,16},{12,20},{16,8},{20,12},{24,0},{28,4},{1,25},{... | collective-permute-start | bytes 294920 | tf_op jit(solution)/shard_map/ppermute | solution.py:485
  5.6 0.5 %collective-permute-start.1 = (bf16[96,512]{1,0:T(8,128)(2,1)S(1)}, bf16[96,512]{1,0:T(8,128)(2,1)S(1)}, u32[]{:S(2)}, u32[]{:S(2)}) collective-permute-start(bf16[96,512]{1,0:T(8,128)(2,1)S(1)} %pack.1.refs_9_), channel_id=1, source_target_pairs={{0,16},{4,20},{8,24},{12,28},{16,0},{20,4},{24,8},{28,12},{1,17},{... | collective-permute-start | bytes 294920 | tf_op jit(solution)/shard_map/ppermute | solution.py:485
  6.1 0.1 collective-permute-start
  6.9 0.0 copy-done.2
  6.9 0.0 copy-done.3
  7.0 0.0 copy-done.4
  7.0 0.0 copy-start.5
  7.0 0.0 copy-start.6
  7.0 0.0 copy-start.8
  7.0 1.1 %prepare.1 = (bf16[4,256,512]{2,1,0:T(8,128)(2,1)S(1)}, f32[4,8,512]{2,1,0:T(8,128)S(1)}, bf16[4,256,512]{2,1,0:T(8,128)(2,1)S(1)}, bf16[4,256,512]{2,1,0:T(8,128)(2,1)S(1)}, f32[128,512]{1,0:T(8,128)S(1)}) custom-call(s32[1]{0:T(128)S(6)} %copy.18.live_ref.refs_0_, bf16[256,2048]{1,0:T(8,128)(2,1)S(1)} %copy-done.3, bf16[256,2048]{1,0:T(8,128)(2,1)S(1)} %copy-done.4, ...), custom_call_target="tpu_custom_call" | custom-call | flops 2000000000 | bytes 3145728 | tf_op jit(solution)/shard_map/prepare/pallas_call | solution.py:142
  8.1 0.0 copy-start.9
  8.1 1.0 %copy-done.9 = bf16[4,256,512]{2,1,0:T(8,128)(2,1)} copy-done((bf16[4,256,512]{2,1,0:T(8,128)(2,1)}, bf16[4,256,512]{2,1,0:T(8,128)(2,1)S(1)}, u32[]{:S(2)}) %copy-start.9) | copy-done | bytes 1048600
  9.0 0.1 collective-permute-done.2.refs_15_
  9.1 2.0 %collective-permute-done.1.refs_13_ = bf16[96,512]{1,0:T(8,128)(2,1)S(1)} collective-permute-done((bf16[96,512]{1,0:T(8,128)(2,1)S(1)}, bf16[96,512]{1,0:T(8,128)(2,1)S(1)}, u32[]{:S(2)}, u32[]{:S(2)}) %collective-permute-start.1) | collective-permute-done | bytes 98336 | tf_op jit(solution)/shard_map/ppermute | solution.py:485
  11.1 0.3 collective-permute-done.refs_11_
  11.4 0.0 collective-permute-start.4
  11.4 0.5 %collective-permute-start.5 = (bf16[96,512]{1,0:T(8,128)(2,1)S(1)}, bf16[96,512]{1,0:T(8,128)(2,1)S(1)}, u32[]{:S(2)}, u32[]{:S(2)}) collective-permute-start(bf16[96,512]{1,0:T(8,128)(2,1)S(1)} %collective-permute-done.1.refs_13_), channel_id=1, source_target_pairs={{0,4},{4,0},{8,12},{12,8},{16,20},{20,16},{24,28},{28,24},{1,5},{5... | collective-permute-start | bytes 294920 | tf_op jit(solution)/shard_map/ppermute | solution.py:485
  11.9 0.0 collective-permute-start.6
  11.9 0.0 collective-permute-done.3.refs_10_
  11.9 0.8 %collective-permute-done.4.refs_12_ = bf16[96,512]{1,0:T(8,128)(2,1)S(1)} collective-permute-done((bf16[96,512]{1,0:T(8,128)(2,1)S(1)}, bf16[96,512]{1,0:T(8,128)(2,1)S(1)}, u32[]{:S(2)}, u32[]{:S(2)}) %collective-permute-start.4) | collective-permute-done | bytes 98336 | tf_op jit(solution)/shard_map/ppermute | solution.py:485
  12.7 0.2 collective-permute-done.5.refs_14_
  12.9 0.4 collective-permute-done.6.refs_16_
  13.2 0.0 copy-done.5
  13.2 0.0 copy-done.6
  13.2 0.0 copy-done.8
  13.2 0.0 copy-start.10
  13.2 1.2 %copy-done.10 = bf16[4,256,512]{2,1,0:T(8,128)(2,1)S(1)} copy-done((bf16[4,256,512]{2,1,0:T(8,128)(2,1)S(1)}, bf16[4,256,512]{2,1,0:T(8,128)(2,1)}, u32[]{:S(2)}) %copy-start.10) | copy-done | bytes 1048600
  14.5 0.0 copy-start.12
  14.5 0.8 %copy-done.12 = f32[64,256]{1,0:T(8,128)S(1)} copy-done((f32[64,256]{1,0:T(8,128)S(1)}, f32[64,256]{1,0:T(8,128)}, u32[]{:S(2)}) %copy-start.12) | copy-done | bytes 65560
  15.3 10.0 %attention.1 = (bf16[4,256,512]{2,1,0:T(8,128)(2,1)S(1)}, bf16[4,2,448,512]{3,2,1,0:T(8,128)(2,1)S(1)}, bf16[768,256]{1,0:T(8,128)(2,1)S(1)}, bf16[256,256]{1,0:...) custom-call(s32[1]{0:T(128)S(6)} %copy.18.live_ref.refs_0_, ...), custom_call_target="tpu_custom_call" | custom-call | flops 3000000000 | bytes 10000000 | tf_op jit(solution)/shard_map/attention/pallas_call | solution.py:310
  25.3 0.0 collective-permute-start.7
  25.3 3.6 %collective-permute-start.10 = (f32[8,128]{1,0:T(8,128)S(1)}, f32[8,128]{1,0:T(8,128)S(1)}, u32[]{:S(2)}, u32[]{:S(2)}) collective-permute-start(f32[8,128]{1,0:T(8,128)S(1)} %get-tuple-element.65.refs_0_), channel_id=1, source_target_pairs={{0,3},{1,2},{2,1},{3,0},{4,7},{5,6},{6,5},{7,4},{8,11},{9,10},{10,... | collective-permute-start | bytes 12296 | tf_op jit(solution)/shard_map/ppermute | solution.py:485
  28.9 0.0 collective-permute-start.9
  28.9 0.8 %collective-permute-start.8 = (f32[8,128]{1,0:T(8,128)S(1)}, f32[8,128]{1,0:T(8,128)S(1)}, u32[]{:S(2)}, u32[]{:S(2)}) collective-permute-start(f32[8,128]{1,0:T(8,128)S(1)} %get-tuple-element.65.refs_0_), channel_id=1, source_target_pairs={{0,1},{1,0},{2,3},{3,2},{4,5},{5,4},{6,7},{7,6},{8,9},{9,8},{10,11... | collective-permute-start | bytes 12296 | tf_op jit(solution)/shard_map/ppermute | solution.py:485
  29.7 1.0 %collective-permute-done.10.refs_3_ = f32[8,128]{1,0:T(8,128)S(1)} collective-permute-done((f32[8,128]{1,0:T(8,128)S(1)}, f32[8,128]{1,0:T(8,128)S(1)}, u32[]{:S(2)}, u32[]{:S(2)}) %collective-permute-start.10) | collective-permute-done | bytes 4128 | tf_op jit(solution)/shard_map/ppermute | solution.py:485
  30.7 2.7 %collective-permute-done.9.refs_2_ = f32[8,128]{1,0:T(8,128)S(1)} collective-permute-done((f32[8,128]{1,0:T(8,128)S(1)}, f32[8,128]{1,0:T(8,128)S(1)}, u32[]{:S(2)}, u32[]{:S(2)}) %collective-permute-start.9) | collective-permute-done | bytes 4128 | tf_op jit(solution)/shard_map/ppermute | solution.py:485
  33.4 0.0 collective-permute-done.8.refs_1_
  33.4 0.0 collective-permute-done.7.came_ref
  33.4 0.1 add.1
  33.5 1.8 %collective-permute-start.11 = (bf16[112,512]{1,0:T(8,128)(2,1)S(1)}, bf16[112,512]{1,0:T(8,128)(2,1)S(1)}, u32[]{:S(2)}, u32[]{:S(2)}) collective-permute-start(bf16[112,512]{1,0:T(8,128)(2,1)S(1)} %get-tuple-element.67), channel_id=1, source_target_pairs={{0,8},{4,12},{8,0},{12,4},{16,24},{20,28},{24,16},{28,20},{1,9},{5... | collective-permute-start | bytes 344072 | tf_op jit(solution)/shard_map/ppermute | solution.py:485
  35.3 0.7 %collective-permute-start.12 = (bf16[112,512]{1,0:T(8,128)(2,1)S(1)}, bf16[112,512]{1,0:T(8,128)(2,1)S(1)}, u32[]{:S(2)}, u32[]{:S(2)}) collective-permute-start(bf16[112,512]{1,0:T(8,128)(2,1)S(1)} %get-tuple-element.68), channel_id=1, source_target_pairs={{0,16},{4,20},{8,24},{12,28},{16,0},{20,4},{24,8},{28,12},{1,17},{... | collective-permute-start | bytes 344072 | tf_op jit(solution)/shard_map/ppermute | solution.py:485
  36.0 1.1 %collective-permute-start.13 = (bf16[112,512]{1,0:T(8,128)(2,1)S(1)}, bf16[112,512]{1,0:T(8,128)(2,1)S(1)}, u32[]{:S(2)}, u32[]{:S(2)}) collective-permute-start(bf16[112,512]{1,0:T(8,128)(2,1)S(1)} %get-tuple-element.69), channel_id=1, source_target_pairs={{0,24},{4,28},{8,16},{12,20},{16,8},{20,12},{24,0},{28,4},{1,25},{... | collective-permute-start | bytes 344072 | tf_op jit(solution)/shard_map/ppermute | solution.py:485
  37.1 3.4 %post.1 = (bf16[256,2048]{1,0:T(8,128)(2,1)}, bf16[256,2048]{1,0:T(8,128)(2,1)}) custom-call(s32[1]{0:T(128)S(6)} %copy.18.live_ref.refs_0_, s32[4]{0:T(128)S(1)} %copy-done.8, bf16[4,256,512]{2,1,0:T(8,128)(2,1)S(1)} %get-tuple-element.70.att_t_ref, bf16[4,2,448,512]{3,2,1,0:T(8,128)(2,1)S(1)} %get-tuple-element.71.ds_ref, ...), custom_call_target="tpu_custom_call" | custom-call | flops 3000000000 | bytes 4000000 | tf_op jit(solution)/shard_map/post/pallas_call | solution.py:379
  40.5 0.0 collective-permute-done.11.refs_1_
  40.5 1.3 %collective-permute-done.12.refs_2_ = bf16[112,512]{1,0:T(8,128)(2,1)S(1)} collective-permute-done((bf16[112,512]{1,0:T(8,128)(2,1)S(1)}, bf16[112,512]{1,0:T(8,128)(2,1)S(1)}, u32[]{:S(2)}, u32[]{:S(2)}) %collective-permute-start.12) | collective-permute-done | bytes 114720 | tf_op jit(solution)/shard_map/ppermute | solution.py:485
  41.8 0.0 collective-permute-done.13.refs_3_
  41.8 0.1 collective-permute-start.14
  41.9 0.8 %finish.1 = (f32[96,256]{1,0:T(8,128)}, f32[96,256]{1,0:T(8,128)}) custom-call(f32[112,512]{1,0:T(8,128)S(1)} %get-tuple-element.82.refs_0_, bf16[112,512]{1,0:T(8,128)(2,1)S(1)} %collective-permute-done.11.refs_1_, bf16[112,512]{1,0:T(8,128)(2,1)S(1)} %collective-permute-done.12.refs_2_, bf16[112,512]{1,0:T(8,128)(2,1)S(1)} %collective-permute-done.13.refs_3_, ...), custom_call_target="tpu_custom_call" | custom-call | flops 100000000 | bytes 1000000 | tf_op jit(solution)/shard_map/finish/pallas_call | solution.py:473
  42.8 0.3 collective-permute-done.14.refs_1_
  43.1 0.5 %gain_grads.1 = (f32[1,128]{1,0:T(1,128)}, f32[1,128]{1,0:T(1,128)}) custom-call(f32[8,128]{1,0:T(8,128)S(1)} %sum_chips.1.refs_0_, f32[8,128]{1,0:T(8,128)S(1)} %collective-permute-done.14.refs_1_, f32[1,128]{1,0:T(1,128)S(1)} %bitcast.10, f32[1,128]{1,0:T(1,128)S(1)} %bitcast.8), custom_call_target="tpu_custom_call" | custom-call | tf_op jit(solution)/shard_map/gain_grads/pallas_call | solution.py:447
  (2 shorter events, 0.0 us)
Async XLA Ops:
  0.6 0.8 %copy-start = (bf16[96,256]{1,0:T(8,128)(2,1)S(1)}, bf16[96,256]{1,0:T(8,128)(2,1)}, u32[]{:S(2)}) copy-start(bf16[96,256]{1,0:T(8,128)(2,1)} %refs_4_.1) | copy-start | bytes 147460
  0.6 0.8 %copy-start.7 = (bf16[96,256]{1,0:T(8,128)(2,1)S(1)}, bf16[96,256]{1,0:T(8,128)(2,1)}, u32[]{:S(2)}) copy-start(bf16[96,256]{1,0:T(8,128)(2,1)} %values_ref) | copy-start | bytes 147460
  0.7 0.8 %copy-start.1 = (f32[128]{0:T(128)S(1)}, f32[128]{0:T(128)}, u32[]{:S(2)}) copy-start(f32[128]{0:T(128)} %param.16) | copy-start | bytes 1540
  0.7 0.9 %copy-start.11 = (f32[64,256]{1,0:T(8,128)}, f32[64,256]{1,0:T(8,128)S(1)}, u32[]{:S(2)}) copy-start(f32[64,256]{1,0:T(8,128)S(1)} %causal.1.refs_8_) | copy-start | bytes 196612
  1.5 5.5 %copy-start.2 = (f32[128]{0:T(128)S(1)}, f32[128]{0:T(128)}, u32[]{:S(2)}) copy-start(f32[128]{0:T(128)} %param.15) | copy-start | bytes 1540
  1.5 5.5 %copy-start.3 = (bf16[256,2048]{1,0:T(8,128)(2,1)S(1)}, bf16[256,2048]{1,0:T(8,128)(2,1)}, u32[]{:S(2)}) copy-start(bf16[256,2048]{1,0:T(8,128)(2,1)} %q_ref.1) | copy-start | bytes 3145732
  1.5 5.5 %copy-start.4 = (bf16[256,2048]{1,0:T(8,128)(2,1)S(1)}, bf16[256,2048]{1,0:T(8,128)(2,1)}, u32[]{:S(2)}) copy-start(bf16[256,2048]{1,0:T(8,128)(2,1)} %do_ref.1) | copy-start | bytes 3145732
  1.6 10.3 %collective-permute-start.3 = (bf16[96,512]{1,0:T(8,128)(2,1)S(1)}, bf16[96,512]{1,0:T(8,128)(2,1)S(1)}, u32[]{:S(2)}, u32[]{:S(2)}) collective-permute-start(bf16[96,512]{1,0:T(8,128)(2,1)S(1)} %pack.1.refs_9_), channel_id=1, source_target_pairs={{0,4},{4,0},{8,12},{12,8},{16,20},{20,16},{24,28},{28,24},{1,5},{5... | collective-permute-start | bytes 294920 | tf_op jit(solution)/shard_map/ppermute | solution.py:485
  2.1 7.0 %collective-permute-start.2 = (bf16[96,512]{1,0:T(8,128)(2,1)S(1)}, bf16[96,512]{1,0:T(8,128)(2,1)S(1)}, u32[]{:S(2)}, u32[]{:S(2)}) collective-permute-start(bf16[96,512]{1,0:T(8,128)(2,1)S(1)} %pack.1.refs_9_), channel_id=1, source_target_pairs={{0,24},{4,28},{8,16},{12,20},{16,8},{20,12},{24,0},{28,4},{1,25},{... | collective-permute-start | bytes 294920 | tf_op jit(solution)/shard_map/ppermute | solution.py:485
  5.6 5.5 %collective-permute-start.1 = (bf16[96,512]{1,0:T(8,128)(2,1)S(1)}, bf16[96,512]{1,0:T(8,128)(2,1)S(1)}, u32[]{:S(2)}, u32[]{:S(2)}) collective-permute-start(bf16[96,512]{1,0:T(8,128)(2,1)S(1)} %pack.1.refs_9_), channel_id=1, source_target_pairs={{0,16},{4,20},{8,24},{12,28},{16,0},{20,4},{24,8},{28,12},{1,17},{... | collective-permute-start | bytes 294920 | tf_op jit(solution)/shard_map/ppermute | solution.py:485
  6.1 5.3 %collective-permute-start = (bf16[96,512]{1,0:T(8,128)(2,1)S(1)}, bf16[96,512]{1,0:T(8,128)(2,1)S(1)}, u32[]{:S(2)}, u32[]{:S(2)}) collective-permute-start(bf16[96,512]{1,0:T(8,128)(2,1)S(1)} %pack.1.refs_9_), channel_id=1, source_target_pairs={{0,8},{4,12},{8,0},{12,4},{16,24},{20,28},{24,16},{28,20},{1,9},{5... | collective-permute-start | bytes 294920 | tf_op jit(solution)/shard_map/ppermute | solution.py:485
  7.0 6.3 %copy-start.5 = (bf16[256,256]{1,0:T(8,128)(2,1)S(1)}, bf16[256,256]{1,0:T(8,128)(2,1)}, u32[]{:S(2)}) copy-start(bf16[256,256]{1,0:T(8,128)(2,1)} %refs_5_.1) | copy-start | bytes 393220
  7.0 6.2 %copy-start.6 = (bf16[256,256]{1,0:T(8,128)(2,1)S(1)}, bf16[256,256]{1,0:T(8,128)(2,1)}, u32[]{:S(2)}) copy-start(bf16[256,256]{1,0:T(8,128)(2,1)} %refs_6_.1) | copy-start | bytes 393220
  7.0 6.2 %copy-start.8 = (s32[4]{0:T(128)S(1)}, s32[4]{0:T(128)}, u32[]{:S(2)}) copy-start(s32[4]{0:T(128)} %prompt_ref.1) | copy-start | bytes 52
  8.1 1.0 %copy-start.9 = (bf16[4,256,512]{2,1,0:T(8,128)(2,1)}, bf16[4,256,512]{2,1,0:T(8,128)(2,1)S(1)}, u32[]{:S(2)}) copy-start(bf16[4,256,512]{2,1,0:T(8,128)(2,1)S(1)} %get-tuple-element.57.refs_4_) | copy-start | bytes 3145732
  11.4 1.3 %collective-permute-start.4 = (bf16[96,512]{1,0:T(8,128)(2,1)S(1)}, bf16[96,512]{1,0:T(8,128)(2,1)S(1)}, u32[]{:S(2)}, u32[]{:S(2)}) collective-permute-start(bf16[96,512]{1,0:T(8,128)(2,1)S(1)} %collective-permute-done.refs_11_), channel_id=1, source_target_pairs={{0,4},{4,0},{8,12},{12,8},{16,20},{20,16},{24,28},{28,24},{1,5},{5... | collective-permute-start | bytes 294920 | tf_op jit(solution)/shard_map/ppermute | solution.py:485
  11.4 1.5 %collective-permute-start.5 = (bf16[96,512]{1,0:T(8,128)(2,1)S(1)}, bf16[96,512]{1,0:T(8,128)(2,1)S(1)}, u32[]{:S(2)}, u32[]{:S(2)}) collective-permute-start(bf16[96,512]{1,0:T(8,128)(2,1)S(1)} %collective-permute-done.1.refs_13_), channel_id=1, source_target_pairs={{0,4},{4,0},{8,12},{12,8},{16,20},{20,16},{24,28},{28,24},{1,5},{5... | collective-permute-start | bytes 294920 | tf_op jit(solution)/shard_map/ppermute | solution.py:485
  11.9 1.3 %collective-permute-start.6 = (bf16[96,512]{1,0:T(8,128)(2,1)S(1)}, bf16[96,512]{1,0:T(8,128)(2,1)S(1)}, u32[]{:S(2)}, u32[]{:S(2)}) collective-permute-start(bf16[96,512]{1,0:T(8,128)(2,1)S(1)} %collective-permute-done.2.refs_15_), channel_id=1, source_target_pairs={{0,4},{4,0},{8,12},{12,8},{16,20},{20,16},{24,28},{28,24},{1,5},{5... | collective-permute-start | bytes 294920 | tf_op jit(solution)/shard_map/ppermute | solution.py:485
  13.2 1.2 %copy-start.10 = (bf16[4,256,512]{2,1,0:T(8,128)(2,1)S(1)}, bf16[4,256,512]{2,1,0:T(8,128)(2,1)}, u32[]{:S(2)}) copy-start(bf16[4,256,512]{2,1,0:T(8,128)(2,1)} %copy-done.9) | copy-start | bytes 3145732
  14.5 0.8 %copy-start.12 = (f32[64,256]{1,0:T(8,128)S(1)}, f32[64,256]{1,0:T(8,128)}, u32[]{:S(2)}) copy-start(f32[64,256]{1,0:T(8,128)} %copy-done.11) | copy-start | bytes 196612
  25.3 8.1 %collective-permute-start.7 = (bf16[384,512]{1,0:T(8,128)(2,1)S(1)}, bf16[384,512]{1,0:T(8,128)(2,1)S(1)}, u32[]{:S(2)}, u32[]{:S(2)}) collective-permute-start(bf16[384,512]{1,0:T(8,128)(2,1)S(1)} %get-tuple-element.64), channel_id=1, source_target_pairs={{0,4},{4,0},{8,12},{12,8},{16,20},{20,16},{24,28},{28,24},{1,5},{5... | collective-permute-start | bytes 1179656 | tf_op jit(solution)/shard_map/ppermute | solution.py:485
  25.3 5.4 %collective-permute-start.10 = (f32[8,128]{1,0:T(8,128)S(1)}, f32[8,128]{1,0:T(8,128)S(1)}, u32[]{:S(2)}, u32[]{:S(2)}) collective-permute-start(f32[8,128]{1,0:T(8,128)S(1)} %get-tuple-element.65.refs_0_), channel_id=1, source_target_pairs={{0,3},{1,2},{2,1},{3,0},{4,7},{5,6},{6,5},{7,4},{8,11},{9,10},{10,... | collective-permute-start | bytes 12296 | tf_op jit(solution)/shard_map/ppermute | solution.py:485
  28.9 4.5 %collective-permute-start.9 = (f32[8,128]{1,0:T(8,128)S(1)}, f32[8,128]{1,0:T(8,128)S(1)}, u32[]{:S(2)}, u32[]{:S(2)}) collective-permute-start(f32[8,128]{1,0:T(8,128)S(1)} %get-tuple-element.65.refs_0_), channel_id=1, source_target_pairs={{0,2},{1,3},{2,0},{3,1},{4,6},{5,7},{6,4},{7,5},{8,10},{9,11},{10,... | collective-permute-start | bytes 12296 | tf_op jit(solution)/shard_map/ppermute | solution.py:485
  28.9 4.5 %collective-permute-start.8 = (f32[8,128]{1,0:T(8,128)S(1)}, f32[8,128]{1,0:T(8,128)S(1)}, u32[]{:S(2)}, u32[]{:S(2)}) collective-permute-start(f32[8,128]{1,0:T(8,128)S(1)} %get-tuple-element.65.refs_0_), channel_id=1, source_target_pairs={{0,1},{1,0},{2,3},{3,2},{4,5},{5,4},{6,7},{7,6},{8,9},{9,8},{10,11... | collective-permute-start | bytes 12296 | tf_op jit(solution)/shard_map/ppermute | solution.py:485
  33.5 7.0 %collective-permute-start.11 = (bf16[112,512]{1,0:T(8,128)(2,1)S(1)}, bf16[112,512]{1,0:T(8,128)(2,1)S(1)}, u32[]{:S(2)}, u32[]{:S(2)}) collective-permute-start(bf16[112,512]{1,0:T(8,128)(2,1)S(1)} %get-tuple-element.67), channel_id=1, source_target_pairs={{0,8},{4,12},{8,0},{12,4},{16,24},{20,28},{24,16},{28,20},{1,9},{5... | collective-permute-start | bytes 344072 | tf_op jit(solution)/shard_map/ppermute | solution.py:485
  35.3 6.5 %collective-permute-start.12 = (bf16[112,512]{1,0:T(8,128)(2,1)S(1)}, bf16[112,512]{1,0:T(8,128)(2,1)S(1)}, u32[]{:S(2)}, u32[]{:S(2)}) collective-permute-start(bf16[112,512]{1,0:T(8,128)(2,1)S(1)} %get-tuple-element.68), channel_id=1, source_target_pairs={{0,16},{4,20},{8,24},{12,28},{16,0},{20,4},{24,8},{28,12},{1,17},{... | collective-permute-start | bytes 344072 | tf_op jit(solution)/shard_map/ppermute | solution.py:485
  36.0 5.8 %collective-permute-start.13 = (bf16[112,512]{1,0:T(8,128)(2,1)S(1)}, bf16[112,512]{1,0:T(8,128)(2,1)S(1)}, u32[]{:S(2)}, u32[]{:S(2)}) collective-permute-start(bf16[112,512]{1,0:T(8,128)(2,1)S(1)} %get-tuple-element.69), channel_id=1, source_target_pairs={{0,24},{4,28},{8,16},{12,20},{16,8},{20,12},{24,0},{28,4},{1,25},{... | collective-permute-start | bytes 344072 | tf_op jit(solution)/shard_map/ppermute | solution.py:485
  41.8 1.2 %collective-permute-start.14 = (f32[8,128]{1,0:T(8,128)S(1)}, f32[8,128]{1,0:T(8,128)S(1)}, u32[]{:S(2)}, u32[]{:S(2)}) collective-permute-start(f32[8,128]{1,0:T(8,128)S(1)} %sum_chips.1.refs_0_), channel_id=1, source_target_pairs={{0,4},{4,0},{8,12},{12,8},{16,20},{20,16},{24,28},{28,24},{1,5},{5... | collective-permute-start | bytes 12296 | tf_op jit(solution)/shard_map/ppermute | solution.py:485

commit v3 on v2

--- a/solution.py
+++ b/solution.py
@@ -156,18 +156,18 @@
 def attention_kernel(*refs, parts, heads):
     live_ref, prompt_ref, me_ref, queries_ref, grads_ref, ck_ref, cv_ref, kg_ref, mask_ref = refs[:9]
     pieces, refs = refs[9:9 + parts], refs[9 + parts:]
-    att_ref, ds_ref, pool_keys, own_keys, dk_ref, dv_ref, term_ref, keep_ref = refs[:8]
-    send_ref, refs = (refs[8], refs[9:]) if parts > 1 else (None, refs[8:])
-    acc, own_acc, pool_values, pool_values_t, own_values_t = refs[:5]
+    att_ref, ds_ref, pool_keys, own_keys, own_acc, term_ref, keep_ref = refs[:7]
+    send_ref, refs = (refs[7], refs[8:]) if parts > 1 else (None, refs[7:])
+    acc, pool_values, pool_values_t, own_values_t = refs[:4]
     size = kg_ref.shape[1]
     width = heads * size
     slots, _, lanes = queries_ref.shape
     per_head = lanes // CHUNK
     count = heads * per_head
-    scores, weights, summed, grads, prob_grads, deltas = (refs[5 + at * count:5 + (at + 1) * count] for at in range(6))
+    weights, grads = refs[4:4 + heads], refs[4 + heads:4 + 2 * heads]
+    scores, summed = refs[4 + 2 * heads:4 + 2 * heads + count], refs[4 + 2 * heads + count:]
     score_scale = 1.0 / math.sqrt(size)
     shard = pieces[0].shape[0]
-    pool_rows = parts * shard
 
     def columns(head):
         return slice(head * size, (head + 1) * size)
@@ -186,94 +186,82 @@
         own_keys[:, columns(head)] = (own_unit * kg_ref[...]).astype(BF16)
         for slot in range(slots):
             own_values_t[slot, head] = cv_ref[slot * CL:(slot + 1) * CL, columns(head)].T
-    alive = live_ref[0]
-
-    def step(turn, carry):
-        now, before = jnp.minimum(turn, alive - 1), jnp.maximum(turn - 1, 0)
-        slot_of = {True: now, False: before}
-        rows_of = {True: prompt_ref[now] * PL, False: prompt_ref[before] * PL}
-        target_of = {
-            True: jnp.where(turn < alive, rows_of[True], pool_rows),
-            False: jnp.where(turn > 0, rows_of[False], pool_rows),
-        }
-        own_of = {True: jnp.where(turn < alive, turn, slots), False: jnp.where(turn > 0, turn - 1, slots)}
-
-        def prompt_rows(at):
-            return pl.ds(pl.multiple_of(at, PL), PL)
-
-        def part(no):
-            head = no // per_head
-            return head, columns(head), slice(no % per_head * CHUNK, (no % per_head + 1) * CHUNK)
-
-        def begin(no, fresh):
-            _, place, span = part(no)
-            keys = jnp.concatenate(
-                [pool_keys[prompt_rows(rows_of[fresh]), place], own_keys[slot_rows(slot_of[fresh]), place]], axis=0
-            )
-            scores[no][...] = dot(keys, queries_ref[slot_of[fresh], place, span])
-
-        def weigh(no, fresh):
-            head, place, _ = part(no)
-            prompt, own = scores[no][:PL, :], scores[no][PL:, :] + mask_ref[...]
-            factor = score_scale * math.log2(math.e)
-            high = jnp.maximum(jnp.max(prompt, axis=0, keepdims=True), jnp.max(own, axis=0, keepdims=True))
-            both = jnp.concatenate([prompt, own], axis=0)
-            half = jnp.exp2((both - high) * factor).astype(BF16)
-            weights[no][...] = half
-            values_t = jnp.concatenate(
-                [pool_values_t[place, prompt_rows(rows_of[fresh])], own_values_t[slot_of[fresh], head]], axis=1
-            )
-            values_t = jnp.concatenate([values_t, jnp.ones((TAIL, PL + CL), BF16)], axis=0)
-            summed[no][...] = dot(values_t, half)
-
-        def attend(no, fresh):
-            _, place, span = part(no)
-            inverse = 1.0 / summed[no][size:size + 1, :]
-            attended = (summed[no][:size, :] * inverse).astype(BF16)
-            att_ref[slot_of[fresh], place, span] = attended
-            scaled = (grads_ref[slot_of[fresh], place, span].astype(F32) * inverse).astype(BF16)
-            grads[no][...] = scaled
-            delta = jnp.sum(scaled.astype(F32) * attended.astype(F32), axis=0, keepdims=True)
-            deltas[no][...] = jnp.broadcast_to(delta, deltas[no].shape)
-            values = jnp.concatenate(
-                [pool_values[prompt_rows(rows_of[fresh]), place], cv_ref[slot_rows(slot_of[fresh]), place]], axis=0
-            )
-            prob_grads[no][...] = dot(values, scaled)
-
-        def back(no, fresh):
-            head, place, span = part(no)
-            half = weights[no][...]
-            score_grad = (half.astype(F32) * (prob_grads[no][...] - deltas[no][0:1, :])).astype(BF16)
-            ds_ref[slot_of[fresh], head, :, span] = score_grad
-            value_grad = dot_nt(half, grads[no][...])
-            key_grad = dot_nt(score_grad, queries_ref[slot_of[fresh], place, span])
-            target = prompt_rows(target_of[fresh])
-            acc[target, place] += key_grad[:PL]
-            acc[target, width + head * size:width + (head + 1) * size] += value_grad[:PL]
-            own_acc[own_of[fresh], head, 0] += key_grad[PL:]
-            own_acc[own_of[fresh], head, 1] += value_grad[PL:]
-
-        stages = (begin, weigh, attend, back)
+
+    def prompt_rows(slot):
+        return pl.ds(pl.multiple_of(prompt_ref[slot] * PL, PL), PL)
+
+    def part(no):
+        head = no // per_head
+        return head, columns(head), slice(no % per_head * CHUNK, (no % per_head + 1) * CHUNK)
+
+    def begin(slot, no):
+        _, place, span = part(no)
+        keys = jnp.concatenate([pool_keys[prompt_rows(slot), place], own_keys[slot_rows(slot), place]], axis=0)
+        scores[no][...] = dot(keys, queries_ref[slot, place, span])
+
+    def weigh(slot, no):
+        head, place, span = part(no)
+        prompt, own = scores[no][:PL, :], scores[no][PL:, :] + mask_ref[...]
+        factor = score_scale * math.log2(math.e)
+        high = jnp.maximum(jnp.max(prompt, axis=0, keepdims=True), jnp.max(own, axis=0, keepdims=True))
+        both = jnp.concatenate([prompt, own], axis=0)
+        half = jnp.exp2((both - high) * factor).astype(BF16)
+        weights[head][:, span] = half
+        values_t = jnp.concatenate([pool_values_t[place, prompt_rows(slot)], own_values_t[slot, head]], axis=1)
+        values_t = jnp.concatenate([values_t, jnp.ones((TAIL, PL + CL), BF16)], axis=0)
+        summed[no][...] = dot(values_t, half)
+
+    def back(slot, no):
+        head, place, span = part(no)
+        inverse = 1.0 / summed[no][size:size + 1, :]
+        attended = (summed[no][:size, :] * inverse).astype(BF16)
+        att_ref[slot, place, span] = attended
+        scaled = (grads_ref[slot, place, span].astype(F32) * inverse).astype(BF16)
+        grads[head][:, span] = scaled
+        delta = jnp.sum(scaled.astype(F32) * attended.astype(F32), axis=0, keepdims=True)
+        values = jnp.concatenate([pool_values[prompt_rows(slot), place], cv_ref[slot_rows(slot), place]], axis=0)
+        score_grad = weights[head][:, span].astype(F32) * (dot(values, scaled) - delta)
+        ds_ref[slot, head, :, span] = score_grad.astype(BF16)
+
+    def close(slot, head):
+        value_grad = dot_nt(weights[head][...], grads[head][...])
+        key_grad = dot_nt(ds_ref[slot, head], queries_ref[slot, columns(head), :])
+        acc[prompt_rows(slot), columns(head)] += key_grad[:PL]
+        acc[prompt_rows(slot), width + head * size:width + (head + 1) * size] += value_grad[:PL]
+        own_acc[slot, head, 0] = key_grad[PL:]
+        own_acc[slot, head, 1] = value_grad[PL:]
+
+    def ticks(now, before):
         for tick in range(count):
-            for number, stage in enumerate(stages):
-                stage((tick - number) % count, tick >= number)
+            if now is not None:
+                begin(now, tick)
+            for number, stage in ((1, weigh), (2, back)):
+                slot = now if tick >= number else before
+                if slot is not None:
+                    stage(slot, (tick - number) % count)
+            done = (tick - 3) % count
+            slot = now if tick >= 3 else before
+            if slot is not None and done % per_head == per_head - 1:
+                close(slot, done // per_head)
+
+    def step(slot, carry):
+        ticks(slot, slot - 1)
         return carry
 
-    lax.fori_loop(0, alive + 1, step, 0)
+    ticks(0, None)
+    lax.fori_loop(1, live_ref[0], step, 0)
+    ticks(None, live_ref[0] - 1)
 
     total = jnp.zeros((1, size), F32)
     for head in range(heads):
-        own_grad = own_acc[:slots, head, 0].reshape(slots * CL, size) * score_scale
-        own_unit, own_recip = unit(ck_ref[:, columns(head)].astype(F32))
-        dk_ref[:, columns(head)] = norm_back(own_grad, own_unit, own_recip, kg_ref[...]).astype(BF16)
-        dv_ref[:, columns(head)] = own_acc[:slots, head, 1].reshape(slots * CL, size).astype(BF16)
+        own_grad = own_acc[:, head, 0].reshape(slots * CL, size)
         total = total + jnp.sum(own_grad * own_keys[:, columns(head)].astype(F32), axis=0, keepdims=True)
-        pool_term = acc[:pool_rows, columns(head)] * pool_keys[:, columns(head)].astype(F32)
-        total = total + jnp.sum(pool_term, axis=0, keepdims=True) * score_scale
-    term_ref[...] = jnp.broadcast_to(total, term_ref.shape)
+        pool_term = acc[:, columns(head)] * pool_keys[:, columns(head)].astype(F32)
+        total = total + jnp.sum(pool_term, axis=0, keepdims=True)
+    term_ref[...] = jnp.broadcast_to(total * score_scale, term_ref.shape)
     if parts == 1:
-        keep_ref[:, :width] = acc[:pool_rows, :width] * score_scale
-        keep_ref[:, width:] = acc[:pool_rows, width:]
+        keep_ref[:, :width] = acc[:, :width] * score_scale
+        keep_ref[:, width:] = acc[:, width:]
     else:
         for piece_no in range(parts):
             place = slice(piece_no // 2 * shard, (piece_no // 2 + 1) * shard)
@@ -290,12 +278,12 @@
     pool_rows = parts * pieces[0].shape[0]
     count = heads * lanes // CHUNK
     span = PL + CL
-    own = jax.ShapeDtypeStruct(keys.shape, BF16)
     out_shape = [
         jax.ShapeDtypeStruct(queries.shape, BF16),
         jax.ShapeDtypeStruct((slots, heads, span, lanes), BF16),
         jax.ShapeDtypeStruct((pool_rows, width), BF16),
-        own, own, own,
+        jax.ShapeDtypeStruct(keys.shape, BF16),
+        jax.ShapeDtypeStruct((slots, heads, 2, CL, size), F32),
         jax.ShapeDtypeStruct((8, size), F32),
     ]
     if parts > 1:
@@ -303,22 +291,21 @@
         out_shape += [jax.ShapeDtypeStruct(half, F32), jax.ShapeDtypeStruct(half, BF16)]
     else:
         out_shape += [jax.ShapeDtypeStruct((pool_rows, 2 * width), F32)]
-    kinds = [
-        ((span, CHUNK), F32), ((span, CHUNK), BF16), ((size + TAIL, CHUNK), F32),
-        ((size, CHUNK), BF16), ((span, CHUNK), F32), ((8, CHUNK), F32),
-    ]
     return pl.pallas_call(
         functools.partial(attention_kernel, parts=parts, heads=heads),
         in_specs=[SMEM_SPEC] * 3 + [VMEM_SPEC] * (6 + parts),
         out_specs=[VMEM_SPEC] * len(out_shape),
         out_shape=out_shape,
         scratch_shapes=[
-            pltpu.VMEM((pool_rows + PL, 2 * width), F32),
-            pltpu.VMEM((slots + 1, heads, 2, CL, size), F32),
+            pltpu.VMEM((pool_rows, 2 * width), F32),
             pltpu.VMEM((pool_rows, width), BF16),
             pltpu.VMEM((width, pool_rows), BF16),
             pltpu.VMEM((slots, heads, size, CL), BF16),
-        ] + [pltpu.VMEM(shape, kind) for shape, kind in kinds for _ in range(count)],
+        ]
+        + [pltpu.VMEM((span, lanes), BF16)] * heads
+        + [pltpu.VMEM((size, lanes), BF16)] * heads
+        + [pltpu.VMEM((span, CHUNK), F32)] * count
+        + [pltpu.VMEM((size + TAIL, CHUNK), F32)] * count,
         compiler_params=params(),
         cost_estimate=cost(3 * 10**9, 10**7),
         name="attention",
@@ -326,8 +313,8 @@
 
 
 def post_kernel(
-    live_ref, prompt_ref, att_t_ref, ds_ref, pool_keys, own_keys_ref, raw_ref, recip_ref, col_ref,
-    att_ref, dq_ref, att_out, dq_out, sems,
+    live_ref, prompt_ref, att_t_ref, ds_ref, pool_keys, own_keys_ref, own_acc, raw_ref, recip_ref, col_ref,
+    ck_ref, kg_ref, att_ref, dq_ref, dk_ref, dv_ref, att_out, dq_out, sems,
 ):
     slots, width, lanes = raw_ref.shape
     size = col_ref.shape[0]
@@ -367,25 +354,38 @@
 
     lax.fori_loop(live_ref[0], slots, dead, 0)
     lax.fori_loop(0, live_ref[0], live, 0)
+    for head in range(heads):
+        columns = slice(head * size, (head + 1) * size)
+        own_grad = own_acc[:, head, 0].reshape(slots * CL, size) * score_scale
+        own_unit, own_recip = unit(ck_ref[:, columns].astype(F32))
+        dk_ref[:, columns] = norm_back(own_grad, own_unit, own_recip, kg_ref[...]).astype(BF16)
+        dv_ref[:, columns] = own_acc[:, head, 1].reshape(slots * CL, size).astype(BF16)
     for slot in range(slots):
         for which in range(2):
             copy_out(slot, which).wait()
 
 
-def post(live_counts, slot_prompts, att_t, score_grads, pool_keys, own_keys, raw, recip, query_col, shape):
+def post(
+    live_counts, slot_prompts, att_t, score_grads, pool_keys, own_keys, own_acc, raw, recip, query_col,
+    keys, key_gain, shape,
+):
     slots = raw.shape[0]
     out = jax.ShapeDtypeStruct(shape, BF16)
+    own = jax.ShapeDtypeStruct(keys.shape, BF16)
     slab = pltpu.VMEM((slots, CL, shape[1]), BF16)
     return pl.pallas_call(
         post_kernel,
-        in_specs=[SMEM_SPEC] * 2 + [VMEM_SPEC] * 7,
-        out_specs=[HBM_SPEC] * 2,
-        out_shape=[out, out],
+        in_specs=[SMEM_SPEC] * 2 + [VMEM_SPEC] * 10,
+        out_specs=[HBM_SPEC] * 2 + [VMEM_SPEC] * 2,
+        out_shape=[out, out, own, own],
         scratch_shapes=[slab, slab, pltpu.SemaphoreType.DMA((2, slots))],
         compiler_params=params(),
         cost_estimate=cost(3 * 10**9, 4 * 10**6),
         name="post",
-    )(live_counts, slot_prompts, att_t, score_grads, pool_keys, own_keys, raw, recip, query_col)
+    )(
+        live_counts, slot_prompts, att_t, score_grads, pool_keys, own_keys, own_acc, raw, recip, query_col,
+        keys, key_gain,
+    )
 
 
 def tree(terms):
@@ -495,12 +495,11 @@
     by_permute = shard % 16 == 0 and grp > 1 and grp & (grp - 1) == 0 and tp & (tp - 1) == 0
     slots, width = slot_prompts.shape[0], comp_keys.shape[1]
     query_gain, key_gain = query_gain.reshape(1, size), key_gain.reshape(1, size)
-    mask = causal()
-    mask, keys_in, values_in = lax.optimization_barrier((mask, prompt_keys, prompt_values))
+    me = lax.axis_index("grp").astype(jnp.int32).reshape(1) if by_permute else jnp.zeros((1,), jnp.int32)
+    mask, me, keys_in, values_in = lax.optimization_barrier((causal(), me, prompt_keys, prompt_values))
     mine = pack(keys_in, values_in, key_gain)
     raw, recip, queries, grads, query_col = prepare(live_counts, comp_queries, out_grad, query_gain, slots, width)
     if by_permute:
-        me = lax.axis_index("grp").astype(jnp.int32).reshape(1)
         even = [mine] + [swap(mine, "grp", step) for step in range(2, grp, 2)]
         odd = [swap(mine, "grp", 1)]
         even, queries, grads, raw, recip, query_col = lax.optimization_barrier(
@@ -509,13 +508,13 @@
         odd += [swap(piece, "grp", 1) for piece in even[1:]]
         pieces = [piece for pair in zip(even, odd) for piece in pair]
     else:
-        me = jnp.zeros((1,), jnp.int32)
         pieces = [lax.all_gather(mine, "grp", axis=0, tiled=True)]
-    att_t, score_grads, pool_keys, own_keys, key_grads, value_grads, term, keep, *send = attention(
+    att_t, score_grads, pool_keys, own_keys, own_acc, term, keep, *send = attention(
         live_counts, slot_prompts, me, queries, grads, comp_keys, comp_values, key_gain, mask, pieces,
     )
-    attended, query_grads = post(
-        live_counts, slot_prompts, att_t, score_grads, pool_keys, own_keys, raw, recip, query_col, comp_queries.shape,
+    attended, query_grads, key_grads, value_grads = post(
+        live_counts, slot_prompts, att_t, score_grads, pool_keys, own_keys, own_acc, raw, recip, query_col,
+        comp_keys, key_gain, comp_queries.shape,
     )
     if by_permute:
         came = swap(send[0], "grp", 1)

time: 43.1 us -> 38.8 us (0.900); the launches traced: 43.6 us -> 38.4 us
  Pallas kernels: 16.1 us -> 7.49 us
  starting transfers between devices: 13.2 us -> 17.5 us
  local copies, waits for them, and re-layouts: 3.83 us -> 0.83 us
  waiting for transfers between devices: 9.04 us -> 11.2 us
    pallas_call x1, Pallas kernels: 10 us -> 2.84 us  [attention(): pl.pallas_call(functools.partial(attention_kernel, parts=parts, heads=hea...]
    ppermute x15, starting transfers between devices: 13.2 us -> 17.5 us  [swap(): lax.ppermute(values, axis, [(i, i ^ step) for i in range(lax.axis_size(ax...]
    unnamed x26 -> x18, local copies, waits for them, and re-layouts: 3.83 us -> 0.83 us
    ppermute x15, waiting for transfers between devices: 9.04 us -> 11.2 us  [swap(): lax.ppermute(values, axis, [(i, i ^ step) for i in range(lax.axis_size(ax...]
    pallas_call x1, Pallas kernels: 1.05 us -> 0.34 us  [prepare(): pl.pallas_call(prepare_kernel, in_specs=[SMEM_SPEC] + [VMEM_SPEC] * 3, ou...]
    pallas_call x1, Pallas kernels: 3.41 us -> 2.72 us  [post(): pl.pallas_call(post_kernel, in_specs=[SMEM_SPEC] * 2 + [VMEM_SPEC] * 10,...]
  transfers between devices with their start and end apart: 15 -> 15, of which waited for: 10 -> 10; matrix products, arithmetic and copies ran while one was open for 0% -> 0% of each run, Pallas kernels for 12% -> 10%
where the time goes in v3:
time: 38.8 us; the launch traced here: 38.4 us
  starting transfers between devices  17.5 us (45%)
  waiting for transfers between devices  11.2 us (29%)
  Pallas kernels  7.49 us (19%)
  between operations  1.44 us (4%)
  local copies, waits for them, and re-layouts  0.83 us (2%)
    ppermute x15, starting transfers between devices, swap(): lax.ppermute(values, axis, [(i, i ^ step) for i in range(lax.axis_size(ax...  17.5 us
    ppermute x15, waiting for transfers between devices, swap(): lax.ppermute(values, axis, [(i, i ^ step) for i in range(lax.axis_size(ax...  11.2 us
    pallas_call x1, Pallas kernels, attention(): pl.pallas_call(functools.partial(attention_kernel, parts=parts, heads=hea...  2.84 us
    pallas_call x1, Pallas kernels, post(): pl.pallas_call(post_kernel, in_specs=[SMEM_SPEC] * 2 + [VMEM_SPEC] * 10,...  2.72 us
    pallas_call x1, Pallas kernels, finish(): pl.pallas_call(finish_kernel, in_specs=[VMEM_SPEC] * (len(blocks) + 2), o...  0.84 us
    unnamed x18, local copies, waits for them, and re-layouts  0.83 us
  transfers between devices with their start and end apart: 15, of which 10 were waited for; matrix products, arithmetic and copies ran while one was open for 0% of the time, Pallas kernels for 10%

profile of v3, /device:TPU:0, one launch (start us, length us, event | category | flops | bytes accessed | tf_op | source)
XLA Modules:
  0.0 38.4 jit_solution(18013772736427997714)
XLA Ops:
  0.6 0.0 copy-start
  0.6 0.0 copy-start.1
  0.7 0.0 copy-start.7
  0.7 0.7 %copy-done = bf16[96,256]{1,0:T(8,128)(2,1)S(1)} copy-done((bf16[96,256]{1,0:T(8,128)(2,1)S(1)}, bf16[96,256]{1,0:T(8,128)(2,1)}, u32[]{:S(2)}) %copy-start) | copy-done | bytes 49176
  1.4 0.0 copy-done.1
  1.4 0.0 copy-done.7
  1.5 0.0 copy-start.2
  1.5 0.0 copy-start.3
  1.5 0.0 copy-start.4
  1.5 0.1 pack.1.refs_9_
  1.6 0.5 %collective-permute-start.3 = (bf16[96,512]{1,0:T(8,128)(2,1)S(1)}, bf16[96,512]{1,0:T(8,128)(2,1)S(1)}, u32[]{:S(2)}, u32[]{:S(2)}) collective-permute-start(bf16[96,512]{1,0:T(8,128)(2,1)S(1)} %pack.1.refs_9_), channel_id=1, source_target_pairs={{0,4},{4,0},{8,12},{12,8},{16,20},{20,16},{24,28},{28,24},{1,5},{5... | collective-permute-start | bytes 294920 | tf_op jit(solution)/shard_map/ppermute | solution.py:485
  2.1 3.5 %collective-permute-start.2 = (bf16[96,512]{1,0:T(8,128)(2,1)S(1)}, bf16[96,512]{1,0:T(8,128)(2,1)S(1)}, u32[]{:S(2)}, u32[]{:S(2)}) collective-permute-start(bf16[96,512]{1,0:T(8,128)(2,1)S(1)} %pack.1.refs_9_), channel_id=1, source_target_pairs={{0,24},{4,28},{8,16},{12,20},{16,8},{20,12},{24,0},{28,4},{1,25},{... | collective-permute-start | bytes 294920 | tf_op jit(solution)/shard_map/ppermute | solution.py:485
  5.6 0.5 %collective-permute-start.1 = (bf16[96,512]{1,0:T(8,128)(2,1)S(1)}, bf16[96,512]{1,0:T(8,128)(2,1)S(1)}, u32[]{:S(2)}, u32[]{:S(2)}) collective-permute-start(bf16[96,512]{1,0:T(8,128)(2,1)S(1)} %pack.1.refs_9_), channel_id=1, source_target_pairs={{0,16},{4,20},{8,24},{12,28},{16,0},{20,4},{24,8},{28,12},{1,17},{... | collective-permute-start | bytes 294920 | tf_op jit(solution)/shard_map/ppermute | solution.py:485
  6.1 0.1 collective-permute-start
  6.9 0.0 copy-done.2
  6.9 0.0 copy-done.3
  7.0 0.0 copy-done.4
  7.0 0.0 copy-start.5
  7.0 0.0 copy-start.6
  7.0 0.0 copy-start.8
  7.0 0.3 prepare.1
  7.4 1.7 %collective-permute-done.2.refs_15_ = bf16[96,512]{1,0:T(8,128)(2,1)S(1)} collective-permute-done((bf16[96,512]{1,0:T(8,128)(2,1)S(1)}, bf16[96,512]{1,0:T(8,128)(2,1)S(1)}, u32[]{:S(2)}, u32[]{:S(2)}) %collective-permute-start.2) | collective-permute-done | bytes 98336 | tf_op jit(solution)/shard_map/ppermute | solution.py:485
  9.1 2.0 %collective-permute-done.1.refs_13_ = bf16[96,512]{1,0:T(8,128)(2,1)S(1)} collective-permute-done((bf16[96,512]{1,0:T(8,128)(2,1)S(1)}, bf16[96,512]{1,0:T(8,128)(2,1)S(1)}, u32[]{:S(2)}, u32[]{:S(2)}) %collective-permute-start.1) | collective-permute-done | bytes 98336 | tf_op jit(solution)/shard_map/ppermute | solution.py:485
  11.1 0.3 collective-permute-done.refs_11_
  11.4 0.0 collective-permute-start.4
  11.4 0.5 %collective-permute-start.5 = (bf16[96,512]{1,0:T(8,128)(2,1)S(1)}, bf16[96,512]{1,0:T(8,128)(2,1)S(1)}, u32[]{:S(2)}, u32[]{:S(2)}) collective-permute-start(bf16[96,512]{1,0:T(8,128)(2,1)S(1)} %collective-permute-done.1.refs_13_), channel_id=1, source_target_pairs={{0,4},{4,0},{8,12},{12,8},{16,20},{20,16},{24,28},{28,24},{1,5},{5... | collective-permute-start | bytes 294920 | tf_op jit(solution)/shard_map/ppermute | solution.py:485
  11.9 0.0 collective-permute-start.6
  11.9 0.0 collective-permute-done.3.refs_10_
  11.9 0.8 %collective-permute-done.4.refs_12_ = bf16[96,512]{1,0:T(8,128)(2,1)S(1)} collective-permute-done((bf16[96,512]{1,0:T(8,128)(2,1)S(1)}, bf16[96,512]{1,0:T(8,128)(2,1)S(1)}, u32[]{:S(2)}, u32[]{:S(2)}) %collective-permute-start.4) | collective-permute-done | bytes 98336 | tf_op jit(solution)/shard_map/ppermute | solution.py:485
  12.7 0.2 collective-permute-done.5.refs_14_
  12.9 0.4 collective-permute-done.6.refs_16_
  13.2 0.0 copy-done.5
  13.2 0.0 copy-done.6
  13.2 0.0 copy-done.8
  13.2 2.8 %attention.1 = (bf16[4,256,512]{2,1,0:T(8,128)(2,1)S(1)}, bf16[4,2,448,512]{3,2,1,0:T(8,128)(2,1)S(1)}, bf16[768,256]{1,0:T(8,128)(2,1)S(1)}, bf16[256,256]{1,0:...) custom-call(s32[1]{0:T(128)S(6)} %copy.18.live_ref.refs_0_, ...), custom_call_target="tpu_custom_call" | custom-call | flops 3000000000 | bytes 10000000 | tf_op jit(solution)/shard_map/attention/pallas_call | solution.py:294
  16.1 1.8 %collective-permute-start.7 = (bf16[384,512]{1,0:T(8,128)(2,1)S(1)}, bf16[384,512]{1,0:T(8,128)(2,1)S(1)}, u32[]{:S(2)}, u32[]{:S(2)}) collective-permute-start(bf16[384,512]{1,0:T(8,128)(2,1)S(1)} %get-tuple-element.67), channel_id=1, source_target_pairs={{0,4},{4,0},{8,12},{12,8},{16,20},{20,16},{24,28},{28,24},{1,5},{5... | collective-permute-start | bytes 1179656 | tf_op jit(solution)/shard_map/ppermute | solution.py:485
  17.9 3.6 %collective-permute-start.10 = (f32[8,128]{1,0:T(8,128)S(1)}, f32[8,128]{1,0:T(8,128)S(1)}, u32[]{:S(2)}, u32[]{:S(2)}) collective-permute-start(f32[8,128]{1,0:T(8,128)S(1)} %get-tuple-element.68.refs_0_), channel_id=1, source_target_pairs={{0,3},{1,2},{2,1},{3,0},{4,7},{5,6},{6,5},{7,4},{8,11},{9,10},{10,... | collective-permute-start | bytes 12296 | tf_op jit(solution)/shard_map/ppermute | solution.py:485
  21.5 0.0 collective-permute-start.9
  21.5 0.8 %collective-permute-start.8 = (f32[8,128]{1,0:T(8,128)S(1)}, f32[8,128]{1,0:T(8,128)S(1)}, u32[]{:S(2)}, u32[]{:S(2)}) collective-permute-start(f32[8,128]{1,0:T(8,128)S(1)} %get-tuple-element.68.refs_0_), channel_id=1, source_target_pairs={{0,1},{1,0},{2,3},{3,2},{4,5},{5,4},{6,7},{7,6},{8,9},{9,8},{10,11... | collective-permute-start | bytes 12296 | tf_op jit(solution)/shard_map/ppermute | solution.py:485
  22.3 1.0 %collective-permute-done.10.refs_3_ = f32[8,128]{1,0:T(8,128)S(1)} collective-permute-done((f32[8,128]{1,0:T(8,128)S(1)}, f32[8,128]{1,0:T(8,128)S(1)}, u32[]{:S(2)}, u32[]{:S(2)}) %collective-permute-start.10) | collective-permute-done | bytes 4128 | tf_op jit(solution)/shard_map/ppermute | solution.py:485
  23.3 2.7 %collective-permute-done.9.refs_2_ = f32[8,128]{1,0:T(8,128)S(1)} collective-permute-done((f32[8,128]{1,0:T(8,128)S(1)}, f32[8,128]{1,0:T(8,128)S(1)}, u32[]{:S(2)}, u32[]{:S(2)}) %collective-permute-start.9) | collective-permute-done | bytes 4128 | tf_op jit(solution)/shard_map/ppermute | solution.py:485
  26.0 0.0 collective-permute-done.8.refs_1_
  26.0 0.0 collective-permute-done.7.came_ref
  26.0 0.1 add.1
  26.1 1.6 %collective-permute-start.11 = (bf16[112,512]{1,0:T(8,128)(2,1)S(1)}, bf16[112,512]{1,0:T(8,128)(2,1)S(1)}, u32[]{:S(2)}, u32[]{:S(2)}) collective-permute-start(bf16[112,512]{1,0:T(8,128)(2,1)S(1)} %get-tuple-element.70), channel_id=1, source_target_pairs={{0,8},{4,12},{8,0},{12,4},{16,24},{20,28},{24,16},{28,20},{1,9},{5... | collective-permute-start | bytes 344072 | tf_op jit(solution)/shard_map/ppermute | solution.py:485
  27.7 3.1 %collective-permute-start.12 = (bf16[112,512]{1,0:T(8,128)(2,1)S(1)}, bf16[112,512]{1,0:T(8,128)(2,1)S(1)}, u32[]{:S(2)}, u32[]{:S(2)}) collective-permute-start(bf16[112,512]{1,0:T(8,128)(2,1)S(1)} %get-tuple-element.71), channel_id=1, source_target_pairs={{0,16},{4,20},{8,24},{12,28},{16,0},{20,4},{24,8},{28,12},{1,17},{... | collective-permute-start | bytes 344072 | tf_op jit(solution)/shard_map/ppermute | solution.py:485
  30.8 1.4 %collective-permute-start.13 = (bf16[112,512]{1,0:T(8,128)(2,1)S(1)}, bf16[112,512]{1,0:T(8,128)(2,1)S(1)}, u32[]{:S(2)}, u32[]{:S(2)}) collective-permute-start(bf16[112,512]{1,0:T(8,128)(2,1)S(1)} %get-tuple-element.72), channel_id=1, source_target_pairs={{0,24},{4,28},{8,16},{12,20},{16,8},{20,12},{24,0},{28,4},{1,25},{... | collective-permute-start | bytes 344072 | tf_op jit(solution)/shard_map/ppermute | solution.py:485
  32.2 2.7 %post.1 = (bf16[256,2048]{1,0:T(8,128)(2,1)}, bf16[256,2048]{1,0:T(8,128)(2,1)}, bf16[256,256]{1,0:T(8,128)(2,1)}, bf16[256,256]{1,0:T(8,128)(2,1)}) custom-call(s32[1]{0:T(128)S(6)} %copy.18.live_ref.refs_0_, s32[4]{0:T(128)S(1)} %copy-done.8, bf16[4,256,512]{2,1,0:T(8,128)(2,1)S(1)} %get-tuple-element.73.att_t_ref, ...), custom_call_target="tpu_custom_call" | custom-call | flops 3000000000 | bytes 4000000 | tf_op jit(solution)/shard_map/post/pallas_call | solution.py:376
  34.9 0.0 collective-permute-done.11.refs_1_
  34.9 0.0 collective-permute-done.12.refs_2_
  34.9 1.8 %collective-permute-done.13.refs_3_ = bf16[112,512]{1,0:T(8,128)(2,1)S(1)} collective-permute-done((bf16[112,512]{1,0:T(8,128)(2,1)S(1)}, bf16[112,512]{1,0:T(8,128)(2,1)S(1)}, u32[]{:S(2)}, u32[]{:S(2)}) %collective-permute-start.13) | collective-permute-done | bytes 114720 | tf_op jit(solution)/shard_map/ppermute | solution.py:485
  36.7 0.0 collective-permute-start.14
  36.7 0.8 %finish.1 = (f32[96,256]{1,0:T(8,128)}, f32[96,256]{1,0:T(8,128)}) custom-call(f32[112,512]{1,0:T(8,128)S(1)} %get-tuple-element.86.refs_0_, bf16[112,512]{1,0:T(8,128)(2,1)S(1)} %collective-permute-done.11.refs_1_, bf16[112,512]{1,0:T(8,128)(2,1)S(1)} %collective-permute-done.12.refs_2_, bf16[112,512]{1,0:T(8,128)(2,1)S(1)} %collective-permute-done.13.refs_3_, ...), custom_call_target="tpu_custom_call" | custom-call | flops 100000000 | bytes 1000000 | tf_op jit(solution)/shard_map/finish/pallas_call | solution.py:473
  37.5 0.3 collective-permute-done.14.refs_1_
  37.9 0.5 %gain_grads.1 = (f32[1,128]{1,0:T(1,128)}, f32[1,128]{1,0:T(1,128)}) custom-call(f32[8,128]{1,0:T(8,128)S(1)} %sum_chips.1.refs_0_, f32[8,128]{1,0:T(8,128)S(1)} %collective-permute-done.14.refs_1_, f32[1,128]{1,0:T(1,128)S(1)} %bitcast.11, f32[1,128]{1,0:T(1,128)S(1)} %bitcast.9), custom_call_target="tpu_custom_call" | custom-call | tf_op jit(solution)/shard_map/gain_grads/pallas_call | solution.py:447
  (2 shorter events, 0.0 us)
Async XLA Ops:
  0.6 0.8 %copy-start = (bf16[96,256]{1,0:T(8,128)(2,1)S(1)}, bf16[96,256]{1,0:T(8,128)(2,1)}, u32[]{:S(2)}) copy-start(bf16[96,256]{1,0:T(8,128)(2,1)} %refs_4_.1) | copy-start | bytes 147460
  0.6 0.8 %copy-start.1 = (f32[128]{0:T(128)S(1)}, f32[128]{0:T(128)}, u32[]{:S(2)}) copy-start(f32[128]{0:T(128)} %param.16) | copy-start | bytes 1540
  0.7 0.8 %copy-start.7 = (bf16[96,256]{1,0:T(8,128)(2,1)S(1)}, bf16[96,256]{1,0:T(8,128)(2,1)}, u32[]{:S(2)}) copy-start(bf16[96,256]{1,0:T(8,128)(2,1)} %values_ref) | copy-start | bytes 147460
  1.5 5.5 %copy-start.2 = (f32[128]{0:T(128)S(1)}, f32[128]{0:T(128)}, u32[]{:S(2)}) copy-start(f32[128]{0:T(128)} %param.15) | copy-start | bytes 1540
  1.5 5.5 %copy-start.3 = (bf16[256,2048]{1,0:T(8,128)(2,1)S(1)}, bf16[256,2048]{1,0:T(8,128)(2,1)}, u32[]{:S(2)}) copy-start(bf16[256,2048]{1,0:T(8,128)(2,1)} %q_ref.1) | copy-start | bytes 3145732
  1.5 5.5 %copy-start.4 = (bf16[256,2048]{1,0:T(8,128)(2,1)S(1)}, bf16[256,2048]{1,0:T(8,128)(2,1)}, u32[]{:S(2)}) copy-start(bf16[256,2048]{1,0:T(8,128)(2,1)} %do_ref.1) | copy-start | bytes 3145732
  1.6 10.3 %collective-permute-start.3 = (bf16[96,512]{1,0:T(8,128)(2,1)S(1)}, bf16[96,512]{1,0:T(8,128)(2,1)S(1)}, u32[]{:S(2)}, u32[]{:S(2)}) collective-permute-start(bf16[96,512]{1,0:T(8,128)(2,1)S(1)} %pack.1.refs_9_), channel_id=1, source_target_pairs={{0,4},{4,0},{8,12},{12,8},{16,20},{20,16},{24,28},{28,24},{1,5},{5... | collective-permute-start | bytes 294920 | tf_op jit(solution)/shard_map/ppermute | solution.py:485
  2.1 7.0 %collective-permute-start.2 = (bf16[96,512]{1,0:T(8,128)(2,1)S(1)}, bf16[96,512]{1,0:T(8,128)(2,1)S(1)}, u32[]{:S(2)}, u32[]{:S(2)}) collective-permute-start(bf16[96,512]{1,0:T(8,128)(2,1)S(1)} %pack.1.refs_9_), channel_id=1, source_target_pairs={{0,24},{4,28},{8,16},{12,20},{16,8},{20,12},{24,0},{28,4},{1,25},{... | collective-permute-start | bytes 294920 | tf_op jit(solution)/shard_map/ppermute | solution.py:485
  5.6 5.5 %collective-permute-start.1 = (bf16[96,512]{1,0:T(8,128)(2,1)S(1)}, bf16[96,512]{1,0:T(8,128)(2,1)S(1)}, u32[]{:S(2)}, u32[]{:S(2)}) collective-permute-start(bf16[96,512]{1,0:T(8,128)(2,1)S(1)} %pack.1.refs_9_), channel_id=1, source_target_pairs={{0,16},{4,20},{8,24},{12,28},{16,0},{20,4},{24,8},{28,12},{1,17},{... | collective-permute-start | bytes 294920 | tf_op jit(solution)/shard_map/ppermute | solution.py:485
  6.1 5.3 %collective-permute-start = (bf16[96,512]{1,0:T(8,128)(2,1)S(1)}, bf16[96,512]{1,0:T(8,128)(2,1)S(1)}, u32[]{:S(2)}, u32[]{:S(2)}) collective-permute-start(bf16[96,512]{1,0:T(8,128)(2,1)S(1)} %pack.1.refs_9_), channel_id=1, source_target_pairs={{0,8},{4,12},{8,0},{12,4},{16,24},{20,28},{24,16},{28,20},{1,9},{5... | collective-permute-start | bytes 294920 | tf_op jit(solution)/shard_map/ppermute | solution.py:485
  7.0 6.3 %copy-start.5 = (bf16[256,256]{1,0:T(8,128)(2,1)S(1)}, bf16[256,256]{1,0:T(8,128)(2,1)}, u32[]{:S(2)}) copy-start(bf16[256,256]{1,0:T(8,128)(2,1)} %refs_6_.1) | copy-start | bytes 393220
  7.0 6.2 %copy-start.6 = (bf16[256,256]{1,0:T(8,128)(2,1)S(1)}, bf16[256,256]{1,0:T(8,128)(2,1)}, u32[]{:S(2)}) copy-start(bf16[256,256]{1,0:T(8,128)(2,1)} %ck_ref.1) | copy-start | bytes 393220
  7.0 6.2 %copy-start.8 = (s32[4]{0:T(128)S(1)}, s32[4]{0:T(128)}, u32[]{:S(2)}) copy-start(s32[4]{0:T(128)} %prompt_ref.1) | copy-start | bytes 52
  11.4 1.3 %collective-permute-start.4 = (bf16[96,512]{1,0:T(8,128)(2,1)S(1)}, bf16[96,512]{1,0:T(8,128)(2,1)S(1)}, u32[]{:S(2)}, u32[]{:S(2)}) collective-permute-start(bf16[96,512]{1,0:T(8,128)(2,1)S(1)} %collective-permute-done.refs_11_), channel_id=1, source_target_pairs={{0,4},{4,0},{8,12},{12,8},{16,20},{20,16},{24,28},{28,24},{1,5},{5... | collective-permute-start | bytes 294920 | tf_op jit(solution)/shard_map/ppermute | solution.py:485
  11.4 1.5 %collective-permute-start.5 = (bf16[96,512]{1,0:T(8,128)(2,1)S(1)}, bf16[96,512]{1,0:T(8,128)(2,1)S(1)}, u32[]{:S(2)}, u32[]{:S(2)}) collective-permute-start(bf16[96,512]{1,0:T(8,128)(2,1)S(1)} %collective-permute-done.1.refs_13_), channel_id=1, source_target_pairs={{0,4},{4,0},{8,12},{12,8},{16,20},{20,16},{24,28},{28,24},{1,5},{5... | collective-permute-start | bytes 294920 | tf_op jit(solution)/shard_map/ppermute | solution.py:485
  11.9 1.3 %collective-permute-start.6 = (bf16[96,512]{1,0:T(8,128)(2,1)S(1)}, bf16[96,512]{1,0:T(8,128)(2,1)S(1)}, u32[]{:S(2)}, u32[]{:S(2)}) collective-permute-start(bf16[96,512]{1,0:T(8,128)(2,1)S(1)} %collective-permute-done.2.refs_15_), channel_id=1, source_target_pairs={{0,4},{4,0},{8,12},{12,8},{16,20},{20,16},{24,28},{28,24},{1,5},{5... | collective-permute-start | bytes 294920 | tf_op jit(solution)/shard_map/ppermute | solution.py:485
  16.1 9.9 %collective-permute-start.7 = (bf16[384,512]{1,0:T(8,128)(2,1)S(1)}, bf16[384,512]{1,0:T(8,128)(2,1)S(1)}, u32[]{:S(2)}, u32[]{:S(2)}) collective-permute-start(bf16[384,512]{1,0:T(8,128)(2,1)S(1)} %get-tuple-element.67), channel_id=1, source_target_pairs={{0,4},{4,0},{8,12},{12,8},{16,20},{20,16},{24,28},{28,24},{1,5},{5... | collective-permute-start | bytes 1179656 | tf_op jit(solution)/shard_map/ppermute | solution.py:485
  17.9 5.4 %collective-permute-start.10 = (f32[8,128]{1,0:T(8,128)S(1)}, f32[8,128]{1,0:T(8,128)S(1)}, u32[]{:S(2)}, u32[]{:S(2)}) collective-permute-start(f32[8,128]{1,0:T(8,128)S(1)} %get-tuple-element.68.refs_0_), channel_id=1, source_target_pairs={{0,3},{1,2},{2,1},{3,0},{4,7},{5,6},{6,5},{7,4},{8,11},{9,10},{10,... | collective-permute-start | bytes 12296 | tf_op jit(solution)/shard_map/ppermute | solution.py:485
  21.5 4.5 %collective-permute-start.9 = (f32[8,128]{1,0:T(8,128)S(1)}, f32[8,128]{1,0:T(8,128)S(1)}, u32[]{:S(2)}, u32[]{:S(2)}) collective-permute-start(f32[8,128]{1,0:T(8,128)S(1)} %get-tuple-element.68.refs_0_), channel_id=1, source_target_pairs={{0,2},{1,3},{2,0},{3,1},{4,6},{5,7},{6,4},{7,5},{8,10},{9,11},{10,... | collective-permute-start | bytes 12296 | tf_op jit(solution)/shard_map/ppermute | solution.py:485
  21.5 4.5 %collective-permute-start.8 = (f32[8,128]{1,0:T(8,128)S(1)}, f32[8,128]{1,0:T(8,128)S(1)}, u32[]{:S(2)}, u32[]{:S(2)}) collective-permute-start(f32[8,128]{1,0:T(8,128)S(1)} %get-tuple-element.68.refs_0_), channel_id=1, source_target_pairs={{0,1},{1,0},{2,3},{3,2},{4,5},{5,4},{6,7},{7,6},{8,9},{9,8},{10,11... | collective-permute-start | bytes 12296 | tf_op jit(solution)/shard_map/ppermute | solution.py:485
  26.1 8.8 %collective-permute-start.11 = (bf16[112,512]{1,0:T(8,128)(2,1)S(1)}, bf16[112,512]{1,0:T(8,128)(2,1)S(1)}, u32[]{:S(2)}, u32[]{:S(2)}) collective-permute-start(bf16[112,512]{1,0:T(8,128)(2,1)S(1)} %get-tuple-element.70), channel_id=1, source_target_pairs={{0,8},{4,12},{8,0},{12,4},{16,24},{20,28},{24,16},{28,20},{1,9},{5... | collective-permute-start | bytes 344072 | tf_op jit(solution)/shard_map/ppermute | solution.py:485
  27.7 7.2 %collective-permute-start.12 = (bf16[112,512]{1,0:T(8,128)(2,1)S(1)}, bf16[112,512]{1,0:T(8,128)(2,1)S(1)}, u32[]{:S(2)}, u32[]{:S(2)}) collective-permute-start(bf16[112,512]{1,0:T(8,128)(2,1)S(1)} %get-tuple-element.71), channel_id=1, source_target_pairs={{0,16},{4,20},{8,24},{12,28},{16,0},{20,4},{24,8},{28,12},{1,17},{... | collective-permute-start | bytes 344072 | tf_op jit(solution)/shard_map/ppermute | solution.py:485
  30.8 5.9 %collective-permute-start.13 = (bf16[112,512]{1,0:T(8,128)(2,1)S(1)}, bf16[112,512]{1,0:T(8,128)(2,1)S(1)}, u32[]{:S(2)}, u32[]{:S(2)}) collective-permute-start(bf16[112,512]{1,0:T(8,128)(2,1)S(1)} %get-tuple-element.72), channel_id=1, source_target_pairs={{0,24},{4,28},{8,16},{12,20},{16,8},{20,12},{24,0},{28,4},{1,25},{... | collective-permute-start | bytes 344072 | tf_op jit(solution)/shard_map/ppermute | solution.py:485
  36.7 1.2 %collective-permute-start.14 = (f32[8,128]{1,0:T(8,128)S(1)}, f32[8,128]{1,0:T(8,128)S(1)}, u32[]{:S(2)}, u32[]{:S(2)}) collective-permute-start(f32[8,128]{1,0:T(8,128)S(1)} %sum_chips.1.refs_0_), channel_id=1, source_target_pairs={{0,4},{4,0},{8,12},{12,8},{16,20},{20,16},{24,28},{28,24},{1,5},{5... | collective-permute-start | bytes 12296 | tf_op jit(solution)/shard_map/ppermute | solution.py:485

commit v4 on v3

--- a/solution.py
+++ b/solution.py
@@ -39,22 +39,14 @@
     return recip * (scaled - unit_rows * jnp.mean(unit_rows * scaled, axis=-1, keepdims=True))
 
 
-def halves(row):
-    upper = row.astype(BF16)
-    return [upper, (row - upper.astype(F32)).astype(BF16)]
-
-
-def gain_rows(term, wide):
-    row = jnp.concatenate([part.astype(F32) for part in halves(term)], axis=1)
-    if wide > row.shape[1]:
-        row = jnp.concatenate([row, jnp.zeros((1, wide - row.shape[1]), F32)], axis=1)
-    rows = jnp.broadcast_to(row, (TAIL, wide))
-    return jnp.where(lax.broadcasted_iota(jnp.int32, rows.shape, 0) == 0, rows, 0.0).astype(BF16)
-
-
-def gain_term(rows, size):
-    row = rows.astype(F32)[0:1]
-    return row[:, :size] + row[:, size:2 * size]
+def gain_rows(term):
+    upper = term.astype(BF16).astype(F32)
+    rows = jnp.concatenate([upper, term - upper, jnp.zeros((TAIL - 2, term.shape[1]), F32)], axis=0)
+    return rows.astype(BF16)
+
+
+def gain_term(rows):
+    return rows[0:1].astype(F32) + rows[1:2].astype(F32)
 
 
 def params(limit=VMEM_LIMIT):
@@ -314,7 +306,7 @@
 
 def post_kernel(
     live_ref, prompt_ref, att_t_ref, ds_ref, pool_keys, own_keys_ref, own_acc, raw_ref, recip_ref, col_ref,
-    ck_ref, kg_ref, att_ref, dq_ref, dk_ref, dv_ref, att_out, dq_out, sems,
+    ck_ref, kg_ref, att_ref, dq_ref, dk_ref, dv_ref, att_out, dq_out, zeros, dk_out, dv_out, sems, own_sems,
 ):
     slots, width, lanes = raw_ref.shape
     size = col_ref.shape[0]
@@ -322,15 +314,13 @@
     group = att_ref.shape[1] // width
     score_scale = 1.0 / math.sqrt(size)
 
-    def copy_out(slot, which):
-        source, target = ((att_out, att_ref), (dq_out, dq_ref))[which]
-        return pltpu.make_async_copy(source.at[slot], target.at[slot_rows(slot), :], sems.at[which, slot])
+    def copy_out(source, slot, which):
+        target = (att_ref, dq_ref)[which]
+        return pltpu.make_async_copy(source, target.at[slot_rows(slot), :], sems.at[which, slot])
 
     def dead(slot, carry):
-        att_out[slot] = jnp.zeros(att_out.shape[1:], BF16)
-        dq_out[slot] = jnp.zeros(dq_out.shape[1:], BF16)
         for which in range(2):
-            copy_out(slot, which).start()
+            copy_out(zeros, slot, which).start()
         return carry
 
     def live(slot, carry):
@@ -349,20 +339,29 @@
                 att_out[slot, :, place] = attended[g * CL:(g + 1) * CL]
                 dq_out[slot, :, place] = query_out[g * CL:(g + 1) * CL]
         for which in range(2):
-            copy_out(slot, which).start()
+            copy_out((att_out, dq_out)[which].at[slot], slot, which).start()
         return carry
 
+    zeros[...] = jnp.zeros_like(zeros)
     lax.fori_loop(live_ref[0], slots, dead, 0)
-    lax.fori_loop(0, live_ref[0], live, 0)
     for head in range(heads):
         columns = slice(head * size, (head + 1) * size)
         own_grad = own_acc[:, head, 0].reshape(slots * CL, size) * score_scale
         own_unit, own_recip = unit(ck_ref[:, columns].astype(F32))
-        dk_ref[:, columns] = norm_back(own_grad, own_unit, own_recip, kg_ref[...]).astype(BF16)
-        dv_ref[:, columns] = own_acc[:, head, 1].reshape(slots * CL, size).astype(BF16)
+        dk_out[:, columns] = norm_back(own_grad, own_unit, own_recip, kg_ref[...]).astype(BF16)
+        dv_out[:, columns] = own_acc[:, head, 1].reshape(slots * CL, size).astype(BF16)
+    own_copies = [
+        pltpu.make_async_copy(dk_out, dk_ref, own_sems.at[0]),
+        pltpu.make_async_copy(dv_out, dv_ref, own_sems.at[1]),
+    ]
+    for copy in own_copies:
+        copy.start()
+    lax.fori_loop(0, live_ref[0], live, 0)
+    for copy in own_copies:
+        copy.wait()
     for slot in range(slots):
         for which in range(2):
-            copy_out(slot, which).wait()
+            copy_out(zeros, slot, which).wait()
 
 
 def post(
@@ -376,9 +375,12 @@
     return pl.pallas_call(
         post_kernel,
         in_specs=[SMEM_SPEC] * 2 + [VMEM_SPEC] * 10,
-        out_specs=[HBM_SPEC] * 2 + [VMEM_SPEC] * 2,
+        out_specs=[HBM_SPEC] * 4,
         out_shape=[out, out, own, own],
-        scratch_shapes=[slab, slab, pltpu.SemaphoreType.DMA((2, slots))],
+        scratch_shapes=[
+            slab, slab, pltpu.VMEM((CL, shape[1]), BF16), pltpu.VMEM(keys.shape, BF16), pltpu.VMEM(keys.shape, BF16),
+            pltpu.SemaphoreType.DMA((2, slots)), pltpu.SemaphoreType.DMA((2,)),
+        ],
         compiler_params=params(),
         cost_estimate=cost(3 * 10**9, 4 * 10**6),
         name="post",
@@ -394,23 +396,26 @@
     return terms[0]
 
 
-def add_kernel(keep_ref, came_ref, *refs, terms, size):
-    tail = gain_rows(tree([ref[0:1, :] for ref in refs[:terms]]), keep_ref.shape[1])
+def add_kernel(keep_ref, came_ref, *refs, terms):
+    tail = gain_rows(tree([ref[0:1, :] for ref in refs[:terms]]))
+    size = tail.shape[1]
     own_ref, send_refs = refs[terms], refs[terms + 1:]
     blocks = len(send_refs) + 1
     shard = keep_ref.shape[0] // blocks
     for at in range(blocks):
         place = slice(at * shard, (at + 1) * shard)
+        ref = send_refs[at - 1] if at > 0 else own_ref
         total = keep_ref[place, :] + came_ref[place, :].astype(F32)
-        ref = send_refs[at - 1] if at > 0 else own_ref
-        ref[:shard, :] = total.astype(ref.dtype)
-        ref[shard:, :] = tail.astype(ref.dtype)
+        for slab in range(keep_ref.shape[1] // size):
+            ref[slab * shard:(slab + 1) * shard, :] = total[:, slab * size:(slab + 1) * size].astype(ref.dtype)
+        ref[ref.shape[0] - TAIL:, :] = tail.astype(ref.dtype)
 
 
 def add(keep, came, terms, blocks):
-    shape = (keep.shape[0] // blocks + TAIL, keep.shape[1])
-    return pl.pallas_call(
-        functools.partial(add_kernel, terms=len(terms), size=terms[0].shape[1]),
+    size = terms[0].shape[1]
+    shape = (keep.size // blocks // size + TAIL, size)
+    return pl.pallas_call(
+        functools.partial(add_kernel, terms=len(terms)),
         in_specs=[VMEM_SPEC] * (2 + len(terms)),
         out_specs=[VMEM_SPEC] * blocks,
         out_shape=[jax.ShapeDtypeStruct(shape, F32)] + [jax.ShapeDtypeStruct(shape, BF16)] * (blocks - 1),
@@ -419,17 +424,17 @@
     )(keep, came, *terms)
 
 
-def chips_kernel(*refs, size):
-    total = tree([gain_term(ref[ref.shape[0] - TAIL:, :], size) for ref in refs[:-1]])
+def chips_kernel(*refs):
+    total = tree([gain_term(ref[ref.shape[0] - TAIL:, :]) for ref in refs[:-1]])
     refs[-1][...] = jnp.broadcast_to(total, refs[-1].shape)
 
 
-def sum_chips(blocks, size):
-    return pl.pallas_call(
-        functools.partial(chips_kernel, size=size),
+def sum_chips(blocks):
+    return pl.pallas_call(
+        chips_kernel,
         in_specs=[VMEM_SPEC] * len(blocks),
         out_specs=VMEM_SPEC,
-        out_shape=jax.ShapeDtypeStruct((8, size), F32),
+        out_shape=jax.ShapeDtypeStruct((8, blocks[0].shape[1]), F32),
         compiler_params=params(),
         name="sum_chips",
     )(*blocks)
@@ -458,14 +463,18 @@
     parts, (raw_ref, kg_ref, key_ref, value_ref) = refs[:-4], refs[-4:]
     size = kg_ref.shape[1]
     shard, width = raw_ref.shape
-    total = parts[0][:shard, :]
-    for ref in parts[1:]:
-        total = total + ref[:shard, :].astype(F32)
-    for head in range(width // size):
-        columns = slice(head * size, (head + 1) * size)
-        unit_rows, recip = unit(raw_ref[:, columns].astype(F32))
-        key_ref[:, columns] = norm_back(total[:, columns], unit_rows, recip, kg_ref[...])
-    value_ref[...] = total[:, width:]
+    heads = width // size
+    for slab in range(2 * heads):
+        rows = slice(slab * shard, (slab + 1) * shard)
+        total = parts[0][rows, :]
+        for ref in parts[1:]:
+            total = total + ref[rows, :].astype(F32)
+        columns = slice(slab % heads * size, (slab % heads + 1) * size)
+        if slab < heads:
+            unit_rows, recip = unit(raw_ref[:, columns].astype(F32))
+            key_ref[:, columns] = norm_back(total, unit_rows, recip, kg_ref[...])
+        else:
+            value_ref[:, columns] = total
 
 
 def finish(blocks, raw, key_gain):
@@ -502,10 +511,9 @@
     if by_permute:
         even = [mine] + [swap(mine, "grp", step) for step in range(2, grp, 2)]
         odd = [swap(mine, "grp", 1)]
-        even, queries, grads, raw, recip, query_col = lax.optimization_barrier(
-            (even, queries, grads, raw, recip, query_col)
-        )
-        odd += [swap(piece, "grp", 1) for piece in even[1:]]
+        for at in range(1, len(even)):
+            even[at], query_col = lax.optimization_barrier((even[at], query_col))
+            odd.append(swap(even[at], "grp", 1))
         pieces = [piece for pair in zip(even, odd) for piece in pair]
     else:
         pieces = [lax.all_gather(mine, "grp", axis=0, tiled=True)]
@@ -518,14 +526,17 @@
     )
     if by_permute:
         came = swap(send[0], "grp", 1)
-        terms = [term] + [swap(term, "tp", step) for step in range(1, tp)]
+        others = {step: swap(term, "tp", step) for step in range(tp - 1, 0, -1)}
+        terms = [term] + [others[step] for step in range(1, tp)]
         own, *blocks = add(keep, came, terms, grp // 2)
-        blocks = [own] + [swap(block, "grp", 2 * at + 2) for at, block in enumerate(blocks)]
+        others = {at: swap(blocks[at], "grp", 2 * at + 2) for at in range(len(blocks) - 1, -1, -1)}
+        blocks = [own] + [others[at] for at in range(len(blocks))]
         blocks, attended = lax.optimization_barrier((blocks, attended))
-        total = sum_chips(blocks, size)
+        total = sum_chips(blocks)
         terms = [total, swap(total, "grp", 1)]
     else:
-        blocks = [lax.psum_scatter(keep, "grp", scatter_dimension=0, tiled=True)]
+        block = lax.psum_scatter(keep, "grp", scatter_dimension=0, tiled=True)
+        blocks = [jnp.concatenate([block[:, at:at + size] for at in range(0, 2 * width, size)], axis=0)]
         terms = [lax.psum(term, ("grp", "tp"))]
     prompt_key_grads, prompt_value_grads = finish(blocks, prompt_keys, key_gain)
     query_gain_grad, key_gain_grad = gain_grads(terms, query_gain, key_gain)

time: 38.8 us -> 38.1 us (0.982); the launches traced: 38.4 us -> 38.2 us
  Pallas kernels: 7.49 us -> 13.9 us
  starting transfers between devices: 17.5 us -> 13.4 us
  waiting for transfers between devices: 11.2 us -> 8.59 us
    pallas_call x1, Pallas kernels: 2.84 us -> 7.56 us  [attention(): pl.pallas_call(functools.partial(attention_kernel, parts=parts, heads=hea...]
    ppermute x15, starting transfers between devices: 17.5 us -> 13.4 us  [swap(): lax.ppermute(values, axis, [(i, i ^ step) for i in range(lax.axis_size(ax...]
    ppermute x15, waiting for transfers between devices: 11.2 us -> 8.59 us  [swap(): lax.ppermute(values, axis, [(i, i ^ step) for i in range(lax.axis_size(ax...]
    pallas_call x1, Pallas kernels: 2.72 us -> 3.68 us  [post(): pl.pallas_call(post_kernel, in_specs=[SMEM_SPEC] * 2 + [VMEM_SPEC] * 10,...]
    pallas_call x1, Pallas kernels: 0.34 us -> 1.06 us  [prepare(): pl.pallas_call(prepare_kernel, in_specs=[SMEM_SPEC] + [VMEM_SPEC] * 3, ou...]
  transfers between devices with their start and end apart: 15 -> 15, of which waited for: 10 -> 8; matrix products, arithmetic and copies ran while one was open for 0% -> 0% of each run, Pallas kernels for 10% -> 15%
where the time goes in v4:
time: 38.1 us; the launch traced here: 38.2 us
  Pallas kernels  13.9 us (36%)
  starting transfers between devices  13.4 us (35%)
  waiting for transfers between devices  8.59 us (23%)
  between operations  1.45 us (4%)
  local copies, waits for them, and re-layouts  0.83 us (2%)
    ppermute x15, starting transfers between devices, swap(): lax.ppermute(values, axis, [(i, i ^ step) for i in range(lax.axis_size(ax...  13.4 us
    ppermute x15, waiting for transfers between devices, swap(): lax.ppermute(values, axis, [(i, i ^ step) for i in range(lax.axis_size(ax...  8.59 us
    pallas_call x1, Pallas kernels, attention(): pl.pallas_call(functools.partial(attention_kernel, parts=parts, heads=hea...  7.56 us
    pallas_call x1, Pallas kernels, post(): pl.pallas_call(post_kernel, in_specs=[SMEM_SPEC] * 2 + [VMEM_SPEC] * 10,...  3.68 us
    pallas_call x1, Pallas kernels, prepare(): pl.pallas_call(prepare_kernel, in_specs=[SMEM_SPEC] + [VMEM_SPEC] * 3, ou...  1.06 us
    pallas_call x1, Pallas kernels, finish(): pl.pallas_call(finish_kernel, in_specs=[VMEM_SPEC] * (len(blocks) + 2), o...  0.84 us
    unnamed x18, local copies, waits for them, and re-layouts  0.83 us
  transfers between devices with their start and end apart: 15, of which 8 were waited for; matrix products, arithmetic and copies ran while one was open for 0% of the time, Pallas kernels for 15%

profile of v4, /device:TPU:0, one launch (start us, length us, event | category | flops | bytes accessed | tf_op | source)
XLA Modules:
  0.0 38.2 jit_solution(7944127749888737815)
XLA Ops:
  0.6 0.0 copy-start
  0.6 0.0 copy-start.1
  0.7 0.0 copy-start.7
  0.7 0.7 %copy-done = bf16[96,256]{1,0:T(8,128)(2,1)S(1)} copy-done((bf16[96,256]{1,0:T(8,128)(2,1)S(1)}, bf16[96,256]{1,0:T(8,128)(2,1)}, u32[]{:S(2)}) %copy-start) | copy-done | bytes 49176
  1.4 0.0 copy-done.1
  1.4 0.0 copy-done.7
  1.5 0.0 copy-start.2
  1.5 0.0 copy-start.3
  1.5 0.0 copy-start.4
  1.5 0.1 pack.1.refs_9_
  1.6 4.0 %collective-permute-start.5 = (bf16[96,512]{1,0:T(8,128)(2,1)S(1)}, bf16[96,512]{1,0:T(8,128)(2,1)S(1)}, u32[]{:S(2)}, u32[]{:S(2)}) collective-permute-start(bf16[96,512]{1,0:T(8,128)(2,1)S(1)} %pack.1.refs_9_), channel_id=1, source_target_pairs={{0,24},{4,28},{8,16},{12,20},{16,8},{20,12},{24,0},{28,4},{1,25},{... | collective-permute-start | bytes 294920 | tf_op jit(solution)/shard_map/ppermute | solution.py:494
  5.6 0.5 %collective-permute-start.3 = (bf16[96,512]{1,0:T(8,128)(2,1)S(1)}, bf16[96,512]{1,0:T(8,128)(2,1)S(1)}, u32[]{:S(2)}, u32[]{:S(2)}) collective-permute-start(bf16[96,512]{1,0:T(8,128)(2,1)S(1)} %pack.1.refs_9_), channel_id=1, source_target_pairs={{0,16},{4,20},{8,24},{12,28},{16,0},{20,4},{24,8},{28,12},{1,17},{... | collective-permute-start | bytes 294920 | tf_op jit(solution)/shard_map/ppermute | solution.py:494
  6.1 0.1 collective-permute-start.1
  6.2 0.0 collective-permute-start
  6.9 0.0 copy-done.2
  6.9 0.0 copy-done.3
  6.9 0.0 copy-done.4
  6.9 0.0 copy-start.5
  6.9 0.0 copy-start.6
  6.9 0.0 copy-start.8
  6.9 1.1 %prepare.1 = (bf16[4,256,512]{2,1,0:T(8,128)(2,1)S(1)}, f32[4,8,512]{2,1,0:T(8,128)S(1)}, bf16[4,256,512]{2,1,0:T(8,128)(2,1)S(1)}, bf16[4,256,512]{2,1,0:T(8,128)(2,1)S(1)}, f32[128,512]{1,0:T(8,128)S(1)}) custom-call(s32[1]{0:T(128)S(6)} %copy.18.live_ref.refs_0_, bf16[256,2048]{1,0:T(8,128)(2,1)S(1)} %copy-done.3, bf16[256,2048]{1,0:T(8,128)(2,1)S(1)} %copy-done.4, ...), custom_call_target="tpu_custom_call" | custom-call | flops 2000000000 | bytes 3145728 | tf_op jit(solution)/shard_map/prepare/pallas_call | solution.py:134
  8.0 2.8 %collective-permute-done.1.refs_11_ = bf16[96,512]{1,0:T(8,128)(2,1)S(1)} collective-permute-done((bf16[96,512]{1,0:T(8,128)(2,1)S(1)}, bf16[96,512]{1,0:T(8,128)(2,1)S(1)}, u32[]{:S(2)}, u32[]{:S(2)}) %collective-permute-start.1) | collective-permute-done | bytes 98336 | tf_op jit(solution)/shard_map/ppermute | solution.py:494
  10.8 0.0 collective-permute-done.3.refs_13_
  10.8 0.0 collective-permute-done.5.refs_15_
  10.8 0.0 collective-permute-start.6
  10.8 0.5 %collective-permute-start.4 = (bf16[96,512]{1,0:T(8,128)(2,1)S(1)}, bf16[96,512]{1,0:T(8,128)(2,1)S(1)}, u32[]{:S(2)}, u32[]{:S(2)}) collective-permute-start(bf16[96,512]{1,0:T(8,128)(2,1)S(1)} %collective-permute-done.3.refs_13_), channel_id=1, source_target_pairs={{0,4},{4,0},{8,12},{12,8},{16,20},{20,16},{24,28},{28,24},{1,5},{5... | collective-permute-start | bytes 294920 | tf_op jit(solution)/shard_map/ppermute | solution.py:494
  11.3 0.1 collective-permute-start.2
  11.4 0.0 collective-permute-done.refs_10_
  11.4 0.7 %collective-permute-done.6.refs_16_ = bf16[96,512]{1,0:T(8,128)(2,1)S(1)} collective-permute-done((bf16[96,512]{1,0:T(8,128)(2,1)S(1)}, bf16[96,512]{1,0:T(8,128)(2,1)S(1)}, u32[]{:S(2)}, u32[]{:S(2)}) %collective-permute-start.6) | collective-permute-done | bytes 98336 | tf_op jit(solution)/shard_map/ppermute | solution.py:494
  12.1 0.2 collective-permute-done.4.refs_14_
  12.3 0.4 collective-permute-done.2.refs_12_
  12.6 0.0 copy-done.5
  12.6 0.0 copy-done.6
  12.6 0.0 copy-done.8
  12.6 7.6 %attention.1 = (bf16[4,256,512]{2,1,0:T(8,128)(2,1)S(1)}, bf16[4,2,448,512]{3,2,1,0:T(8,128)(2,1)S(1)}, bf16[768,256]{1,0:T(8,128)(2,1)S(1)}, bf16[256,256]{1,0:...) custom-call(s32[1]{0:T(128)S(6)} %copy.18.live_ref.refs_0_, ...), custom_call_target="tpu_custom_call" | custom-call | flops 3000000000 | bytes 10000000 | tf_op jit(solution)/shard_map/attention/pallas_call | solution.py:286
  20.2 0.2 collective-permute-start.7
  20.4 3.6 %collective-permute-start.10 = (f32[8,128]{1,0:T(8,128)S(1)}, f32[8,128]{1,0:T(8,128)S(1)}, u32[]{:S(2)}, u32[]{:S(2)}) collective-permute-start(f32[8,128]{1,0:T(8,128)S(1)} %get-tuple-element.62.refs_0_), channel_id=1, source_target_pairs={{0,3},{1,2},{2,1},{3,0},{4,7},{5,6},{6,5},{7,4},{8,11},{9,10},{10,... | collective-permute-start | bytes 12296 | tf_op jit(solution)/shard_map/ppermute | solution.py:494
  24.0 0.0 collective-permute-start.9
  24.0 0.8 %collective-permute-start.8 = (f32[8,128]{1,0:T(8,128)S(1)}, f32[8,128]{1,0:T(8,128)S(1)}, u32[]{:S(2)}, u32[]{:S(2)}) collective-permute-start(f32[8,128]{1,0:T(8,128)S(1)} %get-tuple-element.62.refs_0_), channel_id=1, source_target_pairs={{0,1},{1,0},{2,3},{3,2},{4,5},{5,4},{6,7},{7,6},{8,9},{9,8},{10,11... | collective-permute-start | bytes 12296 | tf_op jit(solution)/shard_map/ppermute | solution.py:494
  24.8 1.0 %collective-permute-done.10.refs_3_ = f32[8,128]{1,0:T(8,128)S(1)} collective-permute-done((f32[8,128]{1,0:T(8,128)S(1)}, f32[8,128]{1,0:T(8,128)S(1)}, u32[]{:S(2)}, u32[]{:S(2)}) %collective-permute-start.10) | collective-permute-done | bytes 4128 | tf_op jit(solution)/shard_map/ppermute | solution.py:494
  25.8 2.7 %collective-permute-done.9.refs_2_ = f32[8,128]{1,0:T(8,128)S(1)} collective-permute-done((f32[8,128]{1,0:T(8,128)S(1)}, f32[8,128]{1,0:T(8,128)S(1)}, u32[]{:S(2)}, u32[]{:S(2)}) %collective-permute-start.9) | collective-permute-done | bytes 4128 | tf_op jit(solution)/shard_map/ppermute | solution.py:494
  28.5 0.0 collective-permute-done.8.refs_1_
  28.5 0.0 collective-permute-done.7.came_ref
  28.5 0.1 add.1
  28.6 1.5 %collective-permute-start.11 = (bf16[400,128]{1,0:T(8,128)(2,1)S(1)}, bf16[400,128]{1,0:T(8,128)(2,1)S(1)}, u32[]{:S(2)}, u32[]{:S(2)}) collective-permute-start(bf16[400,128]{1,0:T(8,128)(2,1)S(1)} %get-tuple-element.64), channel_id=1, source_target_pairs={{0,8},{4,12},{8,0},{12,4},{16,24},{20,28},{24,16},{28,20},{1,9},{5... | collective-permute-start | bytes 307208 | tf_op jit(solution)/shard_map/ppermute | solution.py:494
  30.1 0.7 %collective-permute-start.12 = (bf16[400,128]{1,0:T(8,128)(2,1)S(1)}, bf16[400,128]{1,0:T(8,128)(2,1)S(1)}, u32[]{:S(2)}, u32[]{:S(2)}) collective-permute-start(bf16[400,128]{1,0:T(8,128)(2,1)S(1)} %get-tuple-element.65), channel_id=1, source_target_pairs={{0,16},{4,20},{8,24},{12,28},{16,0},{20,4},{24,8},{28,12},{1,17},{... | collective-permute-start | bytes 307208 | tf_op jit(solution)/shard_map/ppermute | solution.py:494
  30.9 1.3 %collective-permute-start.13 = (bf16[400,128]{1,0:T(8,128)(2,1)S(1)}, bf16[400,128]{1,0:T(8,128)(2,1)S(1)}, u32[]{:S(2)}, u32[]{:S(2)}) collective-permute-start(bf16[400,128]{1,0:T(8,128)(2,1)S(1)} %get-tuple-element.66), channel_id=1, source_target_pairs={{0,24},{4,28},{8,16},{12,20},{16,8},{20,12},{24,0},{28,4},{1,25},{... | collective-permute-start | bytes 307208 | tf_op jit(solution)/shard_map/ppermute | solution.py:494
  32.2 3.7 %post.1 = (bf16[256,2048]{1,0:T(8,128)(2,1)}, bf16[256,2048]{1,0:T(8,128)(2,1)}, bf16[256,256]{1,0:T(8,128)(2,1)}, bf16[256,256]{1,0:T(8,128)(2,1)}) custom-call(s32[1]{0:T(128)S(6)} %copy.18.live_ref.refs_0_, s32[4]{0:T(128)S(1)} %copy-done.8, bf16[4,256,512]{2,1,0:T(8,128)(2,1)S(1)} %get-tuple-element.67.att_t_ref, ...), custom_call_target="tpu_custom_call" | custom-call | flops 3000000000 | bytes 4000000 | tf_op jit(solution)/shard_map/post/pallas_call | solution.py:375
  35.9 0.0 collective-permute-done.11.refs_1_
  35.9 0.0 collective-permute-done.12.refs_2_
  35.9 0.5 %collective-permute-done.13.refs_3_ = bf16[400,128]{1,0:T(8,128)(2,1)S(1)} collective-permute-done((bf16[400,128]{1,0:T(8,128)(2,1)S(1)}, bf16[400,128]{1,0:T(8,128)(2,1)S(1)}, u32[]{:S(2)}, u32[]{:S(2)}) %collective-permute-start.13) | collective-permute-done | bytes 102432 | tf_op jit(solution)/shard_map/ppermute | solution.py:494
  36.4 0.1 collective-permute-start.14
  36.5 0.8 %finish.1 = (f32[96,256]{1,0:T(8,128)}, f32[96,256]{1,0:T(8,128)}) custom-call(f32[400,128]{1,0:T(8,128)S(1)} %get-tuple-element.80.refs_0_, bf16[400,128]{1,0:T(8,128)(2,1)S(1)} %collective-permute-done.11.refs_1_, bf16[400,128]{1,0:T(8,128)(2,1)S(1)} %collective-permute-done.12.refs_2_, bf16[400,128]{1,0:T(8,128)(2,1)S(1)} %collective-permute-done.13.refs_3_, ...), custom_call_target="tpu_custom_call" | custom-call | flops 100000000 | bytes 1000000 | tf_op jit(solution)/shard_map/finish/pallas_call | solution.py:482
  37.3 0.3 collective-permute-done.14.refs_1_
  37.7 0.5 %gain_grads.1 = (f32[1,128]{1,0:T(1,128)}, f32[1,128]{1,0:T(1,128)}) custom-call(f32[8,128]{1,0:T(8,128)S(1)} %sum_chips.1.refs_0_, f32[8,128]{1,0:T(8,128)S(1)} %collective-permute-done.14.refs_1_, f32[1,128]{1,0:T(1,128)S(1)} %bitcast.11, f32[1,128]{1,0:T(1,128)S(1)} %bitcast.9), custom_call_target="tpu_custom_call" | custom-call | tf_op jit(solution)/shard_map/gain_grads/pallas_call | solution.py:452
  (2 shorter events, 0.0 us)
Async XLA Ops:
  0.6 0.8 %copy-start = (bf16[96,256]{1,0:T(8,128)(2,1)S(1)}, bf16[96,256]{1,0:T(8,128)(2,1)}, u32[]{:S(2)}) copy-start(bf16[96,256]{1,0:T(8,128)(2,1)} %refs_4_.1) | copy-start | bytes 147460
  0.6 0.8 %copy-start.1 = (f32[128]{0:T(128)S(1)}, f32[128]{0:T(128)}, u32[]{:S(2)}) copy-start(f32[128]{0:T(128)} %param.16) | copy-start | bytes 1540
  0.7 0.8 %copy-start.7 = (bf16[96,256]{1,0:T(8,128)(2,1)S(1)}, bf16[96,256]{1,0:T(8,128)(2,1)}, u32[]{:S(2)}) copy-start(bf16[96,256]{1,0:T(8,128)(2,1)} %values_ref) | copy-start | bytes 147460
  1.5 5.4 %copy-start.2 = (f32[128]{0:T(128)S(1)}, f32[128]{0:T(128)}, u32[]{:S(2)}) copy-start(f32[128]{0:T(128)} %param.15) | copy-start | bytes 1540
  1.5 5.4 %copy-start.3 = (bf16[256,2048]{1,0:T(8,128)(2,1)S(1)}, bf16[256,2048]{1,0:T(8,128)(2,1)}, u32[]{:S(2)}) copy-start(bf16[256,2048]{1,0:T(8,128)(2,1)} %q_ref.1) | copy-start | bytes 3145732
  1.5 5.4 %copy-start.4 = (bf16[256,2048]{1,0:T(8,128)(2,1)S(1)}, bf16[256,2048]{1,0:T(8,128)(2,1)}, u32[]{:S(2)}) copy-start(bf16[256,2048]{1,0:T(8,128)(2,1)} %do_ref.1) | copy-start | bytes 3145732
  1.6 9.2 %collective-permute-start.5 = (bf16[96,512]{1,0:T(8,128)(2,1)S(1)}, bf16[96,512]{1,0:T(8,128)(2,1)S(1)}, u32[]{:S(2)}, u32[]{:S(2)}) collective-permute-start(bf16[96,512]{1,0:T(8,128)(2,1)S(1)} %pack.1.refs_9_), channel_id=1, source_target_pairs={{0,24},{4,28},{8,16},{12,20},{16,8},{20,12},{24,0},{28,4},{1,25},{... | collective-permute-start | bytes 294920 | tf_op jit(solution)/shard_map/ppermute | solution.py:494
  5.6 5.2 %collective-permute-start.3 = (bf16[96,512]{1,0:T(8,128)(2,1)S(1)}, bf16[96,512]{1,0:T(8,128)(2,1)S(1)}, u32[]{:S(2)}, u32[]{:S(2)}) collective-permute-start(bf16[96,512]{1,0:T(8,128)(2,1)S(1)} %pack.1.refs_9_), channel_id=1, source_target_pairs={{0,16},{4,20},{8,24},{12,28},{16,0},{20,4},{24,8},{28,12},{1,17},{... | collective-permute-start | bytes 294920 | tf_op jit(solution)/shard_map/ppermute | solution.py:494
  6.1 4.7 %collective-permute-start.1 = (bf16[96,512]{1,0:T(8,128)(2,1)S(1)}, bf16[96,512]{1,0:T(8,128)(2,1)S(1)}, u32[]{:S(2)}, u32[]{:S(2)}) collective-permute-start(bf16[96,512]{1,0:T(8,128)(2,1)S(1)} %pack.1.refs_9_), channel_id=1, source_target_pairs={{0,8},{4,12},{8,0},{12,4},{16,24},{20,28},{24,16},{28,20},{1,9},{5... | collective-permute-start | bytes 294920 | tf_op jit(solution)/shard_map/ppermute | solution.py:494
  6.2 5.2 %collective-permute-start = (bf16[96,512]{1,0:T(8,128)(2,1)S(1)}, bf16[96,512]{1,0:T(8,128)(2,1)S(1)}, u32[]{:S(2)}, u32[]{:S(2)}) collective-permute-start(bf16[96,512]{1,0:T(8,128)(2,1)S(1)} %pack.1.refs_9_), channel_id=1, source_target_pairs={{0,4},{4,0},{8,12},{12,8},{16,20},{20,16},{24,28},{28,24},{1,5},{5... | collective-permute-start | bytes 294920 | tf_op jit(solution)/shard_map/ppermute | solution.py:494
  6.9 5.7 %copy-start.5 = (bf16[256,256]{1,0:T(8,128)(2,1)S(1)}, bf16[256,256]{1,0:T(8,128)(2,1)}, u32[]{:S(2)}) copy-start(bf16[256,256]{1,0:T(8,128)(2,1)} %refs_6_.1) | copy-start | bytes 393220
  6.9 5.7 %copy-start.6 = (bf16[256,256]{1,0:T(8,128)(2,1)S(1)}, bf16[256,256]{1,0:T(8,128)(2,1)}, u32[]{:S(2)}) copy-start(bf16[256,256]{1,0:T(8,128)(2,1)} %ck_ref.1) | copy-start | bytes 393220
  6.9 5.7 %copy-start.8 = (s32[4]{0:T(128)S(1)}, s32[4]{0:T(128)}, u32[]{:S(2)}) copy-start(s32[4]{0:T(128)} %prompt_ref.1) | copy-start | bytes 52
  10.8 1.3 %collective-permute-start.6 = (bf16[96,512]{1,0:T(8,128)(2,1)S(1)}, bf16[96,512]{1,0:T(8,128)(2,1)S(1)}, u32[]{:S(2)}, u32[]{:S(2)}) collective-permute-start(bf16[96,512]{1,0:T(8,128)(2,1)S(1)} %collective-permute-done.5.refs_15_), channel_id=1, source_target_pairs={{0,4},{4,0},{8,12},{12,8},{16,20},{20,16},{24,28},{28,24},{1,5},{5... | collective-permute-start | bytes 294920 | tf_op jit(solution)/shard_map/ppermute | solution.py:494
  10.8 1.4 %collective-permute-start.4 = (bf16[96,512]{1,0:T(8,128)(2,1)S(1)}, bf16[96,512]{1,0:T(8,128)(2,1)S(1)}, u32[]{:S(2)}, u32[]{:S(2)}) collective-permute-start(bf16[96,512]{1,0:T(8,128)(2,1)S(1)} %collective-permute-done.3.refs_13_), channel_id=1, source_target_pairs={{0,4},{4,0},{8,12},{12,8},{16,20},{20,16},{24,28},{28,24},{1,5},{5... | collective-permute-start | bytes 294920 | tf_op jit(solution)/shard_map/ppermute | solution.py:494
  11.3 1.3 %collective-permute-start.2 = (bf16[96,512]{1,0:T(8,128)(2,1)S(1)}, bf16[96,512]{1,0:T(8,128)(2,1)S(1)}, u32[]{:S(2)}, u32[]{:S(2)}) collective-permute-start(bf16[96,512]{1,0:T(8,128)(2,1)S(1)} %collective-permute-done.1.refs_11_), channel_id=1, source_target_pairs={{0,4},{4,0},{8,12},{12,8},{16,20},{20,16},{24,28},{28,24},{1,5},{5... | collective-permute-start | bytes 294920 | tf_op jit(solution)/shard_map/ppermute | solution.py:494
  20.2 8.3 %collective-permute-start.7 = (bf16[384,512]{1,0:T(8,128)(2,1)S(1)}, bf16[384,512]{1,0:T(8,128)(2,1)S(1)}, u32[]{:S(2)}, u32[]{:S(2)}) collective-permute-start(bf16[384,512]{1,0:T(8,128)(2,1)S(1)} %get-tuple-element.61), channel_id=1, source_target_pairs={{0,4},{4,0},{8,12},{12,8},{16,20},{20,16},{24,28},{28,24},{1,5},{5... | collective-permute-start | bytes 1179656 | tf_op jit(solution)/shard_map/ppermute | solution.py:494
  20.4 5.4 %collective-permute-start.10 = (f32[8,128]{1,0:T(8,128)S(1)}, f32[8,128]{1,0:T(8,128)S(1)}, u32[]{:S(2)}, u32[]{:S(2)}) collective-permute-start(f32[8,128]{1,0:T(8,128)S(1)} %get-tuple-element.62.refs_0_), channel_id=1, source_target_pairs={{0,3},{1,2},{2,1},{3,0},{4,7},{5,6},{6,5},{7,4},{8,11},{9,10},{10,... | collective-permute-start | bytes 12296 | tf_op jit(solution)/shard_map/ppermute | solution.py:494
  24.0 4.5 %collective-permute-start.9 = (f32[8,128]{1,0:T(8,128)S(1)}, f32[8,128]{1,0:T(8,128)S(1)}, u32[]{:S(2)}, u32[]{:S(2)}) collective-permute-start(f32[8,128]{1,0:T(8,128)S(1)} %get-tuple-element.62.refs_0_), channel_id=1, source_target_pairs={{0,2},{1,3},{2,0},{3,1},{4,6},{5,7},{6,4},{7,5},{8,10},{9,11},{10,... | collective-permute-start | bytes 12296 | tf_op jit(solution)/shard_map/ppermute | solution.py:494
  24.0 4.5 %collective-permute-start.8 = (f32[8,128]{1,0:T(8,128)S(1)}, f32[8,128]{1,0:T(8,128)S(1)}, u32[]{:S(2)}, u32[]{:S(2)}) collective-permute-start(f32[8,128]{1,0:T(8,128)S(1)} %get-tuple-element.62.refs_0_), channel_id=1, source_target_pairs={{0,1},{1,0},{2,3},{3,2},{4,5},{5,4},{6,7},{7,6},{8,9},{9,8},{10,11... | collective-permute-start | bytes 12296 | tf_op jit(solution)/shard_map/ppermute | solution.py:494
  28.6 7.2 %collective-permute-start.11 = (bf16[400,128]{1,0:T(8,128)(2,1)S(1)}, bf16[400,128]{1,0:T(8,128)(2,1)S(1)}, u32[]{:S(2)}, u32[]{:S(2)}) collective-permute-start(bf16[400,128]{1,0:T(8,128)(2,1)S(1)} %get-tuple-element.64), channel_id=1, source_target_pairs={{0,8},{4,12},{8,0},{12,4},{16,24},{20,28},{24,16},{28,20},{1,9},{5... | collective-permute-start | bytes 307208 | tf_op jit(solution)/shard_map/ppermute | solution.py:494
  30.1 5.8 %collective-permute-start.12 = (bf16[400,128]{1,0:T(8,128)(2,1)S(1)}, bf16[400,128]{1,0:T(8,128)(2,1)S(1)}, u32[]{:S(2)}, u32[]{:S(2)}) collective-permute-start(bf16[400,128]{1,0:T(8,128)(2,1)S(1)} %get-tuple-element.65), channel_id=1, source_target_pairs={{0,16},{4,20},{8,24},{12,28},{16,0},{20,4},{24,8},{28,12},{1,17},{... | collective-permute-start | bytes 307208 | tf_op jit(solution)/shard_map/ppermute | solution.py:494
  30.9 5.6 %collective-permute-start.13 = (bf16[400,128]{1,0:T(8,128)(2,1)S(1)}, bf16[400,128]{1,0:T(8,128)(2,1)S(1)}, u32[]{:S(2)}, u32[]{:S(2)}) collective-permute-start(bf16[400,128]{1,0:T(8,128)(2,1)S(1)} %get-tuple-element.66), channel_id=1, source_target_pairs={{0,24},{4,28},{8,16},{12,20},{16,8},{20,12},{24,0},{28,4},{1,25},{... | collective-permute-start | bytes 307208 | tf_op jit(solution)/shard_map/ppermute | solution.py:494
  36.4 1.2 %collective-permute-start.14 = (f32[8,128]{1,0:T(8,128)S(1)}, f32[8,128]{1,0:T(8,128)S(1)}, u32[]{:S(2)}, u32[]{:S(2)}) collective-permute-start(f32[8,128]{1,0:T(8,128)S(1)} %sum_chips.1.refs_0_), channel_id=1, source_target_pairs={{0,4},{4,0},{8,12},{12,8},{16,20},{20,16},{24,28},{28,24},{1,5},{5... | collective-permute-start | bytes 12296 | tf_op jit(solution)/shard_map/ppermute | solution.py:494

commit v5 on v4

--- a/solution.py
+++ b/solution.py
@@ -396,48 +396,85 @@
     return terms[0]
 
 
-def add_kernel(keep_ref, came_ref, *refs, terms):
-    tail = gain_rows(tree([ref[0:1, :] for ref in refs[:terms]]))
+def first_partner(me):
+    return 1 + me % 2, 2 - me % 2
+
+
+def stack_slabs(total, size):
+    return jnp.concatenate([total[:, at:at + size] for at in range(0, total.shape[1], size)], axis=0)
+
+
+def add_kernel(me_ref, keep_ref, came_ref, *refs):
+    terms, (own_ref, later_ref, send_ref) = refs[:-3], refs[-3:]
+    tail = gain_rows(tree([ref[0:1, :] for ref in terms[:1] + terms[:0:-1]]))
     size = tail.shape[1]
-    own_ref, send_refs = refs[terms], refs[terms + 1:]
-    blocks = len(send_refs) + 1
-    shard = keep_ref.shape[0] // blocks
-    for at in range(blocks):
-        place = slice(at * shard, (at + 1) * shard)
-        ref = send_refs[at - 1] if at > 0 else own_ref
-        total = keep_ref[place, :] + came_ref[place, :].astype(F32)
-        for slab in range(keep_ref.shape[1] // size):
-            ref[slab * shard:(slab + 1) * shard, :] = total[:, slab * size:(slab + 1) * size].astype(ref.dtype)
-        ref[ref.shape[0] - TAIL:, :] = tail.astype(ref.dtype)
-
-
-def add(keep, came, terms, blocks):
+    shard = keep_ref.shape[0] // 4
+    block = own_ref.shape[0] - TAIL
+    near, far = first_partner(me_ref[0])
+
+    def total(number):
+        rows = pl.ds(pl.multiple_of(number * shard, shard), shard)
+        return stack_slabs(keep_ref[rows, :] + came_ref[rows, :].astype(F32), size)
+
+    own_ref[:block, :] = total(0)
+    own_ref[block:, :] = tail.astype(F32)
+    later_ref[...] = total(far)
+    send_ref[:block, :] = total(near).astype(BF16)
+    send_ref[block:2 * block, :] = total(3).astype(BF16)
+    send_ref[2 * block:, :] = tail
+
+
+def add(me, keep, came, terms):
     size = terms[0].shape[1]
-    shape = (keep.size // blocks // size + TAIL, size)
-    return pl.pallas_call(
-        functools.partial(add_kernel, terms=len(terms)),
-        in_specs=[VMEM_SPEC] * (2 + len(terms)),
-        out_specs=[VMEM_SPEC] * blocks,
-        out_shape=[jax.ShapeDtypeStruct(shape, F32)] + [jax.ShapeDtypeStruct(shape, BF16)] * (blocks - 1),
+    block = keep.size // 4 // size
+    return pl.pallas_call(
+        add_kernel,
+        in_specs=[SMEM_SPEC] + [VMEM_SPEC] * (2 + len(terms)),
+        out_specs=[VMEM_SPEC] * 3,
+        out_shape=[
+            jax.ShapeDtypeStruct((block + TAIL, size), F32),
+            jax.ShapeDtypeStruct((block, size), F32),
+            jax.ShapeDtypeStruct((2 * block + TAIL, size), BF16),
+        ],
         compiler_params=params(),
         name="add",
-    )(keep, came, *terms)
-
-
-def chips_kernel(*refs):
-    total = tree([gain_term(ref[ref.shape[0] - TAIL:, :]) for ref in refs[:-1]])
-    refs[-1][...] = jnp.broadcast_to(total, refs[-1].shape)
-
-
-def sum_chips(blocks):
+    )(me, keep, came, *terms)
+
+
+def relay_kernel(own_ref, later_ref, came_ref, out_ref, send_ref):
+    block = later_ref.shape[0]
+    out_ref[:block, :] = own_ref[:block, :] + came_ref[:block, :].astype(F32)
+    tail = gain_rows(gain_term(own_ref[block:, :]) + gain_term(came_ref[2 * block:, :]))
+    out_ref[block:, :] = tail.astype(F32)
+    send_ref[:block, :] = (later_ref[...] + came_ref[block:2 * block, :].astype(F32)).astype(BF16)
+    send_ref[block:, :] = tail
+
+
+def relay(own, later, came):
+    return pl.pallas_call(
+        relay_kernel,
+        in_specs=[VMEM_SPEC] * 3,
+        out_specs=[VMEM_SPEC] * 2,
+        out_shape=[jax.ShapeDtypeStruct(own.shape, F32), jax.ShapeDtypeStruct(own.shape, BF16)],
+        compiler_params=params(),
+        name="relay",
+    )(own, later, came)
+
+
+def chips_kernel(own_ref, came_ref, out_ref):
+    total = gain_term(own_ref[own_ref.shape[0] - TAIL:, :]) + gain_term(came_ref[came_ref.shape[0] - TAIL:, :])
+    out_ref[...] = jnp.broadcast_to(total, out_ref.shape)
+
+
+def sum_chips(own, came):
     return pl.pallas_call(
         chips_kernel,
-        in_specs=[VMEM_SPEC] * len(blocks),
+        in_specs=[VMEM_SPEC] * 2,
         out_specs=VMEM_SPEC,
-        out_shape=jax.ShapeDtypeStruct((8, blocks[0].shape[1]), F32),
+        out_shape=jax.ShapeDtypeStruct((8, own.shape[1]), F32),
         compiler_params=params(),
         name="sum_chips",
-    )(*blocks)
+    )(own, came)
 
 
 def last_kernel(*refs):
@@ -490,8 +527,9 @@
     )(*blocks, raw, key_gain)
 
 
-def swap(values, axis, step):
-    return lax.ppermute(values, axis, [(i, i ^ step) for i in range(lax.axis_size(axis))])
+def swap(values, axis, step, odd_step=None):
+    steps = (step, step if odd_step is None else odd_step)
+    return lax.ppermute(values, axis, [(i, i ^ steps[i % 2]) for i in range(lax.axis_size(axis))])
 
 
 def local(
@@ -501,7 +539,7 @@
     grp, tp = lax.axis_size("grp"), lax.axis_size("tp")
     shard = prompt_keys.shape[0]
     size = query_gain.shape[0]
-    by_permute = shard % 16 == 0 and grp > 1 and grp & (grp - 1) == 0 and tp & (tp - 1) == 0
+    by_permute = shard % 16 == 0 and grp == 8 and tp & (tp - 1) == 0
     slots, width = slot_prompts.shape[0], comp_keys.shape[1]
     query_gain, key_gain = query_gain.reshape(1, size), key_gain.reshape(1, size)
     me = lax.axis_index("grp").astype(jnp.int32).reshape(1) if by_permute else jnp.zeros((1,), jnp.int32)
@@ -526,13 +564,13 @@
     )
     if by_permute:
         came = swap(send[0], "grp", 1)
-        others = {step: swap(term, "tp", step) for step in range(tp - 1, 0, -1)}
-        terms = [term] + [others[step] for step in range(1, tp)]
-        own, *blocks = add(keep, came, terms, grp // 2)
-        others = {at: swap(blocks[at], "grp", 2 * at + 2) for at in range(len(blocks) - 1, -1, -1)}
-        blocks = [own] + [others[at] for at in range(len(blocks))]
-        blocks, attended = lax.optimization_barrier((blocks, attended))
-        total = sum_chips(blocks)
+        terms = [term] + [swap(term, "tp", step) for step in range(tp - 1, 0, -1)]
+        own, later, sent = add(me, keep, came, terms)
+        came = swap(sent, "grp", 2, 4)
+        came, attended = lax.optimization_barrier((came, attended))
+        own, sent = relay(own, later, came)
+        blocks = [own, swap(sent, "grp", 4, 2)]
+        total = sum_chips(*blocks)
         terms = [total, swap(total, "grp", 1)]
     else:
         block = lax.psum_scatter(keep, "grp", scatter_dimension=0, tiled=True)

time: 38.1 us -> 41.6 us (1.092); the launches traced: 38.2 us -> 42.4 us
  waiting for transfers between devices: 8.59 us -> 17 us
  Pallas kernels: 13.9 us -> 7.02 us
  starting transfers between devices: 13.4 us -> 16.1 us
    ppermute x15 -> x14, waiting for transfers between devices: 8.59 us -> 17 us  [swap(): lax.ppermute(values, axis, [(i, i ^ steps[i % 2]) for i in range(lax.axis...]
    pallas_call x1, Pallas kernels: 7.56 us -> 2.85 us  [attention(): pl.pallas_call(functools.partial(attention_kernel, parts=parts, heads=hea...]
    ppermute x15 -> x14, starting transfers between devices: 13.4 us -> 16.1 us  [swap(): lax.ppermute(values, axis, [(i, i ^ steps[i % 2]) for i in range(lax.axis...]
    pallas_call x1, Pallas kernels: 3.68 us -> 2.21 us  [post(): pl.pallas_call(post_kernel, in_specs=[SMEM_SPEC] * 2 + [VMEM_SPEC] * 10,...]
    pallas_call x1, Pallas kernels: 1.06 us -> 0.34 us  [prepare(): pl.pallas_call(prepare_kernel, in_specs=[SMEM_SPEC] + [VMEM_SPEC] * 3, ou...]
  transfers between devices with their start and end apart: 15 -> 14, of which waited for: 8 -> 9; matrix products, arithmetic and copies ran while one was open for 0% -> 0% of each run, Pallas kernels for 15% -> 8%
where the time goes in v5:
time: 41.6 us; the launch traced here: 42.4 us
  waiting for transfers between devices  17 us (41%)
  starting transfers between devices  16.1 us (39%)
  Pallas kernels  7.02 us (17%)
  between operations  1.44 us (3%)
  local copies, waits for them, and re-layouts  0.82 us (2%)
    ppermute x14, waiting for transfers between devices, swap(): lax.ppermute(values, axis, [(i, i ^ steps[i % 2]) for i in range(lax.axis...  17 us
    ppermute x14, starting transfers between devices, swap(): lax.ppermute(values, axis, [(i, i ^ steps[i % 2]) for i in range(lax.axis...  16.1 us
    pallas_call x1, Pallas kernels, attention(): pl.pallas_call(functools.partial(attention_kernel, parts=parts, heads=hea...  2.85 us
    pallas_call x1, Pallas kernels, post(): pl.pallas_call(post_kernel, in_specs=[SMEM_SPEC] * 2 + [VMEM_SPEC] * 10,...  2.21 us
    pallas_call x1, Pallas kernels, finish(): pl.pallas_call(finish_kernel, in_specs=[VMEM_SPEC] * (len(blocks) + 2), o...  0.84 us
  transfers between devices with their start and end apart: 14, of which 9 were waited for; matrix products, arithmetic and copies ran while one was open for 0% of the time, Pallas kernels for 8%

profile of v5, /device:TPU:0, one launch (start us, length us, event | category | flops | bytes accessed | tf_op | source)
XLA Modules:
  0.0 42.4 jit_solution(8432583251784516903)
XLA Ops:
  0.6 0.0 copy-start.1
  0.6 0.0 copy-start.6
  0.7 0.0 copy-start.7
  0.7 0.6 %copy-done.1 = f32[128]{0:T(128)S(1)} copy-done((f32[128]{0:T(128)S(1)}, f32[128]{0:T(128)}, u32[]{:S(2)}) %copy-start.1) | copy-done | bytes 536
  1.3 0.2 copy-done.6
  1.5 0.0 copy-done.7
  1.5 0.0 copy-start
  1.5 0.0 copy-start.2
  1.5 0.0 copy-start.3
  1.5 0.1 pack.1.refs_9_
  1.6 4.0 %collective-permute-start.5 = (bf16[96,512]{1,0:T(8,128)(2,1)S(1)}, bf16[96,512]{1,0:T(8,128)(2,1)S(1)}, u32[]{:S(2)}, u32[]{:S(2)}) collective-permute-start(bf16[96,512]{1,0:T(8,128)(2,1)S(1)} %pack.1.refs_9_), channel_id=1, source_target_pairs={{0,24},{4,28},{8,16},{12,20},{16,8},{20,12},{24,0},{28,4},{1,25},{... | collective-permute-start | bytes 294920 | tf_op jit(solution)/shard_map/ppermute | solution.py:532
  5.6 0.5 %collective-permute-start.3 = (bf16[96,512]{1,0:T(8,128)(2,1)S(1)}, bf16[96,512]{1,0:T(8,128)(2,1)S(1)}, u32[]{:S(2)}, u32[]{:S(2)}) collective-permute-start(bf16[96,512]{1,0:T(8,128)(2,1)S(1)} %pack.1.refs_9_), channel_id=1, source_target_pairs={{0,16},{4,20},{8,24},{12,28},{16,0},{20,4},{24,8},{28,12},{1,17},{... | collective-permute-start | bytes 294920 | tf_op jit(solution)/shard_map/ppermute | solution.py:532
  6.1 0.1 collective-permute-start.1
  6.2 0.0 collective-permute-start
  6.9 0.0 copy-done
  6.9 0.0 copy-done.2
  6.9 0.0 copy-done.3
  6.9 0.0 copy-start.4
  6.9 0.0 copy-start.5
  6.9 0.0 copy-start.8
  6.9 0.3 prepare.1
  7.3 3.5 %collective-permute-done.1.refs_11_ = bf16[96,512]{1,0:T(8,128)(2,1)S(1)} collective-permute-done((bf16[96,512]{1,0:T(8,128)(2,1)S(1)}, bf16[96,512]{1,0:T(8,128)(2,1)S(1)}, u32[]{:S(2)}, u32[]{:S(2)}) %collective-permute-start.1) | collective-permute-done | bytes 98336 | tf_op jit(solution)/shard_map/ppermute | solution.py:532
  10.8 0.0 collective-permute-done.3.refs_13_
  10.8 0.0 collective-permute-done.5.refs_15_
  10.8 0.0 collective-permute-start.6
  10.8 0.5 %collective-permute-start.4 = (bf16[96,512]{1,0:T(8,128)(2,1)S(1)}, bf16[96,512]{1,0:T(8,128)(2,1)S(1)}, u32[]{:S(2)}, u32[]{:S(2)}) collective-permute-start(bf16[96,512]{1,0:T(8,128)(2,1)S(1)} %collective-permute-done.3.refs_13_), channel_id=1, source_target_pairs={{0,4},{4,0},{8,12},{12,8},{16,20},{20,16},{24,28},{28,24},{1,5},{5... | collective-permute-start | bytes 294920 | tf_op jit(solution)/shard_map/ppermute | solution.py:532
  11.3 0.1 collective-permute-start.2
  11.4 0.0 collective-permute-done.refs_10_
  11.4 0.7 %collective-permute-done.6.refs_16_ = bf16[96,512]{1,0:T(8,128)(2,1)S(1)} collective-permute-done((bf16[96,512]{1,0:T(8,128)(2,1)S(1)}, bf16[96,512]{1,0:T(8,128)(2,1)S(1)}, u32[]{:S(2)}, u32[]{:S(2)}) %collective-permute-start.6) | collective-permute-done | bytes 98336 | tf_op jit(solution)/shard_map/ppermute | solution.py:532
  12.1 0.2 collective-permute-done.4.refs_14_
  12.3 0.4 collective-permute-done.2.refs_12_
  12.6 0.0 copy-done.4
  12.6 0.0 copy-done.5
  12.6 0.0 copy-done.8
  12.6 2.9 %attention.1 = (bf16[4,256,512]{2,1,0:T(8,128)(2,1)S(1)}, bf16[4,2,448,512]{3,2,1,0:T(8,128)(2,1)S(1)}, bf16[768,256]{1,0:T(8,128)(2,1)S(1)}, bf16[256,256]{1,0:...) custom-call(s32[1]{0:T(128)S(6)} %copy.18.live_ref.refs_0_, ...), custom_call_target="tpu_custom_call" | custom-call | flops 3000000000 | bytes 10000000 | tf_op jit(solution)/shard_map/attention/pallas_call | solution.py:286
  15.5 5.0 %collective-permute-start.7 = (bf16[384,512]{1,0:T(8,128)(2,1)S(1)}, bf16[384,512]{1,0:T(8,128)(2,1)S(1)}, u32[]{:S(2)}, u32[]{:S(2)}) collective-permute-start(bf16[384,512]{1,0:T(8,128)(2,1)S(1)} %get-tuple-element.59), channel_id=1, source_target_pairs={{0,4},{4,0},{8,12},{12,8},{16,20},{20,16},{24,28},{28,24},{1,5},{5... | collective-permute-start | bytes 1179656 | tf_op jit(solution)/shard_map/ppermute | solution.py:532
  20.5 1.6 %collective-permute-start.10 = (f32[8,128]{1,0:T(8,128)S(1)}, f32[8,128]{1,0:T(8,128)S(1)}, u32[]{:S(2)}, u32[]{:S(2)}) collective-permute-start(f32[8,128]{1,0:T(8,128)S(1)} %get-tuple-element.60.refs_0_), channel_id=1, source_target_pairs={{0,1},{1,0},{2,3},{3,2},{4,5},{5,4},{6,7},{7,6},{8,9},{9,8},{10,11... | collective-permute-start | bytes 12296 | tf_op jit(solution)/shard_map/ppermute | solution.py:532
  22.0 2.6 %collective-permute-start.9 = (f32[8,128]{1,0:T(8,128)S(1)}, f32[8,128]{1,0:T(8,128)S(1)}, u32[]{:S(2)}, u32[]{:S(2)}) collective-permute-start(f32[8,128]{1,0:T(8,128)S(1)} %get-tuple-element.60.refs_0_), channel_id=1, source_target_pairs={{0,2},{1,3},{2,0},{3,1},{4,6},{5,7},{6,4},{7,5},{8,10},{9,11},{10,... | collective-permute-start | bytes 12296 | tf_op jit(solution)/shard_map/ppermute | solution.py:532
  24.6 0.2 collective-permute-start.8
  24.8 0.0 collective-permute-done.10.refs_3_
  24.8 1.7 %collective-permute-done.9.refs_2_ = f32[8,128]{1,0:T(8,128)S(1)} collective-permute-done((f32[8,128]{1,0:T(8,128)S(1)}, f32[8,128]{1,0:T(8,128)S(1)}, u32[]{:S(2)}, u32[]{:S(2)}) %collective-permute-start.9) | collective-permute-done | bytes 4128 | tf_op jit(solution)/shard_map/ppermute | solution.py:532
  26.5 3.5 %collective-permute-done.8.refs_1_ = f32[8,128]{1,0:T(8,128)S(1)} collective-permute-done((f32[8,128]{1,0:T(8,128)S(1)}, f32[8,128]{1,0:T(8,128)S(1)}, u32[]{:S(2)}, u32[]{:S(2)}) %collective-permute-start.8) | collective-permute-done | bytes 4128 | tf_op jit(solution)/shard_map/ppermute | solution.py:532
  30.0 0.0 collective-permute-done.7.came_ref
  30.0 0.1 add.1
  30.1 1.5 %collective-permute-start.11 = (bf16[784,128]{1,0:T(8,128)(2,1)S(1)}, bf16[784,128]{1,0:T(8,128)(2,1)S(1)}, u32[]{:S(2)}, u32[]{:S(2)}) collective-permute-start(bf16[784,128]{1,0:T(8,128)(2,1)S(1)} %get-tuple-element.61), channel_id=1, source_target_pairs={{0,8},{4,20},{8,0},{12,28},{16,24},{20,4},{24,16},{28,12},{1,9},{5... | collective-permute-start | bytes 602120 | tf_op jit(solution)/shard_map/ppermute | solution.py:532
  31.6 2.2 %post.1 = (bf16[256,2048]{1,0:T(8,128)(2,1)}, bf16[256,2048]{1,0:T(8,128)(2,1)}, bf16[256,256]{1,0:T(8,128)(2,1)}, bf16[256,256]{1,0:T(8,128)(2,1)}) custom-call(s32[1]{0:T(128)S(6)} %copy.18.live_ref.refs_0_, s32[4]{0:T(128)S(1)} %copy-done.8, bf16[4,256,512]{2,1,0:T(8,128)(2,1)S(1)} %get-tuple-element.62.att_t_ref, ...), custom_call_target="tpu_custom_call" | custom-call | flops 3000000000 | bytes 4000000 | tf_op jit(solution)/shard_map/post/pallas_call | solution.py:375
  33.9 2.0 %collective-permute-done.11.came_ref = bf16[784,128]{1,0:T(8,128)(2,1)S(1)} collective-permute-done((bf16[784,128]{1,0:T(8,128)(2,1)S(1)}, bf16[784,128]{1,0:T(8,128)(2,1)S(1)}, u32[]{:S(2)}, u32[]{:S(2)}) %collective-permute-start.11) | collective-permute-done | bytes 200736 | tf_op jit(solution)/shard_map/ppermute | solution.py:532
  35.9 0.1 relay.1
  36.0 0.1 collective-permute-start.12
  36.0 4.6 %collective-permute-done.12.refs_1_.came_ref = bf16[400,128]{1,0:T(8,128)(2,1)S(1)} collective-permute-done((bf16[400,128]{1,0:T(8,128)(2,1)S(1)}, bf16[400,128]{1,0:T(8,128)(2,1)S(1)}, u32[]{:S(2)}, u32[]{:S(2)}) %collective-permute-start.12) | collective-permute-done | bytes 102432 | tf_op jit(solution)/shard_map/ppermute | solution.py:532
  40.7 0.0 collective-permute-start.13
  40.7 0.8 %finish.1 = (f32[96,256]{1,0:T(8,128)}, f32[96,256]{1,0:T(8,128)}) custom-call(f32[400,128]{1,0:T(8,128)S(1)} %get-tuple-element.78.refs_0_.own_ref, bf16[400,128]{1,0:T(8,128)(2,1)S(1)} %collective-permute-done.12.refs_1_.came_ref, bf16[96,256]{1,0:T(8,128)(2,1)S(1)} %copy-done.7, f32[1,128]{1,0:T(1,128)S(1)} %bitcast.10), custom_call_target="tpu_custom_call" | custom-call | flops 100000000 | bytes 1000000 | tf_op jit(solution)/shard_map/finish/pallas_call | solution.py:519
  41.5 0.3 collective-permute-done.13.refs_1_
  41.9 0.5 %gain_grads.1 = (f32[1,128]{1,0:T(1,128)}, f32[1,128]{1,0:T(1,128)}) custom-call(f32[8,128]{1,0:T(8,128)S(1)} %sum_chips.1.refs_0_, f32[8,128]{1,0:T(8,128)S(1)} %collective-permute-done.13.refs_1_, f32[1,128]{1,0:T(1,128)S(1)} %bitcast.6, f32[1,128]{1,0:T(1,128)S(1)} %bitcast.11), custom_call_target="tpu_custom_call" | custom-call | tf_op jit(solution)/shard_map/gain_grads/pallas_call | solution.py:489
  (2 shorter events, 0.0 us)
Async XLA Ops:
  0.6 0.7 %copy-start.1 = (f32[128]{0:T(128)S(1)}, f32[128]{0:T(128)}, u32[]{:S(2)}) copy-start(f32[128]{0:T(128)} %param.16) | copy-start | bytes 1540
  0.6 0.8 %copy-start.6 = (bf16[96,256]{1,0:T(8,128)(2,1)S(1)}, bf16[96,256]{1,0:T(8,128)(2,1)}, u32[]{:S(2)}) copy-start(bf16[96,256]{1,0:T(8,128)(2,1)} %values_ref) | copy-start | bytes 147460
  0.7 0.8 %copy-start.7 = (bf16[96,256]{1,0:T(8,128)(2,1)S(1)}, bf16[96,256]{1,0:T(8,128)(2,1)}, u32[]{:S(2)}) copy-start(bf16[96,256]{1,0:T(8,128)(2,1)} %refs_2_.1) | copy-start | bytes 147460
  1.5 5.4 %copy-start = (f32[128]{0:T(128)S(1)}, f32[128]{0:T(128)}, u32[]{:S(2)}) copy-start(f32[128]{0:T(128)} %param.15) | copy-start | bytes 1540
  1.5 5.4 %copy-start.2 = (bf16[256,2048]{1,0:T(8,128)(2,1)S(1)}, bf16[256,2048]{1,0:T(8,128)(2,1)}, u32[]{:S(2)}) copy-start(bf16[256,2048]{1,0:T(8,128)(2,1)} %q_ref.1) | copy-start | bytes 3145732
  1.5 5.4 %copy-start.3 = (bf16[256,2048]{1,0:T(8,128)(2,1)S(1)}, bf16[256,2048]{1,0:T(8,128)(2,1)}, u32[]{:S(2)}) copy-start(bf16[256,2048]{1,0:T(8,128)(2,1)} %do_ref.1) | copy-start | bytes 3145732
  1.6 9.2 %collective-permute-start.5 = (bf16[96,512]{1,0:T(8,128)(2,1)S(1)}, bf16[96,512]{1,0:T(8,128)(2,1)S(1)}, u32[]{:S(2)}, u32[]{:S(2)}) collective-permute-start(bf16[96,512]{1,0:T(8,128)(2,1)S(1)} %pack.1.refs_9_), channel_id=1, source_target_pairs={{0,24},{4,28},{8,16},{12,20},{16,8},{20,12},{24,0},{28,4},{1,25},{... | collective-permute-start | bytes 294920 | tf_op jit(solution)/shard_map/ppermute | solution.py:532
  5.6 5.2 %collective-permute-start.3 = (bf16[96,512]{1,0:T(8,128)(2,1)S(1)}, bf16[96,512]{1,0:T(8,128)(2,1)S(1)}, u32[]{:S(2)}, u32[]{:S(2)}) collective-permute-start(bf16[96,512]{1,0:T(8,128)(2,1)S(1)} %pack.1.refs_9_), channel_id=1, source_target_pairs={{0,16},{4,20},{8,24},{12,28},{16,0},{20,4},{24,8},{28,12},{1,17},{... | collective-permute-start | bytes 294920 | tf_op jit(solution)/shard_map/ppermute | solution.py:532
  6.1 4.7 %collective-permute-start.1 = (bf16[96,512]{1,0:T(8,128)(2,1)S(1)}, bf16[96,512]{1,0:T(8,128)(2,1)S(1)}, u32[]{:S(2)}, u32[]{:S(2)}) collective-permute-start(bf16[96,512]{1,0:T(8,128)(2,1)S(1)} %pack.1.refs_9_), channel_id=1, source_target_pairs={{0,8},{4,12},{8,0},{12,4},{16,24},{20,28},{24,16},{28,20},{1,9},{5... | collective-permute-start | bytes 294920 | tf_op jit(solution)/shard_map/ppermute | solution.py:532
  6.2 5.2 %collective-permute-start = (bf16[96,512]{1,0:T(8,128)(2,1)S(1)}, bf16[96,512]{1,0:T(8,128)(2,1)S(1)}, u32[]{:S(2)}, u32[]{:S(2)}) collective-permute-start(bf16[96,512]{1,0:T(8,128)(2,1)S(1)} %pack.1.refs_9_), channel_id=1, source_target_pairs={{0,4},{4,0},{8,12},{12,8},{16,20},{20,16},{24,28},{28,24},{1,5},{5... | collective-permute-start | bytes 294920 | tf_op jit(solution)/shard_map/ppermute | solution.py:532
  6.9 5.7 %copy-start.4 = (bf16[256,256]{1,0:T(8,128)(2,1)S(1)}, bf16[256,256]{1,0:T(8,128)(2,1)}, u32[]{:S(2)}) copy-start(bf16[256,256]{1,0:T(8,128)(2,1)} %refs_6_.1) | copy-start | bytes 393220
  6.9 5.7 %copy-start.5 = (bf16[256,256]{1,0:T(8,128)(2,1)S(1)}, bf16[256,256]{1,0:T(8,128)(2,1)}, u32[]{:S(2)}) copy-start(bf16[256,256]{1,0:T(8,128)(2,1)} %ck_ref.1) | copy-start | bytes 393220
  6.9 5.7 %copy-start.8 = (s32[4]{0:T(128)S(1)}, s32[4]{0:T(128)}, u32[]{:S(2)}) copy-start(s32[4]{0:T(128)} %prompt_ref.1) | copy-start | bytes 52
  10.8 1.3 %collective-permute-start.6 = (bf16[96,512]{1,0:T(8,128)(2,1)S(1)}, bf16[96,512]{1,0:T(8,128)(2,1)S(1)}, u32[]{:S(2)}, u32[]{:S(2)}) collective-permute-start(bf16[96,512]{1,0:T(8,128)(2,1)S(1)} %collective-permute-done.5.refs_15_), channel_id=1, source_target_pairs={{0,4},{4,0},{8,12},{12,8},{16,20},{20,16},{24,28},{28,24},{1,5},{5... | collective-permute-start | bytes 294920 | tf_op jit(solution)/shard_map/ppermute | solution.py:532
  10.8 1.4 %collective-permute-start.4 = (bf16[96,512]{1,0:T(8,128)(2,1)S(1)}, bf16[96,512]{1,0:T(8,128)(2,1)S(1)}, u32[]{:S(2)}, u32[]{:S(2)}) collective-permute-start(bf16[96,512]{1,0:T(8,128)(2,1)S(1)} %collective-permute-done.3.refs_13_), channel_id=1, source_target_pairs={{0,4},{4,0},{8,12},{12,8},{16,20},{20,16},{24,28},{28,24},{1,5},{5... | collective-permute-start | bytes 294920 | tf_op jit(solution)/shard_map/ppermute | solution.py:532
  11.3 1.3 %collective-permute-start.2 = (bf16[96,512]{1,0:T(8,128)(2,1)S(1)}, bf16[96,512]{1,0:T(8,128)(2,1)S(1)}, u32[]{:S(2)}, u32[]{:S(2)}) collective-permute-start(bf16[96,512]{1,0:T(8,128)(2,1)S(1)} %collective-permute-done.1.refs_11_), channel_id=1, source_target_pairs={{0,4},{4,0},{8,12},{12,8},{16,20},{20,16},{24,28},{28,24},{1,5},{5... | collective-permute-start | bytes 294920 | tf_op jit(solution)/shard_map/ppermute | solution.py:532
  15.5 14.6 %collective-permute-start.7 = (bf16[384,512]{1,0:T(8,128)(2,1)S(1)}, bf16[384,512]{1,0:T(8,128)(2,1)S(1)}, u32[]{:S(2)}, u32[]{:S(2)}) collective-permute-start(bf16[384,512]{1,0:T(8,128)(2,1)S(1)} %get-tuple-element.59), channel_id=1, source_target_pairs={{0,4},{4,0},{8,12},{12,8},{16,20},{20,16},{24,28},{28,24},{1,5},{5... | collective-permute-start | bytes 1179656 | tf_op jit(solution)/shard_map/ppermute | solution.py:532
  20.5 4.4 %collective-permute-start.10 = (f32[8,128]{1,0:T(8,128)S(1)}, f32[8,128]{1,0:T(8,128)S(1)}, u32[]{:S(2)}, u32[]{:S(2)}) collective-permute-start(f32[8,128]{1,0:T(8,128)S(1)} %get-tuple-element.60.refs_0_), channel_id=1, source_target_pairs={{0,1},{1,0},{2,3},{3,2},{4,5},{5,4},{6,7},{7,6},{8,9},{9,8},{10,11... | collective-permute-start | bytes 12296 | tf_op jit(solution)/shard_map/ppermute | solution.py:532
  22.0 4.5 %collective-permute-start.9 = (f32[8,128]{1,0:T(8,128)S(1)}, f32[8,128]{1,0:T(8,128)S(1)}, u32[]{:S(2)}, u32[]{:S(2)}) collective-permute-start(f32[8,128]{1,0:T(8,128)S(1)} %get-tuple-element.60.refs_0_), channel_id=1, source_target_pairs={{0,2},{1,3},{2,0},{3,1},{4,6},{5,7},{6,4},{7,5},{8,10},{9,11},{10,... | collective-permute-start | bytes 12296 | tf_op jit(solution)/shard_map/ppermute | solution.py:532
  24.6 5.4 %collective-permute-start.8 = (f32[8,128]{1,0:T(8,128)S(1)}, f32[8,128]{1,0:T(8,128)S(1)}, u32[]{:S(2)}, u32[]{:S(2)}) collective-permute-start(f32[8,128]{1,0:T(8,128)S(1)} %get-tuple-element.60.refs_0_), channel_id=1, source_target_pairs={{0,3},{1,2},{2,1},{3,0},{4,7},{5,6},{6,5},{7,4},{8,11},{9,10},{10,... | collective-permute-start | bytes 12296 | tf_op jit(solution)/shard_map/ppermute | solution.py:532
  30.1 5.8 %collective-permute-start.11 = (bf16[784,128]{1,0:T(8,128)(2,1)S(1)}, bf16[784,128]{1,0:T(8,128)(2,1)S(1)}, u32[]{:S(2)}, u32[]{:S(2)}) collective-permute-start(bf16[784,128]{1,0:T(8,128)(2,1)S(1)} %get-tuple-element.61), channel_id=1, source_target_pairs={{0,8},{4,20},{8,0},{12,28},{16,24},{20,4},{24,16},{28,12},{1,9},{5... | collective-permute-start | bytes 602120 | tf_op jit(solution)/shard_map/ppermute | solution.py:532
  36.0 4.7 %collective-permute-start.12 = (bf16[400,128]{1,0:T(8,128)(2,1)S(1)}, bf16[400,128]{1,0:T(8,128)(2,1)S(1)}, u32[]{:S(2)}, u32[]{:S(2)}) collective-permute-start(bf16[400,128]{1,0:T(8,128)(2,1)S(1)} %get-tuple-element.79), channel_id=1, source_target_pairs={{0,16},{4,12},{8,24},{12,4},{16,0},{20,28},{24,8},{28,20},{1,17},{... | collective-permute-start | bytes 307208 | tf_op jit(solution)/shard_map/ppermute | solution.py:532
  40.7 1.2 %collective-permute-start.13 = (f32[8,128]{1,0:T(8,128)S(1)}, f32[8,128]{1,0:T(8,128)S(1)}, u32[]{:S(2)}, u32[]{:S(2)}) collective-permute-start(f32[8,128]{1,0:T(8,128)S(1)} %sum_chips.1.refs_0_), channel_id=1, source_target_pairs={{0,4},{4,0},{8,12},{12,8},{16,20},{20,16},{24,28},{28,24},{1,5},{5... | collective-permute-start | bytes 12296 | tf_op jit(solution)/shard_map/ppermute | solution.py:532

commit v6 on v4

--- a/solution.py
+++ b/solution.py
@@ -304,24 +304,88 @@
     )(live_counts, slot_prompts, me, queries, grads, keys, values, key_gain, mask, *pieces)
 
 
+def copy_slots(live_ref, zeros, out, target, sems):
+    slots = out.shape[0]
+
+    def copy(source, slot):
+        return pltpu.make_async_copy(source, target.at[slot_rows(slot), :], sems.at[slot])
+
+    def dead(slot, carry):
+        copy(zeros, slot).start()
+        return carry
+
+    def wait():
+        for slot in range(slots):
+            copy(zeros, slot).wait()
+
+    zeros[...] = jnp.zeros_like(zeros)
+    lax.fori_loop(live_ref[0], slots, dead, 0)
+    return lambda slot: copy(out.at[slot], slot).start(), wait
+
+
+def turn_kernel(
+    live_ref, att_t_ref, own_acc, ck_ref, kg_ref, att_ref, dk_ref, dv_ref, att_out, zeros, dk_out, dv_out, sems, own_sems,
+):
+    slots, width, _ = att_t_ref.shape
+    size = kg_ref.shape[1]
+    heads = width // size
+    group = att_ref.shape[1] // width
+    start, wait = copy_slots(live_ref, zeros, att_out, att_ref, sems)
+
+    def live(slot, carry):
+        for head in range(heads):
+            attended = att_t_ref[slot, head * size:(head + 1) * size, :].T
+            for g, place in enumerate(head_columns(head, group, size)):
+                att_out[slot, :, place] = attended[g * CL:(g + 1) * CL]
+        start(slot)
+        return carry
+
+    lax.fori_loop(0, live_ref[0], live, 0)
+    for head in range(heads):
+        columns = slice(head * size, (head + 1) * size)
+        own_grad = own_acc[:, head, 0].reshape(slots * CL, size) * (1.0 / math.sqrt(size))
+        own_unit, own_recip = unit(ck_ref[:, columns].astype(F32))
+        dk_out[:, columns] = norm_back(own_grad, own_unit, own_recip, kg_ref[...]).astype(BF16)
+        dv_out[:, columns] = own_acc[:, head, 1].reshape(slots * CL, size).astype(BF16)
+    own_copies = [
+        pltpu.make_async_copy(dk_out, dk_ref, own_sems.at[0]),
+        pltpu.make_async_copy(dv_out, dv_ref, own_sems.at[1]),
+    ]
+    for copy in own_copies:
+        copy.start()
+    for copy in own_copies:
+        copy.wait()
+    wait()
+
+
+def turn(live_counts, att_t, own_acc, keys, key_gain, shape):
+    slots = att_t.shape[0]
+    own = jax.ShapeDtypeStruct(keys.shape, BF16)
+    own_slab = pltpu.VMEM(keys.shape, BF16)
+    return pl.pallas_call(
+        turn_kernel,
+        in_specs=[SMEM_SPEC] + [VMEM_SPEC] * 4,
+        out_specs=[HBM_SPEC] * 3,
+        out_shape=[jax.ShapeDtypeStruct(shape, BF16), own, own],
+        scratch_shapes=[
+            pltpu.VMEM((slots, CL, shape[1]), BF16), pltpu.VMEM((CL, shape[1]), BF16), own_slab, own_slab,
+            pltpu.SemaphoreType.DMA((slots,)), pltpu.SemaphoreType.DMA((2,)),
+        ],
+        compiler_params=params(),
+        cost_estimate=cost(2 * 10**9, 2 * 10**6),
+        name="turn",
+    )(live_counts, att_t, own_acc, keys, key_gain)
+
+
 def post_kernel(
-    live_ref, prompt_ref, att_t_ref, ds_ref, pool_keys, own_keys_ref, own_acc, raw_ref, recip_ref, col_ref,
-    ck_ref, kg_ref, att_ref, dq_ref, dk_ref, dv_ref, att_out, dq_out, zeros, dk_out, dv_out, sems, own_sems,
+    live_ref, prompt_ref, ds_ref, pool_keys, own_keys_ref, raw_ref, recip_ref, col_ref, dq_ref, dq_out, zeros, sems,
 ):
     slots, width, lanes = raw_ref.shape
     size = col_ref.shape[0]
     heads = width // size
-    group = att_ref.shape[1] // width
+    group = dq_ref.shape[1] // width
     score_scale = 1.0 / math.sqrt(size)
-
-    def copy_out(source, slot, which):
-        target = (att_ref, dq_ref)[which]
-        return pltpu.make_async_copy(source, target.at[slot_rows(slot), :], sems.at[which, slot])
-
-    def dead(slot, carry):
-        for which in range(2):
-            copy_out(zeros, slot, which).start()
-        return carry
+    start, wait = copy_slots(live_ref, zeros, dq_out, dq_ref, sems)
 
     def live(slot, carry):
         rows = pl.ds(pl.multiple_of(prompt_ref[slot] * PL, PL), PL)
@@ -334,60 +398,30 @@
             scaled = query_grad * col_ref[...]
             mean = jnp.mean(query_unit * scaled, axis=0, keepdims=True)
             query_out = (recip * (scaled - query_unit * mean)).astype(BF16).T
-            attended = att_t_ref[slot, columns, :].T
             for g, place in enumerate(head_columns(head, group, size)):
-                att_out[slot, :, place] = attended[g * CL:(g + 1) * CL]
                 dq_out[slot, :, place] = query_out[g * CL:(g + 1) * CL]
-        for which in range(2):
-            copy_out((att_out, dq_out)[which].at[slot], slot, which).start()
+        start(slot)
         return carry
 
-    zeros[...] = jnp.zeros_like(zeros)
-    lax.fori_loop(live_ref[0], slots, dead, 0)
-    for head in range(heads):
-        columns = slice(head * size, (head + 1) * size)
-        own_grad = own_acc[:, head, 0].reshape(slots * CL, size) * score_scale
-        own_unit, own_recip = unit(ck_ref[:, columns].astype(F32))
-        dk_out[:, columns] = norm_back(own_grad, own_unit, own_recip, kg_ref[...]).astype(BF16)
-        dv_out[:, columns] = own_acc[:, head, 1].reshape(slots * CL, size).astype(BF16)
-    own_copies = [
-        pltpu.make_async_copy(dk_out, dk_ref, own_sems.at[0]),
-        pltpu.make_async_copy(dv_out, dv_ref, own_sems.at[1]),
-    ]
-    for copy in own_copies:
-        copy.start()
     lax.fori_loop(0, live_ref[0], live, 0)
-    for copy in own_copies:
-        copy.wait()
-    for slot in range(slots):
-        for which in range(2):
-            copy_out(zeros, slot, which).wait()
-
-
-def post(
-    live_counts, slot_prompts, att_t, score_grads, pool_keys, own_keys, own_acc, raw, recip, query_col,
-    keys, key_gain, shape,
-):
+    wait()
+
+
+def post(live_counts, slot_prompts, score_grads, pool_keys, own_keys, raw, recip, query_col, shape):
     slots = raw.shape[0]
-    out = jax.ShapeDtypeStruct(shape, BF16)
-    own = jax.ShapeDtypeStruct(keys.shape, BF16)
-    slab = pltpu.VMEM((slots, CL, shape[1]), BF16)
     return pl.pallas_call(
         post_kernel,
-        in_specs=[SMEM_SPEC] * 2 + [VMEM_SPEC] * 10,
-        out_specs=[HBM_SPEC] * 4,
-        out_shape=[out, out, own, own],
+        in_specs=[SMEM_SPEC] * 2 + [VMEM_SPEC] * 6,
+        out_specs=HBM_SPEC,
+        out_shape=jax.ShapeDtypeStruct(shape, BF16),
         scratch_shapes=[
-            slab, slab, pltpu.VMEM((CL, shape[1]), BF16), pltpu.VMEM(keys.shape, BF16), pltpu.VMEM(keys.shape, BF16),
-            pltpu.SemaphoreType.DMA((2, slots)), pltpu.SemaphoreType.DMA((2,)),
+            pltpu.VMEM((slots, CL, shape[1]), BF16), pltpu.VMEM((CL, shape[1]), BF16),
+            pltpu.SemaphoreType.DMA((slots,)),
         ],
         compiler_params=params(),
         cost_estimate=cost(3 * 10**9, 4 * 10**6),
         name="post",
-    )(
-        live_counts, slot_prompts, att_t, score_grads, pool_keys, own_keys, own_acc, raw, recip, query_col,
-        keys, key_gain,
-    )
+    )(live_counts, slot_prompts, score_grads, pool_keys, own_keys, raw, recip, query_col)
 
 
 def tree(terms):
@@ -425,7 +459,8 @@
 
 
 def chips_kernel(*refs):
-    total = tree([gain_term(ref[ref.shape[0] - TAIL:, :]) for ref in refs[:-1]])
+    parts = [gain_term(ref[ref.shape[0] - TAIL:, :]) for ref in refs[:-1]]
+    total = tree(parts[:1] + parts[:0:-1])
     refs[-1][...] = jnp.broadcast_to(total, refs[-1].shape)
 
 
@@ -520,18 +555,18 @@
     att_t, score_grads, pool_keys, own_keys, own_acc, term, keep, *send = attention(
         live_counts, slot_prompts, me, queries, grads, comp_keys, comp_values, key_gain, mask, pieces,
     )
-    attended, query_grads, key_grads, value_grads = post(
-        live_counts, slot_prompts, att_t, score_grads, pool_keys, own_keys, own_acc, raw, recip, query_col,
-        comp_keys, key_gain, comp_queries.shape,
+    attended, key_grads, value_grads = turn(live_counts, att_t, own_acc, comp_keys, key_gain, comp_queries.shape)
+    query_grads = post(
+        live_counts, slot_prompts, score_grads, pool_keys, own_keys, raw, recip, query_col, comp_queries.shape,
     )
     if by_permute:
         came = swap(send[0], "grp", 1)
-        others = {step: swap(term, "tp", step) for step in range(tp - 1, 0, -1)}
-        terms = [term] + [others[step] for step in range(1, tp)]
+        terms = [term] + [swap(term, "tp", step) for step in range(1, tp)]
+        terms, attended = lax.optimization_barrier((terms, attended))
         own, *blocks = add(keep, came, terms, grp // 2)
-        others = {at: swap(blocks[at], "grp", 2 * at + 2) for at in range(len(blocks) - 1, -1, -1)}
-        blocks = [own] + [others[at] for at in range(len(blocks))]
-        blocks, attended = lax.optimization_barrier((blocks, attended))
+        blocks = [swap(block, "grp", 2 * at + 2) for at, block in enumerate(blocks)]
+        blocks, query_grads = lax.optimization_barrier((blocks, query_grads))
+        blocks = [own] + blocks[::-1]
         total = sum_chips(blocks)
         terms = [total, swap(total, "grp", 1)]
     else:

time: 38.1 us -> 38.3 us (level)
  Pallas kernels: 13.9 us -> 10.1 us
  starting transfers between devices: 13.4 us -> 16.5 us
  waiting for transfers between devices: 8.59 us -> 9.17 us
    pallas_call x1, Pallas kernels: 7.56 us -> 4.4 us  [attention(): pl.pallas_call(functools.partial(attention_kernel, parts=parts, heads=hea...]
    ppermute x15, starting transfers between devices: 13.4 us -> 16.5 us  [swap(): lax.ppermute(values, axis, [(i, i ^ step) for i in range(lax.axis_size(ax...]
    ppermute x15, waiting for transfers between devices: 8.59 us -> 9.17 us  [swap(): lax.ppermute(values, axis, [(i, i ^ step) for i in range(lax.axis_size(ax...]
    pallas_call x1, Pallas kernels: 1.06 us -> 0.58 us  [prepare(): pl.pallas_call(prepare_kernel, in_specs=[SMEM_SPEC] + [VMEM_SPEC] * 3, ou...]
    pallas_call x1 -> x2, Pallas kernels: 3.68 us -> 3.52 us  [the longest x1 2.24 us: post(): pl.pallas_call(post_kernel, in_specs=[SMEM_SPEC] * 2 + [VMEM_SPEC] * 6, o...]
  transfers between devices with their start and end apart: 15 -> 15, of which waited for: 8 -> 8; matrix products, arithmetic and copies ran while one was open for 0% -> 0% of each run, Pallas kernels for 15% -> 13%
where the time goes in v6:
time: 38.3 us; the launch traced here: 38.1 us
  starting transfers between devices  16.5 us (43%)
  Pallas kernels  10.1 us (26%)
  waiting for transfers between devices  9.17 us (24%)
  between operations  1.46 us (4%)
  local copies, waits for them, and re-layouts  0.83 us (2%)
    ppermute x15, starting transfers between devices, swap(): lax.ppermute(values, axis, [(i, i ^ step) for i in range(lax.axis_size(ax...  16.5 us
    ppermute x15, waiting for transfers between devices, swap(): lax.ppermute(values, axis, [(i, i ^ step) for i in range(lax.axis_size(ax...  9.17 us
    pallas_call x1, Pallas kernels, attention(): pl.pallas_call(functools.partial(attention_kernel, parts=parts, heads=hea...  4.4 us
    pallas_call x1, Pallas kernels, post(): pl.pallas_call(post_kernel, in_specs=[SMEM_SPEC] * 2 + [VMEM_SPEC] * 6, o...  2.24 us
    pallas_call x1, Pallas kernels, turn(): pl.pallas_call(turn_kernel, in_specs=[SMEM_SPEC] + [VMEM_SPEC] * 4, out_s...  1.28 us
    pallas_call x1, Pallas kernels, finish(): pl.pallas_call(finish_kernel, in_specs=[VMEM_SPEC] * (len(blocks) + 2), o...  0.84 us
    unnamed x18, local copies, waits for them, and re-layouts  0.83 us
  transfers between devices with their start and end apart: 15, of which 8 were waited for; matrix products, arithmetic and copies ran while one was open for 0% of the time, Pallas kernels for 13%

profile of v6, /device:TPU:0, one launch (start us, length us, event | category | flops | bytes accessed | tf_op | source)
XLA Modules:
  0.0 38.1 jit_solution(10806522534045813008)
XLA Ops:
  0.6 0.0 copy-start
  0.6 0.0 copy-start.1
  0.7 0.0 copy-start.7
  0.7 0.7 %copy-done = bf16[96,256]{1,0:T(8,128)(2,1)S(1)} copy-done((bf16[96,256]{1,0:T(8,128)(2,1)S(1)}, bf16[96,256]{1,0:T(8,128)(2,1)}, u32[]{:S(2)}) %copy-start) | copy-done | bytes 49176
  1.4 0.0 copy-done.1
  1.4 0.0 copy-done.7
  1.5 0.0 copy-start.2
  1.5 0.0 copy-start.3
  1.5 0.0 copy-start.4
  1.5 0.1 pack.1.refs_9_
  1.6 4.0 %collective-permute-start.5 = (bf16[96,512]{1,0:T(8,128)(2,1)S(1)}, bf16[96,512]{1,0:T(8,128)(2,1)S(1)}, u32[]{:S(2)}, u32[]{:S(2)}) collective-permute-start(bf16[96,512]{1,0:T(8,128)(2,1)S(1)} %pack.1.refs_9_), channel_id=1, source_target_pairs={{0,24},{4,28},{8,16},{12,20},{16,8},{20,12},{24,0},{28,4},{1,25},{... | collective-permute-start | bytes 294920 | tf_op jit(solution)/shard_map/ppermute | solution.py:529
  5.6 0.5 %collective-permute-start.3 = (bf16[96,512]{1,0:T(8,128)(2,1)S(1)}, bf16[96,512]{1,0:T(8,128)(2,1)S(1)}, u32[]{:S(2)}, u32[]{:S(2)}) collective-permute-start(bf16[96,512]{1,0:T(8,128)(2,1)S(1)} %pack.1.refs_9_), channel_id=1, source_target_pairs={{0,16},{4,20},{8,24},{12,28},{16,0},{20,4},{24,8},{28,12},{1,17},{... | collective-permute-start | bytes 294920 | tf_op jit(solution)/shard_map/ppermute | solution.py:529
  6.1 0.1 collective-permute-start.1
  6.2 0.0 collective-permute-start
  6.9 0.0 copy-done.2
  6.9 0.0 copy-done.3
  6.9 0.0 copy-done.4
  6.9 0.0 copy-start.5
  6.9 0.0 copy-start.6
  6.9 0.0 copy-start.8
  6.9 0.6 %prepare.1 = (bf16[4,256,512]{2,1,0:T(8,128)(2,1)S(1)}, f32[4,8,512]{2,1,0:T(8,128)S(1)}, bf16[4,256,512]{2,1,0:T(8,128)(2,1)S(1)}, bf16[4,256,512]{2,1,0:T(8,128)(2,1)S(1)}, f32[128,512]{1,0:T(8,128)S(1)}) custom-call(s32[1]{0:T(128)S(6)} %copy.18.live_ref.refs_0_, bf16[256,2048]{1,0:T(8,128)(2,1)S(1)} %copy-done.3, bf16[256,2048]{1,0:T(8,128)(2,1)S(1)} %copy-done.4, ...), custom_call_target="tpu_custom_call" | custom-call | flops 2000000000 | bytes 3145728 | tf_op jit(solution)/shard_map/prepare/pallas_call | solution.py:134
  7.5 3.3 %collective-permute-done.1.refs_11_ = bf16[96,512]{1,0:T(8,128)(2,1)S(1)} collective-permute-done((bf16[96,512]{1,0:T(8,128)(2,1)S(1)}, bf16[96,512]{1,0:T(8,128)(2,1)S(1)}, u32[]{:S(2)}, u32[]{:S(2)}) %collective-permute-start.1) | collective-permute-done | bytes 98336 | tf_op jit(solution)/shard_map/ppermute | solution.py:529
  10.8 0.0 collective-permute-done.3.refs_13_
  10.8 0.0 collective-permute-done.5.refs_15_
  10.8 0.0 collective-permute-start.6
  10.8 0.5 %collective-permute-start.4 = (bf16[96,512]{1,0:T(8,128)(2,1)S(1)}, bf16[96,512]{1,0:T(8,128)(2,1)S(1)}, u32[]{:S(2)}, u32[]{:S(2)}) collective-permute-start(bf16[96,512]{1,0:T(8,128)(2,1)S(1)} %collective-permute-done.3.refs_13_), channel_id=1, source_target_pairs={{0,4},{4,0},{8,12},{12,8},{16,20},{20,16},{24,28},{28,24},{1,5},{5... | collective-permute-start | bytes 294920 | tf_op jit(solution)/shard_map/ppermute | solution.py:529
  11.3 0.1 collective-permute-start.2
  11.4 0.0 collective-permute-done.refs_10_
  11.4 0.7 %collective-permute-done.6.refs_16_ = bf16[96,512]{1,0:T(8,128)(2,1)S(1)} collective-permute-done((bf16[96,512]{1,0:T(8,128)(2,1)S(1)}, bf16[96,512]{1,0:T(8,128)(2,1)S(1)}, u32[]{:S(2)}, u32[]{:S(2)}) %collective-permute-start.6) | collective-permute-done | bytes 98336 | tf_op jit(solution)/shard_map/ppermute | solution.py:529
  12.1 0.2 collective-permute-done.4.refs_14_
  12.3 0.4 collective-permute-done.2.refs_12_
  12.6 0.0 copy-done.5
  12.6 0.0 copy-done.6
  12.6 0.0 copy-done.8
  12.6 4.4 %attention.1 = (bf16[4,256,512]{2,1,0:T(8,128)(2,1)S(1)}, bf16[4,2,448,512]{3,2,1,0:T(8,128)(2,1)S(1)}, bf16[768,256]{1,0:T(8,128)(2,1)S(1)}, bf16[256,256]{1,0:...) custom-call(s32[1]{0:T(128)S(6)} %copy.18.live_ref.refs_0_, ...), custom_call_target="tpu_custom_call" | custom-call | flops 3000000000 | bytes 10000000 | tf_op jit(solution)/shard_map/attention/pallas_call | solution.py:286
  17.0 3.3 %collective-permute-start.10 = (bf16[384,512]{1,0:T(8,128)(2,1)S(1)}, bf16[384,512]{1,0:T(8,128)(2,1)S(1)}, u32[]{:S(2)}, u32[]{:S(2)}) collective-permute-start(bf16[384,512]{1,0:T(8,128)(2,1)S(1)} %get-tuple-element.69), channel_id=1, source_target_pairs={{0,4},{4,0},{8,12},{12,8},{16,20},{20,16},{24,28},{28,24},{1,5},{5... | collective-permute-start | bytes 1179656 | tf_op jit(solution)/shard_map/ppermute | solution.py:529
  20.3 3.6 %collective-permute-start.9 = (f32[8,128]{1,0:T(8,128)S(1)}, f32[8,128]{1,0:T(8,128)S(1)}, u32[]{:S(2)}, u32[]{:S(2)}) collective-permute-start(f32[8,128]{1,0:T(8,128)S(1)} %get-tuple-element.70.refs_0_), channel_id=1, source_target_pairs={{0,3},{1,2},{2,1},{3,0},{4,7},{5,6},{6,5},{7,4},{8,11},{9,10},{10,... | collective-permute-start | bytes 12296 | tf_op jit(solution)/shard_map/ppermute | solution.py:529
  24.0 0.0 collective-permute-start.8
  24.0 0.8 %collective-permute-start.7 = (f32[8,128]{1,0:T(8,128)S(1)}, f32[8,128]{1,0:T(8,128)S(1)}, u32[]{:S(2)}, u32[]{:S(2)}) collective-permute-start(f32[8,128]{1,0:T(8,128)S(1)} %get-tuple-element.70.refs_0_), channel_id=1, source_target_pairs={{0,1},{1,0},{2,3},{3,2},{4,5},{5,4},{6,7},{7,6},{8,9},{9,8},{10,11... | collective-permute-start | bytes 12296 | tf_op jit(solution)/shard_map/ppermute | solution.py:529
  24.7 1.3 %turn.1 = (bf16[256,2048]{1,0:T(8,128)(2,1)}, bf16[256,256]{1,0:T(8,128)(2,1)}, bf16[256,256]{1,0:T(8,128)(2,1)}) custom-call(s32[1]{0:T(128)S(6)} %copy.18.live_ref.refs_0_, bf16[4,256,512]{2,1,0:T(8,128)(2,1)S(1)} %get-tuple-element.64.att_t_ref, f32[4,2,2,64,128]{4,3,2,1,0:T(8,128)S(1)} %get-tuple-element.65.own_acc, bf16[256,256]{1,0:T(8,128)(2,1)S(1)} %copy-done.6, ...), custom_call_target="tpu_custom_call" | custom-call | flops 2000000000 | bytes 2000000 | tf_op jit(solution)/shard_map/turn/pallas_call | solution.py:365
  26.0 0.0 collective-permute-done.9.refs_3_
  26.0 2.4 %collective-permute-done.8.refs_2_ = f32[8,128]{1,0:T(8,128)S(1)} collective-permute-done((f32[8,128]{1,0:T(8,128)S(1)}, f32[8,128]{1,0:T(8,128)S(1)}, u32[]{:S(2)}, u32[]{:S(2)}) %collective-permute-start.8) | collective-permute-done | bytes 4128 | tf_op jit(solution)/shard_map/ppermute | solution.py:529
  28.5 0.0 collective-permute-done.7.refs_1_
  28.5 0.0 collective-permute-done.10.came_ref
  28.5 0.1 add.1
  28.6 1.5 %collective-permute-start.11 = (bf16[400,128]{1,0:T(8,128)(2,1)S(1)}, bf16[400,128]{1,0:T(8,128)(2,1)S(1)}, u32[]{:S(2)}, u32[]{:S(2)}) collective-permute-start(bf16[400,128]{1,0:T(8,128)(2,1)S(1)} %get-tuple-element.74), channel_id=1, source_target_pairs={{0,8},{4,12},{8,0},{12,4},{16,24},{20,28},{24,16},{28,20},{1,9},{5... | collective-permute-start | bytes 307208 | tf_op jit(solution)/shard_map/ppermute | solution.py:529
  30.0 0.7 %collective-permute-start.12 = (bf16[400,128]{1,0:T(8,128)(2,1)S(1)}, bf16[400,128]{1,0:T(8,128)(2,1)S(1)}, u32[]{:S(2)}, u32[]{:S(2)}) collective-permute-start(bf16[400,128]{1,0:T(8,128)(2,1)S(1)} %get-tuple-element.75), channel_id=1, source_target_pairs={{0,16},{4,20},{8,24},{12,28},{16,0},{20,4},{24,8},{28,12},{1,17},{... | collective-permute-start | bytes 307208 | tf_op jit(solution)/shard_map/ppermute | solution.py:529
  30.7 1.4 %collective-permute-start.13 = (bf16[400,128]{1,0:T(8,128)(2,1)S(1)}, bf16[400,128]{1,0:T(8,128)(2,1)S(1)}, u32[]{:S(2)}, u32[]{:S(2)}) collective-permute-start(bf16[400,128]{1,0:T(8,128)(2,1)S(1)} %get-tuple-element.76), channel_id=1, source_target_pairs={{0,24},{4,28},{8,16},{12,20},{16,8},{20,12},{24,0},{28,4},{1,25},{... | collective-permute-start | bytes 307208 | tf_op jit(solution)/shard_map/ppermute | solution.py:529
  32.1 2.2 %post.1 = bf16[256,2048]{1,0:T(8,128)(2,1)} custom-call(s32[1]{0:T(128)S(6)} %copy.18.live_ref.refs_0_, s32[4]{0:T(128)S(1)} %copy-done.8, bf16[4,2,448,512]{3,2,1,0:T(8,128)(2,1)S(1)} %get-tuple-element.77.ds_ref, bf16[768,256]{1,0:T(8,128)(2,1)S(1)} %get-tuple-element.78.pool_keys, bf16[256,256]{1,0:T(8,128)(2,1)S(1)} %get-tuple-element.79.own_keys_ref, ...), custom_call_target="tpu_custom_call" | custom-call | flops 3000000000 | bytes 4000000 | tf_op jit(solution)/shard_map/post/pallas_call | solution.py:412
  34.4 0.0 collective-permute-done.11.refs_3_
  34.4 0.8 %collective-permute-done.12.refs_2_ = bf16[400,128]{1,0:T(8,128)(2,1)S(1)} collective-permute-done((bf16[400,128]{1,0:T(8,128)(2,1)S(1)}, bf16[400,128]{1,0:T(8,128)(2,1)S(1)}, u32[]{:S(2)}, u32[]{:S(2)}) %collective-permute-start.12) | collective-permute-done | bytes 102432 | tf_op jit(solution)/shard_map/ppermute | solution.py:529
  35.2 1.1 %collective-permute-done.13.refs_1_ = bf16[400,128]{1,0:T(8,128)(2,1)S(1)} collective-permute-done((bf16[400,128]{1,0:T(8,128)(2,1)S(1)}, bf16[400,128]{1,0:T(8,128)(2,1)S(1)}, u32[]{:S(2)}, u32[]{:S(2)}) %collective-permute-start.13) | collective-permute-done | bytes 102432 | tf_op jit(solution)/shard_map/ppermute | solution.py:529
  36.3 0.1 collective-permute-start.14
  36.4 0.8 %finish.1 = (f32[96,256]{1,0:T(8,128)}, f32[96,256]{1,0:T(8,128)}) custom-call(f32[400,128]{1,0:T(8,128)S(1)} %get-tuple-element.86.refs_0_, bf16[400,128]{1,0:T(8,128)(2,1)S(1)} %collective-permute-done.13.refs_1_, bf16[400,128]{1,0:T(8,128)(2,1)S(1)} %collective-permute-done.12.refs_2_, bf16[400,128]{1,0:T(8,128)(2,1)S(1)} %collective-permute-done.11.refs_3_, ...), custom_call_target="tpu_custom_call" | custom-call | flops 100000000 | bytes 1000000 | tf_op jit(solution)/shard_map/finish/pallas_call | solution.py:517
  37.2 0.3 collective-permute-done.14.refs_1_
  37.5 0.5 %gain_grads.1 = (f32[1,128]{1,0:T(1,128)}, f32[1,128]{1,0:T(1,128)}) custom-call(f32[8,128]{1,0:T(8,128)S(1)} %sum_chips.1.refs_0_, f32[8,128]{1,0:T(8,128)S(1)} %collective-permute-done.14.refs_1_, f32[1,128]{1,0:T(1,128)S(1)} %bitcast.11, f32[1,128]{1,0:T(1,128)S(1)} %bitcast.9), custom_call_target="tpu_custom_call" | custom-call | tf_op jit(solution)/shard_map/gain_grads/pallas_call | solution.py:487
  (2 shorter events, 0.0 us)
Async XLA Ops:
  0.6 0.8 %copy-start = (bf16[96,256]{1,0:T(8,128)(2,1)S(1)}, bf16[96,256]{1,0:T(8,128)(2,1)}, u32[]{:S(2)}) copy-start(bf16[96,256]{1,0:T(8,128)(2,1)} %refs_4_.1) | copy-start | bytes 147460
  0.6 0.8 %copy-start.1 = (f32[128]{0:T(128)S(1)}, f32[128]{0:T(128)}, u32[]{:S(2)}) copy-start(f32[128]{0:T(128)} %param.16) | copy-start | bytes 1540
  0.7 0.8 %copy-start.7 = (bf16[96,256]{1,0:T(8,128)(2,1)S(1)}, bf16[96,256]{1,0:T(8,128)(2,1)}, u32[]{:S(2)}) copy-start(bf16[96,256]{1,0:T(8,128)(2,1)} %values_ref) | copy-start | bytes 147460
  1.5 5.4 %copy-start.2 = (f32[128]{0:T(128)S(1)}, f32[128]{0:T(128)}, u32[]{:S(2)}) copy-start(f32[128]{0:T(128)} %param.15) | copy-start | bytes 1540
  1.5 5.4 %copy-start.3 = (bf16[256,2048]{1,0:T(8,128)(2,1)S(1)}, bf16[256,2048]{1,0:T(8,128)(2,1)}, u32[]{:S(2)}) copy-start(bf16[256,2048]{1,0:T(8,128)(2,1)} %q_ref.1) | copy-start | bytes 3145732
  1.5 5.4 %copy-start.4 = (bf16[256,2048]{1,0:T(8,128)(2,1)S(1)}, bf16[256,2048]{1,0:T(8,128)(2,1)}, u32[]{:S(2)}) copy-start(bf16[256,2048]{1,0:T(8,128)(2,1)} %do_ref.1) | copy-start | bytes 3145732
  1.6 9.2 %collective-permute-start.5 = (bf16[96,512]{1,0:T(8,128)(2,1)S(1)}, bf16[96,512]{1,0:T(8,128)(2,1)S(1)}, u32[]{:S(2)}, u32[]{:S(2)}) collective-permute-start(bf16[96,512]{1,0:T(8,128)(2,1)S(1)} %pack.1.refs_9_), channel_id=1, source_target_pairs={{0,24},{4,28},{8,16},{12,20},{16,8},{20,12},{24,0},{28,4},{1,25},{... | collective-permute-start | bytes 294920 | tf_op jit(solution)/shard_map/ppermute | solution.py:529
  5.6 5.2 %collective-permute-start.3 = (bf16[96,512]{1,0:T(8,128)(2,1)S(1)}, bf16[96,512]{1,0:T(8,128)(2,1)S(1)}, u32[]{:S(2)}, u32[]{:S(2)}) collective-permute-start(bf16[96,512]{1,0:T(8,128)(2,1)S(1)} %pack.1.refs_9_), channel_id=1, source_target_pairs={{0,16},{4,20},{8,24},{12,28},{16,0},{20,4},{24,8},{28,12},{1,17},{... | collective-permute-start | bytes 294920 | tf_op jit(solution)/shard_map/ppermute | solution.py:529
  6.1 4.7 %collective-permute-start.1 = (bf16[96,512]{1,0:T(8,128)(2,1)S(1)}, bf16[96,512]{1,0:T(8,128)(2,1)S(1)}, u32[]{:S(2)}, u32[]{:S(2)}) collective-permute-start(bf16[96,512]{1,0:T(8,128)(2,1)S(1)} %pack.1.refs_9_), channel_id=1, source_target_pairs={{0,8},{4,12},{8,0},{12,4},{16,24},{20,28},{24,16},{28,20},{1,9},{5... | collective-permute-start | bytes 294920 | tf_op jit(solution)/shard_map/ppermute | solution.py:529
  6.2 5.2 %collective-permute-start = (bf16[96,512]{1,0:T(8,128)(2,1)S(1)}, bf16[96,512]{1,0:T(8,128)(2,1)S(1)}, u32[]{:S(2)}, u32[]{:S(2)}) collective-permute-start(bf16[96,512]{1,0:T(8,128)(2,1)S(1)} %pack.1.refs_9_), channel_id=1, source_target_pairs={{0,4},{4,0},{8,12},{12,8},{16,20},{20,16},{24,28},{28,24},{1,5},{5... | collective-permute-start | bytes 294920 | tf_op jit(solution)/shard_map/ppermute | solution.py:529
  6.9 5.7 %copy-start.5 = (bf16[256,256]{1,0:T(8,128)(2,1)S(1)}, bf16[256,256]{1,0:T(8,128)(2,1)}, u32[]{:S(2)}) copy-start(bf16[256,256]{1,0:T(8,128)(2,1)} %refs_6_.1) | copy-start | bytes 393220
  6.9 5.7 %copy-start.6 = (bf16[256,256]{1,0:T(8,128)(2,1)S(1)}, bf16[256,256]{1,0:T(8,128)(2,1)}, u32[]{:S(2)}) copy-start(bf16[256,256]{1,0:T(8,128)(2,1)} %ck_ref.1) | copy-start | bytes 393220
  6.9 5.7 %copy-start.8 = (s32[4]{0:T(128)S(1)}, s32[4]{0:T(128)}, u32[]{:S(2)}) copy-start(s32[4]{0:T(128)} %prompt_ref.1) | copy-start | bytes 52
  10.8 1.3 %collective-permute-start.6 = (bf16[96,512]{1,0:T(8,128)(2,1)S(1)}, bf16[96,512]{1,0:T(8,128)(2,1)S(1)}, u32[]{:S(2)}, u32[]{:S(2)}) collective-permute-start(bf16[96,512]{1,0:T(8,128)(2,1)S(1)} %collective-permute-done.5.refs_15_), channel_id=1, source_target_pairs={{0,4},{4,0},{8,12},{12,8},{16,20},{20,16},{24,28},{28,24},{1,5},{5... | collective-permute-start | bytes 294920 | tf_op jit(solution)/shard_map/ppermute | solution.py:529
  10.8 1.4 %collective-permute-start.4 = (bf16[96,512]{1,0:T(8,128)(2,1)S(1)}, bf16[96,512]{1,0:T(8,128)(2,1)S(1)}, u32[]{:S(2)}, u32[]{:S(2)}) collective-permute-start(bf16[96,512]{1,0:T(8,128)(2,1)S(1)} %collective-permute-done.3.refs_13_), channel_id=1, source_target_pairs={{0,4},{4,0},{8,12},{12,8},{16,20},{20,16},{24,28},{28,24},{1,5},{5... | collective-permute-start | bytes 294920 | tf_op jit(solution)/shard_map/ppermute | solution.py:529
  11.3 1.3 %collective-permute-start.2 = (bf16[96,512]{1,0:T(8,128)(2,1)S(1)}, bf16[96,512]{1,0:T(8,128)(2,1)S(1)}, u32[]{:S(2)}, u32[]{:S(2)}) collective-permute-start(bf16[96,512]{1,0:T(8,128)(2,1)S(1)} %collective-permute-done.1.refs_11_), channel_id=1, source_target_pairs={{0,4},{4,0},{8,12},{12,8},{16,20},{20,16},{24,28},{28,24},{1,5},{5... | collective-permute-start | bytes 294920 | tf_op jit(solution)/shard_map/ppermute | solution.py:529
  17.0 11.4 %collective-permute-start.10 = (bf16[384,512]{1,0:T(8,128)(2,1)S(1)}, bf16[384,512]{1,0:T(8,128)(2,1)S(1)}, u32[]{:S(2)}, u32[]{:S(2)}) collective-permute-start(bf16[384,512]{1,0:T(8,128)(2,1)S(1)} %get-tuple-element.69), channel_id=1, source_target_pairs={{0,4},{4,0},{8,12},{12,8},{16,20},{20,16},{24,28},{28,24},{1,5},{5... | collective-permute-start | bytes 1179656 | tf_op jit(solution)/shard_map/ppermute | solution.py:529
  20.3 5.7 %collective-permute-start.9 = (f32[8,128]{1,0:T(8,128)S(1)}, f32[8,128]{1,0:T(8,128)S(1)}, u32[]{:S(2)}, u32[]{:S(2)}) collective-permute-start(f32[8,128]{1,0:T(8,128)S(1)} %get-tuple-element.70.refs_0_), channel_id=1, source_target_pairs={{0,3},{1,2},{2,1},{3,0},{4,7},{5,6},{6,5},{7,4},{8,11},{9,10},{10,... | collective-permute-start | bytes 12296 | tf_op jit(solution)/shard_map/ppermute | solution.py:529
  24.0 4.5 %collective-permute-start.8 = (f32[8,128]{1,0:T(8,128)S(1)}, f32[8,128]{1,0:T(8,128)S(1)}, u32[]{:S(2)}, u32[]{:S(2)}) collective-permute-start(f32[8,128]{1,0:T(8,128)S(1)} %get-tuple-element.70.refs_0_), channel_id=1, source_target_pairs={{0,2},{1,3},{2,0},{3,1},{4,6},{5,7},{6,4},{7,5},{8,10},{9,11},{10,... | collective-permute-start | bytes 12296 | tf_op jit(solution)/shard_map/ppermute | solution.py:529
  24.0 4.5 %collective-permute-start.7 = (f32[8,128]{1,0:T(8,128)S(1)}, f32[8,128]{1,0:T(8,128)S(1)}, u32[]{:S(2)}, u32[]{:S(2)}) collective-permute-start(f32[8,128]{1,0:T(8,128)S(1)} %get-tuple-element.70.refs_0_), channel_id=1, source_target_pairs={{0,1},{1,0},{2,3},{3,2},{4,5},{5,4},{6,7},{7,6},{8,9},{9,8},{10,11... | collective-permute-start | bytes 12296 | tf_op jit(solution)/shard_map/ppermute | solution.py:529
  28.6 5.8 %collective-permute-start.11 = (bf16[400,128]{1,0:T(8,128)(2,1)S(1)}, bf16[400,128]{1,0:T(8,128)(2,1)S(1)}, u32[]{:S(2)}, u32[]{:S(2)}) collective-permute-start(bf16[400,128]{1,0:T(8,128)(2,1)S(1)} %get-tuple-element.74), channel_id=1, source_target_pairs={{0,8},{4,12},{8,0},{12,4},{16,24},{20,28},{24,16},{28,20},{1,9},{5... | collective-permute-start | bytes 307208 | tf_op jit(solution)/shard_map/ppermute | solution.py:529
  30.0 5.2 %collective-permute-start.12 = (bf16[400,128]{1,0:T(8,128)(2,1)S(1)}, bf16[400,128]{1,0:T(8,128)(2,1)S(1)}, u32[]{:S(2)}, u32[]{:S(2)}) collective-permute-start(bf16[400,128]{1,0:T(8,128)(2,1)S(1)} %get-tuple-element.75), channel_id=1, source_target_pairs={{0,16},{4,20},{8,24},{12,28},{16,0},{20,4},{24,8},{28,12},{1,17},{... | collective-permute-start | bytes 307208 | tf_op jit(solution)/shard_map/ppermute | solution.py:529
  30.7 5.6 %collective-permute-start.13 = (bf16[400,128]{1,0:T(8,128)(2,1)S(1)}, bf16[400,128]{1,0:T(8,128)(2,1)S(1)}, u32[]{:S(2)}, u32[]{:S(2)}) collective-permute-start(bf16[400,128]{1,0:T(8,128)(2,1)S(1)} %get-tuple-element.76), channel_id=1, source_target_pairs={{0,24},{4,28},{8,16},{12,20},{16,8},{20,12},{24,0},{28,4},{1,25},{... | collective-permute-start | bytes 307208 | tf_op jit(solution)/shard_map/ppermute | solution.py:529
  36.3 1.2 %collective-permute-start.14 = (f32[8,128]{1,0:T(8,128)S(1)}, f32[8,128]{1,0:T(8,128)S(1)}, u32[]{:S(2)}, u32[]{:S(2)}) collective-permute-start(f32[8,128]{1,0:T(8,128)S(1)} %sum_chips.1.refs_0_), channel_id=1, source_target_pairs={{0,4},{4,0},{8,12},{12,8},{16,20},{20,16},{24,28},{28,24},{1,5},{5... | collective-permute-start | bytes 12296 | tf_op jit(solution)/shard_map/ppermute | solution.py:529

commit v7 on v6

--- a/solution.py
+++ b/solution.py
@@ -12,7 +12,7 @@
 CL = 64
 EPS = 1e-06
 TAIL = 16
-CHUNK = 256
+CHUNK = 512
 VMEM_LIMIT = 24 * 1024 * 1024
 F32 = jnp.float32
 BF16 = jnp.bfloat16
@@ -231,8 +231,9 @@
                 slot = now if tick >= number else before
                 if slot is not None:
                     stage(slot, (tick - number) % count)
-            done = (tick - 3) % count
-            slot = now if tick >= 3 else before
+            wait = 3 if per_head > 1 else 2
+            done = (tick - wait) % count
+            slot = now if tick >= wait else before
             if slot is not None and done % per_head == per_head - 1:
                 close(slot, done // per_head)
 
@@ -438,7 +439,7 @@
     shard = keep_ref.shape[0] // blocks
     for at in range(blocks):
         place = slice(at * shard, (at + 1) * shard)
-        ref = send_refs[at - 1] if at > 0 else own_ref
+        ref = send_refs[blocks - 1 - at] if at > 0 else own_ref
         total = keep_ref[place, :] + came_ref[place, :].astype(F32)
         for slab in range(keep_ref.shape[1] // size):
             ref[slab * shard:(slab + 1) * shard, :] = total[:, slab * size:(slab + 1) * size].astype(ref.dtype)
@@ -564,9 +565,9 @@
         terms = [term] + [swap(term, "tp", step) for step in range(1, tp)]
         terms, attended = lax.optimization_barrier((terms, attended))
         own, *blocks = add(keep, came, terms, grp // 2)
-        blocks = [swap(block, "grp", 2 * at + 2) for at, block in enumerate(blocks)]
+        blocks = [swap(block, "grp", grp - 2 - 2 * at) for at, block in enumerate(blocks)]
         blocks, query_grads = lax.optimization_barrier((blocks, query_grads))
-        blocks = [own] + blocks[::-1]
+        blocks = [own] + blocks
         total = sum_chips(blocks)
         terms = [total, swap(total, "grp", 1)]
     else:

time: 38.3 us -> 38.1 us (level)
  Pallas kernels: 10.1 us -> 12.4 us
  starting transfers between devices: 16.5 us -> 14.9 us
  waiting for transfers between devices: 9.17 us -> 8.21 us
    ppermute x15, starting transfers between devices: 16.5 us -> 14.9 us  [swap(): lax.ppermute(values, axis, [(i, i ^ step) for i in range(lax.axis_size(ax...]
    pallas_call x1, Pallas kernels: 4.4 us -> 5.95 us  [attention(): pl.pallas_call(functools.partial(attention_kernel, parts=parts, heads=hea...]
    ppermute x15, waiting for transfers between devices: 9.17 us -> 8.21 us  [swap(): lax.ppermute(values, axis, [(i, i ^ step) for i in range(lax.axis_size(ax...]
    pallas_call x1, Pallas kernels: 2.24 us -> 2.7 us  [post(): pl.pallas_call(post_kernel, in_specs=[SMEM_SPEC] * 2 + [VMEM_SPEC] * 6, o...]
  transfers between devices with their start and end apart: 15 -> 15, of which waited for: 8 -> 9; matrix products, arithmetic and copies ran while one was open for 0% -> 0% of each run, Pallas kernels for 13% -> 15%
where the time goes in v7:
time: 38.1 us; the launch traced here: 37.8 us
  starting transfers between devices  14.9 us (39%)
  Pallas kernels  12.4 us (33%)
  waiting for transfers between devices  8.21 us (22%)
  between operations  1.46 us (4%)
  local copies, waits for them, and re-layouts  0.82 us (2%)
    ppermute x15, starting transfers between devices, swap(): lax.ppermute(values, axis, [(i, i ^ step) for i in range(lax.axis_size(ax...  14.9 us
    ppermute x15, waiting for transfers between devices, swap(): lax.ppermute(values, axis, [(i, i ^ step) for i in range(lax.axis_size(ax...  8.21 us
    pallas_call x1, Pallas kernels, attention(): pl.pallas_call(functools.partial(attention_kernel, parts=parts, heads=hea...  5.95 us
    pallas_call x1, Pallas kernels, post(): pl.pallas_call(post_kernel, in_specs=[SMEM_SPEC] * 2 + [VMEM_SPEC] * 6, o...  2.7 us
    pallas_call x1, Pallas kernels, turn(): pl.pallas_call(turn_kernel, in_specs=[SMEM_SPEC] + [VMEM_SPEC] * 4, out_s...  1.39 us
    pallas_call x1, Pallas kernels, finish(): pl.pallas_call(finish_kernel, in_specs=[VMEM_SPEC] * (len(blocks) + 2), o...  0.84 us
    unnamed x18, local copies, waits for them, and re-layouts  0.82 us
    pallas_call x1, Pallas kernels, prepare(): pl.pallas_call(prepare_kernel, in_specs=[SMEM_SPEC] + [VMEM_SPEC] * 3, ou...  0.82 us
  transfers between devices with their start and end apart: 15, of which 9 were waited for; matrix products, arithmetic and copies ran while one was open for 0% of the time, Pallas kernels for 15%

profile of v7, /device:TPU:0, one launch (start us, length us, event | category | flops | bytes accessed | tf_op | source)
XLA Modules:
  0.0 37.8 jit_solution(11388165281653599123)
XLA Ops:
  0.6 0.0 copy-start
  0.6 0.0 copy-start.1
  0.7 0.0 copy-start.7
  0.7 0.7 %copy-done = bf16[96,256]{1,0:T(8,128)(2,1)S(1)} copy-done((bf16[96,256]{1,0:T(8,128)(2,1)S(1)}, bf16[96,256]{1,0:T(8,128)(2,1)}, u32[]{:S(2)}) %copy-start) | copy-done | bytes 49176
  1.4 0.0 copy-done.1
  1.4 0.0 copy-done.7
  1.5 0.0 copy-start.2
  1.5 0.0 copy-start.3
  1.5 0.0 copy-start.4
  1.5 0.1 pack.1.refs_9_
  1.6 4.0 %collective-permute-start.5 = (bf16[96,512]{1,0:T(8,128)(2,1)S(1)}, bf16[96,512]{1,0:T(8,128)(2,1)S(1)}, u32[]{:S(2)}, u32[]{:S(2)}) collective-permute-start(bf16[96,512]{1,0:T(8,128)(2,1)S(1)} %pack.1.refs_9_), channel_id=1, source_target_pairs={{0,24},{4,28},{8,16},{12,20},{16,8},{20,12},{24,0},{28,4},{1,25},{... | collective-permute-start | bytes 294920 | tf_op jit(solution)/shard_map/ppermute | solution.py:530
  5.6 0.5 %collective-permute-start.3 = (bf16[96,512]{1,0:T(8,128)(2,1)S(1)}, bf16[96,512]{1,0:T(8,128)(2,1)S(1)}, u32[]{:S(2)}, u32[]{:S(2)}) collective-permute-start(bf16[96,512]{1,0:T(8,128)(2,1)S(1)} %pack.1.refs_9_), channel_id=1, source_target_pairs={{0,16},{4,20},{8,24},{12,28},{16,0},{20,4},{24,8},{28,12},{1,17},{... | collective-permute-start | bytes 294920 | tf_op jit(solution)/shard_map/ppermute | solution.py:530
  6.1 0.1 collective-permute-start.1
  6.2 0.0 collective-permute-start
  6.9 0.0 copy-done.2
  6.9 0.0 copy-done.3
  6.9 0.0 copy-done.4
  6.9 0.0 copy-start.5
  6.9 0.0 copy-start.6
  6.9 0.0 copy-start.8
  6.9 0.8 %prepare.1 = (bf16[4,256,512]{2,1,0:T(8,128)(2,1)S(1)}, f32[4,8,512]{2,1,0:T(8,128)S(1)}, bf16[4,256,512]{2,1,0:T(8,128)(2,1)S(1)}, bf16[4,256,512]{2,1,0:T(8,128)(2,1)S(1)}, f32[128,512]{1,0:T(8,128)S(1)}) custom-call(s32[1]{0:T(128)S(6)} %copy.18.live_ref.refs_0_, bf16[256,2048]{1,0:T(8,128)(2,1)S(1)} %copy-done.3, bf16[256,2048]{1,0:T(8,128)(2,1)S(1)} %copy-done.4, ...), custom_call_target="tpu_custom_call" | custom-call | flops 2000000000 | bytes 3145728 | tf_op jit(solution)/shard_map/prepare/pallas_call | solution.py:134
  7.8 3.0 %collective-permute-done.1.refs_11_ = bf16[96,512]{1,0:T(8,128)(2,1)S(1)} collective-permute-done((bf16[96,512]{1,0:T(8,128)(2,1)S(1)}, bf16[96,512]{1,0:T(8,128)(2,1)S(1)}, u32[]{:S(2)}, u32[]{:S(2)}) %collective-permute-start.1) | collective-permute-done | bytes 98336 | tf_op jit(solution)/shard_map/ppermute | solution.py:530
  10.8 0.0 collective-permute-done.3.refs_13_
  10.8 0.0 collective-permute-done.5.refs_15_
  10.8 0.0 collective-permute-start.6
  10.8 0.5 %collective-permute-start.4 = (bf16[96,512]{1,0:T(8,128)(2,1)S(1)}, bf16[96,512]{1,0:T(8,128)(2,1)S(1)}, u32[]{:S(2)}, u32[]{:S(2)}) collective-permute-start(bf16[96,512]{1,0:T(8,128)(2,1)S(1)} %collective-permute-done.3.refs_13_), channel_id=1, source_target_pairs={{0,4},{4,0},{8,12},{12,8},{16,20},{20,16},{24,28},{28,24},{1,5},{5... | collective-permute-start | bytes 294920 | tf_op jit(solution)/shard_map/ppermute | solution.py:530
  11.3 0.1 collective-permute-start.2
  11.4 0.0 collective-permute-done.refs_10_
  11.4 0.7 %collective-permute-done.6.refs_16_ = bf16[96,512]{1,0:T(8,128)(2,1)S(1)} collective-permute-done((bf16[96,512]{1,0:T(8,128)(2,1)S(1)}, bf16[96,512]{1,0:T(8,128)(2,1)S(1)}, u32[]{:S(2)}, u32[]{:S(2)}) %collective-permute-start.6) | collective-permute-done | bytes 98336 | tf_op jit(solution)/shard_map/ppermute | solution.py:530
  12.1 0.2 collective-permute-done.4.refs_14_
  12.3 0.4 collective-permute-done.2.refs_12_
  12.6 0.0 copy-done.5
  12.6 0.0 copy-done.6
  12.6 0.0 copy-done.8
  12.6 6.0 %attention.1 = (bf16[4,256,512]{2,1,0:T(8,128)(2,1)S(1)}, bf16[4,2,448,512]{3,2,1,0:T(8,128)(2,1)S(1)}, bf16[768,256]{1,0:T(8,128)(2,1)S(1)}, bf16[256,256]{1,0:...) custom-call(s32[1]{0:T(128)S(6)} %copy.18.live_ref.refs_0_, ...), custom_call_target="tpu_custom_call" | custom-call | flops 3000000000 | bytes 10000000 | tf_op jit(solution)/shard_map/attention/pallas_call | solution.py:287
  18.6 1.7 %collective-permute-start.10 = (bf16[384,512]{1,0:T(8,128)(2,1)S(1)}, bf16[384,512]{1,0:T(8,128)(2,1)S(1)}, u32[]{:S(2)}, u32[]{:S(2)}) collective-permute-start(bf16[384,512]{1,0:T(8,128)(2,1)S(1)} %get-tuple-element.69), channel_id=1, source_target_pairs={{0,4},{4,0},{8,12},{12,8},{16,20},{20,16},{24,28},{28,24},{1,5},{5... | collective-permute-start | bytes 1179656 | tf_op jit(solution)/shard_map/ppermute | solution.py:530
  20.3 3.6 %collective-permute-start.9 = (f32[8,128]{1,0:T(8,128)S(1)}, f32[8,128]{1,0:T(8,128)S(1)}, u32[]{:S(2)}, u32[]{:S(2)}) collective-permute-start(f32[8,128]{1,0:T(8,128)S(1)} %get-tuple-element.70.refs_0_), channel_id=1, source_target_pairs={{0,3},{1,2},{2,1},{3,0},{4,7},{5,6},{6,5},{7,4},{8,11},{9,10},{10,... | collective-permute-start | bytes 12296 | tf_op jit(solution)/shard_map/ppermute | solution.py:530
  23.9 0.0 collective-permute-start.8
  23.9 0.8 %collective-permute-start.7 = (f32[8,128]{1,0:T(8,128)S(1)}, f32[8,128]{1,0:T(8,128)S(1)}, u32[]{:S(2)}, u32[]{:S(2)}) collective-permute-start(f32[8,128]{1,0:T(8,128)S(1)} %get-tuple-element.70.refs_0_), channel_id=1, source_target_pairs={{0,1},{1,0},{2,3},{3,2},{4,5},{5,4},{6,7},{7,6},{8,9},{9,8},{10,11... | collective-permute-start | bytes 12296 | tf_op jit(solution)/shard_map/ppermute | solution.py:530
  24.7 1.4 %turn.1 = (bf16[256,2048]{1,0:T(8,128)(2,1)}, bf16[256,256]{1,0:T(8,128)(2,1)}, bf16[256,256]{1,0:T(8,128)(2,1)}) custom-call(s32[1]{0:T(128)S(6)} %copy.18.live_ref.refs_0_, bf16[4,256,512]{2,1,0:T(8,128)(2,1)S(1)} %get-tuple-element.64.att_t_ref, f32[4,2,2,64,128]{4,3,2,1,0:T(8,128)S(1)} %get-tuple-element.65.own_acc, bf16[256,256]{1,0:T(8,128)(2,1)S(1)} %copy-done.6, ...), custom_call_target="tpu_custom_call" | custom-call | flops 2000000000 | bytes 2000000 | tf_op jit(solution)/shard_map/turn/pallas_call | solution.py:366
  26.1 0.0 collective-permute-done.9.refs_3_
  26.1 2.3 %collective-permute-done.8.refs_2_ = f32[8,128]{1,0:T(8,128)S(1)} collective-permute-done((f32[8,128]{1,0:T(8,128)S(1)}, f32[8,128]{1,0:T(8,128)S(1)}, u32[]{:S(2)}, u32[]{:S(2)}) %collective-permute-start.8) | collective-permute-done | bytes 4128 | tf_op jit(solution)/shard_map/ppermute | solution.py:530
  28.4 0.0 collective-permute-done.7.refs_1_
  28.4 0.0 collective-permute-done.10.came_ref
  28.4 0.1 add.1
  28.5 1.7 %collective-permute-start.11 = (bf16[400,128]{1,0:T(8,128)(2,1)S(1)}, bf16[400,128]{1,0:T(8,128)(2,1)S(1)}, u32[]{:S(2)}, u32[]{:S(2)}) collective-permute-start(bf16[400,128]{1,0:T(8,128)(2,1)S(1)} %get-tuple-element.74), channel_id=1, source_target_pairs={{0,24},{4,28},{8,16},{12,20},{16,8},{20,12},{24,0},{28,4},{1,25},{... | collective-permute-start | bytes 307208 | tf_op jit(solution)/shard_map/ppermute | solution.py:530
  30.2 1.2 %collective-permute-start.12 = (bf16[400,128]{1,0:T(8,128)(2,1)S(1)}, bf16[400,128]{1,0:T(8,128)(2,1)S(1)}, u32[]{:S(2)}, u32[]{:S(2)}) collective-permute-start(bf16[400,128]{1,0:T(8,128)(2,1)S(1)} %get-tuple-element.75), channel_id=1, source_target_pairs={{0,16},{4,20},{8,24},{12,28},{16,0},{20,4},{24,8},{28,12},{1,17},{... | collective-permute-start | bytes 307208 | tf_op jit(solution)/shard_map/ppermute | solution.py:530
  31.4 0.6 %collective-permute-start.13 = (bf16[400,128]{1,0:T(8,128)(2,1)S(1)}, bf16[400,128]{1,0:T(8,128)(2,1)S(1)}, u32[]{:S(2)}, u32[]{:S(2)}) collective-permute-start(bf16[400,128]{1,0:T(8,128)(2,1)S(1)} %get-tuple-element.76), channel_id=1, source_target_pairs={{0,8},{4,12},{8,0},{12,4},{16,24},{20,28},{24,16},{28,20},{1,9},{5... | collective-permute-start | bytes 307208 | tf_op jit(solution)/shard_map/ppermute | solution.py:530
  32.1 2.7 %post.1 = bf16[256,2048]{1,0:T(8,128)(2,1)} custom-call(s32[1]{0:T(128)S(6)} %copy.18.live_ref.refs_0_, s32[4]{0:T(128)S(1)} %copy-done.8, bf16[4,2,448,512]{3,2,1,0:T(8,128)(2,1)S(1)} %get-tuple-element.77.ds_ref, bf16[768,256]{1,0:T(8,128)(2,1)S(1)} %get-tuple-element.78.pool_keys, bf16[256,256]{1,0:T(8,128)(2,1)S(1)} %get-tuple-element.79.own_keys_ref, ...), custom_call_target="tpu_custom_call" | custom-call | flops 3000000000 | bytes 4000000 | tf_op jit(solution)/shard_map/post/pallas_call | solution.py:413
  34.8 0.2 collective-permute-done.11.refs_1_
  35.0 0.6 %collective-permute-done.12.refs_2_ = bf16[400,128]{1,0:T(8,128)(2,1)S(1)} collective-permute-done((bf16[400,128]{1,0:T(8,128)(2,1)S(1)}, bf16[400,128]{1,0:T(8,128)(2,1)S(1)}, u32[]{:S(2)}, u32[]{:S(2)}) %collective-permute-start.12) | collective-permute-done | bytes 102432 | tf_op jit(solution)/shard_map/ppermute | solution.py:530
  35.5 0.5 %collective-permute-done.13.refs_3_ = bf16[400,128]{1,0:T(8,128)(2,1)S(1)} collective-permute-done((bf16[400,128]{1,0:T(8,128)(2,1)S(1)}, bf16[400,128]{1,0:T(8,128)(2,1)S(1)}, u32[]{:S(2)}, u32[]{:S(2)}) %collective-permute-start.13) | collective-permute-done | bytes 102432 | tf_op jit(solution)/shard_map/ppermute | solution.py:530
  36.1 0.1 collective-permute-start.14
  36.2 0.8 %finish.1 = (f32[96,256]{1,0:T(8,128)}, f32[96,256]{1,0:T(8,128)}) custom-call(f32[400,128]{1,0:T(8,128)S(1)} %get-tuple-element.86.refs_0_, bf16[400,128]{1,0:T(8,128)(2,1)S(1)} %collective-permute-done.11.refs_1_, bf16[400,128]{1,0:T(8,128)(2,1)S(1)} %collective-permute-done.12.refs_2_, bf16[400,128]{1,0:T(8,128)(2,1)S(1)} %collective-permute-done.13.refs_3_, ...), custom_call_target="tpu_custom_call" | custom-call | flops 100000000 | bytes 1000000 | tf_op jit(solution)/shard_map/finish/pallas_call | solution.py:518
  37.0 0.3 collective-permute-done.14.refs_1_
  37.3 0.5 %gain_grads.1 = (f32[1,128]{1,0:T(1,128)}, f32[1,128]{1,0:T(1,128)}) custom-call(f32[8,128]{1,0:T(8,128)S(1)} %sum_chips.1.refs_0_, f32[8,128]{1,0:T(8,128)S(1)} %collective-permute-done.14.refs_1_, f32[1,128]{1,0:T(1,128)S(1)} %bitcast.11, f32[1,128]{1,0:T(1,128)S(1)} %bitcast.9), custom_call_target="tpu_custom_call" | custom-call | tf_op jit(solution)/shard_map/gain_grads/pallas_call | solution.py:488
  (2 shorter events, 0.0 us)
Async XLA Ops:
  0.6 0.8 %copy-start = (bf16[96,256]{1,0:T(8,128)(2,1)S(1)}, bf16[96,256]{1,0:T(8,128)(2,1)}, u32[]{:S(2)}) copy-start(bf16[96,256]{1,0:T(8,128)(2,1)} %refs_4_.1) | copy-start | bytes 147460
  0.6 0.8 %copy-start.1 = (f32[128]{0:T(128)S(1)}, f32[128]{0:T(128)}, u32[]{:S(2)}) copy-start(f32[128]{0:T(128)} %param.16) | copy-start | bytes 1540
  0.7 0.8 %copy-start.7 = (bf16[96,256]{1,0:T(8,128)(2,1)S(1)}, bf16[96,256]{1,0:T(8,128)(2,1)}, u32[]{:S(2)}) copy-start(bf16[96,256]{1,0:T(8,128)(2,1)} %values_ref) | copy-start | bytes 147460
  1.5 5.4 %copy-start.2 = (f32[128]{0:T(128)S(1)}, f32[128]{0:T(128)}, u32[]{:S(2)}) copy-start(f32[128]{0:T(128)} %param.15) | copy-start | bytes 1540
  1.5 5.4 %copy-start.3 = (bf16[256,2048]{1,0:T(8,128)(2,1)S(1)}, bf16[256,2048]{1,0:T(8,128)(2,1)}, u32[]{:S(2)}) copy-start(bf16[256,2048]{1,0:T(8,128)(2,1)} %q_ref.1) | copy-start | bytes 3145732
  1.5 5.4 %copy-start.4 = (bf16[256,2048]{1,0:T(8,128)(2,1)S(1)}, bf16[256,2048]{1,0:T(8,128)(2,1)}, u32[]{:S(2)}) copy-start(bf16[256,2048]{1,0:T(8,128)(2,1)} %do_ref.1) | copy-start | bytes 3145732
  1.6 9.2 %collective-permute-start.5 = (bf16[96,512]{1,0:T(8,128)(2,1)S(1)}, bf16[96,512]{1,0:T(8,128)(2,1)S(1)}, u32[]{:S(2)}, u32[]{:S(2)}) collective-permute-start(bf16[96,512]{1,0:T(8,128)(2,1)S(1)} %pack.1.refs_9_), channel_id=1, source_target_pairs={{0,24},{4,28},{8,16},{12,20},{16,8},{20,12},{24,0},{28,4},{1,25},{... | collective-permute-start | bytes 294920 | tf_op jit(solution)/shard_map/ppermute | solution.py:530
  5.6 5.2 %collective-permute-start.3 = (bf16[96,512]{1,0:T(8,128)(2,1)S(1)}, bf16[96,512]{1,0:T(8,128)(2,1)S(1)}, u32[]{:S(2)}, u32[]{:S(2)}) collective-permute-start(bf16[96,512]{1,0:T(8,128)(2,1)S(1)} %pack.1.refs_9_), channel_id=1, source_target_pairs={{0,16},{4,20},{8,24},{12,28},{16,0},{20,4},{24,8},{28,12},{1,17},{... | collective-permute-start | bytes 294920 | tf_op jit(solution)/shard_map/ppermute | solution.py:530
  6.1 4.7 %collective-permute-start.1 = (bf16[96,512]{1,0:T(8,128)(2,1)S(1)}, bf16[96,512]{1,0:T(8,128)(2,1)S(1)}, u32[]{:S(2)}, u32[]{:S(2)}) collective-permute-start(bf16[96,512]{1,0:T(8,128)(2,1)S(1)} %pack.1.refs_9_), channel_id=1, source_target_pairs={{0,8},{4,12},{8,0},{12,4},{16,24},{20,28},{24,16},{28,20},{1,9},{5... | collective-permute-start | bytes 294920 | tf_op jit(solution)/shard_map/ppermute | solution.py:530
  6.2 5.2 %collective-permute-start = (bf16[96,512]{1,0:T(8,128)(2,1)S(1)}, bf16[96,512]{1,0:T(8,128)(2,1)S(1)}, u32[]{:S(2)}, u32[]{:S(2)}) collective-permute-start(bf16[96,512]{1,0:T(8,128)(2,1)S(1)} %pack.1.refs_9_), channel_id=1, source_target_pairs={{0,4},{4,0},{8,12},{12,8},{16,20},{20,16},{24,28},{28,24},{1,5},{5... | collective-permute-start | bytes 294920 | tf_op jit(solution)/shard_map/ppermute | solution.py:530
  6.9 5.7 %copy-start.5 = (bf16[256,256]{1,0:T(8,128)(2,1)S(1)}, bf16[256,256]{1,0:T(8,128)(2,1)}, u32[]{:S(2)}) copy-start(bf16[256,256]{1,0:T(8,128)(2,1)} %refs_6_.1) | copy-start | bytes 393220
  6.9 5.7 %copy-start.6 = (bf16[256,256]{1,0:T(8,128)(2,1)S(1)}, bf16[256,256]{1,0:T(8,128)(2,1)}, u32[]{:S(2)}) copy-start(bf16[256,256]{1,0:T(8,128)(2,1)} %ck_ref.1) | copy-start | bytes 393220
  6.9 5.7 %copy-start.8 = (s32[4]{0:T(128)S(1)}, s32[4]{0:T(128)}, u32[]{:S(2)}) copy-start(s32[4]{0:T(128)} %prompt_ref.1) | copy-start | bytes 52
  10.8 1.3 %collective-permute-start.6 = (bf16[96,512]{1,0:T(8,128)(2,1)S(1)}, bf16[96,512]{1,0:T(8,128)(2,1)S(1)}, u32[]{:S(2)}, u32[]{:S(2)}) collective-permute-start(bf16[96,512]{1,0:T(8,128)(2,1)S(1)} %collective-permute-done.5.refs_15_), channel_id=1, source_target_pairs={{0,4},{4,0},{8,12},{12,8},{16,20},{20,16},{24,28},{28,24},{1,5},{5... | collective-permute-start | bytes 294920 | tf_op jit(solution)/shard_map/ppermute | solution.py:530
  10.8 1.4 %collective-permute-start.4 = (bf16[96,512]{1,0:T(8,128)(2,1)S(1)}, bf16[96,512]{1,0:T(8,128)(2,1)S(1)}, u32[]{:S(2)}, u32[]{:S(2)}) collective-permute-start(bf16[96,512]{1,0:T(8,128)(2,1)S(1)} %collective-permute-done.3.refs_13_), channel_id=1, source_target_pairs={{0,4},{4,0},{8,12},{12,8},{16,20},{20,16},{24,28},{28,24},{1,5},{5... | collective-permute-start | bytes 294920 | tf_op jit(solution)/shard_map/ppermute | solution.py:530
  11.3 1.3 %collective-permute-start.2 = (bf16[96,512]{1,0:T(8,128)(2,1)S(1)}, bf16[96,512]{1,0:T(8,128)(2,1)S(1)}, u32[]{:S(2)}, u32[]{:S(2)}) collective-permute-start(bf16[96,512]{1,0:T(8,128)(2,1)S(1)} %collective-permute-done.1.refs_11_), channel_id=1, source_target_pairs={{0,4},{4,0},{8,12},{12,8},{16,20},{20,16},{24,28},{28,24},{1,5},{5... | collective-permute-start | bytes 294920 | tf_op jit(solution)/shard_map/ppermute | solution.py:530
  18.6 9.8 %collective-permute-start.10 = (bf16[384,512]{1,0:T(8,128)(2,1)S(1)}, bf16[384,512]{1,0:T(8,128)(2,1)S(1)}, u32[]{:S(2)}, u32[]{:S(2)}) collective-permute-start(bf16[384,512]{1,0:T(8,128)(2,1)S(1)} %get-tuple-element.69), channel_id=1, source_target_pairs={{0,4},{4,0},{8,12},{12,8},{16,20},{20,16},{24,28},{28,24},{1,5},{5... | collective-permute-start | bytes 1179656 | tf_op jit(solution)/shard_map/ppermute | solution.py:530
  20.3 5.8 %collective-permute-start.9 = (f32[8,128]{1,0:T(8,128)S(1)}, f32[8,128]{1,0:T(8,128)S(1)}, u32[]{:S(2)}, u32[]{:S(2)}) collective-permute-start(f32[8,128]{1,0:T(8,128)S(1)} %get-tuple-element.70.refs_0_), channel_id=1, source_target_pairs={{0,3},{1,2},{2,1},{3,0},{4,7},{5,6},{6,5},{7,4},{8,11},{9,10},{10,... | collective-permute-start | bytes 12296 | tf_op jit(solution)/shard_map/ppermute | solution.py:530
  23.9 4.5 %collective-permute-start.8 = (f32[8,128]{1,0:T(8,128)S(1)}, f32[8,128]{1,0:T(8,128)S(1)}, u32[]{:S(2)}, u32[]{:S(2)}) collective-permute-start(f32[8,128]{1,0:T(8,128)S(1)} %get-tuple-element.70.refs_0_), channel_id=1, source_target_pairs={{0,2},{1,3},{2,0},{3,1},{4,6},{5,7},{6,4},{7,5},{8,10},{9,11},{10,... | collective-permute-start | bytes 12296 | tf_op jit(solution)/shard_map/ppermute | solution.py:530
  23.9 4.5 %collective-permute-start.7 = (f32[8,128]{1,0:T(8,128)S(1)}, f32[8,128]{1,0:T(8,128)S(1)}, u32[]{:S(2)}, u32[]{:S(2)}) collective-permute-start(f32[8,128]{1,0:T(8,128)S(1)} %get-tuple-element.70.refs_0_), channel_id=1, source_target_pairs={{0,1},{1,0},{2,3},{3,2},{4,5},{5,4},{6,7},{7,6},{8,9},{9,8},{10,11... | collective-permute-start | bytes 12296 | tf_op jit(solution)/shard_map/ppermute | solution.py:530
  28.5 6.4 %collective-permute-start.11 = (bf16[400,128]{1,0:T(8,128)(2,1)S(1)}, bf16[400,128]{1,0:T(8,128)(2,1)S(1)}, u32[]{:S(2)}, u32[]{:S(2)}) collective-permute-start(bf16[400,128]{1,0:T(8,128)(2,1)S(1)} %get-tuple-element.74), channel_id=1, source_target_pairs={{0,24},{4,28},{8,16},{12,20},{16,8},{20,12},{24,0},{28,4},{1,25},{... | collective-permute-start | bytes 307208 | tf_op jit(solution)/shard_map/ppermute | solution.py:530
  30.2 5.4 %collective-permute-start.12 = (bf16[400,128]{1,0:T(8,128)(2,1)S(1)}, bf16[400,128]{1,0:T(8,128)(2,1)S(1)}, u32[]{:S(2)}, u32[]{:S(2)}) collective-permute-start(bf16[400,128]{1,0:T(8,128)(2,1)S(1)} %get-tuple-element.75), channel_id=1, source_target_pairs={{0,16},{4,20},{8,24},{12,28},{16,0},{20,4},{24,8},{28,12},{1,17},{... | collective-permute-start | bytes 307208 | tf_op jit(solution)/shard_map/ppermute | solution.py:530
  31.4 4.7 %collective-permute-start.13 = (bf16[400,128]{1,0:T(8,128)(2,1)S(1)}, bf16[400,128]{1,0:T(8,128)(2,1)S(1)}, u32[]{:S(2)}, u32[]{:S(2)}) collective-permute-start(bf16[400,128]{1,0:T(8,128)(2,1)S(1)} %get-tuple-element.76), channel_id=1, source_target_pairs={{0,8},{4,12},{8,0},{12,4},{16,24},{20,28},{24,16},{28,20},{1,9},{5... | collective-permute-start | bytes 307208 | tf_op jit(solution)/shard_map/ppermute | solution.py:530
  36.1 1.2 %collective-permute-start.14 = (f32[8,128]{1,0:T(8,128)S(1)}, f32[8,128]{1,0:T(8,128)S(1)}, u32[]{:S(2)}, u32[]{:S(2)}) collective-permute-start(f32[8,128]{1,0:T(8,128)S(1)} %sum_chips.1.refs_0_), channel_id=1, source_target_pairs={{0,4},{4,0},{8,12},{12,8},{16,20},{20,16},{24,28},{28,24},{1,5},{5... | collective-permute-start | bytes 12296 | tf_op jit(solution)/shard_map/ppermute | solution.py:530

commit v8 on v7

--- a/solution.py
+++ b/solution.py
@@ -103,7 +103,7 @@
     return pl.ds(pl.multiple_of(slot * CL, CL), CL)
 
 
-def prepare_kernel(live_ref, q_ref, do_ref, qg_ref, raw_ref, recip_ref, queries_ref, grads_ref, col_ref):
+def prepare_kernel(live_ref, q_ref, do_ref, qg_ref, raw_ref, recip_ref, queries_ref, grads_ref, col_ref, rows_ref):
     size = col_ref.shape[0]
     heads = raw_ref.shape[1] // size
     group = q_ref.shape[1] // raw_ref.shape[1]
@@ -120,7 +120,9 @@
             raw = half.astype(F32)
             recip = lax.rsqrt(jnp.mean(raw * raw, axis=0, keepdims=True) + EPS)
             recip_ref[slot, head:head + 1, :] = recip
-            queries_ref[slot, rows, :] = (raw * recip * col_ref[...]).astype(BF16)
+            queries = (raw * recip * col_ref[...]).astype(BF16)
+            queries_ref[slot, rows, :] = queries
+            rows_ref[slot, head] = queries.T
             grads_ref[slot, rows, :] = jnp.concatenate([do_ref[slot_rows(slot), place] for place in places], axis=0).T
         return carry
 
@@ -134,10 +136,11 @@
     return pl.pallas_call(
         prepare_kernel,
         in_specs=[SMEM_SPEC] + [VMEM_SPEC] * 3,
-        out_specs=[VMEM_SPEC] * 5,
+        out_specs=[VMEM_SPEC] * 6,
         out_shape=[
             turned, jax.ShapeDtypeStruct((slots, 8, lanes), F32), turned, turned,
             jax.ShapeDtypeStruct((size, lanes), F32),
+            jax.ShapeDtypeStruct((slots, width // size, lanes, size), BF16),
         ],
         compiler_params=params(),
         cost_estimate=cost(2 * 10**9, 6 * queries.size),
@@ -146,8 +149,8 @@
 
 
 def attention_kernel(*refs, parts, heads):
-    live_ref, prompt_ref, me_ref, queries_ref, grads_ref, ck_ref, cv_ref, kg_ref, mask_ref = refs[:9]
-    pieces, refs = refs[9:9 + parts], refs[9 + parts:]
+    live_ref, prompt_ref, me_ref, queries_ref, query_rows, grads_ref, ck_ref, cv_ref, kg_ref, mask_ref = refs[:10]
+    pieces, refs = refs[10:10 + parts], refs[10 + parts:]
     att_ref, ds_ref, pool_keys, own_keys, own_acc, term_ref, keep_ref = refs[:7]
     send_ref, refs = (refs[7], refs[8:]) if parts > 1 else (None, refs[7:])
     acc, pool_values, pool_values_t, own_values_t = refs[:4]
@@ -217,7 +220,7 @@
 
     def close(slot, head):
         value_grad = dot_nt(weights[head][...], grads[head][...])
-        key_grad = dot_nt(ds_ref[slot, head], queries_ref[slot, columns(head), :])
+        key_grad = dot(ds_ref[slot, head], query_rows[slot, head])
         acc[prompt_rows(slot), columns(head)] += key_grad[:PL]
         acc[prompt_rows(slot), width + head * size:width + (head + 1) * size] += value_grad[:PL]
         own_acc[slot, head, 0] = key_grad[PL:]
@@ -263,7 +266,7 @@
             ref[place, width:] = acc[piece_rows(piece_no), width:].astype(ref.dtype)
 
 
-def attention(live_counts, slot_prompts, me, queries, grads, keys, values, key_gain, mask, pieces):
+def attention(live_counts, slot_prompts, me, queries, query_rows, grads, keys, values, key_gain, mask, pieces):
     size = key_gain.shape[1]
     slots, width, lanes = queries.shape
     heads = width // size
@@ -286,7 +289,7 @@
         out_shape += [jax.ShapeDtypeStruct((pool_rows, 2 * width), F32)]
     return pl.pallas_call(
         functools.partial(attention_kernel, parts=parts, heads=heads),
-        in_specs=[SMEM_SPEC] * 3 + [VMEM_SPEC] * (6 + parts),
+        in_specs=[SMEM_SPEC] * 3 + [VMEM_SPEC] * (7 + parts),
         out_specs=[VMEM_SPEC] * len(out_shape),
         out_shape=out_shape,
         scratch_shapes=[
@@ -302,7 +305,7 @@
         compiler_params=params(),
         cost_estimate=cost(3 * 10**9, 10**7),
         name="attention",
-    )(live_counts, slot_prompts, me, queries, grads, keys, values, key_gain, mask, *pieces)
+    )(live_counts, slot_prompts, me, queries, query_rows, grads, keys, values, key_gain, mask, *pieces)
 
 
 def copy_slots(live_ref, zeros, out, target, sems):
@@ -543,18 +546,21 @@
     me = lax.axis_index("grp").astype(jnp.int32).reshape(1) if by_permute else jnp.zeros((1,), jnp.int32)
     mask, me, keys_in, values_in = lax.optimization_barrier((causal(), me, prompt_keys, prompt_values))
     mine = pack(keys_in, values_in, key_gain)
-    raw, recip, queries, grads, query_col = prepare(live_counts, comp_queries, out_grad, query_gain, slots, width)
+    raw, recip, queries, grads, query_col, query_rows = prepare(live_counts, comp_queries, out_grad, query_gain, slots, width)
     if by_permute:
         even = [mine] + [swap(mine, "grp", step) for step in range(2, grp, 2)]
-        odd = [swap(mine, "grp", 1)]
-        for at in range(1, len(even)):
-            even[at], query_col = lax.optimization_barrier((even[at], query_col))
-            odd.append(swap(even[at], "grp", 1))
+        odd = [swap(mine, "grp", 1)] + [None] * (len(even) - 1)
+        for at in range(len(even) - 1, 0, -1):
+            if at == 1:
+                even[at], query_col, odd[-1] = lax.optimization_barrier((even[at], query_col, odd[-1]))
+            else:
+                even[at], query_col = lax.optimization_barrier((even[at], query_col))
+            odd[at] = swap(even[at], "grp", 1)
         pieces = [piece for pair in zip(even, odd) for piece in pair]
     else:
         pieces = [lax.all_gather(mine, "grp", axis=0, tiled=True)]
     att_t, score_grads, pool_keys, own_keys, own_acc, term, keep, *send = attention(
-        live_counts, slot_prompts, me, queries, grads, comp_keys, comp_values, key_gain, mask, pieces,
+        live_counts, slot_prompts, me, queries, query_rows, grads, comp_keys, comp_values, key_gain, mask, pieces,
     )
     attended, key_grads, value_grads = turn(live_counts, att_t, own_acc, comp_keys, key_gain, comp_queries.shape)
     query_grads = post(

time: 38.1 us -> 37.7 us (0.990)
  Pallas kernels: 12.4 us -> 12.8 us
  transfers between devices with their start and end apart: 15 -> 15, of which waited for: 9 -> 9; matrix products, arithmetic and copies ran while one was open for 0% -> 0% of each run, Pallas kernels for 15% -> 16%
where the time goes in v8:
time: 37.7 us
  starting transfers between devices  14.7 us (39%)
  Pallas kernels  12.8 us (34%)
  waiting for transfers between devices  7.92 us (21%)
  between operations  1.46 us (4%)
  local copies, waits for them, and re-layouts  0.82 us (2%)
    ppermute x15, starting transfers between devices, swap(): lax.ppermute(values, axis, [(i, i ^ step) for i in range(lax.axis_size(ax...  14.7 us
    ppermute x15, waiting for transfers between devices, swap(): lax.ppermute(values, axis, [(i, i ^ step) for i in range(lax.axis_size(ax...  7.92 us
    pallas_call x1, Pallas kernels, attention(): pl.pallas_call(functools.partial(attention_kernel, parts=parts, heads=hea...  5.95 us
    pallas_call x1, Pallas kernels, post(): pl.pallas_call(post_kernel, in_specs=[SMEM_SPEC] * 2 + [VMEM_SPEC] * 6, o...  2.69 us
    pallas_call x1, Pallas kernels, turn(): pl.pallas_call(turn_kernel, in_specs=[SMEM_SPEC] + [VMEM_SPEC] * 4, out_s...  1.39 us
    pallas_call x1, Pallas kernels, prepare(): pl.pallas_call(prepare_kernel, in_specs=[SMEM_SPEC] + [VMEM_SPEC] * 3, ou...  1.15 us
    pallas_call x1, Pallas kernels, finish(): pl.pallas_call(finish_kernel, in_specs=[VMEM_SPEC] * (len(blocks) + 2), o...  0.84 us
    unnamed x18, local copies, waits for them, and re-layouts  0.82 us
  transfers between devices with their start and end apart: 15, of which 9 were waited for; matrix products, arithmetic and copies ran while one was open for 0% of the time, Pallas kernels for 16%

profile of v8, /device:TPU:0, one launch (start us, length us, event | category | flops | bytes accessed | tf_op | source)
XLA Modules:
  0.0 37.7 jit_solution(14631937805628842042)
XLA Ops:
  0.6 0.0 copy-start
  0.6 0.0 copy-start.1
  0.7 0.0 copy-start.7
  0.7 0.7 %copy-done = bf16[96,256]{1,0:T(8,128)(2,1)S(1)} copy-done((bf16[96,256]{1,0:T(8,128)(2,1)S(1)}, bf16[96,256]{1,0:T(8,128)(2,1)}, u32[]{:S(2)}) %copy-start) | copy-done | bytes 49176
  1.4 0.0 copy-done.1
  1.4 0.0 copy-done.7
  1.5 0.0 copy-start.2
  1.5 0.0 copy-start.3
  1.5 0.0 copy-start.4
  1.5 0.1 pack.1.refs_10_
  1.6 4.0 %collective-permute-start.3 = (bf16[96,512]{1,0:T(8,128)(2,1)S(1)}, bf16[96,512]{1,0:T(8,128)(2,1)S(1)}, u32[]{:S(2)}, u32[]{:S(2)}) collective-permute-start(bf16[96,512]{1,0:T(8,128)(2,1)S(1)} %pack.1.refs_10_), channel_id=1, source_target_pairs={{0,24},{4,28},{8,16},{12,20},{16,8},{20,12},{24,0},{28,4},{1,25},{... | collective-permute-start | bytes 294920 | tf_op jit(solution)/shard_map/ppermute | solution.py:533
  5.6 0.5 %collective-permute-start.2 = (bf16[96,512]{1,0:T(8,128)(2,1)S(1)}, bf16[96,512]{1,0:T(8,128)(2,1)S(1)}, u32[]{:S(2)}, u32[]{:S(2)}) collective-permute-start(bf16[96,512]{1,0:T(8,128)(2,1)S(1)} %pack.1.refs_10_), channel_id=1, source_target_pairs={{0,16},{4,20},{8,24},{12,28},{16,0},{20,4},{24,8},{28,12},{1,17},{... | collective-permute-start | bytes 294920 | tf_op jit(solution)/shard_map/ppermute | solution.py:533
  6.1 0.1 collective-permute-start.1
  6.9 0.0 copy-done.2
  6.9 0.0 copy-done.3
  6.9 0.0 copy-done.4
  6.9 0.0 copy-start.5
  6.9 0.0 copy-start.6
  6.9 0.0 copy-start.8
  6.9 1.2 %prepare.1 = (bf16[4,256,512]{2,1,0:T(8,128)(2,1)S(1)}, f32[4,8,512]{2,1,0:T(8,128)S(1)}, bf16[4,256,512]{2,1,0:T(8,128)(2,1)S(1)}, bf16[4,256,512]{2,1,0:T(8,12...) custom-call(s32[1]{0:T(128)S(6)} %copy.18.live_ref.refs_0_, bf16[256,2048]{1,0:T(8,128)(2,1)S(1)} %copy-done.3, ...), custom_call_target="tpu_custom_call" | custom-call | flops 2000000000 | bytes 3145728 | tf_op jit(solution)/shard_map/prepare/pallas_call | solution.py:136
  8.1 0.7 %collective-permute-done.3.refs_16_ = bf16[96,512]{1,0:T(8,128)(2,1)S(1)} collective-permute-done((bf16[96,512]{1,0:T(8,128)(2,1)S(1)}, bf16[96,512]{1,0:T(8,128)(2,1)S(1)}, u32[]{:S(2)}, u32[]{:S(2)}) %collective-permute-start.3) | collective-permute-done | bytes 98336 | tf_op jit(solution)/shard_map/ppermute | solution.py:533
  8.7 0.0 collective-permute-start.4
  8.8 0.5 %collective-permute-start = (bf16[96,512]{1,0:T(8,128)(2,1)S(1)}, bf16[96,512]{1,0:T(8,128)(2,1)S(1)}, u32[]{:S(2)}, u32[]{:S(2)}) collective-permute-start(bf16[96,512]{1,0:T(8,128)(2,1)S(1)} %pack.1.refs_10_), channel_id=1, source_target_pairs={{0,4},{4,0},{8,12},{12,8},{16,20},{20,16},{24,28},{28,24},{1,5},{5... | collective-permute-start | bytes 294920 | tf_op jit(solution)/shard_map/ppermute | solution.py:533
  9.3 1.2 %collective-permute-done.2.refs_14_ = bf16[96,512]{1,0:T(8,128)(2,1)S(1)} collective-permute-done((bf16[96,512]{1,0:T(8,128)(2,1)S(1)}, bf16[96,512]{1,0:T(8,128)(2,1)S(1)}, u32[]{:S(2)}, u32[]{:S(2)}) %collective-permute-start.2) | collective-permute-done | bytes 98336 | tf_op jit(solution)/shard_map/ppermute | solution.py:533
  10.5 0.0 collective-permute-start.6
  10.5 0.3 collective-permute-done.1.refs_12_
  10.8 0.0 collective-permute-done.4.refs_17_
  10.8 0.2 collective-permute-start.5
  11.0 0.0 collective-permute-done.refs_11_
  11.0 0.8 %collective-permute-done.6.refs_15_ = bf16[96,512]{1,0:T(8,128)(2,1)S(1)} collective-permute-done((bf16[96,512]{1,0:T(8,128)(2,1)S(1)}, bf16[96,512]{1,0:T(8,128)(2,1)S(1)}, u32[]{:S(2)}, u32[]{:S(2)}) %collective-permute-start.6) | collective-permute-done | bytes 98336 | tf_op jit(solution)/shard_map/ppermute | solution.py:533
  11.8 0.3 collective-permute-done.5.refs_13_
  12.1 0.0 copy-done.5
  12.1 0.0 copy-done.6
  12.1 0.0 copy-done.8
  12.1 5.9 %attention.1 = (bf16[4,256,512]{2,1,0:T(8,128)(2,1)S(1)}, bf16[4,2,448,512]{3,2,1,0:T(8,128)(2,1)S(1)}, bf16[768,256]{1,0:T(8,128)(2,1)S(1)}, bf16[256,256]{1,0:...) custom-call(s32[1]{0:T(128)S(6)} %copy.18.live_ref.refs_0_, ...), custom_call_target="tpu_custom_call" | custom-call | flops 3000000000 | bytes 10000000 | tf_op jit(solution)/shard_map/attention/pallas_call | solution.py:290
  18.1 0.1 collective-permute-start.10
  18.1 3.8 %collective-permute-start.9 = (f32[8,128]{1,0:T(8,128)S(1)}, f32[8,128]{1,0:T(8,128)S(1)}, u32[]{:S(2)}, u32[]{:S(2)}) collective-permute-start(f32[8,128]{1,0:T(8,128)S(1)} %get-tuple-element.74.refs_0_), channel_id=1, source_target_pairs={{0,3},{1,2},{2,1},{3,0},{4,7},{5,6},{6,5},{7,4},{8,11},{9,10},{10,... | collective-permute-start | bytes 12296 | tf_op jit(solution)/shard_map/ppermute | solution.py:533
  21.9 0.0 collective-permute-start.8
  21.9 0.7 %collective-permute-start.7 = (f32[8,128]{1,0:T(8,128)S(1)}, f32[8,128]{1,0:T(8,128)S(1)}, u32[]{:S(2)}, u32[]{:S(2)}) collective-permute-start(f32[8,128]{1,0:T(8,128)S(1)} %get-tuple-element.74.refs_0_), channel_id=1, source_target_pairs={{0,1},{1,0},{2,3},{3,2},{4,5},{5,4},{6,7},{7,6},{8,9},{9,8},{10,11... | collective-permute-start | bytes 12296 | tf_op jit(solution)/shard_map/ppermute | solution.py:533
  22.6 1.4 %turn.1 = (bf16[256,2048]{1,0:T(8,128)(2,1)}, bf16[256,256]{1,0:T(8,128)(2,1)}, bf16[256,256]{1,0:T(8,128)(2,1)}) custom-call(s32[1]{0:T(128)S(6)} %copy.18.live_ref.refs_0_, bf16[4,256,512]{2,1,0:T(8,128)(2,1)S(1)} %get-tuple-element.68.att_t_ref, f32[4,2,2,64,128]{4,3,2,1,0:T(8,128)S(1)} %get-tuple-element.69.own_acc, bf16[256,256]{1,0:T(8,128)(2,1)S(1)} %copy-done.6, ...), custom_call_target="tpu_custom_call" | custom-call | flops 2000000000 | bytes 2000000 | tf_op jit(solution)/shard_map/turn/pallas_call | solution.py:369
  24.0 0.0 collective-permute-done.9.refs_3_
  24.0 2.4 %collective-permute-done.8.refs_2_ = f32[8,128]{1,0:T(8,128)S(1)} collective-permute-done((f32[8,128]{1,0:T(8,128)S(1)}, f32[8,128]{1,0:T(8,128)S(1)}, u32[]{:S(2)}, u32[]{:S(2)}) %collective-permute-start.8) | collective-permute-done | bytes 4128 | tf_op jit(solution)/shard_map/ppermute | solution.py:533
  26.4 0.0 collective-permute-done.7.refs_1_
  26.4 0.0 collective-permute-done.10.came_ref
  26.4 0.1 add.1
  26.5 4.2 %collective-permute-start.11 = (bf16[400,128]{1,0:T(8,128)(2,1)S(1)}, bf16[400,128]{1,0:T(8,128)(2,1)S(1)}, u32[]{:S(2)}, u32[]{:S(2)}) collective-permute-start(bf16[400,128]{1,0:T(8,128)(2,1)S(1)} %get-tuple-element.78), channel_id=1, source_target_pairs={{0,24},{4,28},{8,16},{12,20},{16,8},{20,12},{24,0},{28,4},{1,25},{... | collective-permute-start | bytes 307208 | tf_op jit(solution)/shard_map/ppermute | solution.py:533
  30.7 0.6 %collective-permute-start.12 = (bf16[400,128]{1,0:T(8,128)(2,1)S(1)}, bf16[400,128]{1,0:T(8,128)(2,1)S(1)}, u32[]{:S(2)}, u32[]{:S(2)}) collective-permute-start(bf16[400,128]{1,0:T(8,128)(2,1)S(1)} %get-tuple-element.79), channel_id=1, source_target_pairs={{0,16},{4,20},{8,24},{12,28},{16,0},{20,4},{24,8},{28,12},{1,17},{... | collective-permute-start | bytes 307208 | tf_op jit(solution)/shard_map/ppermute | solution.py:533
  31.3 0.1 collective-permute-start.13
  31.3 2.7 %post.1 = bf16[256,2048]{1,0:T(8,128)(2,1)} custom-call(s32[1]{0:T(128)S(6)} %copy.18.live_ref.refs_0_, s32[4]{0:T(128)S(1)} %copy-done.8, bf16[4,2,448,512]{3,2,1,0:T(8,128)(2,1)S(1)} %get-tuple-element.81.ds_ref, bf16[768,256]{1,0:T(8,128)(2,1)S(1)} %get-tuple-element.82.pool_keys, bf16[256,256]{1,0:T(8,128)(2,1)S(1)} %get-tuple-element.83.own_keys_ref, ...), custom_call_target="tpu_custom_call" | custom-call | flops 3000000000 | bytes 4000000 | tf_op jit(solution)/shard_map/post/pallas_call | solution.py:416
  34.0 0.0 collective-permute-done.11.refs_1_
  34.0 1.3 %collective-permute-done.12.refs_2_ = bf16[400,128]{1,0:T(8,128)(2,1)S(1)} collective-permute-done((bf16[400,128]{1,0:T(8,128)(2,1)S(1)}, bf16[400,128]{1,0:T(8,128)(2,1)S(1)}, u32[]{:S(2)}, u32[]{:S(2)}) %collective-permute-start.12) | collective-permute-done | bytes 102432 | tf_op jit(solution)/shard_map/ppermute | solution.py:533
  35.3 0.6 %collective-permute-done.13.refs_3_ = bf16[400,128]{1,0:T(8,128)(2,1)S(1)} collective-permute-done((bf16[400,128]{1,0:T(8,128)(2,1)S(1)}, bf16[400,128]{1,0:T(8,128)(2,1)S(1)}, u32[]{:S(2)}, u32[]{:S(2)}) %collective-permute-start.13) | collective-permute-done | bytes 102432 | tf_op jit(solution)/shard_map/ppermute | solution.py:533
  35.9 0.1 collective-permute-start.14
  36.0 0.8 %finish.1 = (f32[96,256]{1,0:T(8,128)}, f32[96,256]{1,0:T(8,128)}) custom-call(f32[400,128]{1,0:T(8,128)S(1)} %get-tuple-element.90.refs_0_, bf16[400,128]{1,0:T(8,128)(2,1)S(1)} %collective-permute-done.11.refs_1_, bf16[400,128]{1,0:T(8,128)(2,1)S(1)} %collective-permute-done.12.refs_2_, bf16[400,128]{1,0:T(8,128)(2,1)S(1)} %collective-permute-done.13.refs_3_, ...), custom_call_target="tpu_custom_call" | custom-call | flops 100000000 | bytes 1000000 | tf_op jit(solution)/shard_map/finish/pallas_call | solution.py:521
  36.9 0.3 collective-permute-done.14.refs_1_
  37.2 0.5 %gain_grads.1 = (f32[1,128]{1,0:T(1,128)}, f32[1,128]{1,0:T(1,128)}) custom-call(f32[8,128]{1,0:T(8,128)S(1)} %sum_chips.1.refs_0_, f32[8,128]{1,0:T(8,128)S(1)} %collective-permute-done.14.refs_1_, f32[1,128]{1,0:T(1,128)S(1)} %bitcast.11, f32[1,128]{1,0:T(1,128)S(1)} %bitcast.9), custom_call_target="tpu_custom_call" | custom-call | tf_op jit(solution)/shard_map/gain_grads/pallas_call | solution.py:491
  (2 shorter events, 0.0 us)
Async XLA Ops:
  0.6 0.8 %copy-start = (bf16[96,256]{1,0:T(8,128)(2,1)S(1)}, bf16[96,256]{1,0:T(8,128)(2,1)}, u32[]{:S(2)}) copy-start(bf16[96,256]{1,0:T(8,128)(2,1)} %refs_4_.1) | copy-start | bytes 147460
  0.6 0.8 %copy-start.1 = (f32[128]{0:T(128)S(1)}, f32[128]{0:T(128)}, u32[]{:S(2)}) copy-start(f32[128]{0:T(128)} %param.16) | copy-start | bytes 1540
  0.7 0.8 %copy-start.7 = (bf16[96,256]{1,0:T(8,128)(2,1)S(1)}, bf16[96,256]{1,0:T(8,128)(2,1)}, u32[]{:S(2)}) copy-start(bf16[96,256]{1,0:T(8,128)(2,1)} %values_ref) | copy-start | bytes 147460
  1.5 5.4 %copy-start.2 = (f32[128]{0:T(128)S(1)}, f32[128]{0:T(128)}, u32[]{:S(2)}) copy-start(f32[128]{0:T(128)} %param.15) | copy-start | bytes 1540
  1.5 5.4 %copy-start.3 = (bf16[256,2048]{1,0:T(8,128)(2,1)S(1)}, bf16[256,2048]{1,0:T(8,128)(2,1)}, u32[]{:S(2)}) copy-start(bf16[256,2048]{1,0:T(8,128)(2,1)} %q_ref.1) | copy-start | bytes 3145732
  1.5 5.4 %copy-start.4 = (bf16[256,2048]{1,0:T(8,128)(2,1)S(1)}, bf16[256,2048]{1,0:T(8,128)(2,1)}, u32[]{:S(2)}) copy-start(bf16[256,2048]{1,0:T(8,128)(2,1)} %do_ref.1) | copy-start | bytes 3145732
  1.6 7.1 %collective-permute-start.3 = (bf16[96,512]{1,0:T(8,128)(2,1)S(1)}, bf16[96,512]{1,0:T(8,128)(2,1)S(1)}, u32[]{:S(2)}, u32[]{:S(2)}) collective-permute-start(bf16[96,512]{1,0:T(8,128)(2,1)S(1)} %pack.1.refs_10_), channel_id=1, source_target_pairs={{0,24},{4,28},{8,16},{12,20},{16,8},{20,12},{24,0},{28,4},{1,25},{... | collective-permute-start | bytes 294920 | tf_op jit(solution)/shard_map/ppermute | solution.py:533
  5.6 4.9 %collective-permute-start.2 = (bf16[96,512]{1,0:T(8,128)(2,1)S(1)}, bf16[96,512]{1,0:T(8,128)(2,1)S(1)}, u32[]{:S(2)}, u32[]{:S(2)}) collective-permute-start(bf16[96,512]{1,0:T(8,128)(2,1)S(1)} %pack.1.refs_10_), channel_id=1, source_target_pairs={{0,16},{4,20},{8,24},{12,28},{16,0},{20,4},{24,8},{28,12},{1,17},{... | collective-permute-start | bytes 294920 | tf_op jit(solution)/shard_map/ppermute | solution.py:533
  6.1 4.7 %collective-permute-start.1 = (bf16[96,512]{1,0:T(8,128)(2,1)S(1)}, bf16[96,512]{1,0:T(8,128)(2,1)S(1)}, u32[]{:S(2)}, u32[]{:S(2)}) collective-permute-start(bf16[96,512]{1,0:T(8,128)(2,1)S(1)} %pack.1.refs_10_), channel_id=1, source_target_pairs={{0,8},{4,12},{8,0},{12,4},{16,24},{20,28},{24,16},{28,20},{1,9},{5... | collective-permute-start | bytes 294920 | tf_op jit(solution)/shard_map/ppermute | solution.py:533
  6.9 5.2 %copy-start.5 = (bf16[256,256]{1,0:T(8,128)(2,1)S(1)}, bf16[256,256]{1,0:T(8,128)(2,1)}, u32[]{:S(2)}) copy-start(bf16[256,256]{1,0:T(8,128)(2,1)} %refs_7_.1) | copy-start | bytes 393220
  6.9 5.2 %copy-start.6 = (bf16[256,256]{1,0:T(8,128)(2,1)S(1)}, bf16[256,256]{1,0:T(8,128)(2,1)}, u32[]{:S(2)}) copy-start(bf16[256,256]{1,0:T(8,128)(2,1)} %ck_ref.1) | copy-start | bytes 393220
  6.9 5.2 %copy-start.8 = (s32[4]{0:T(128)S(1)}, s32[4]{0:T(128)}, u32[]{:S(2)}) copy-start(s32[4]{0:T(128)} %prompt_ref.1) | copy-start | bytes 52
  8.7 2.0 %collective-permute-start.4 = (bf16[96,512]{1,0:T(8,128)(2,1)S(1)}, bf16[96,512]{1,0:T(8,128)(2,1)S(1)}, u32[]{:S(2)}, u32[]{:S(2)}) collective-permute-start(bf16[96,512]{1,0:T(8,128)(2,1)S(1)} %collective-permute-done.3.refs_16_), channel_id=1, source_target_pairs={{0,4},{4,0},{8,12},{12,8},{16,20},{20,16},{24,28},{28,24},{1,5},{5... | collective-permute-start | bytes 294920 | tf_op jit(solution)/shard_map/ppermute | solution.py:533
  8.8 2.2 %collective-permute-start = (bf16[96,512]{1,0:T(8,128)(2,1)S(1)}, bf16[96,512]{1,0:T(8,128)(2,1)S(1)}, u32[]{:S(2)}, u32[]{:S(2)}) collective-permute-start(bf16[96,512]{1,0:T(8,128)(2,1)S(1)} %pack.1.refs_10_), channel_id=1, source_target_pairs={{0,4},{4,0},{8,12},{12,8},{16,20},{20,16},{24,28},{28,24},{1,5},{5... | collective-permute-start | bytes 294920 | tf_op jit(solution)/shard_map/ppermute | solution.py:533
  10.5 1.3 %collective-permute-start.6 = (bf16[96,512]{1,0:T(8,128)(2,1)S(1)}, bf16[96,512]{1,0:T(8,128)(2,1)S(1)}, u32[]{:S(2)}, u32[]{:S(2)}) collective-permute-start(bf16[96,512]{1,0:T(8,128)(2,1)S(1)} %collective-permute-done.2.refs_14_), channel_id=1, source_target_pairs={{0,4},{4,0},{8,12},{12,8},{16,20},{20,16},{24,28},{28,24},{1,5},{5... | collective-permute-start | bytes 294920 | tf_op jit(solution)/shard_map/ppermute | solution.py:533
  10.8 1.3 %collective-permute-start.5 = (bf16[96,512]{1,0:T(8,128)(2,1)S(1)}, bf16[96,512]{1,0:T(8,128)(2,1)S(1)}, u32[]{:S(2)}, u32[]{:S(2)}) collective-permute-start(bf16[96,512]{1,0:T(8,128)(2,1)S(1)} %collective-permute-done.1.refs_12_), channel_id=1, source_target_pairs={{0,4},{4,0},{8,12},{12,8},{16,20},{20,16},{24,28},{28,24},{1,5},{5... | collective-permute-start | bytes 294920 | tf_op jit(solution)/shard_map/ppermute | solution.py:533
  18.1 8.3 %collective-permute-start.10 = (bf16[384,512]{1,0:T(8,128)(2,1)S(1)}, bf16[384,512]{1,0:T(8,128)(2,1)S(1)}, u32[]{:S(2)}, u32[]{:S(2)}) collective-permute-start(bf16[384,512]{1,0:T(8,128)(2,1)S(1)} %get-tuple-element.73), channel_id=1, source_target_pairs={{0,4},{4,0},{8,12},{12,8},{16,20},{20,16},{24,28},{28,24},{1,5},{5... | collective-permute-start | bytes 1179656 | tf_op jit(solution)/shard_map/ppermute | solution.py:533
  18.1 5.9 %collective-permute-start.9 = (f32[8,128]{1,0:T(8,128)S(1)}, f32[8,128]{1,0:T(8,128)S(1)}, u32[]{:S(2)}, u32[]{:S(2)}) collective-permute-start(f32[8,128]{1,0:T(8,128)S(1)} %get-tuple-element.74.refs_0_), channel_id=1, source_target_pairs={{0,3},{1,2},{2,1},{3,0},{4,7},{5,6},{6,5},{7,4},{8,11},{9,10},{10,... | collective-permute-start | bytes 12296 | tf_op jit(solution)/shard_map/ppermute | solution.py:533
  21.9 4.5 %collective-permute-start.8 = (f32[8,128]{1,0:T(8,128)S(1)}, f32[8,128]{1,0:T(8,128)S(1)}, u32[]{:S(2)}, u32[]{:S(2)}) collective-permute-start(f32[8,128]{1,0:T(8,128)S(1)} %get-tuple-element.74.refs_0_), channel_id=1, source_target_pairs={{0,2},{1,3},{2,0},{3,1},{4,6},{5,7},{6,4},{7,5},{8,10},{9,11},{10,... | collective-permute-start | bytes 12296 | tf_op jit(solution)/shard_map/ppermute | solution.py:533
  21.9 4.5 %collective-permute-start.7 = (f32[8,128]{1,0:T(8,128)S(1)}, f32[8,128]{1,0:T(8,128)S(1)}, u32[]{:S(2)}, u32[]{:S(2)}) collective-permute-start(f32[8,128]{1,0:T(8,128)S(1)} %get-tuple-element.74.refs_0_), channel_id=1, source_target_pairs={{0,1},{1,0},{2,3},{3,2},{4,5},{5,4},{6,7},{7,6},{8,9},{9,8},{10,11... | collective-permute-start | bytes 12296 | tf_op jit(solution)/shard_map/ppermute | solution.py:533
  26.5 7.5 %collective-permute-start.11 = (bf16[400,128]{1,0:T(8,128)(2,1)S(1)}, bf16[400,128]{1,0:T(8,128)(2,1)S(1)}, u32[]{:S(2)}, u32[]{:S(2)}) collective-permute-start(bf16[400,128]{1,0:T(8,128)(2,1)S(1)} %get-tuple-element.78), channel_id=1, source_target_pairs={{0,24},{4,28},{8,16},{12,20},{16,8},{20,12},{24,0},{28,4},{1,25},{... | collective-permute-start | bytes 307208 | tf_op jit(solution)/shard_map/ppermute | solution.py:533
  30.7 4.7 %collective-permute-start.12 = (bf16[400,128]{1,0:T(8,128)(2,1)S(1)}, bf16[400,128]{1,0:T(8,128)(2,1)S(1)}, u32[]{:S(2)}, u32[]{:S(2)}) collective-permute-start(bf16[400,128]{1,0:T(8,128)(2,1)S(1)} %get-tuple-element.79), channel_id=1, source_target_pairs={{0,16},{4,20},{8,24},{12,28},{16,0},{20,4},{24,8},{28,12},{1,17},{... | collective-permute-start | bytes 307208 | tf_op jit(solution)/shard_map/ppermute | solution.py:533
  31.3 4.7 %collective-permute-start.13 = (bf16[400,128]{1,0:T(8,128)(2,1)S(1)}, bf16[400,128]{1,0:T(8,128)(2,1)S(1)}, u32[]{:S(2)}, u32[]{:S(2)}) collective-permute-start(bf16[400,128]{1,0:T(8,128)(2,1)S(1)} %get-tuple-element.80), channel_id=1, source_target_pairs={{0,8},{4,12},{8,0},{12,4},{16,24},{20,28},{24,16},{28,20},{1,9},{5... | collective-permute-start | bytes 307208 | tf_op jit(solution)/shard_map/ppermute | solution.py:533
  35.9 1.2 %collective-permute-start.14 = (f32[8,128]{1,0:T(8,128)S(1)}, f32[8,128]{1,0:T(8,128)S(1)}, u32[]{:S(2)}, u32[]{:S(2)}) collective-permute-start(f32[8,128]{1,0:T(8,128)S(1)} %sum_chips.1.refs_0_), channel_id=1, source_target_pairs={{0,4},{4,0},{8,12},{12,8},{16,20},{20,16},{24,28},{28,24},{1,5},{5... | collective-permute-start | bytes 12296 | tf_op jit(solution)/shard_map/ppermute | solution.py:533

commit v9 on v7

--- a/solution.py
+++ b/solution.py
@@ -145,19 +145,36 @@
     )(live_counts, queries, out_grad, query_gain)
 
 
+def give_pieces(acc, me_ref, parts, keep_ref, send_ref, scale):
+    if parts == 1:
+        keep_ref[...] = acc[...] * scale
+        return
+    shard = acc.shape[0] // parts
+    for piece_no in range(parts):
+        rows = pl.ds(pl.multiple_of((me_ref[0] ^ piece_no) * shard, shard), shard)
+        place = slice(piece_no // 2 * shard, (piece_no // 2 + 1) * shard)
+        ref = keep_ref if piece_no % 2 == 0 else send_ref
+        ref[place, :] = (acc[rows, :] * scale).astype(ref.dtype)
+
+
+def piece_shapes(pool_rows, width, parts):
+    if parts == 1:
+        return [jax.ShapeDtypeStruct((pool_rows, width), F32)]
+    return [jax.ShapeDtypeStruct((pool_rows // 2, width), kind) for kind in (F32, BF16)]
+
+
 def attention_kernel(*refs, parts, heads):
     live_ref, prompt_ref, me_ref, queries_ref, grads_ref, ck_ref, cv_ref, kg_ref, mask_ref = refs[:9]
     pieces, refs = refs[9:9 + parts], refs[9 + parts:]
-    att_ref, ds_ref, pool_keys, own_keys, own_acc, term_ref, keep_ref = refs[:7]
-    send_ref, refs = (refs[7], refs[8:]) if parts > 1 else (None, refs[7:])
+    att_ref, ds_ref, weights, grads, pool_keys, own_keys, own_acc, term_ref, keep_ref = refs[:9]
+    send_ref, refs = (refs[9], refs[10:]) if parts > 1 else (None, refs[9:])
     acc, pool_values, pool_values_t, own_values_t = refs[:4]
     size = kg_ref.shape[1]
     width = heads * size
     slots, _, lanes = queries_ref.shape
     per_head = lanes // CHUNK
     count = heads * per_head
-    weights, grads = refs[4:4 + heads], refs[4 + heads:4 + 2 * heads]
-    scores, summed = refs[4 + 2 * heads:4 + 2 * heads + count], refs[4 + 2 * heads + count:]
+    scores, summed = refs[4:4 + count], refs[4 + count:]
     score_scale = 1.0 / math.sqrt(size)
     shard = pieces[0].shape[0]
 
@@ -198,7 +215,7 @@
         high = jnp.maximum(jnp.max(prompt, axis=0, keepdims=True), jnp.max(own, axis=0, keepdims=True))
         both = jnp.concatenate([prompt, own], axis=0)
         half = jnp.exp2((both - high) * factor).astype(BF16)
-        weights[head][:, span] = half
+        weights[slot, head, :, span] = half
         values_t = jnp.concatenate([pool_values_t[place, prompt_rows(slot)], own_values_t[slot, head]], axis=1)
         values_t = jnp.concatenate([values_t, jnp.ones((TAIL, PL + CL), BF16)], axis=0)
         summed[no][...] = dot(values_t, half)
@@ -209,19 +226,16 @@
         attended = (summed[no][:size, :] * inverse).astype(BF16)
         att_ref[slot, place, span] = attended
         scaled = (grads_ref[slot, place, span].astype(F32) * inverse).astype(BF16)
-        grads[head][:, span] = scaled
+        grads[slot, place, span] = scaled
         delta = jnp.sum(scaled.astype(F32) * attended.astype(F32), axis=0, keepdims=True)
         values = jnp.concatenate([pool_values[prompt_rows(slot), place], cv_ref[slot_rows(slot), place]], axis=0)
-        score_grad = weights[head][:, span].astype(F32) * (dot(values, scaled) - delta)
+        score_grad = weights[slot, head, :, span].astype(F32) * (dot(values, scaled) - delta)
         ds_ref[slot, head, :, span] = score_grad.astype(BF16)
 
     def close(slot, head):
-        value_grad = dot_nt(weights[head][...], grads[head][...])
         key_grad = dot_nt(ds_ref[slot, head], queries_ref[slot, columns(head), :])
         acc[prompt_rows(slot), columns(head)] += key_grad[:PL]
-        acc[prompt_rows(slot), width + head * size:width + (head + 1) * size] += value_grad[:PL]
-        own_acc[slot, head, 0] = key_grad[PL:]
-        own_acc[slot, head, 1] = value_grad[PL:]
+        own_acc[slot, head] = key_grad[PL:]
 
     def ticks(now, before):
         for tick in range(count):
@@ -247,20 +261,12 @@
 
     total = jnp.zeros((1, size), F32)
     for head in range(heads):
-        own_grad = own_acc[:, head, 0].reshape(slots * CL, size)
+        own_grad = own_acc[:, head].reshape(slots * CL, size)
         total = total + jnp.sum(own_grad * own_keys[:, columns(head)].astype(F32), axis=0, keepdims=True)
         pool_term = acc[:, columns(head)] * pool_keys[:, columns(head)].astype(F32)
         total = total + jnp.sum(pool_term, axis=0, keepdims=True)
     term_ref[...] = jnp.broadcast_to(total * score_scale, term_ref.shape)
-    if parts == 1:
-        keep_ref[:, :width] = acc[:, :width] * score_scale
-        keep_ref[:, width:] = acc[:, width:]
-    else:
-        for piece_no in range(parts):
-            place = slice(piece_no // 2 * shard, (piece_no // 2 + 1) * shard)
-            ref = keep_ref if piece_no % 2 == 0 else send_ref
-            ref[place, :width] = (acc[piece_rows(piece_no), :width] * score_scale).astype(ref.dtype)
-            ref[place, width:] = acc[piece_rows(piece_no), width:].astype(ref.dtype)
+    give_pieces(acc, me_ref, parts, keep_ref, send_ref, score_scale)
 
 
 def attention(live_counts, slot_prompts, me, queries, grads, keys, values, key_gain, mask, pieces):
@@ -271,32 +277,26 @@
     pool_rows = parts * pieces[0].shape[0]
     count = heads * lanes // CHUNK
     span = PL + CL
+    per_slot = jax.ShapeDtypeStruct((slots, heads, span, lanes), BF16)
+    turned = jax.ShapeDtypeStruct(queries.shape, BF16)
     out_shape = [
-        jax.ShapeDtypeStruct(queries.shape, BF16),
-        jax.ShapeDtypeStruct((slots, heads, span, lanes), BF16),
+        turned, per_slot, per_slot, turned,
         jax.ShapeDtypeStruct((pool_rows, width), BF16),
         jax.ShapeDtypeStruct(keys.shape, BF16),
-        jax.ShapeDtypeStruct((slots, heads, 2, CL, size), F32),
+        jax.ShapeDtypeStruct((slots, heads, CL, size), F32),
         jax.ShapeDtypeStruct((8, size), F32),
-    ]
-    if parts > 1:
-        half = (pool_rows // 2, 2 * width)
-        out_shape += [jax.ShapeDtypeStruct(half, F32), jax.ShapeDtypeStruct(half, BF16)]
-    else:
-        out_shape += [jax.ShapeDtypeStruct((pool_rows, 2 * width), F32)]
+    ] + piece_shapes(pool_rows, width, parts)
     return pl.pallas_call(
         functools.partial(attention_kernel, parts=parts, heads=heads),
         in_specs=[SMEM_SPEC] * 3 + [VMEM_SPEC] * (6 + parts),
         out_specs=[VMEM_SPEC] * len(out_shape),
         out_shape=out_shape,
         scratch_shapes=[
-            pltpu.VMEM((pool_rows, 2 * width), F32),
+            pltpu.VMEM((pool_rows, width), F32),
             pltpu.VMEM((pool_rows, width), BF16),
             pltpu.VMEM((width, pool_rows), BF16),
             pltpu.VMEM((slots, heads, size, CL), BF16),
         ]
-        + [pltpu.VMEM((span, lanes), BF16)] * heads
-        + [pltpu.VMEM((size, lanes), BF16)] * heads
         + [pltpu.VMEM((span, CHUNK), F32)] * count
         + [pltpu.VMEM((size + TAIL, CHUNK), F32)] * count,
         compiler_params=params(),
@@ -305,6 +305,43 @@
     )(live_counts, slot_prompts, me, queries, grads, keys, values, key_gain, mask, *pieces)
 
 
+def values_kernel(live_ref, prompt_ref, me_ref, weights, grads, own_acc, keep_ref, *refs, parts):
+    send_ref, acc = refs if parts > 1 else (None, refs[0])
+    slots, heads, _, _ = weights.shape
+    size = own_acc.shape[3]
+    acc[...] = jnp.zeros_like(acc)
+    own_acc[...] = jnp.zeros_like(own_acc)
+
+    def live(slot, carry):
+        rows = pl.ds(pl.multiple_of(prompt_ref[slot] * PL, PL), PL)
+        for head in range(heads):
+            columns = slice(head * size, (head + 1) * size)
+            value_grad = dot_nt(weights[slot, head], grads[slot, columns, :])
+            acc[rows, columns] += value_grad[:PL]
+            own_acc[slot, head] = value_grad[PL:]
+        return carry
+
+    lax.fori_loop(0, live_ref[0], live, 0)
+    give_pieces(acc, me_ref, parts, keep_ref, send_ref, 1.0)
+
+
+def value_grads(live_counts, slot_prompts, me, weights, grads, pool_rows, parts):
+    slots, heads, _, _ = weights.shape
+    width = grads.shape[1]
+    out_shape = [jax.ShapeDtypeStruct((slots, heads, CL, width // heads), F32)]
+    out_shape += piece_shapes(pool_rows, width, parts)
+    return pl.pallas_call(
+        functools.partial(values_kernel, parts=parts),
+        in_specs=[SMEM_SPEC] * 3 + [VMEM_SPEC] * 2,
+        out_specs=[VMEM_SPEC] * len(out_shape),
+        out_shape=out_shape,
+        scratch_shapes=[pltpu.VMEM((pool_rows, width), F32)],
+        compiler_params=params(),
+        cost_estimate=cost(2 * 10**9, 10**6),
+        name="values",
+    )(live_counts, slot_prompts, me, weights, grads)
+
+
 def copy_slots(live_ref, zeros, out, target, sems):
     slots = out.shape[0]
 
@@ -325,7 +362,7 @@
 
 
 def turn_kernel(
-    live_ref, att_t_ref, own_acc, ck_ref, kg_ref, att_ref, dk_ref, dv_ref, att_out, zeros, dk_out, dv_out, sems, own_sems,
+    live_ref, att_t_ref, own_keys, ck_ref, kg_ref, att_ref, dk_ref, att_out, zeros, dk_out, sems, own_sem,
 ):
     slots, width, _ = att_t_ref.shape
     size = kg_ref.shape[1]
@@ -344,42 +381,35 @@
     lax.fori_loop(0, live_ref[0], live, 0)
     for head in range(heads):
         columns = slice(head * size, (head + 1) * size)
-        own_grad = own_acc[:, head, 0].reshape(slots * CL, size) * (1.0 / math.sqrt(size))
+        own_grad = own_keys[:, head].reshape(slots * CL, size) * (1.0 / math.sqrt(size))
         own_unit, own_recip = unit(ck_ref[:, columns].astype(F32))
         dk_out[:, columns] = norm_back(own_grad, own_unit, own_recip, kg_ref[...]).astype(BF16)
-        dv_out[:, columns] = own_acc[:, head, 1].reshape(slots * CL, size).astype(BF16)
-    own_copies = [
-        pltpu.make_async_copy(dk_out, dk_ref, own_sems.at[0]),
-        pltpu.make_async_copy(dv_out, dv_ref, own_sems.at[1]),
-    ]
-    for copy in own_copies:
-        copy.start()
-    for copy in own_copies:
-        copy.wait()
+    own_copy = pltpu.make_async_copy(dk_out, dk_ref, own_sem)
+    own_copy.start()
+    own_copy.wait()
     wait()
 
 
-def turn(live_counts, att_t, own_acc, keys, key_gain, shape):
+def turn(live_counts, att_t, own_keys, keys, key_gain, shape):
     slots = att_t.shape[0]
-    own = jax.ShapeDtypeStruct(keys.shape, BF16)
-    own_slab = pltpu.VMEM(keys.shape, BF16)
     return pl.pallas_call(
         turn_kernel,
         in_specs=[SMEM_SPEC] + [VMEM_SPEC] * 4,
-        out_specs=[HBM_SPEC] * 3,
-        out_shape=[jax.ShapeDtypeStruct(shape, BF16), own, own],
+        out_specs=[HBM_SPEC] * 2,
+        out_shape=[jax.ShapeDtypeStruct(shape, BF16), jax.ShapeDtypeStruct(keys.shape, BF16)],
         scratch_shapes=[
-            pltpu.VMEM((slots, CL, shape[1]), BF16), pltpu.VMEM((CL, shape[1]), BF16), own_slab, own_slab,
-            pltpu.SemaphoreType.DMA((slots,)), pltpu.SemaphoreType.DMA((2,)),
+            pltpu.VMEM((slots, CL, shape[1]), BF16), pltpu.VMEM((CL, shape[1]), BF16), pltpu.VMEM(keys.shape, BF16),
+            pltpu.SemaphoreType.DMA((slots,)), pltpu.SemaphoreType.DMA,
         ],
         compiler_params=params(),
-        cost_estimate=cost(2 * 10**9, 2 * 10**6),
+        cost_estimate=cost(4 * 10**11, 2 * 10**6),
         name="turn",
-    )(live_counts, att_t, own_acc, keys, key_gain)
+    )(live_counts, att_t, own_keys, keys, key_gain)
 
 
 def post_kernel(
-    live_ref, prompt_ref, ds_ref, pool_keys, own_keys_ref, raw_ref, recip_ref, col_ref, dq_ref, dq_out, zeros, sems,
+    live_ref, prompt_ref, ds_ref, pool_keys, own_keys_ref, own_values, raw_ref, recip_ref, col_ref,
+    dq_ref, dv_ref, dq_out, zeros, dv_out, sems, own_sem,
 ):
     slots, width, lanes = raw_ref.shape
     size = col_ref.shape[0]
@@ -387,6 +417,10 @@
     group = dq_ref.shape[1] // width
     score_scale = 1.0 / math.sqrt(size)
     start, wait = copy_slots(live_ref, zeros, dq_out, dq_ref, sems)
+    for head in range(heads):
+        dv_out[:, head * size:(head + 1) * size] = own_values[:, head].reshape(slots * CL, size).astype(BF16)
+    own_copy = pltpu.make_async_copy(dv_out, dv_ref, own_sem)
+    own_copy.start()
 
     def live(slot, carry):
         rows = pl.ds(pl.multiple_of(prompt_ref[slot] * PL, PL), PL)
@@ -405,24 +439,25 @@
         return carry
 
     lax.fori_loop(0, live_ref[0], live, 0)
+    own_copy.wait()
     wait()
 
 
-def post(live_counts, slot_prompts, score_grads, pool_keys, own_keys, raw, recip, query_col, shape):
+def post(live_counts, slot_prompts, score_grads, pool_keys, own_keys, own_values, raw, recip, query_col, shape):
     slots = raw.shape[0]
     return pl.pallas_call(
         post_kernel,
-        in_specs=[SMEM_SPEC] * 2 + [VMEM_SPEC] * 6,
-        out_specs=HBM_SPEC,
-        out_shape=jax.ShapeDtypeStruct(shape, BF16),
+        in_specs=[SMEM_SPEC] * 2 + [VMEM_SPEC] * 7,
+        out_specs=[HBM_SPEC] * 2,
+        out_shape=[jax.ShapeDtypeStruct(shape, BF16), jax.ShapeDtypeStruct(own_keys.shape, BF16)],
         scratch_shapes=[
-            pltpu.VMEM((slots, CL, shape[1]), BF16), pltpu.VMEM((CL, shape[1]), BF16),
-            pltpu.SemaphoreType.DMA((slots,)),
+            pltpu.VMEM((slots, CL, shape[1]), BF16), pltpu.VMEM((CL, shape[1]), BF16), pltpu.VMEM(own_keys.shape, BF16),
+            pltpu.SemaphoreType.DMA((slots,)), pltpu.SemaphoreType.DMA,
         ],
         compiler_params=params(),
         cost_estimate=cost(3 * 10**9, 4 * 10**6),
         name="post",
-    )(live_counts, slot_prompts, score_grads, pool_keys, own_keys, raw, recip, query_col)
+    )(live_counts, slot_prompts, score_grads, pool_keys, own_keys, own_values, raw, recip, query_col)
 
 
 def tree(terms):
@@ -431,32 +466,37 @@
     return terms[0]
 
 
-def add_kernel(keep_ref, came_ref, *refs, terms):
+def add_kernel(*refs, terms):
+    halves, refs = (refs[:2], refs[2:4]), refs[4:]
     tail = gain_rows(tree([ref[0:1, :] for ref in refs[:terms]]))
     size = tail.shape[1]
     own_ref, send_refs = refs[terms], refs[terms + 1:]
     blocks = len(send_refs) + 1
-    shard = keep_ref.shape[0] // blocks
+    rows, width = halves[0][0].shape
+    shard = rows // blocks
+    heads = width // size
     for at in range(blocks):
         place = slice(at * shard, (at + 1) * shard)
         ref = send_refs[blocks - 1 - at] if at > 0 else own_ref
-        total = keep_ref[place, :] + came_ref[place, :].astype(F32)
-        for slab in range(keep_ref.shape[1] // size):
-            ref[slab * shard:(slab + 1) * shard, :] = total[:, slab * size:(slab + 1) * size].astype(ref.dtype)
-        ref[ref.shape[0] - TAIL:, :] = tail.astype(ref.dtype)
-
-
-def add(keep, came, terms, blocks):
+        for slab in range(2 * heads):
+            keep_ref, came_ref = halves[slab // heads]
+            columns = slice(slab % heads * size, (slab % heads + 1) * size)
+            total = keep_ref[place, columns] + came_ref[place, columns].astype(F32)
+            ref[slab * shard:(slab + 1) * shard, :] = total.astype(ref.dtype)
+        ref[2 * heads * shard:, :] = tail.astype(ref.dtype)
+
+
+def add(keys, values, terms, blocks):
     size = terms[0].shape[1]
-    shape = (keep.size // blocks // size + TAIL, size)
+    shape = (2 * keys[0].size // blocks // size + TAIL, size)
     return pl.pallas_call(
         functools.partial(add_kernel, terms=len(terms)),
-        in_specs=[VMEM_SPEC] * (2 + len(terms)),
+        in_specs=[VMEM_SPEC] * (4 + len(terms)),
         out_specs=[VMEM_SPEC] * blocks,
         out_shape=[jax.ShapeDtypeStruct(shape, F32)] + [jax.ShapeDtypeStruct(shape, BF16)] * (blocks - 1),
         compiler_params=params(),
         name="add",
-    )(keep, came, *terms)
+    )(*keys, *values, *terms)
 
 
 def chips_kernel(*refs):
@@ -546,38 +586,47 @@
     raw, recip, queries, grads, query_col = prepare(live_counts, comp_queries, out_grad, query_gain, slots, width)
     if by_permute:
         even = [mine] + [swap(mine, "grp", step) for step in range(2, grp, 2)]
-        odd = [swap(mine, "grp", 1)]
-        for at in range(1, len(even)):
-            even[at], query_col = lax.optimization_barrier((even[at], query_col))
-            odd.append(swap(even[at], "grp", 1))
+        odd = [swap(mine, "grp", 1)] + [None] * (len(even) - 1)
+        for at in range(len(even) - 1, 0, -1):
+            if at == 1:
+                even[at], query_col, odd[-1] = lax.optimization_barrier((even[at], query_col, odd[-1]))
+            else:
+                even[at], query_col = lax.optimization_barrier((even[at], query_col))
+            odd[at] = swap(even[at], "grp", 1)
         pieces = [piece for pair in zip(even, odd) for piece in pair]
     else:
         pieces = [lax.all_gather(mine, "grp", axis=0, tiled=True)]
-    att_t, score_grads, pool_keys, own_keys, own_acc, term, keep, *send = attention(
+    att_t, score_grads, weights, grads, pool_keys, own_keys, own_key_acc, term, *key_pieces = attention(
         live_counts, slot_prompts, me, queries, grads, comp_keys, comp_values, key_gain, mask, pieces,
     )
-    attended, key_grads, value_grads = turn(live_counts, att_t, own_acc, comp_keys, key_gain, comp_queries.shape)
-    query_grads = post(
-        live_counts, slot_prompts, score_grads, pool_keys, own_keys, raw, recip, query_col, comp_queries.shape,
+    if by_permute:
+        terms = [term] + [swap(term, "tp", step) for step in range(1, tp)]
+    own_value_acc, *value_pieces = value_grads(
+        live_counts, slot_prompts, me, weights, grads, pool_keys.shape[0], len(pieces),
+    )
+    attended, comp_key_grads = turn(live_counts, att_t, own_key_acc, comp_keys, key_gain, comp_queries.shape)
+    query_grads, comp_value_grads = post(
+        live_counts, slot_prompts, score_grads, pool_keys, own_keys, own_value_acc, raw, recip, query_col,
+        comp_queries.shape,
     )
     if by_permute:
-        came = swap(send[0], "grp", 1)
-        terms = [term] + [swap(term, "tp", step) for step in range(1, tp)]
+        key_pieces, value_pieces = ((keep, swap(send, "grp", 1)) for keep, send in (key_pieces, value_pieces))
         terms, attended = lax.optimization_barrier((terms, attended))
-        own, *blocks = add(keep, came, terms, grp // 2)
+        own, *blocks = add(key_pieces, value_pieces, terms, grp // 2)
         blocks = [swap(block, "grp", grp - 2 - 2 * at) for at, block in enumerate(blocks)]
         blocks, query_grads = lax.optimization_barrier((blocks, query_grads))
         blocks = [own] + blocks
         total = sum_chips(blocks)
         terms = [total, swap(total, "grp", 1)]
     else:
-        block = lax.psum_scatter(keep, "grp", scatter_dimension=0, tiled=True)
+        pool_grads = jnp.concatenate(key_pieces + value_pieces, axis=1)
+        block = lax.psum_scatter(pool_grads, "grp", scatter_dimension=0, tiled=True)
         blocks = [jnp.concatenate([block[:, at:at + size] for at in range(0, 2 * width, size)], axis=0)]
         terms = [lax.psum(term, ("grp", "tp"))]
     prompt_key_grads, prompt_value_grads = finish(blocks, prompt_keys, key_gain)
     query_gain_grad, key_gain_grad = gain_grads(terms, query_gain, key_gain)
     return (
-        attended, query_grads, key_grads, value_grads, prompt_key_grads, prompt_value_grads,
+        attended, query_grads, comp_key_grads, comp_value_grads, prompt_key_grads, prompt_value_grads,
         query_gain_grad.reshape(size), key_gain_grad.reshape(size),
     )
 

time: 38.1 us -> 39.3 us (1.031); the launches traced: 37.8 us -> 38.6 us
  Pallas kernels: 12.4 us -> 18.5 us
  waiting for transfers between devices: 8.21 us -> 4.51 us
  starting transfers between devices: 14.9 us -> 13.3 us
    ppermute x15 -> x16, waiting for transfers between devices: 8.21 us -> 4.51 us  [swap(): lax.ppermute(values, axis, [(i, i ^ step) for i in range(lax.axis_size(ax...]
    pallas_call x1 -> x2, Pallas kernels: 2.7 us -> 6.13 us  [the longest x1 3.2 us: post(): pl.pallas_call(post_kernel, in_specs=[SMEM_SPEC] * 2 + [VMEM_SPEC] * 7, o...]
    ppermute x15 -> x16, starting transfers between devices: 14.9 us -> 13.3 us  [swap(): lax.ppermute(values, axis, [(i, i ^ step) for i in range(lax.axis_size(ax...]
    pallas_call x1, Pallas kernels: 5.95 us -> 7.23 us  [attention(): pl.pallas_call(functools.partial(attention_kernel, parts=parts, heads=hea...]
    pallas_call x1, Pallas kernels: 0.09 us -> 1.11 us  [add(): pl.pallas_call(functools.partial(add_kernel, terms=len(terms)), in_specs=...]
    unnamed x18 -> x20, local copies, waits for them, and re-layouts: 0.82 us -> 0.83 us
  transfers between devices with their start and end apart: 15 -> 16, of which waited for: 9 -> 8; matrix products, arithmetic and copies ran while one was open for 0% -> 0% of each run, Pallas kernels for 15% -> 25%
where the time goes in v9:
time: 39.3 us; the launch traced here: 38.6 us
  Pallas kernels  18.5 us (47%)
  starting transfers between devices  13.3 us (34%)
  waiting for transfers between devices  4.51 us (11%)
  between operations  1.49 us (4%)
  local copies, waits for them, and re-layouts  0.83 us (2%)
    ppermute x16, starting transfers between devices, swap(): lax.ppermute(values, axis, [(i, i ^ step) for i in range(lax.axis_size(ax...  13.3 us
    pallas_call x1, Pallas kernels, attention(): pl.pallas_call(functools.partial(attention_kernel, parts=parts, heads=hea...  7.23 us
    ppermute x16, waiting for transfers between devices, swap(): lax.ppermute(values, axis, [(i, i ^ step) for i in range(lax.axis_size(ax...  4.51 us
    pallas_call x1, Pallas kernels, post(): pl.pallas_call(post_kernel, in_specs=[SMEM_SPEC] * 2 + [VMEM_SPEC] * 7, o...  3.2 us
    pallas_call x1, Pallas kernels, value_grads(): pl.pallas_call(functools.partial(values_kernel, parts=parts), in_specs=[S...  2.93 us
    pallas_call x1, Pallas kernels, turn(): pl.pallas_call(turn_kernel, in_specs=[SMEM_SPEC] + [VMEM_SPEC] * 4, out_s...  1.45 us
    pallas_call x1, Pallas kernels, add(): pl.pallas_call(functools.partial(add_kernel, terms=len(terms)), in_specs=...  1.11 us
    pallas_call x1, Pallas kernels, prepare(): pl.pallas_call(prepare_kernel, in_specs=[SMEM_SPEC] + [VMEM_SPEC] * 3, ou...  1.05 us
  transfers between devices with their start and end apart: 16, of which 8 were waited for; matrix products, arithmetic and copies ran while one was open for 0% of the time, Pallas kernels for 25%

profile of v9, /device:TPU:0, one launch (start us, length us, event | category | flops | bytes accessed | tf_op | source)
XLA Modules:
  0.0 38.6 jit_solution(8648005243803130962)
XLA Ops:
  0.6 0.0 copy-start
  0.6 0.0 copy-start.1
  0.7 0.0 copy-start.8
  0.7 0.7 %copy-done = bf16[96,256]{1,0:T(8,128)(2,1)S(1)} copy-done((bf16[96,256]{1,0:T(8,128)(2,1)S(1)}, bf16[96,256]{1,0:T(8,128)(2,1)}, u32[]{:S(2)}) %copy-start) | copy-done | bytes 49176
  1.4 0.0 copy-done.1
  1.4 0.0 copy-done.8
  1.5 0.0 copy-start.2
  1.5 0.0 copy-start.4
  1.5 0.0 copy-start.5
  1.5 0.1 pack.1.refs_9_
  1.6 4.0 %collective-permute-start.3 = (bf16[96,512]{1,0:T(8,128)(2,1)S(1)}, bf16[96,512]{1,0:T(8,128)(2,1)S(1)}, u32[]{:S(2)}, u32[]{:S(2)}) collective-permute-start(bf16[96,512]{1,0:T(8,128)(2,1)S(1)} %pack.1.refs_9_), channel_id=1, source_target_pairs={{0,24},{4,28},{8,16},{12,20},{16,8},{20,12},{24,0},{28,4},{1,25},{... | collective-permute-start | bytes 294920 | tf_op jit(solution)/shard_map/ppermute | solution.py:570
  5.6 0.5 %collective-permute-start.2 = (bf16[96,512]{1,0:T(8,128)(2,1)S(1)}, bf16[96,512]{1,0:T(8,128)(2,1)S(1)}, u32[]{:S(2)}, u32[]{:S(2)}) collective-permute-start(bf16[96,512]{1,0:T(8,128)(2,1)S(1)} %pack.1.refs_9_), channel_id=1, source_target_pairs={{0,16},{4,20},{8,24},{12,28},{16,0},{20,4},{24,8},{28,12},{1,17},{... | collective-permute-start | bytes 294920 | tf_op jit(solution)/shard_map/ppermute | solution.py:570
  6.1 0.1 collective-permute-start.1
  6.9 0.0 copy-done.2
  6.9 0.0 copy-done.4
  6.9 0.0 copy-done.5
  6.9 0.0 copy-start.6
  6.9 0.0 copy-start.7
  6.9 0.0 copy-start.9
  6.9 1.1 %prepare.1 = (bf16[4,256,512]{2,1,0:T(8,128)(2,1)S(1)}, f32[4,8,512]{2,1,0:T(8,128)S(1)}, bf16[4,256,512]{2,1,0:T(8,128)(2,1)S(1)}, bf16[4,256,512]{2,1,0:T(8,128)(2,1)S(1)}, f32[128,512]{1,0:T(8,128)S(1)}) custom-call(s32[1]{0:T(128)S(6)} %copy.18.live_ref.refs_0_, bf16[256,2048]{1,0:T(8,128)(2,1)S(1)} %copy-done.4, bf16[256,2048]{1,0:T(8,128)(2,1)S(1)} %copy-done.5, ...), custom_call_target="tpu_custom_call" | custom-call | flops 2000000000 | bytes 3145728 | tf_op jit(solution)/shard_map/prepare/pallas_call | solution.py:134
  8.0 0.8 %collective-permute-done.3.refs_15_ = bf16[96,512]{1,0:T(8,128)(2,1)S(1)} collective-permute-done((bf16[96,512]{1,0:T(8,128)(2,1)S(1)}, bf16[96,512]{1,0:T(8,128)(2,1)S(1)}, u32[]{:S(2)}, u32[]{:S(2)}) %collective-permute-start.3) | collective-permute-done | bytes 98336 | tf_op jit(solution)/shard_map/ppermute | solution.py:570
  8.7 0.0 collective-permute-start.4
  8.8 0.5 %collective-permute-start = (bf16[96,512]{1,0:T(8,128)(2,1)S(1)}, bf16[96,512]{1,0:T(8,128)(2,1)S(1)}, u32[]{:S(2)}, u32[]{:S(2)}) collective-permute-start(bf16[96,512]{1,0:T(8,128)(2,1)S(1)} %pack.1.refs_9_), channel_id=1, source_target_pairs={{0,4},{4,0},{8,12},{12,8},{16,20},{20,16},{24,28},{28,24},{1,5},{5... | collective-permute-start | bytes 294920 | tf_op jit(solution)/shard_map/ppermute | solution.py:570
  9.3 1.2 %collective-permute-done.2.refs_13_ = bf16[96,512]{1,0:T(8,128)(2,1)S(1)} collective-permute-done((bf16[96,512]{1,0:T(8,128)(2,1)S(1)}, bf16[96,512]{1,0:T(8,128)(2,1)S(1)}, u32[]{:S(2)}, u32[]{:S(2)}) %collective-permute-start.2) | collective-permute-done | bytes 98336 | tf_op jit(solution)/shard_map/ppermute | solution.py:570
  10.5 0.0 collective-permute-start.6
  10.5 0.3 collective-permute-done.1.refs_11_
  10.8 0.0 collective-permute-done.4.refs_16_
  10.8 0.2 collective-permute-start.5
  11.0 0.0 collective-permute-done.refs_10_
  11.0 0.8 %collective-permute-done.6.refs_14_ = bf16[96,512]{1,0:T(8,128)(2,1)S(1)} collective-permute-done((bf16[96,512]{1,0:T(8,128)(2,1)S(1)}, bf16[96,512]{1,0:T(8,128)(2,1)S(1)}, u32[]{:S(2)}, u32[]{:S(2)}) %collective-permute-start.6) | collective-permute-done | bytes 98336 | tf_op jit(solution)/shard_map/ppermute | solution.py:570
  11.8 0.3 collective-permute-done.5.refs_12_
  12.1 0.0 copy-done.6
  12.1 0.0 copy-done.7
  12.1 0.0 copy-done.9
  12.1 7.2 %attention.1 = (bf16[4,256,512]{2,1,0:T(8,128)(2,1)S(1)}, bf16[4,2,448,512]{3,2,1,0:T(8,128)(2,1)S(1)}, bf16[4,2,448,512]{3,2,1,0:T(8,128)(2,1)S(1)}, bf16[4,256...) custom-call(s32[1]{0:T(128)S(6)} %copy.18.live_ref.refs_0_, ...), custom_call_target="tpu_custom_call" | custom-call | flops 3000000000 | bytes 10000000 | tf_op jit(solution)/shard_map/attention/pallas_call | solution.py:289
  19.3 3.7 %collective-permute-start.9 = (f32[8,128]{1,0:T(8,128)}, f32[8,128]{1,0:T(8,128)}, u32[]{:S(2)}, u32[]{:S(2)}) collective-permute-start(f32[8,128]{1,0:T(8,128)} %get-tuple-element.82.refs_4_), channel_id=1, source_target_pairs={{0,3},{1,2},{2,1},{3,0},{4,7},{5,6},{6,5},{7,4},{8,11},{9,10},{10,... | collective-permute-start | bytes 12296 | tf_op jit(solution)/shard_map/ppermute | solution.py:570
  23.0 0.0 collective-permute-start.8
  23.0 0.7 %collective-permute-start.7 = (f32[8,128]{1,0:T(8,128)}, f32[8,128]{1,0:T(8,128)}, u32[]{:S(2)}, u32[]{:S(2)}) collective-permute-start(f32[8,128]{1,0:T(8,128)} %get-tuple-element.82.refs_4_), channel_id=1, source_target_pairs={{0,1},{1,0},{2,3},{3,2},{4,5},{5,4},{6,7},{7,6},{8,9},{9,8},{10,11... | collective-permute-start | bytes 12296 | tf_op jit(solution)/shard_map/ppermute | solution.py:570
  23.7 0.0 collective-permute-start.10
  23.7 2.9 %values.1 = (f32[4,2,64,128]{3,2,1,0:T(8,128)S(1)}, f32[384,256]{1,0:T(8,128)S(1)}, bf16[384,256]{1,0:T(8,128)(2,1)}) custom-call(s32[1]{0:T(128)S(6)} %copy.18.live_ref.refs_0_, s32[4]{0:T(128)S(1)} %copy-done.9, s32[1]{0:T(128)} %bitcast.refs_2_.me_ref, bf16[4,2,448,512]{3,2,1,0:T(8,128)(2,1)S(1)} %get-tuple-element.78.weights, ...), custom_call_target="tpu_custom_call" | custom-call | flops 2000000000 | bytes 1000000 | tf_op jit(solution)/shard_map/values/pallas_call | solution.py:333
  26.7 0.0 collective-permute-start.11
  26.7 1.5 %turn.1 = (bf16[256,2048]{1,0:T(8,128)(2,1)}, bf16[256,256]{1,0:T(8,128)(2,1)}) custom-call(s32[1]{0:T(128)S(6)} %copy.18.live_ref.refs_0_, bf16[4,256,512]{2,1,0:T(8,128)(2,1)S(1)} %get-tuple-element.72.att_t_ref, f32[4,2,64,128]{3,2,1,0:T(8,128)S(1)} %get-tuple-element.73.own_keys, bf16[256,256]{1,0:T(8,128)(2,1)S(1)} %copy-done.7, f32[1,128]{1,0:T(1,128)S(1)} %bitcast.7), custom_call_target="tpu_custom_call" | custom-call | flops 399999991808 | bytes 2000000 | tf_op jit(solution)/shard_map/turn/pallas_call | solution.py:395
  28.1 0.0 collective-permute-done.9.refs_7_
  28.1 0.0 collective-permute-done.8.refs_6_
  28.1 0.0 collective-permute-done.7.refs_5_
  28.2 0.0 collective-permute-done.10.refs_1_
  28.2 0.3 collective-permute-done.11.refs_3_
  28.5 1.1 %add.1 = (f32[400,128]{1,0:T(8,128)S(1)}, bf16[400,128]{1,0:T(8,128)(2,1)S(1)}, bf16[400,128]{1,0:T(8,128)(2,1)S(1)}, bf16[400,128]{1,0:T(8,128)(2,1)S(1)}) custom-call(f32[384,256]{1,0:T(8,128)S(1)} %get-tuple-element.76.refs_0_, bf16[384,256]{1,0:T(8,128)(2,1)} %collective-permute-done.10.refs_1_, f32[384,256]{1,0:T(8,128)S(1)} %get-tuple-element.80.refs_2_, ...), custom_call_target="tpu_custom_call" | custom-call | tf_op jit(solution)/shard_map/add/pallas_call | solution.py:492
  29.6 0.1 collective-permute-start.12
  29.6 1.2 %collective-permute-start.13 = (bf16[400,128]{1,0:T(8,128)(2,1)S(1)}, bf16[400,128]{1,0:T(8,128)(2,1)S(1)}, u32[]{:S(2)}, u32[]{:S(2)}) collective-permute-start(bf16[400,128]{1,0:T(8,128)(2,1)S(1)} %get-tuple-element.87), channel_id=1, source_target_pairs={{0,16},{4,20},{8,24},{12,28},{16,0},{20,4},{24,8},{28,12},{1,17},{... | collective-permute-start | bytes 307208 | tf_op jit(solution)/shard_map/ppermute | solution.py:570
  30.8 2.3 %collective-permute-start.14 = (bf16[400,128]{1,0:T(8,128)(2,1)S(1)}, bf16[400,128]{1,0:T(8,128)(2,1)S(1)}, u32[]{:S(2)}, u32[]{:S(2)}) collective-permute-start(bf16[400,128]{1,0:T(8,128)(2,1)S(1)} %get-tuple-element.88), channel_id=1, source_target_pairs={{0,8},{4,12},{8,0},{12,4},{16,24},{20,28},{24,16},{28,20},{1,9},{5... | collective-permute-start | bytes 307208 | tf_op jit(solution)/shard_map/ppermute | solution.py:570
  33.1 0.0 copy-start.3
  33.1 3.2 %post.1 = (bf16[256,2048]{1,0:T(8,128)(2,1)}, bf16[256,256]{1,0:T(8,128)(2,1)}) custom-call(s32[1]{0:T(128)S(6)} %copy.18.live_ref.refs_0_, s32[4]{0:T(128)S(1)} %copy-done.9, bf16[4,2,448,512]{3,2,1,0:T(8,128)(2,1)S(1)} %get-tuple-element.89.ds_ref, bf16[768,256]{1,0:T(8,128)(2,1)S(1)} %get-tuple-element.90.pool_keys, ...), custom_call_target="tpu_custom_call" | custom-call | flops 3000000000 | bytes 4000000 | tf_op jit(solution)/shard_map/post/pallas_call | solution.py:448
  36.3 0.0 collective-permute-done.12.refs_1_
  36.3 0.5 %collective-permute-done.13.refs_2_ = bf16[400,128]{1,0:T(8,128)(2,1)S(1)} collective-permute-done((bf16[400,128]{1,0:T(8,128)(2,1)S(1)}, bf16[400,128]{1,0:T(8,128)(2,1)S(1)}, u32[]{:S(2)}, u32[]{:S(2)}) %collective-permute-start.13) | collective-permute-done | bytes 102432 | tf_op jit(solution)/shard_map/ppermute | solution.py:570
  36.8 0.0 collective-permute-done.14.refs_3_
  36.8 0.1 collective-permute-start.15
  36.9 0.8 %finish.1 = (f32[96,256]{1,0:T(8,128)}, f32[96,256]{1,0:T(8,128)}) custom-call(f32[400,128]{1,0:T(8,128)S(1)} %get-tuple-element.100.refs_0_, bf16[400,128]{1,0:T(8,128)(2,1)S(1)} %collective-permute-done.12.refs_1_, bf16[400,128]{1,0:T(8,128)(2,1)S(1)} %collective-permute-done.13.refs_2_, bf16[400,128]{1,0:T(8,128)(2,1)S(1)} %collective-permute-done.14.refs_3_, ...), custom_call_target="tpu_custom_call" | custom-call | flops 100000000 | bytes 1000000 | tf_op jit(solution)/shard_map/finish/pallas_call | solution.py:558
  37.8 0.3 collective-permute-done.15.refs_1_
  38.1 0.0 copy-done.3
  38.1 0.5 %gain_grads.1 = (f32[1,128]{1,0:T(1,128)}, f32[1,128]{1,0:T(1,128)}) custom-call(f32[8,128]{1,0:T(8,128)S(1)} %sum_chips.1.refs_0_, f32[8,128]{1,0:T(8,128)S(1)} %collective-permute-done.15.refs_1_, f32[1,128]{1,0:T(1,128)S(1)} %bitcast.11, f32[1,128]{1,0:T(1,128)S(1)} %bitcast.9), custom_call_target="tpu_custom_call" | custom-call | tf_op jit(solution)/shard_map/gain_grads/pallas_call | solution.py:528
  (2 shorter events, 0.0 us)
Async XLA Ops:
  0.6 0.8 %copy-start = (bf16[96,256]{1,0:T(8,128)(2,1)S(1)}, bf16[96,256]{1,0:T(8,128)(2,1)}, u32[]{:S(2)}) copy-start(bf16[96,256]{1,0:T(8,128)(2,1)} %refs_4_.1) | copy-start | bytes 147460
  0.6 0.8 %copy-start.1 = (f32[128]{0:T(128)S(1)}, f32[128]{0:T(128)}, u32[]{:S(2)}) copy-start(f32[128]{0:T(128)} %param.16) | copy-start | bytes 1540
  0.7 0.8 %copy-start.8 = (bf16[96,256]{1,0:T(8,128)(2,1)S(1)}, bf16[96,256]{1,0:T(8,128)(2,1)}, u32[]{:S(2)}) copy-start(bf16[96,256]{1,0:T(8,128)(2,1)} %values_ref) | copy-start | bytes 147460
  1.5 5.4 %copy-start.2 = (f32[128]{0:T(128)S(1)}, f32[128]{0:T(128)}, u32[]{:S(2)}) copy-start(f32[128]{0:T(128)} %param.15) | copy-start | bytes 1540
  1.5 5.4 %copy-start.4 = (bf16[256,2048]{1,0:T(8,128)(2,1)S(1)}, bf16[256,2048]{1,0:T(8,128)(2,1)}, u32[]{:S(2)}) copy-start(bf16[256,2048]{1,0:T(8,128)(2,1)} %q_ref.1) | copy-start | bytes 3145732
  1.5 5.4 %copy-start.5 = (bf16[256,2048]{1,0:T(8,128)(2,1)S(1)}, bf16[256,2048]{1,0:T(8,128)(2,1)}, u32[]{:S(2)}) copy-start(bf16[256,2048]{1,0:T(8,128)(2,1)} %do_ref.1) | copy-start | bytes 3145732
  1.6 7.1 %collective-permute-start.3 = (bf16[96,512]{1,0:T(8,128)(2,1)S(1)}, bf16[96,512]{1,0:T(8,128)(2,1)S(1)}, u32[]{:S(2)}, u32[]{:S(2)}) collective-permute-start(bf16[96,512]{1,0:T(8,128)(2,1)S(1)} %pack.1.refs_9_), channel_id=1, source_target_pairs={{0,24},{4,28},{8,16},{12,20},{16,8},{20,12},{24,0},{28,4},{1,25},{... | collective-permute-start | bytes 294920 | tf_op jit(solution)/shard_map/ppermute | solution.py:570
  5.6 4.9 %collective-permute-start.2 = (bf16[96,512]{1,0:T(8,128)(2,1)S(1)}, bf16[96,512]{1,0:T(8,128)(2,1)S(1)}, u32[]{:S(2)}, u32[]{:S(2)}) collective-permute-start(bf16[96,512]{1,0:T(8,128)(2,1)S(1)} %pack.1.refs_9_), channel_id=1, source_target_pairs={{0,16},{4,20},{8,24},{12,28},{16,0},{20,4},{24,8},{28,12},{1,17},{... | collective-permute-start | bytes 294920 | tf_op jit(solution)/shard_map/ppermute | solution.py:570
  6.1 4.7 %collective-permute-start.1 = (bf16[96,512]{1,0:T(8,128)(2,1)S(1)}, bf16[96,512]{1,0:T(8,128)(2,1)S(1)}, u32[]{:S(2)}, u32[]{:S(2)}) collective-permute-start(bf16[96,512]{1,0:T(8,128)(2,1)S(1)} %pack.1.refs_9_), channel_id=1, source_target_pairs={{0,8},{4,12},{8,0},{12,4},{16,24},{20,28},{24,16},{28,20},{1,9},{5... | collective-permute-start | bytes 294920 | tf_op jit(solution)/shard_map/ppermute | solution.py:570
  6.9 5.2 %copy-start.6 = (bf16[256,256]{1,0:T(8,128)(2,1)S(1)}, bf16[256,256]{1,0:T(8,128)(2,1)}, u32[]{:S(2)}) copy-start(bf16[256,256]{1,0:T(8,128)(2,1)} %refs_6_.1) | copy-start | bytes 393220
  6.9 5.2 %copy-start.7 = (bf16[256,256]{1,0:T(8,128)(2,1)S(1)}, bf16[256,256]{1,0:T(8,128)(2,1)}, u32[]{:S(2)}) copy-start(bf16[256,256]{1,0:T(8,128)(2,1)} %ck_ref.1) | copy-start | bytes 393220
  6.9 5.2 %copy-start.9 = (s32[4]{0:T(128)S(1)}, s32[4]{0:T(128)}, u32[]{:S(2)}) copy-start(s32[4]{0:T(128)} %prompt_ref.3) | copy-start | bytes 52
  8.7 2.0 %collective-permute-start.4 = (bf16[96,512]{1,0:T(8,128)(2,1)S(1)}, bf16[96,512]{1,0:T(8,128)(2,1)S(1)}, u32[]{:S(2)}, u32[]{:S(2)}) collective-permute-start(bf16[96,512]{1,0:T(8,128)(2,1)S(1)} %collective-permute-done.3.refs_15_), channel_id=1, source_target_pairs={{0,4},{4,0},{8,12},{12,8},{16,20},{20,16},{24,28},{28,24},{1,5},{5... | collective-permute-start | bytes 294920 | tf_op jit(solution)/shard_map/ppermute | solution.py:570
  8.8 2.2 %collective-permute-start = (bf16[96,512]{1,0:T(8,128)(2,1)S(1)}, bf16[96,512]{1,0:T(8,128)(2,1)S(1)}, u32[]{:S(2)}, u32[]{:S(2)}) collective-permute-start(bf16[96,512]{1,0:T(8,128)(2,1)S(1)} %pack.1.refs_9_), channel_id=1, source_target_pairs={{0,4},{4,0},{8,12},{12,8},{16,20},{20,16},{24,28},{28,24},{1,5},{5... | collective-permute-start | bytes 294920 | tf_op jit(solution)/shard_map/ppermute | solution.py:570
  10.5 1.3 %collective-permute-start.6 = (bf16[96,512]{1,0:T(8,128)(2,1)S(1)}, bf16[96,512]{1,0:T(8,128)(2,1)S(1)}, u32[]{:S(2)}, u32[]{:S(2)}) collective-permute-start(bf16[96,512]{1,0:T(8,128)(2,1)S(1)} %collective-permute-done.2.refs_13_), channel_id=1, source_target_pairs={{0,4},{4,0},{8,12},{12,8},{16,20},{20,16},{24,28},{28,24},{1,5},{5... | collective-permute-start | bytes 294920 | tf_op jit(solution)/shard_map/ppermute | solution.py:570
  10.8 1.3 %collective-permute-start.5 = (bf16[96,512]{1,0:T(8,128)(2,1)S(1)}, bf16[96,512]{1,0:T(8,128)(2,1)S(1)}, u32[]{:S(2)}, u32[]{:S(2)}) collective-permute-start(bf16[96,512]{1,0:T(8,128)(2,1)S(1)} %collective-permute-done.1.refs_11_), channel_id=1, source_target_pairs={{0,4},{4,0},{8,12},{12,8},{16,20},{20,16},{24,28},{28,24},{1,5},{5... | collective-permute-start | bytes 294920 | tf_op jit(solution)/shard_map/ppermute | solution.py:570
  19.3 8.8 %collective-permute-start.9 = (f32[8,128]{1,0:T(8,128)}, f32[8,128]{1,0:T(8,128)}, u32[]{:S(2)}, u32[]{:S(2)}) collective-permute-start(f32[8,128]{1,0:T(8,128)} %get-tuple-element.82.refs_4_), channel_id=1, source_target_pairs={{0,3},{1,2},{2,1},{3,0},{4,7},{5,6},{6,5},{7,4},{8,11},{9,10},{10,... | collective-permute-start | bytes 12296 | tf_op jit(solution)/shard_map/ppermute | solution.py:570
  23.0 5.1 %collective-permute-start.8 = (f32[8,128]{1,0:T(8,128)}, f32[8,128]{1,0:T(8,128)}, u32[]{:S(2)}, u32[]{:S(2)}) collective-permute-start(f32[8,128]{1,0:T(8,128)} %get-tuple-element.82.refs_4_), channel_id=1, source_target_pairs={{0,2},{1,3},{2,0},{3,1},{4,6},{5,7},{6,4},{7,5},{8,10},{9,11},{10,... | collective-permute-start | bytes 12296 | tf_op jit(solution)/shard_map/ppermute | solution.py:570
  23.0 5.1 %collective-permute-start.7 = (f32[8,128]{1,0:T(8,128)}, f32[8,128]{1,0:T(8,128)}, u32[]{:S(2)}, u32[]{:S(2)}) collective-permute-start(f32[8,128]{1,0:T(8,128)} %get-tuple-element.82.refs_4_), channel_id=1, source_target_pairs={{0,1},{1,0},{2,3},{3,2},{4,5},{5,4},{6,7},{7,6},{8,9},{9,8},{10,11... | collective-permute-start | bytes 12296 | tf_op jit(solution)/shard_map/ppermute | solution.py:570
  23.7 4.4 %collective-permute-start.10 = (bf16[384,256]{1,0:T(8,128)(2,1)}, bf16[384,256]{1,0:T(8,128)(2,1)}, u32[]{:S(2)}, u32[]{:S(2)}) collective-permute-start(bf16[384,256]{1,0:T(8,128)(2,1)} %get-tuple-element.77), channel_id=1, source_target_pairs={{0,4},{4,0},{8,12},{12,8},{16,20},{20,16},{24,28},{28,24},{1,5},{5... | collective-permute-start | bytes 589832 | tf_op jit(solution)/shard_map/ppermute | solution.py:570
  26.7 1.8 %collective-permute-start.11 = (bf16[384,256]{1,0:T(8,128)(2,1)}, bf16[384,256]{1,0:T(8,128)(2,1)}, u32[]{:S(2)}, u32[]{:S(2)}) collective-permute-start(bf16[384,256]{1,0:T(8,128)(2,1)} %get-tuple-element.81), channel_id=1, source_target_pairs={{0,4},{4,0},{8,12},{12,8},{16,20},{20,16},{24,28},{28,24},{1,5},{5... | collective-permute-start | bytes 589832 | tf_op jit(solution)/shard_map/ppermute | solution.py:570
  29.6 6.8 %collective-permute-start.12 = (bf16[400,128]{1,0:T(8,128)(2,1)S(1)}, bf16[400,128]{1,0:T(8,128)(2,1)S(1)}, u32[]{:S(2)}, u32[]{:S(2)}) collective-permute-start(bf16[400,128]{1,0:T(8,128)(2,1)S(1)} %get-tuple-element.86), channel_id=1, source_target_pairs={{0,24},{4,28},{8,16},{12,20},{16,8},{20,12},{24,0},{28,4},{1,25},{... | collective-permute-start | bytes 307208 | tf_op jit(solution)/shard_map/ppermute | solution.py:570
  29.6 7.2 %collective-permute-start.13 = (bf16[400,128]{1,0:T(8,128)(2,1)S(1)}, bf16[400,128]{1,0:T(8,128)(2,1)S(1)}, u32[]{:S(2)}, u32[]{:S(2)}) collective-permute-start(bf16[400,128]{1,0:T(8,128)(2,1)S(1)} %get-tuple-element.87), channel_id=1, source_target_pairs={{0,16},{4,20},{8,24},{12,28},{16,0},{20,4},{24,8},{28,12},{1,17},{... | collective-permute-start | bytes 307208 | tf_op jit(solution)/shard_map/ppermute | solution.py:570
  30.8 6.0 %collective-permute-start.14 = (bf16[400,128]{1,0:T(8,128)(2,1)S(1)}, bf16[400,128]{1,0:T(8,128)(2,1)S(1)}, u32[]{:S(2)}, u32[]{:S(2)}) collective-permute-start(bf16[400,128]{1,0:T(8,128)(2,1)S(1)} %get-tuple-element.88), channel_id=1, source_target_pairs={{0,8},{4,12},{8,0},{12,4},{16,24},{20,28},{24,16},{28,20},{1,9},{5... | collective-permute-start | bytes 307208 | tf_op jit(solution)/shard_map/ppermute | solution.py:570
  33.1 5.0 %copy-start.3 = (f32[128]{0:T(128)S(1)}, f32[128]{0:T(128)}, u32[]{:S(2)}) copy-start(f32[128]{0:T(128)} %param.15) | copy-start | bytes 1540
  36.8 1.2 %collective-permute-start.15 = (f32[8,128]{1,0:T(8,128)S(1)}, f32[8,128]{1,0:T(8,128)S(1)}, u32[]{:S(2)}, u32[]{:S(2)}) collective-permute-start(f32[8,128]{1,0:T(8,128)S(1)} %sum_chips.1.refs_0_), channel_id=1, source_target_pairs={{0,4},{4,0},{8,12},{12,8},{16,20},{20,16},{24,28},{28,24},{1,5},{5... | collective-permute-start | bytes 12296 | tf_op jit(solution)/shard_map/ppermute | solution.py:570

commit v10 on v8

--- a/solution.py
+++ b/solution.py
@@ -376,7 +376,7 @@
             pltpu.SemaphoreType.DMA((slots,)), pltpu.SemaphoreType.DMA((2,)),
         ],
         compiler_params=params(),
-        cost_estimate=cost(2 * 10**9, 2 * 10**6),
+        cost_estimate=cost(6 * 10**9, 2 * 10**6),
         name="turn",
     )(live_counts, att_t, own_acc, keys, key_gain)
 

time: 37.7 us -> 37.3 us (0.989)
  Pallas kernels: 12.8 us -> 10.4 us
  starting transfers between devices: 14.7 us -> 15.8 us
  waiting for transfers between devices: 7.92 us -> 8.89 us
    pallas_call x1, Pallas kernels: 5.95 us -> 4.45 us  [attention(): pl.pallas_call(functools.partial(attention_kernel, parts=parts, heads=hea...]
    ppermute x15, starting transfers between devices: 14.7 us -> 15.8 us  [swap(): lax.ppermute(values, axis, [(i, i ^ step) for i in range(lax.axis_size(ax...]
    ppermute x15, waiting for transfers between devices: 7.92 us -> 8.89 us  [swap(): lax.ppermute(values, axis, [(i, i ^ step) for i in range(lax.axis_size(ax...]
    pallas_call x1, Pallas kernels: 2.69 us -> 2.24 us  [post(): pl.pallas_call(post_kernel, in_specs=[SMEM_SPEC] * 2 + [VMEM_SPEC] * 6, o...]
  transfers between devices with their start and end apart: 15 -> 15, of which waited for: 9 -> 9; matrix products, arithmetic and copies ran while one was open for 0% -> 0% of each run, Pallas kernels for 16% -> 14%
where the time goes in v10:
time: 37.3 us
  starting transfers between devices  15.8 us (42%)
  Pallas kernels  10.4 us (28%)
  waiting for transfers between devices  8.89 us (24%)
  between operations  1.46 us (4%)
  local copies, waits for them, and re-layouts  0.82 us (2%)
    ppermute x15, starting transfers between devices, swap(): lax.ppermute(values, axis, [(i, i ^ step) for i in range(lax.axis_size(ax...  15.8 us
    ppermute x15, waiting for transfers between devices, swap(): lax.ppermute(values, axis, [(i, i ^ step) for i in range(lax.axis_size(ax...  8.89 us
    pallas_call x1, Pallas kernels, attention(): pl.pallas_call(functools.partial(attention_kernel, parts=parts, heads=hea...  4.45 us
    pallas_call x1, Pallas kernels, post(): pl.pallas_call(post_kernel, in_specs=[SMEM_SPEC] * 2 + [VMEM_SPEC] * 6, o...  2.24 us
    pallas_call x1, Pallas kernels, turn(): pl.pallas_call(turn_kernel, in_specs=[SMEM_SPEC] + [VMEM_SPEC] * 4, out_s...  1.28 us
    pallas_call x1, Pallas kernels, finish(): pl.pallas_call(finish_kernel, in_specs=[VMEM_SPEC] * (len(blocks) + 2), o...  0.84 us
    unnamed x18, local copies, waits for them, and re-layouts  0.82 us
    pallas_call x1, Pallas kernels, prepare(): pl.pallas_call(prepare_kernel, in_specs=[SMEM_SPEC] + [VMEM_SPEC] * 3, ou...  0.8 us
  transfers between devices with their start and end apart: 15, of which 9 were waited for; matrix products, arithmetic and copies ran while one was open for 0% of the time, Pallas kernels for 14%

profile of v10, /device:TPU:0, one launch (start us, length us, event | category | flops | bytes accessed | tf_op | source)
XLA Modules:
  0.0 37.3 jit_solution(9761154595299205173)
XLA Ops:
  0.6 0.0 copy-start
  0.6 0.0 copy-start.1
  0.7 0.0 copy-start.7
  0.7 0.7 %copy-done = bf16[96,256]{1,0:T(8,128)(2,1)S(1)} copy-done((bf16[96,256]{1,0:T(8,128)(2,1)S(1)}, bf16[96,256]{1,0:T(8,128)(2,1)}, u32[]{:S(2)}) %copy-start) | copy-done | bytes 49176
  1.4 0.0 copy-done.1
  1.4 0.0 copy-done.7
  1.5 0.0 copy-start.2
  1.5 0.0 copy-start.3
  1.5 0.0 copy-start.4
  1.5 0.1 pack.1.refs_10_
  1.6 4.0 %collective-permute-start.3 = (bf16[96,512]{1,0:T(8,128)(2,1)S(1)}, bf16[96,512]{1,0:T(8,128)(2,1)S(1)}, u32[]{:S(2)}, u32[]{:S(2)}) collective-permute-start(bf16[96,512]{1,0:T(8,128)(2,1)S(1)} %pack.1.refs_10_), channel_id=1, source_target_pairs={{0,24},{4,28},{8,16},{12,20},{16,8},{20,12},{24,0},{28,4},{1,25},{... | collective-permute-start | bytes 294920 | tf_op jit(solution)/shard_map/ppermute | solution.py:533
  5.6 0.5 %collective-permute-start.2 = (bf16[96,512]{1,0:T(8,128)(2,1)S(1)}, bf16[96,512]{1,0:T(8,128)(2,1)S(1)}, u32[]{:S(2)}, u32[]{:S(2)}) collective-permute-start(bf16[96,512]{1,0:T(8,128)(2,1)S(1)} %pack.1.refs_10_), channel_id=1, source_target_pairs={{0,16},{4,20},{8,24},{12,28},{16,0},{20,4},{24,8},{28,12},{1,17},{... | collective-permute-start | bytes 294920 | tf_op jit(solution)/shard_map/ppermute | solution.py:533
  6.1 0.1 collective-permute-start.1
  6.9 0.0 copy-done.2
  6.9 0.0 copy-done.3
  6.9 0.0 copy-done.4
  6.9 0.0 copy-start.5
  6.9 0.0 copy-start.6
  6.9 0.0 copy-start.8
  6.9 0.8 %prepare.1 = (bf16[4,256,512]{2,1,0:T(8,128)(2,1)S(1)}, f32[4,8,512]{2,1,0:T(8,128)S(1)}, bf16[4,256,512]{2,1,0:T(8,128)(2,1)S(1)}, bf16[4,256,512]{2,1,0:T(8,12...) custom-call(s32[1]{0:T(128)S(6)} %copy.18.live_ref.refs_0_, bf16[256,2048]{1,0:T(8,128)(2,1)S(1)} %copy-done.3, ...), custom_call_target="tpu_custom_call" | custom-call | flops 2000000000 | bytes 3145728 | tf_op jit(solution)/shard_map/prepare/pallas_call | solution.py:136
  7.7 1.0 %collective-permute-done.3.refs_16_ = bf16[96,512]{1,0:T(8,128)(2,1)S(1)} collective-permute-done((bf16[96,512]{1,0:T(8,128)(2,1)S(1)}, bf16[96,512]{1,0:T(8,128)(2,1)S(1)}, u32[]{:S(2)}, u32[]{:S(2)}) %collective-permute-start.3) | collective-permute-done | bytes 98336 | tf_op jit(solution)/shard_map/ppermute | solution.py:533
  8.7 0.0 collective-permute-start.4
  8.8 0.5 %collective-permute-start = (bf16[96,512]{1,0:T(8,128)(2,1)S(1)}, bf16[96,512]{1,0:T(8,128)(2,1)S(1)}, u32[]{:S(2)}, u32[]{:S(2)}) collective-permute-start(bf16[96,512]{1,0:T(8,128)(2,1)S(1)} %pack.1.refs_10_), channel_id=1, source_target_pairs={{0,4},{4,0},{8,12},{12,8},{16,20},{20,16},{24,28},{28,24},{1,5},{5... | collective-permute-start | bytes 294920 | tf_op jit(solution)/shard_map/ppermute | solution.py:533
  9.3 1.2 %collective-permute-done.2.refs_14_ = bf16[96,512]{1,0:T(8,128)(2,1)S(1)} collective-permute-done((bf16[96,512]{1,0:T(8,128)(2,1)S(1)}, bf16[96,512]{1,0:T(8,128)(2,1)S(1)}, u32[]{:S(2)}, u32[]{:S(2)}) %collective-permute-start.2) | collective-permute-done | bytes 98336 | tf_op jit(solution)/shard_map/ppermute | solution.py:533
  10.5 0.0 collective-permute-start.6
  10.5 0.3 collective-permute-done.1.refs_12_
  10.8 0.0 collective-permute-done.4.refs_17_
  10.8 0.2 collective-permute-start.5
  11.0 0.0 collective-permute-done.refs_11_
  11.0 0.8 %collective-permute-done.6.refs_15_ = bf16[96,512]{1,0:T(8,128)(2,1)S(1)} collective-permute-done((bf16[96,512]{1,0:T(8,128)(2,1)S(1)}, bf16[96,512]{1,0:T(8,128)(2,1)S(1)}, u32[]{:S(2)}, u32[]{:S(2)}) %collective-permute-start.6) | collective-permute-done | bytes 98336 | tf_op jit(solution)/shard_map/ppermute | solution.py:533
  11.8 0.3 collective-permute-done.5.refs_13_
  12.1 0.0 copy-done.5
  12.1 0.0 copy-done.6
  12.1 0.0 copy-done.8
  12.1 4.5 %attention.1 = (bf16[4,256,512]{2,1,0:T(8,128)(2,1)S(1)}, bf16[4,2,448,512]{3,2,1,0:T(8,128)(2,1)S(1)}, bf16[768,256]{1,0:T(8,128)(2,1)S(1)}, bf16[256,256]{1,0:...) custom-call(s32[1]{0:T(128)S(6)} %copy.18.live_ref.refs_0_, ...), custom_call_target="tpu_custom_call" | custom-call | flops 3000000000 | bytes 10000000 | tf_op jit(solution)/shard_map/attention/pallas_call | solution.py:290
  16.6 3.8 %collective-permute-start.9 = (f32[8,128]{1,0:T(8,128)S(1)}, f32[8,128]{1,0:T(8,128)S(1)}, u32[]{:S(2)}, u32[]{:S(2)}) collective-permute-start(f32[8,128]{1,0:T(8,128)S(1)} %get-tuple-element.74.refs_0_), channel_id=1, source_target_pairs={{0,3},{1,2},{2,1},{3,0},{4,7},{5,6},{6,5},{7,4},{8,11},{9,10},{10,... | collective-permute-start | bytes 12296 | tf_op jit(solution)/shard_map/ppermute | solution.py:533
  20.3 0.0 collective-permute-start.8
  20.3 0.7 %collective-permute-start.7 = (f32[8,128]{1,0:T(8,128)S(1)}, f32[8,128]{1,0:T(8,128)S(1)}, u32[]{:S(2)}, u32[]{:S(2)}) collective-permute-start(f32[8,128]{1,0:T(8,128)S(1)} %get-tuple-element.74.refs_0_), channel_id=1, source_target_pairs={{0,1},{1,0},{2,3},{3,2},{4,5},{5,4},{6,7},{7,6},{8,9},{9,8},{10,11... | collective-permute-start | bytes 12296 | tf_op jit(solution)/shard_map/ppermute | solution.py:533
  21.0 0.0 collective-permute-start.10
  21.0 1.3 %turn.1 = (bf16[256,2048]{1,0:T(8,128)(2,1)}, bf16[256,256]{1,0:T(8,128)(2,1)}, bf16[256,256]{1,0:T(8,128)(2,1)}) custom-call(s32[1]{0:T(128)S(6)} %copy.18.live_ref.refs_0_, bf16[4,256,512]{2,1,0:T(8,128)(2,1)S(1)} %get-tuple-element.68.att_t_ref, f32[4,2,2,64,128]{4,3,2,1,0:T(8,128)S(1)} %get-tuple-element.69.own_acc, bf16[256,256]{1,0:T(8,128)(2,1)S(1)} %copy-done.6, ...), custom_call_target="tpu_custom_call" | custom-call | flops 6000000000 | bytes 2000000 | tf_op jit(solution)/shard_map/turn/pallas_call | solution.py:369
  22.3 0.0 collective-permute-done.9.refs_3_
  22.3 2.5 %collective-permute-done.8.refs_2_ = f32[8,128]{1,0:T(8,128)S(1)} collective-permute-done((f32[8,128]{1,0:T(8,128)S(1)}, f32[8,128]{1,0:T(8,128)S(1)}, u32[]{:S(2)}, u32[]{:S(2)}) %collective-permute-start.8) | collective-permute-done | bytes 4128 | tf_op jit(solution)/shard_map/ppermute | solution.py:533
  24.8 0.0 collective-permute-done.7.refs_1_
  24.8 0.0 collective-permute-done.10.came_ref
  24.8 0.1 add.1
  24.9 2.7 %collective-permute-start.11 = (bf16[400,128]{1,0:T(8,128)(2,1)S(1)}, bf16[400,128]{1,0:T(8,128)(2,1)S(1)}, u32[]{:S(2)}, u32[]{:S(2)}) collective-permute-start(bf16[400,128]{1,0:T(8,128)(2,1)S(1)} %get-tuple-element.78), channel_id=1, source_target_pairs={{0,24},{4,28},{8,16},{12,20},{16,8},{20,12},{24,0},{28,4},{1,25},{... | collective-permute-start | bytes 307208 | tf_op jit(solution)/shard_map/ppermute | solution.py:533
  27.6 3.3 %collective-permute-start.12 = (bf16[400,128]{1,0:T(8,128)(2,1)S(1)}, bf16[400,128]{1,0:T(8,128)(2,1)S(1)}, u32[]{:S(2)}, u32[]{:S(2)}) collective-permute-start(bf16[400,128]{1,0:T(8,128)(2,1)S(1)} %get-tuple-element.79), channel_id=1, source_target_pairs={{0,16},{4,20},{8,24},{12,28},{16,0},{20,4},{24,8},{28,12},{1,17},{... | collective-permute-start | bytes 307208 | tf_op jit(solution)/shard_map/ppermute | solution.py:533
  30.9 0.0 collective-permute-start.13
  30.9 2.2 %post.1 = bf16[256,2048]{1,0:T(8,128)(2,1)} custom-call(s32[1]{0:T(128)S(6)} %copy.18.live_ref.refs_0_, s32[4]{0:T(128)S(1)} %copy-done.8, bf16[4,2,448,512]{3,2,1,0:T(8,128)(2,1)S(1)} %get-tuple-element.81.ds_ref, bf16[768,256]{1,0:T(8,128)(2,1)S(1)} %get-tuple-element.82.pool_keys, bf16[256,256]{1,0:T(8,128)(2,1)S(1)} %get-tuple-element.83.own_keys_ref, ...), custom_call_target="tpu_custom_call" | custom-call | flops 3000000000 | bytes 4000000 | tf_op jit(solution)/shard_map/post/pallas_call | solution.py:416
  33.1 0.0 collective-permute-done.11.refs_1_
  33.2 0.7 %collective-permute-done.12.refs_2_ = bf16[400,128]{1,0:T(8,128)(2,1)S(1)} collective-permute-done((bf16[400,128]{1,0:T(8,128)(2,1)S(1)}, bf16[400,128]{1,0:T(8,128)(2,1)S(1)}, u32[]{:S(2)}, u32[]{:S(2)}) %collective-permute-start.12) | collective-permute-done | bytes 102432 | tf_op jit(solution)/shard_map/ppermute | solution.py:533
  33.9 1.7 %collective-permute-done.13.refs_3_ = bf16[400,128]{1,0:T(8,128)(2,1)S(1)} collective-permute-done((bf16[400,128]{1,0:T(8,128)(2,1)S(1)}, bf16[400,128]{1,0:T(8,128)(2,1)S(1)}, u32[]{:S(2)}, u32[]{:S(2)}) %collective-permute-start.13) | collective-permute-done | bytes 102432 | tf_op jit(solution)/shard_map/ppermute | solution.py:533
  35.6 0.1 collective-permute-start.14
  35.7 0.8 %finish.1 = (f32[96,256]{1,0:T(8,128)}, f32[96,256]{1,0:T(8,128)}) custom-call(f32[400,128]{1,0:T(8,128)S(1)} %get-tuple-element.90.refs_0_, bf16[400,128]{1,0:T(8,128)(2,1)S(1)} %collective-permute-done.11.refs_1_, bf16[400,128]{1,0:T(8,128)(2,1)S(1)} %collective-permute-done.12.refs_2_, bf16[400,128]{1,0:T(8,128)(2,1)S(1)} %collective-permute-done.13.refs_3_, ...), custom_call_target="tpu_custom_call" | custom-call | flops 100000000 | bytes 1000000 | tf_op jit(solution)/shard_map/finish/pallas_call | solution.py:521
  36.5 0.3 collective-permute-done.14.refs_1_
  36.8 0.5 %gain_grads.1 = (f32[1,128]{1,0:T(1,128)}, f32[1,128]{1,0:T(1,128)}) custom-call(f32[8,128]{1,0:T(8,128)S(1)} %sum_chips.1.refs_0_, f32[8,128]{1,0:T(8,128)S(1)} %collective-permute-done.14.refs_1_, f32[1,128]{1,0:T(1,128)S(1)} %bitcast.11, f32[1,128]{1,0:T(1,128)S(1)} %bitcast.9), custom_call_target="tpu_custom_call" | custom-call | tf_op jit(solution)/shard_map/gain_grads/pallas_call | solution.py:491
  (2 shorter events, 0.0 us)
Async XLA Ops:
  0.6 0.8 %copy-start = (bf16[96,256]{1,0:T(8,128)(2,1)S(1)}, bf16[96,256]{1,0:T(8,128)(2,1)}, u32[]{:S(2)}) copy-start(bf16[96,256]{1,0:T(8,128)(2,1)} %refs_4_.1) | copy-start | bytes 147460
  0.6 0.8 %copy-start.1 = (f32[128]{0:T(128)S(1)}, f32[128]{0:T(128)}, u32[]{:S(2)}) copy-start(f32[128]{0:T(128)} %param.16) | copy-start | bytes 1540
  0.7 0.8 %copy-start.7 = (bf16[96,256]{1,0:T(8,128)(2,1)S(1)}, bf16[96,256]{1,0:T(8,128)(2,1)}, u32[]{:S(2)}) copy-start(bf16[96,256]{1,0:T(8,128)(2,1)} %values_ref) | copy-start | bytes 147460
  1.5 5.4 %copy-start.2 = (f32[128]{0:T(128)S(1)}, f32[128]{0:T(128)}, u32[]{:S(2)}) copy-start(f32[128]{0:T(128)} %param.15) | copy-start | bytes 1540
  1.5 5.4 %copy-start.3 = (bf16[256,2048]{1,0:T(8,128)(2,1)S(1)}, bf16[256,2048]{1,0:T(8,128)(2,1)}, u32[]{:S(2)}) copy-start(bf16[256,2048]{1,0:T(8,128)(2,1)} %q_ref.1) | copy-start | bytes 3145732
  1.5 5.4 %copy-start.4 = (bf16[256,2048]{1,0:T(8,128)(2,1)S(1)}, bf16[256,2048]{1,0:T(8,128)(2,1)}, u32[]{:S(2)}) copy-start(bf16[256,2048]{1,0:T(8,128)(2,1)} %do_ref.1) | copy-start | bytes 3145732
  1.6 7.1 %collective-permute-start.3 = (bf16[96,512]{1,0:T(8,128)(2,1)S(1)}, bf16[96,512]{1,0:T(8,128)(2,1)S(1)}, u32[]{:S(2)}, u32[]{:S(2)}) collective-permute-start(bf16[96,512]{1,0:T(8,128)(2,1)S(1)} %pack.1.refs_10_), channel_id=1, source_target_pairs={{0,24},{4,28},{8,16},{12,20},{16,8},{20,12},{24,0},{28,4},{1,25},{... | collective-permute-start | bytes 294920 | tf_op jit(solution)/shard_map/ppermute | solution.py:533
  5.6 4.9 %collective-permute-start.2 = (bf16[96,512]{1,0:T(8,128)(2,1)S(1)}, bf16[96,512]{1,0:T(8,128)(2,1)S(1)}, u32[]{:S(2)}, u32[]{:S(2)}) collective-permute-start(bf16[96,512]{1,0:T(8,128)(2,1)S(1)} %pack.1.refs_10_), channel_id=1, source_target_pairs={{0,16},{4,20},{8,24},{12,28},{16,0},{20,4},{24,8},{28,12},{1,17},{... | collective-permute-start | bytes 294920 | tf_op jit(solution)/shard_map/ppermute | solution.py:533
  6.1 4.7 %collective-permute-start.1 = (bf16[96,512]{1,0:T(8,128)(2,1)S(1)}, bf16[96,512]{1,0:T(8,128)(2,1)S(1)}, u32[]{:S(2)}, u32[]{:S(2)}) collective-permute-start(bf16[96,512]{1,0:T(8,128)(2,1)S(1)} %pack.1.refs_10_), channel_id=1, source_target_pairs={{0,8},{4,12},{8,0},{12,4},{16,24},{20,28},{24,16},{28,20},{1,9},{5... | collective-permute-start | bytes 294920 | tf_op jit(solution)/shard_map/ppermute | solution.py:533
  6.9 5.2 %copy-start.5 = (bf16[256,256]{1,0:T(8,128)(2,1)S(1)}, bf16[256,256]{1,0:T(8,128)(2,1)}, u32[]{:S(2)}) copy-start(bf16[256,256]{1,0:T(8,128)(2,1)} %refs_7_.1) | copy-start | bytes 393220
  6.9 5.2 %copy-start.6 = (bf16[256,256]{1,0:T(8,128)(2,1)S(1)}, bf16[256,256]{1,0:T(8,128)(2,1)}, u32[]{:S(2)}) copy-start(bf16[256,256]{1,0:T(8,128)(2,1)} %ck_ref.1) | copy-start | bytes 393220
  6.9 5.2 %copy-start.8 = (s32[4]{0:T(128)S(1)}, s32[4]{0:T(128)}, u32[]{:S(2)}) copy-start(s32[4]{0:T(128)} %prompt_ref.1) | copy-start | bytes 52
  8.7 2.0 %collective-permute-start.4 = (bf16[96,512]{1,0:T(8,128)(2,1)S(1)}, bf16[96,512]{1,0:T(8,128)(2,1)S(1)}, u32[]{:S(2)}, u32[]{:S(2)}) collective-permute-start(bf16[96,512]{1,0:T(8,128)(2,1)S(1)} %collective-permute-done.3.refs_16_), channel_id=1, source_target_pairs={{0,4},{4,0},{8,12},{12,8},{16,20},{20,16},{24,28},{28,24},{1,5},{5... | collective-permute-start | bytes 294920 | tf_op jit(solution)/shard_map/ppermute | solution.py:533
  8.8 2.2 %collective-permute-start = (bf16[96,512]{1,0:T(8,128)(2,1)S(1)}, bf16[96,512]{1,0:T(8,128)(2,1)S(1)}, u32[]{:S(2)}, u32[]{:S(2)}) collective-permute-start(bf16[96,512]{1,0:T(8,128)(2,1)S(1)} %pack.1.refs_10_), channel_id=1, source_target_pairs={{0,4},{4,0},{8,12},{12,8},{16,20},{20,16},{24,28},{28,24},{1,5},{5... | collective-permute-start | bytes 294920 | tf_op jit(solution)/shard_map/ppermute | solution.py:533
  10.5 1.3 %collective-permute-start.6 = (bf16[96,512]{1,0:T(8,128)(2,1)S(1)}, bf16[96,512]{1,0:T(8,128)(2,1)S(1)}, u32[]{:S(2)}, u32[]{:S(2)}) collective-permute-start(bf16[96,512]{1,0:T(8,128)(2,1)S(1)} %collective-permute-done.2.refs_14_), channel_id=1, source_target_pairs={{0,4},{4,0},{8,12},{12,8},{16,20},{20,16},{24,28},{28,24},{1,5},{5... | collective-permute-start | bytes 294920 | tf_op jit(solution)/shard_map/ppermute | solution.py:533
  10.8 1.3 %collective-permute-start.5 = (bf16[96,512]{1,0:T(8,128)(2,1)S(1)}, bf16[96,512]{1,0:T(8,128)(2,1)S(1)}, u32[]{:S(2)}, u32[]{:S(2)}) collective-permute-start(bf16[96,512]{1,0:T(8,128)(2,1)S(1)} %collective-permute-done.1.refs_12_), channel_id=1, source_target_pairs={{0,4},{4,0},{8,12},{12,8},{16,20},{20,16},{24,28},{28,24},{1,5},{5... | collective-permute-start | bytes 294920 | tf_op jit(solution)/shard_map/ppermute | solution.py:533
  16.6 5.7 %collective-permute-start.9 = (f32[8,128]{1,0:T(8,128)S(1)}, f32[8,128]{1,0:T(8,128)S(1)}, u32[]{:S(2)}, u32[]{:S(2)}) collective-permute-start(f32[8,128]{1,0:T(8,128)S(1)} %get-tuple-element.74.refs_0_), channel_id=1, source_target_pairs={{0,3},{1,2},{2,1},{3,0},{4,7},{5,6},{6,5},{7,4},{8,11},{9,10},{10,... | collective-permute-start | bytes 12296 | tf_op jit(solution)/shard_map/ppermute | solution.py:533
  20.3 4.5 %collective-permute-start.8 = (f32[8,128]{1,0:T(8,128)S(1)}, f32[8,128]{1,0:T(8,128)S(1)}, u32[]{:S(2)}, u32[]{:S(2)}) collective-permute-start(f32[8,128]{1,0:T(8,128)S(1)} %get-tuple-element.74.refs_0_), channel_id=1, source_target_pairs={{0,2},{1,3},{2,0},{3,1},{4,6},{5,7},{6,4},{7,5},{8,10},{9,11},{10,... | collective-permute-start | bytes 12296 | tf_op jit(solution)/shard_map/ppermute | solution.py:533
  20.3 4.5 %collective-permute-start.7 = (f32[8,128]{1,0:T(8,128)S(1)}, f32[8,128]{1,0:T(8,128)S(1)}, u32[]{:S(2)}, u32[]{:S(2)}) collective-permute-start(f32[8,128]{1,0:T(8,128)S(1)} %get-tuple-element.74.refs_0_), channel_id=1, source_target_pairs={{0,1},{1,0},{2,3},{3,2},{4,5},{5,4},{6,7},{7,6},{8,9},{9,8},{10,11... | collective-permute-start | bytes 12296 | tf_op jit(solution)/shard_map/ppermute | solution.py:533
  21.0 3.8 %collective-permute-start.10 = (bf16[384,512]{1,0:T(8,128)(2,1)S(1)}, bf16[384,512]{1,0:T(8,128)(2,1)S(1)}, u32[]{:S(2)}, u32[]{:S(2)}) collective-permute-start(bf16[384,512]{1,0:T(8,128)(2,1)S(1)} %get-tuple-element.73), channel_id=1, source_target_pairs={{0,4},{4,0},{8,12},{12,8},{16,20},{20,16},{24,28},{28,24},{1,5},{5... | collective-permute-start | bytes 1179656 | tf_op jit(solution)/shard_map/ppermute | solution.py:533
  24.9 8.2 %collective-permute-start.11 = (bf16[400,128]{1,0:T(8,128)(2,1)S(1)}, bf16[400,128]{1,0:T(8,128)(2,1)S(1)}, u32[]{:S(2)}, u32[]{:S(2)}) collective-permute-start(bf16[400,128]{1,0:T(8,128)(2,1)S(1)} %get-tuple-element.78), channel_id=1, source_target_pairs={{0,24},{4,28},{8,16},{12,20},{16,8},{20,12},{24,0},{28,4},{1,25},{... | collective-permute-start | bytes 307208 | tf_op jit(solution)/shard_map/ppermute | solution.py:533
  27.6 6.3 %collective-permute-start.12 = (bf16[400,128]{1,0:T(8,128)(2,1)S(1)}, bf16[400,128]{1,0:T(8,128)(2,1)S(1)}, u32[]{:S(2)}, u32[]{:S(2)}) collective-permute-start(bf16[400,128]{1,0:T(8,128)(2,1)S(1)} %get-tuple-element.79), channel_id=1, source_target_pairs={{0,16},{4,20},{8,24},{12,28},{16,0},{20,4},{24,8},{28,12},{1,17},{... | collective-permute-start | bytes 307208 | tf_op jit(solution)/shard_map/ppermute | solution.py:533
  30.9 4.7 %collective-permute-start.13 = (bf16[400,128]{1,0:T(8,128)(2,1)S(1)}, bf16[400,128]{1,0:T(8,128)(2,1)S(1)}, u32[]{:S(2)}, u32[]{:S(2)}) collective-permute-start(bf16[400,128]{1,0:T(8,128)(2,1)S(1)} %get-tuple-element.80), channel_id=1, source_target_pairs={{0,8},{4,12},{8,0},{12,4},{16,24},{20,28},{24,16},{28,20},{1,9},{5... | collective-permute-start | bytes 307208 | tf_op jit(solution)/shard_map/ppermute | solution.py:533
  35.6 1.2 %collective-permute-start.14 = (f32[8,128]{1,0:T(8,128)S(1)}, f32[8,128]{1,0:T(8,128)S(1)}, u32[]{:S(2)}, u32[]{:S(2)}) collective-permute-start(f32[8,128]{1,0:T(8,128)S(1)} %sum_chips.1.refs_0_), channel_id=1, source_target_pairs={{0,4},{4,0},{8,12},{12,8},{16,20},{20,16},{24,28},{28,24},{1,5},{5... | collective-permute-start | bytes 12296 | tf_op jit(solution)/shard_map/ppermute | solution.py:533

commit v11 on v9

--- a/solution.py
+++ b/solution.py
@@ -402,7 +402,7 @@
             pltpu.SemaphoreType.DMA((slots,)), pltpu.SemaphoreType.DMA,
         ],
         compiler_params=params(),
-        cost_estimate=cost(4 * 10**11, 2 * 10**6),
+        cost_estimate=cost(6 * 10**9, 2 * 10**6),
         name="turn",
     )(live_counts, att_t, own_keys, keys, key_gain)
 

time: 39.3 us -> 37.2 us (0.947); the launches traced: 38.6 us -> 37.1 us
  Pallas kernels: 18.5 us -> 16.1 us
  waiting for transfers between devices: 4.51 us -> 5.2 us
    pallas_call x1, Pallas kernels: 1.11 us -> 0.08 us  [add(): pl.pallas_call(functools.partial(add_kernel, terms=len(terms)), in_specs=...]
    ppermute x16, waiting for transfers between devices: 4.51 us -> 5.2 us  [swap(): lax.ppermute(values, axis, [(i, i ^ step) for i in range(lax.axis_size(ax...]
    pallas_call x1, Pallas kernels: 2.93 us -> 2.25 us  [value_grads(): pl.pallas_call(functools.partial(values_kernel, parts=parts), in_specs=[S...]
    pallas_call x1, Pallas kernels: 7.23 us -> 6.6 us  [attention(): pl.pallas_call(functools.partial(attention_kernel, parts=parts, heads=hea...]
    unnamed x20 -> x18, local copies, waits for them, and re-layouts: 0.83 us -> 0.82 us
  transfers between devices with their start and end apart: 16 -> 16, of which waited for: 8 -> 7; matrix products, arithmetic and copies ran while one was open for 0% -> 0% of each run, Pallas kernels for 25% -> 24%
where the time goes in v11:
time: 37.2 us; the launch traced here: 37.1 us
  Pallas kernels  16.1 us (43%)
  starting transfers between devices  13.5 us (36%)
  waiting for transfers between devices  5.2 us (14%)
  between operations  1.49 us (4%)
  local copies, waits for them, and re-layouts  0.82 us (2%)
    ppermute x16, starting transfers between devices, swap(): lax.ppermute(values, axis, [(i, i ^ step) for i in range(lax.axis_size(ax...  13.5 us
    pallas_call x1, Pallas kernels, attention(): pl.pallas_call(functools.partial(attention_kernel, parts=parts, heads=hea...  6.6 us
    ppermute x16, waiting for transfers between devices, swap(): lax.ppermute(values, axis, [(i, i ^ step) for i in range(lax.axis_size(ax...  5.2 us
    pallas_call x1, Pallas kernels, post(): pl.pallas_call(post_kernel, in_specs=[SMEM_SPEC] * 2 + [VMEM_SPEC] * 7, o...  3.17 us
    pallas_call x1, Pallas kernels, value_grads(): pl.pallas_call(functools.partial(values_kernel, parts=parts), in_specs=[S...  2.25 us
    pallas_call x1, Pallas kernels, turn(): pl.pallas_call(turn_kernel, in_specs=[SMEM_SPEC] + [VMEM_SPEC] * 4, out_s...  1.46 us
    pallas_call x1, Pallas kernels, prepare(): pl.pallas_call(prepare_kernel, in_specs=[SMEM_SPEC] + [VMEM_SPEC] * 3, ou...  1.06 us
    pallas_call x1, Pallas kernels, finish(): pl.pallas_call(finish_kernel, in_specs=[VMEM_SPEC] * (len(blocks) + 2), o...  0.84 us
  transfers between devices with their start and end apart: 16, of which 7 were waited for; matrix products, arithmetic and copies ran while one was open for 0% of the time, Pallas kernels for 24%

profile of v11, /device:TPU:0, one launch (start us, length us, event | category | flops | bytes accessed | tf_op | source)
XLA Modules:
  0.0 37.1 jit_solution(503510998944647435)
XLA Ops:
  0.6 0.0 copy-start
  0.6 0.0 copy-start.1
  0.7 0.0 copy-start.7
  0.7 0.7 %copy-done = bf16[96,256]{1,0:T(8,128)(2,1)S(1)} copy-done((bf16[96,256]{1,0:T(8,128)(2,1)S(1)}, bf16[96,256]{1,0:T(8,128)(2,1)}, u32[]{:S(2)}) %copy-start) | copy-done | bytes 49176
  1.4 0.0 copy-done.1
  1.4 0.0 copy-done.7
  1.5 0.0 copy-start.2
  1.5 0.0 copy-start.3
  1.5 0.0 copy-start.4
  1.5 0.1 pack.1.refs_9_
  1.6 4.0 %collective-permute-start.3 = (bf16[96,512]{1,0:T(8,128)(2,1)S(1)}, bf16[96,512]{1,0:T(8,128)(2,1)S(1)}, u32[]{:S(2)}, u32[]{:S(2)}) collective-permute-start(bf16[96,512]{1,0:T(8,128)(2,1)S(1)} %pack.1.refs_9_), channel_id=1, source_target_pairs={{0,24},{4,28},{8,16},{12,20},{16,8},{20,12},{24,0},{28,4},{1,25},{... | collective-permute-start | bytes 294920 | tf_op jit(solution)/shard_map/ppermute | solution.py:570
  5.6 0.5 %collective-permute-start.2 = (bf16[96,512]{1,0:T(8,128)(2,1)S(1)}, bf16[96,512]{1,0:T(8,128)(2,1)S(1)}, u32[]{:S(2)}, u32[]{:S(2)}) collective-permute-start(bf16[96,512]{1,0:T(8,128)(2,1)S(1)} %pack.1.refs_9_), channel_id=1, source_target_pairs={{0,16},{4,20},{8,24},{12,28},{16,0},{20,4},{24,8},{28,12},{1,17},{... | collective-permute-start | bytes 294920 | tf_op jit(solution)/shard_map/ppermute | solution.py:570
  6.1 0.1 collective-permute-start.1
  6.9 0.0 copy-done.2
  6.9 0.0 copy-done.3
  6.9 0.0 copy-done.4
  6.9 0.0 copy-start.5
  6.9 0.0 copy-start.6
  6.9 0.0 copy-start.8
  6.9 1.1 %prepare.1 = (bf16[4,256,512]{2,1,0:T(8,128)(2,1)S(1)}, f32[4,8,512]{2,1,0:T(8,128)S(1)}, bf16[4,256,512]{2,1,0:T(8,128)(2,1)S(1)}, bf16[4,256,512]{2,1,0:T(8,128)(2,1)S(1)}, f32[128,512]{1,0:T(8,128)S(1)}) custom-call(s32[1]{0:T(128)S(6)} %copy.18.live_ref.refs_0_, bf16[256,2048]{1,0:T(8,128)(2,1)S(1)} %copy-done.3, bf16[256,2048]{1,0:T(8,128)(2,1)S(1)} %copy-done.4, ...), custom_call_target="tpu_custom_call" | custom-call | flops 2000000000 | bytes 3145728 | tf_op jit(solution)/shard_map/prepare/pallas_call | solution.py:134
  8.0 0.8 %collective-permute-done.3.refs_15_ = bf16[96,512]{1,0:T(8,128)(2,1)S(1)} collective-permute-done((bf16[96,512]{1,0:T(8,128)(2,1)S(1)}, bf16[96,512]{1,0:T(8,128)(2,1)S(1)}, u32[]{:S(2)}, u32[]{:S(2)}) %collective-permute-start.3) | collective-permute-done | bytes 98336 | tf_op jit(solution)/shard_map/ppermute | solution.py:570
  8.7 0.0 collective-permute-start.4
  8.8 0.5 %collective-permute-start = (bf16[96,512]{1,0:T(8,128)(2,1)S(1)}, bf16[96,512]{1,0:T(8,128)(2,1)S(1)}, u32[]{:S(2)}, u32[]{:S(2)}) collective-permute-start(bf16[96,512]{1,0:T(8,128)(2,1)S(1)} %pack.1.refs_9_), channel_id=1, source_target_pairs={{0,4},{4,0},{8,12},{12,8},{16,20},{20,16},{24,28},{28,24},{1,5},{5... | collective-permute-start | bytes 294920 | tf_op jit(solution)/shard_map/ppermute | solution.py:570
  9.3 1.2 %collective-permute-done.2.refs_13_ = bf16[96,512]{1,0:T(8,128)(2,1)S(1)} collective-permute-done((bf16[96,512]{1,0:T(8,128)(2,1)S(1)}, bf16[96,512]{1,0:T(8,128)(2,1)S(1)}, u32[]{:S(2)}, u32[]{:S(2)}) %collective-permute-start.2) | collective-permute-done | bytes 98336 | tf_op jit(solution)/shard_map/ppermute | solution.py:570
  10.5 0.0 collective-permute-start.6
  10.5 0.3 collective-permute-done.1.refs_11_
  10.8 0.0 collective-permute-done.4.refs_16_
  10.8 0.2 collective-permute-start.5
  11.0 0.0 collective-permute-done.refs_10_
  11.0 0.8 %collective-permute-done.6.refs_14_ = bf16[96,512]{1,0:T(8,128)(2,1)S(1)} collective-permute-done((bf16[96,512]{1,0:T(8,128)(2,1)S(1)}, bf16[96,512]{1,0:T(8,128)(2,1)S(1)}, u32[]{:S(2)}, u32[]{:S(2)}) %collective-permute-start.6) | collective-permute-done | bytes 98336 | tf_op jit(solution)/shard_map/ppermute | solution.py:570
  11.8 0.3 collective-permute-done.5.refs_12_
  12.1 0.0 copy-done.5
  12.1 0.0 copy-done.6
  12.1 0.0 copy-done.8
  12.1 6.6 %attention.1 = (bf16[4,256,512]{2,1,0:T(8,128)(2,1)S(1)}, bf16[4,2,448,512]{3,2,1,0:T(8,128)(2,1)S(1)}, bf16[4,2,448,512]{3,2,1,0:T(8,128)(2,1)S(1)}, bf16[4,256...) custom-call(s32[1]{0:T(128)S(6)} %copy.18.live_ref.refs_0_, ...), custom_call_target="tpu_custom_call" | custom-call | flops 3000000000 | bytes 10000000 | tf_op jit(solution)/shard_map/attention/pallas_call | solution.py:289
  18.7 3.8 %collective-permute-start.9 = (f32[8,128]{1,0:T(8,128)S(1)}, f32[8,128]{1,0:T(8,128)S(1)}, u32[]{:S(2)}, u32[]{:S(2)}) collective-permute-start(f32[8,128]{1,0:T(8,128)S(1)} %get-tuple-element.82.refs_4_), channel_id=1, source_target_pairs={{0,3},{1,2},{2,1},{3,0},{4,7},{5,6},{6,5},{7,4},{8,11},{9,10},{10,... | collective-permute-start | bytes 12296 | tf_op jit(solution)/shard_map/ppermute | solution.py:570
  22.5 0.0 collective-permute-start.8
  22.5 0.7 %collective-permute-start.7 = (f32[8,128]{1,0:T(8,128)S(1)}, f32[8,128]{1,0:T(8,128)S(1)}, u32[]{:S(2)}, u32[]{:S(2)}) collective-permute-start(f32[8,128]{1,0:T(8,128)S(1)} %get-tuple-element.82.refs_4_), channel_id=1, source_target_pairs={{0,1},{1,0},{2,3},{3,2},{4,5},{5,4},{6,7},{7,6},{8,9},{9,8},{10,11... | collective-permute-start | bytes 12296 | tf_op jit(solution)/shard_map/ppermute | solution.py:570
  23.2 0.0 collective-permute-start.10
  23.2 2.2 %values.1 = (f32[4,2,64,128]{3,2,1,0:T(8,128)S(1)}, f32[384,256]{1,0:T(8,128)S(1)}, bf16[384,256]{1,0:T(8,128)(2,1)S(1)}) custom-call(s32[1]{0:T(128)S(6)} %copy.18.live_ref.refs_0_, s32[4]{0:T(128)S(1)} %copy-done.8, s32[1]{0:T(128)} %bitcast.refs_2_.me_ref, bf16[4,2,448,512]{3,2,1,0:T(8,128)(2,1)S(1)} %get-tuple-element.78.weights, ...), custom_call_target="tpu_custom_call" | custom-call | flops 2000000000 | bytes 1000000 | tf_op jit(solution)/shard_map/values/pallas_call | solution.py:333
  25.4 0.1 collective-permute-start.11
  25.5 1.5 %turn.1 = (bf16[256,2048]{1,0:T(8,128)(2,1)}, bf16[256,256]{1,0:T(8,128)(2,1)}) custom-call(s32[1]{0:T(128)S(6)} %copy.18.live_ref.refs_0_, bf16[4,256,512]{2,1,0:T(8,128)(2,1)S(1)} %get-tuple-element.72.att_t_ref, f32[4,2,64,128]{3,2,1,0:T(8,128)S(1)} %get-tuple-element.73.own_keys, bf16[256,256]{1,0:T(8,128)(2,1)S(1)} %copy-done.6, f32[1,128]{1,0:T(1,128)S(1)} %bitcast.7), custom_call_target="tpu_custom_call" | custom-call | flops 6000000000 | bytes 2000000 | tf_op jit(solution)/shard_map/turn/pallas_call | solution.py:395
  27.0 0.0 collective-permute-done.9.refs_7_
  27.0 0.0 collective-permute-done.8.refs_6_
  27.0 0.0 collective-permute-done.7.refs_5_
  27.0 0.0 collective-permute-done.10.refs_1_
  27.0 0.0 collective-permute-done.11.refs_3_
  27.0 0.1 add.1
  27.1 2.0 %collective-permute-start.12 = (bf16[400,128]{1,0:T(8,128)(2,1)S(1)}, bf16[400,128]{1,0:T(8,128)(2,1)S(1)}, u32[]{:S(2)}, u32[]{:S(2)}) collective-permute-start(bf16[400,128]{1,0:T(8,128)(2,1)S(1)} %get-tuple-element.86), channel_id=1, source_target_pairs={{0,24},{4,28},{8,16},{12,20},{16,8},{20,12},{24,0},{28,4},{1,25},{... | collective-permute-start | bytes 307208 | tf_op jit(solution)/shard_map/ppermute | solution.py:570
  29.1 0.0 collective-permute-start.13
  29.1 1.6 %collective-permute-start.14 = (bf16[400,128]{1,0:T(8,128)(2,1)S(1)}, bf16[400,128]{1,0:T(8,128)(2,1)S(1)}, u32[]{:S(2)}, u32[]{:S(2)}) collective-permute-start(bf16[400,128]{1,0:T(8,128)(2,1)S(1)} %get-tuple-element.88), channel_id=1, source_target_pairs={{0,8},{4,12},{8,0},{12,4},{16,24},{20,28},{24,16},{28,20},{1,9},{5... | collective-permute-start | bytes 307208 | tf_op jit(solution)/shard_map/ppermute | solution.py:570
  30.7 3.2 %post.1 = (bf16[256,2048]{1,0:T(8,128)(2,1)}, bf16[256,256]{1,0:T(8,128)(2,1)}) custom-call(s32[1]{0:T(128)S(6)} %copy.18.live_ref.refs_0_, s32[4]{0:T(128)S(1)} %copy-done.8, bf16[4,2,448,512]{3,2,1,0:T(8,128)(2,1)S(1)} %get-tuple-element.89.ds_ref, bf16[768,256]{1,0:T(8,128)(2,1)S(1)} %get-tuple-element.90.pool_keys, ...), custom_call_target="tpu_custom_call" | custom-call | flops 3000000000 | bytes 4000000 | tf_op jit(solution)/shard_map/post/pallas_call | solution.py:448
  33.8 0.0 collective-permute-done.12.refs_1_
  33.8 1.5 %collective-permute-done.13.refs_2_ = bf16[400,128]{1,0:T(8,128)(2,1)S(1)} collective-permute-done((bf16[400,128]{1,0:T(8,128)(2,1)S(1)}, bf16[400,128]{1,0:T(8,128)(2,1)S(1)}, u32[]{:S(2)}, u32[]{:S(2)}) %collective-permute-start.13) | collective-permute-done | bytes 102432 | tf_op jit(solution)/shard_map/ppermute | solution.py:570
  35.3 0.0 collective-permute-done.14.refs_3_
  35.3 0.1 collective-permute-start.15
  35.4 0.8 %finish.1 = (f32[96,256]{1,0:T(8,128)}, f32[96,256]{1,0:T(8,128)}) custom-call(f32[400,128]{1,0:T(8,128)S(1)} %get-tuple-element.100.refs_0_, bf16[400,128]{1,0:T(8,128)(2,1)S(1)} %collective-permute-done.12.refs_1_, bf16[400,128]{1,0:T(8,128)(2,1)S(1)} %collective-permute-done.13.refs_2_, bf16[400,128]{1,0:T(8,128)(2,1)S(1)} %collective-permute-done.14.refs_3_, ...), custom_call_target="tpu_custom_call" | custom-call | flops 100000000 | bytes 1000000 | tf_op jit(solution)/shard_map/finish/pallas_call | solution.py:558
  36.2 0.3 collective-permute-done.15.refs_1_
  36.6 0.5 %gain_grads.1 = (f32[1,128]{1,0:T(1,128)}, f32[1,128]{1,0:T(1,128)}) custom-call(f32[8,128]{1,0:T(8,128)S(1)} %sum_chips.1.refs_0_, f32[8,128]{1,0:T(8,128)S(1)} %collective-permute-done.15.refs_1_, f32[1,128]{1,0:T(1,128)S(1)} %bitcast.11, f32[1,128]{1,0:T(1,128)S(1)} %bitcast.9), custom_call_target="tpu_custom_call" | custom-call | tf_op jit(solution)/shard_map/gain_grads/pallas_call | solution.py:528
  (2 shorter events, 0.0 us)
Async XLA Ops:
  0.6 0.8 %copy-start = (bf16[96,256]{1,0:T(8,128)(2,1)S(1)}, bf16[96,256]{1,0:T(8,128)(2,1)}, u32[]{:S(2)}) copy-start(bf16[96,256]{1,0:T(8,128)(2,1)} %refs_4_.1) | copy-start | bytes 147460
  0.6 0.8 %copy-start.1 = (f32[128]{0:T(128)S(1)}, f32[128]{0:T(128)}, u32[]{:S(2)}) copy-start(f32[128]{0:T(128)} %param.16) | copy-start | bytes 1540
  0.7 0.8 %copy-start.7 = (bf16[96,256]{1,0:T(8,128)(2,1)S(1)}, bf16[96,256]{1,0:T(8,128)(2,1)}, u32[]{:S(2)}) copy-start(bf16[96,256]{1,0:T(8,128)(2,1)} %values_ref) | copy-start | bytes 147460
  1.5 5.4 %copy-start.2 = (f32[128]{0:T(128)S(1)}, f32[128]{0:T(128)}, u32[]{:S(2)}) copy-start(f32[128]{0:T(128)} %param.15) | copy-start | bytes 1540
  1.5 5.4 %copy-start.3 = (bf16[256,2048]{1,0:T(8,128)(2,1)S(1)}, bf16[256,2048]{1,0:T(8,128)(2,1)}, u32[]{:S(2)}) copy-start(bf16[256,2048]{1,0:T(8,128)(2,1)} %q_ref.1) | copy-start | bytes 3145732
  1.5 5.4 %copy-start.4 = (bf16[256,2048]{1,0:T(8,128)(2,1)S(1)}, bf16[256,2048]{1,0:T(8,128)(2,1)}, u32[]{:S(2)}) copy-start(bf16[256,2048]{1,0:T(8,128)(2,1)} %do_ref.1) | copy-start | bytes 3145732
  1.6 7.1 %collective-permute-start.3 = (bf16[96,512]{1,0:T(8,128)(2,1)S(1)}, bf16[96,512]{1,0:T(8,128)(2,1)S(1)}, u32[]{:S(2)}, u32[]{:S(2)}) collective-permute-start(bf16[96,512]{1,0:T(8,128)(2,1)S(1)} %pack.1.refs_9_), channel_id=1, source_target_pairs={{0,24},{4,28},{8,16},{12,20},{16,8},{20,12},{24,0},{28,4},{1,25},{... | collective-permute-start | bytes 294920 | tf_op jit(solution)/shard_map/ppermute | solution.py:570
  5.6 4.9 %collective-permute-start.2 = (bf16[96,512]{1,0:T(8,128)(2,1)S(1)}, bf16[96,512]{1,0:T(8,128)(2,1)S(1)}, u32[]{:S(2)}, u32[]{:S(2)}) collective-permute-start(bf16[96,512]{1,0:T(8,128)(2,1)S(1)} %pack.1.refs_9_), channel_id=1, source_target_pairs={{0,16},{4,20},{8,24},{12,28},{16,0},{20,4},{24,8},{28,12},{1,17},{... | collective-permute-start | bytes 294920 | tf_op jit(solution)/shard_map/ppermute | solution.py:570
  6.1 4.7 %collective-permute-start.1 = (bf16[96,512]{1,0:T(8,128)(2,1)S(1)}, bf16[96,512]{1,0:T(8,128)(2,1)S(1)}, u32[]{:S(2)}, u32[]{:S(2)}) collective-permute-start(bf16[96,512]{1,0:T(8,128)(2,1)S(1)} %pack.1.refs_9_), channel_id=1, source_target_pairs={{0,8},{4,12},{8,0},{12,4},{16,24},{20,28},{24,16},{28,20},{1,9},{5... | collective-permute-start | bytes 294920 | tf_op jit(solution)/shard_map/ppermute | solution.py:570
  6.9 5.2 %copy-start.5 = (bf16[256,256]{1,0:T(8,128)(2,1)S(1)}, bf16[256,256]{1,0:T(8,128)(2,1)}, u32[]{:S(2)}) copy-start(bf16[256,256]{1,0:T(8,128)(2,1)} %refs_6_.1) | copy-start | bytes 393220
  6.9 5.2 %copy-start.6 = (bf16[256,256]{1,0:T(8,128)(2,1)S(1)}, bf16[256,256]{1,0:T(8,128)(2,1)}, u32[]{:S(2)}) copy-start(bf16[256,256]{1,0:T(8,128)(2,1)} %ck_ref.1) | copy-start | bytes 393220
  6.9 5.2 %copy-start.8 = (s32[4]{0:T(128)S(1)}, s32[4]{0:T(128)}, u32[]{:S(2)}) copy-start(s32[4]{0:T(128)} %prompt_ref.3) | copy-start | bytes 52
  8.7 2.0 %collective-permute-start.4 = (bf16[96,512]{1,0:T(8,128)(2,1)S(1)}, bf16[96,512]{1,0:T(8,128)(2,1)S(1)}, u32[]{:S(2)}, u32[]{:S(2)}) collective-permute-start(bf16[96,512]{1,0:T(8,128)(2,1)S(1)} %collective-permute-done.3.refs_15_), channel_id=1, source_target_pairs={{0,4},{4,0},{8,12},{12,8},{16,20},{20,16},{24,28},{28,24},{1,5},{5... | collective-permute-start | bytes 294920 | tf_op jit(solution)/shard_map/ppermute | solution.py:570
  8.8 2.2 %collective-permute-start = (bf16[96,512]{1,0:T(8,128)(2,1)S(1)}, bf16[96,512]{1,0:T(8,128)(2,1)S(1)}, u32[]{:S(2)}, u32[]{:S(2)}) collective-permute-start(bf16[96,512]{1,0:T(8,128)(2,1)S(1)} %pack.1.refs_9_), channel_id=1, source_target_pairs={{0,4},{4,0},{8,12},{12,8},{16,20},{20,16},{24,28},{28,24},{1,5},{5... | collective-permute-start | bytes 294920 | tf_op jit(solution)/shard_map/ppermute | solution.py:570
  10.5 1.3 %collective-permute-start.6 = (bf16[96,512]{1,0:T(8,128)(2,1)S(1)}, bf16[96,512]{1,0:T(8,128)(2,1)S(1)}, u32[]{:S(2)}, u32[]{:S(2)}) collective-permute-start(bf16[96,512]{1,0:T(8,128)(2,1)S(1)} %collective-permute-done.2.refs_13_), channel_id=1, source_target_pairs={{0,4},{4,0},{8,12},{12,8},{16,20},{20,16},{24,28},{28,24},{1,5},{5... | collective-permute-start | bytes 294920 | tf_op jit(solution)/shard_map/ppermute | solution.py:570
  10.8 1.3 %collective-permute-start.5 = (bf16[96,512]{1,0:T(8,128)(2,1)S(1)}, bf16[96,512]{1,0:T(8,128)(2,1)S(1)}, u32[]{:S(2)}, u32[]{:S(2)}) collective-permute-start(bf16[96,512]{1,0:T(8,128)(2,1)S(1)} %collective-permute-done.1.refs_11_), channel_id=1, source_target_pairs={{0,4},{4,0},{8,12},{12,8},{16,20},{20,16},{24,28},{28,24},{1,5},{5... | collective-permute-start | bytes 294920 | tf_op jit(solution)/shard_map/ppermute | solution.py:570
  18.7 8.3 %collective-permute-start.9 = (f32[8,128]{1,0:T(8,128)S(1)}, f32[8,128]{1,0:T(8,128)S(1)}, u32[]{:S(2)}, u32[]{:S(2)}) collective-permute-start(f32[8,128]{1,0:T(8,128)S(1)} %get-tuple-element.82.refs_4_), channel_id=1, source_target_pairs={{0,3},{1,2},{2,1},{3,0},{4,7},{5,6},{6,5},{7,4},{8,11},{9,10},{10,... | collective-permute-start | bytes 12296 | tf_op jit(solution)/shard_map/ppermute | solution.py:570
  22.5 4.5 %collective-permute-start.8 = (f32[8,128]{1,0:T(8,128)S(1)}, f32[8,128]{1,0:T(8,128)S(1)}, u32[]{:S(2)}, u32[]{:S(2)}) collective-permute-start(f32[8,128]{1,0:T(8,128)S(1)} %get-tuple-element.82.refs_4_), channel_id=1, source_target_pairs={{0,2},{1,3},{2,0},{3,1},{4,6},{5,7},{6,4},{7,5},{8,10},{9,11},{10,... | collective-permute-start | bytes 12296 | tf_op jit(solution)/shard_map/ppermute | solution.py:570
  22.5 4.5 %collective-permute-start.7 = (f32[8,128]{1,0:T(8,128)S(1)}, f32[8,128]{1,0:T(8,128)S(1)}, u32[]{:S(2)}, u32[]{:S(2)}) collective-permute-start(f32[8,128]{1,0:T(8,128)S(1)} %get-tuple-element.82.refs_4_), channel_id=1, source_target_pairs={{0,1},{1,0},{2,3},{3,2},{4,5},{5,4},{6,7},{7,6},{8,9},{9,8},{10,11... | collective-permute-start | bytes 12296 | tf_op jit(solution)/shard_map/ppermute | solution.py:570
  23.2 3.8 %collective-permute-start.10 = (bf16[384,256]{1,0:T(8,128)(2,1)S(1)}, bf16[384,256]{1,0:T(8,128)(2,1)S(1)}, u32[]{:S(2)}, u32[]{:S(2)}) collective-permute-start(bf16[384,256]{1,0:T(8,128)(2,1)S(1)} %get-tuple-element.77), channel_id=1, source_target_pairs={{0,4},{4,0},{8,12},{12,8},{16,20},{20,16},{24,28},{28,24},{1,5},{5... | collective-permute-start | bytes 589832 | tf_op jit(solution)/shard_map/ppermute | solution.py:570
  25.4 1.6 %collective-permute-start.11 = (bf16[384,256]{1,0:T(8,128)(2,1)S(1)}, bf16[384,256]{1,0:T(8,128)(2,1)S(1)}, u32[]{:S(2)}, u32[]{:S(2)}) collective-permute-start(bf16[384,256]{1,0:T(8,128)(2,1)S(1)} %get-tuple-element.81), channel_id=1, source_target_pairs={{0,4},{4,0},{8,12},{12,8},{16,20},{20,16},{24,28},{28,24},{1,5},{5... | collective-permute-start | bytes 589832 | tf_op jit(solution)/shard_map/ppermute | solution.py:570
  27.1 6.7 %collective-permute-start.12 = (bf16[400,128]{1,0:T(8,128)(2,1)S(1)}, bf16[400,128]{1,0:T(8,128)(2,1)S(1)}, u32[]{:S(2)}, u32[]{:S(2)}) collective-permute-start(bf16[400,128]{1,0:T(8,128)(2,1)S(1)} %get-tuple-element.86), channel_id=1, source_target_pairs={{0,24},{4,28},{8,16},{12,20},{16,8},{20,12},{24,0},{28,4},{1,25},{... | collective-permute-start | bytes 307208 | tf_op jit(solution)/shard_map/ppermute | solution.py:570
  29.1 6.2 %collective-permute-start.13 = (bf16[400,128]{1,0:T(8,128)(2,1)S(1)}, bf16[400,128]{1,0:T(8,128)(2,1)S(1)}, u32[]{:S(2)}, u32[]{:S(2)}) collective-permute-start(bf16[400,128]{1,0:T(8,128)(2,1)S(1)} %get-tuple-element.87), channel_id=1, source_target_pairs={{0,16},{4,20},{8,24},{12,28},{16,0},{20,4},{24,8},{28,12},{1,17},{... | collective-permute-start | bytes 307208 | tf_op jit(solution)/shard_map/ppermute | solution.py:570
  29.1 6.2 %collective-permute-start.14 = (bf16[400,128]{1,0:T(8,128)(2,1)S(1)}, bf16[400,128]{1,0:T(8,128)(2,1)S(1)}, u32[]{:S(2)}, u32[]{:S(2)}) collective-permute-start(bf16[400,128]{1,0:T(8,128)(2,1)S(1)} %get-tuple-element.88), channel_id=1, source_target_pairs={{0,8},{4,12},{8,0},{12,4},{16,24},{20,28},{24,16},{28,20},{1,9},{5... | collective-permute-start | bytes 307208 | tf_op jit(solution)/shard_map/ppermute | solution.py:570
  35.3 1.2 %collective-permute-start.15 = (f32[8,128]{1,0:T(8,128)S(1)}, f32[8,128]{1,0:T(8,128)S(1)}, u32[]{:S(2)}, u32[]{:S(2)}) collective-permute-start(f32[8,128]{1,0:T(8,128)S(1)} %sum_chips.1.refs_0_), channel_id=1, source_target_pairs={{0,4},{4,0},{8,12},{12,8},{16,20},{20,16},{24,28},{28,24},{1,5},{5... | collective-permute-start | bytes 12296 | tf_op jit(solution)/shard_map/ppermute | solution.py:570
